TPU v7x, 128 devices: a whole 4x4x4 slice. The times are simulated.
128 devices in a mesh: group: 4 (over x), local: 32 (over z, y, core).
Axes of the slice: x: 4, y: 4, z: 4, core: 2. Of those that a mesh axis runs over, the one named last changes fastest.
Arguments:
- x_q: bfloat16 [2048, 4096], P(('group', 'local')), may hold values from -6 to 6
- x_scale: float32 [2048, 32], P(('group', 'local')), may hold values from 0.25 to 4, as said below
- cotangent: bfloat16 [2048, 4096], P(('group', 'local')), may hold values from -6 to 6
- gates: bfloat16 [2048, 8], P(('group', 'local')), may hold values from 0.049804688 to 0.5
- experts: int32 [2048, 8], P(('group', 'local')), may hold values from 0 to 63, as said below
- replicas: int32 [2048, 8], P(('group', 'local')), may hold values from 0 to 1, as said below
- slots: int32 [2048, 8], P(('group', 'local')), may hold values from 0 to 255, as said below
- w_gate_q: bfloat16 [8192, 32, 768], P('group', 'local'), may hold values from -0.09375 to 0.09375
- w_up_q: bfloat16 [8192, 32, 768], P('group', 'local'), may hold values from -0.09375 to 0.09375
- w_down_q: bfloat16 [8192, 32, 768], P('group', 'local'), may hold values from -0.21875 to 0.21875
- gate_scales: float32 [64, 32, 6], P('group', 'local'), may hold values from 0.5 to 2, as said below
- up_scales: float32 [64, 32, 6], P('group', 'local'), may hold values from 0.5 to 2, as said below
- down_scales: float32 [64, 32, 6], P('group', 'local'), may hold values from 0.5 to 2, as said below
Outputs:
- grad_tokens: bfloat16 [2048, 4096], P(('group', 'local'))
- grad_gates: bfloat16 [2048, 8], P(('group', 'local'))
- grad_gate: bfloat16 [8192, 32, 768], P('group', 'local')
- grad_up: bfloat16 [8192, 32, 768], P('group', 'local')
- grad_down: bfloat16 [8192, 32, 768], P('group', 'local')
Inputs may be any that keep to these rules, and one draw needn't show every extreme that they name: Each token names 8 distinct experts; no expert is named more than 2 * 2 times by the tokens of one device (aligned blocks of 16 tokens). `replicas`: the copies of the tokens of one device reach one replica device at most 2 times; in every block some replica device receives exactly 2. `slots`: the slot of a copy is the number of earlier copies, in token order and then choice order, that go to the same replica device. `x_scale`: every entry is a power of two. `gate_scales`: every entry is a power of two. `up_scales`: every entry is a power of two. `down_scales`: every entry is a power of two.
All inputs are finite; a program needn't handle non-finite values.
Results may differ from a plain program's by a relative error of at most 0.0075.
Values may be sent and summed in bfloat16 or wider, within the bound.
No kernel may reach another device: no remote copies, remote signals or barrier semaphores. Data moves between devices by JAX's collectives and lax.ppermute only.
A program may use at most 128 MiB of HBM per device.

v0:
```python
import jax
import jax.numpy as jnp
from jax import lax
from jax.sharding import PartitionSpec as P

CAP = 192


def partner(block, axis, apart):
    count = lax.axis_size(axis)
    route = []
    for low in range(count):
        high = low | 1 << apart
        if high != low and high < count:
            route += [(low, high), (high, low)]
    return lax.ppermute(block, axis, route)


def contract_rows(left, right):
    return lax.dot_general(
        left, right, (((0,), (0,)), ((), ())), preferred_element_type=jnp.float32
    )


def contract_last(left, right):
    return lax.dot_general(
        left, right, (((1,), (1,)), ((), ())), preferred_element_type=jnp.float32
    )


def expert_backward(rows_x, rows_dy, rows_gate, w_gate, w_up, w_down):
    act_a = jnp.dot(rows_x, w_gate, preferred_element_type=jnp.float32)
    act_b = jnp.dot(rows_x, w_up, preferred_element_type=jnp.float32)
    sigma = jax.nn.sigmoid(act_a)
    silu_a = act_a * sigma
    hidden = (silu_a * act_b).astype(jnp.bfloat16)
    output = contract_last(hidden, w_down)
    grad_gate_rows = jnp.sum(rows_dy.astype(jnp.float32) * output, axis=1).astype(jnp.bfloat16)
    scaled = (rows_gate.astype(jnp.float32)[:, None] * rows_dy.astype(jnp.float32)).astype(
        jnp.bfloat16
    )
    d_hidden = jnp.dot(scaled, w_down, preferred_element_type=jnp.float32)
    d_gate_act = (d_hidden * act_b * sigma * (1.0 + act_a * (1.0 - sigma))).astype(jnp.bfloat16)
    d_up_act = (d_hidden * silu_a).astype(jnp.bfloat16)
    grad_rows = (contract_last(d_gate_act, w_gate) + contract_last(d_up_act, w_up)).astype(
        jnp.bfloat16
    )
    term_gate = contract_rows(rows_x, d_gate_act).astype(jnp.bfloat16)
    term_up = contract_rows(rows_x, d_up_act).astype(jnp.bfloat16)
    term_down = contract_rows(scaled, hidden).astype(jnp.bfloat16)
    return (grad_rows, grad_gate_rows, term_gate, term_up, term_down)


def dequant_half(quant, scales):
    scale = jnp.repeat(jnp.repeat(scales[:, 0, :], 128, axis=0), 128, axis=1)
    return (quant[:, 0, :].astype(jnp.float32) * scale).astype(jnp.bfloat16)


def shards(
    x_q,
    x_scale,
    cotangent,
    gates,
    experts,
    replicas,
    slots,
    w_gate_q,
    w_up_q,
    w_down_q,
    gate_scales,
    up_scales,
    down_scales,
):
    n_group = lax.axis_size("group")
    n_local = lax.axis_size("local")
    n_dev = n_group * n_local
    tok_count, width = x_q.shape
    top_count = experts.shape[1]
    copies = tok_count * top_count
    per_pair = copies * 2 // n_dev
    arrivals = n_dev * per_pair
    tokens = (x_q.astype(jnp.float32) * jnp.repeat(x_scale, 128, axis=1)).astype(jnp.bfloat16)
    expert_flat = experts.reshape(-1)
    replica_flat = replicas.reshape(-1)
    slot_flat = slots.reshape(-1)
    gate_flat = gates.reshape(-1)
    target = (2 * (expert_flat // n_local) + replica_flat) * n_local + expert_flat % n_local
    onehot = (target[:, None] == jnp.arange(n_dev, dtype=jnp.int32)[None, :]).astype(jnp.int32)
    earlier = jnp.cumsum(onehot, axis=0) - onehot
    position = jnp.sum(earlier * onehot, axis=1)
    source_rows = jnp.arange(copies, dtype=jnp.int32) // top_count
    copy_x = tokens[source_rows]
    copy_dy = cotangent[source_rows]
    send_index = target * per_pair + position
    send_x = jnp.zeros((arrivals, width), jnp.bfloat16).at[send_index].set(copy_x)
    send_dy = jnp.zeros((arrivals, width), jnp.bfloat16).at[send_index].set(copy_dy)
    send_gate = jnp.zeros((arrivals,), jnp.bfloat16).at[send_index].set(gate_flat)
    send_slot = jnp.full((arrivals,), -1, jnp.int32).at[send_index].set(slot_flat)
    pack_x = send_x.reshape(n_dev, per_pair, width)
    pack_dy = send_dy.reshape(n_dev, per_pair, width)
    pack_gate = send_gate.reshape(n_dev, per_pair)
    pack_slot = send_slot.reshape(n_dev, per_pair)
    received = (
        lax.all_to_all(pack_x, ("group", "local"), split_axis=0, concat_axis=0, tiled=True),
        lax.all_to_all(pack_dy, ("group", "local"), split_axis=0, concat_axis=0, tiled=True),
        lax.all_to_all(pack_gate, ("group", "local"), split_axis=0, concat_axis=0, tiled=True),
        lax.all_to_all(pack_slot, ("group", "local"), split_axis=0, concat_axis=0, tiled=True),
    )
    recv_x = received[0].reshape(arrivals, width)
    recv_dy = received[1].reshape(arrivals, width)
    recv_gate = received[2].reshape(arrivals)
    recv_slot = received[3].reshape(arrivals)
    live = (recv_slot >= 0) & (recv_slot < CAP)
    half_index = lax.axis_index("group") % 2
    w_gate = dequant_half(w_gate_q, gate_scales)
    w_up = dequant_half(w_up_q, up_scales)
    w_down = dequant_half(w_down_q, down_scales)
    half_width = w_gate.shape[0]

    def ordered(mine, theirs, axis):
        return jnp.where(
            half_index == 0,
            jnp.concatenate([mine, theirs], axis),
            jnp.concatenate([theirs, mine], axis),
        )

    place = jnp.where(live, recv_slot, CAP)
    rows_x = jnp.zeros((CAP, width), jnp.bfloat16).at[place].set(recv_x, mode="drop")
    rows_dy = jnp.zeros((CAP, width), jnp.bfloat16).at[place].set(recv_dy, mode="drop")
    rows_gate = jnp.zeros((CAP,), jnp.bfloat16).at[place].set(recv_gate, mode="drop")
    peer_gate_w, peer_up_w, peer_down_w = partner((w_gate, w_up, w_down), "group", 0)
    out_dx, out_gate, term_gate, term_up, term_down = expert_backward(
        rows_x,
        rows_dy,
        rows_gate,
        ordered(w_gate, peer_gate_w, 0),
        ordered(w_up, peer_up_w, 0),
        ordered(w_down, peer_down_w, 0),
    )
    keep_start = half_index * half_width
    give_start = (1 - half_index) * half_width
    given = partner(
        (
            lax.dynamic_slice_in_dim(term_gate, give_start, half_width, 0),
            lax.dynamic_slice_in_dim(term_up, give_start, half_width, 0),
            lax.dynamic_slice_in_dim(term_down, give_start, half_width, 0),
        ),
        "group",
        0,
    )
    terms = (term_gate, term_up, term_down)
    grads = [
        (
            lax.dynamic_slice_in_dim(term, keep_start, half_width, 0).astype(jnp.float32)
            + other.astype(jnp.float32)
        ).astype(jnp.bfloat16)
        for term, other in zip(terms, given)
    ]
    pick = jnp.where(live, recv_slot, 0)
    back_x = jnp.where(live[:, None], out_dx[pick], jnp.zeros((arrivals, width), jnp.bfloat16))
    back_gate = jnp.where(live, out_gate[pick], jnp.zeros((arrivals,), jnp.bfloat16))
    ret_x = back_x.reshape(n_dev, per_pair, width)
    ret_gate = back_gate.reshape(n_dev, per_pair)
    returned = (
        lax.all_to_all(ret_x, ("group", "local"), split_axis=0, concat_axis=0, tiled=True),
        lax.all_to_all(ret_gate, ("group", "local"), split_axis=0, concat_axis=0, tiled=True),
    )
    flat_dx = returned[0].reshape(arrivals, width)
    flat_gate = returned[1].reshape(arrivals)
    copy_dx = flat_dx[send_index]
    copy_gate = flat_gate[send_index]
    grad_tokens = (
        copy_dx.reshape(tok_count, top_count, width)
        .astype(jnp.float32)
        .sum(axis=1)
        .astype(jnp.bfloat16)
    )
    grad_gates = copy_gate.reshape(tok_count, top_count)
    return (
        grad_tokens,
        grad_gates,
        grads[0][:, None, :],
        grads[1][:, None, :],
        grads[2][:, None, :],
    )


def solution(mesh):
    in_specs = (
        P(("group", "local"), None),
        P(("group", "local"), None),
        P(("group", "local"), None),
        P(("group", "local"), None),
        P(("group", "local"), None),
        P(("group", "local"), None),
        P(("group", "local"), None),
        P("group", "local", None),
        P("group", "local", None),
        P("group", "local", None),
        P("group", "local", None),
        P("group", "local", None),
        P("group", "local", None),
    )
    out_specs = (
        P(("group", "local"), None),
        P(("group", "local"), None),
        P("group", "local", None),
        P("group", "local", None),
        P("group", "local", None),
    )
    return jax.shard_map(shards, mesh=mesh, in_specs=in_specs, out_specs=out_specs, check_vma=False)
```

profile of v0, /device:TPU:0, one launch (start us, length us, event | category | flops | bytes accessed | tf_op | source)
XLA Modules:
  0.0 595.4 jit_solution(4691830912392451655)
XLA Ops:
  6.1 11.1 %all-to-all-start.1 = ((bf16[128,1,2]{2,1,0:T(2,128)(2,1)}), bf16[128,1,2]{2,1,0:T(2,128)(2,1)S(1)}, u32[]{:S(2)}, u32[]{:S(2)}) async-start(bf16[128,1,2]{2,1,0:T(2,128)(2,1)} %all_to_all.33), calls=%async_computation.1 | async-start | bytes 131072 | tf_op jit(solution)/shard_map/all_to_all | solution.py:106
  21.7 4.7 all-to-all-done.1
  26.5 5.0 all-to-all-start
  31.5 5.8 scatter_custom_fusion.5
  40.7 9.5 %all-to-all-start.3 = ((bf16[128,2,4096]{2,1,0:T(2,128)(2,1)}), bf16[128,2,4096]{2,1,0:T(2,128)(2,1)}, u32[]{:S(2)}, u32[]{:S(2)}) async-start(bf16[128,2,4096]{2,1,0:T(2,128)(2,1)} %reshape.391), calls=%async_computation.3 | async-start | bytes 4194304 | tf_op jit(solution)/shard_map/all_to_all | solution.py:104
  64.3 5.8 scatter_custom_fusion.3
  72.7 7.9 %all-to-all-done.3 = bf16[128,2,4096]{2,1,0:T(2,128)(2,1)} async-done(((bf16[128,2,4096]{2,1,0:T(2,128)(2,1)}), bf16[128,2,4096]{2,1,0:T(2,128)(2,1)}, u32[]{:S(2)}, u32[]{:S(2)}) %all-to-all-start.3) | async-done | bytes 2097184 | tf_op jit(solution)/shard_map/all_to_all | solution.py:104
  80.7 5.8 all-to-all-start.2
  101.3 4.9 scatter_custom_fusion.6
  106.2 131.8 %all-to-all-done.2 = bf16[128,2,4096]{2,1,0:T(2,128)(2,1)} async-done(((bf16[128,2,4096]{2,1,0:T(2,128)(2,1)}), bf16[128,2,4096]{2,1,0:T(2,128)(2,1)}, u32[]{:S(2)}, u32[]{:S(2)}) %all-to-all-start.2) | async-done | bytes 2097184 | tf_op jit(solution)/shard_map/all_to_all | solution.py:105
  242.1 5.1 scatter_custom_fusion.4
  247.2 7.3 %fusion.9 = f32[192,768]{1,0:T(8,128)S(1)} fusion(bf16[192,4096]{1,0:T(8,128)(2,1)S(1)} %scatter_custom_fusion.6, bf16[2048,768]{0,1:T(8,128)(2,1)} %collective-permute-done.2, bf16[2048,768]{0,1:T(8,128)(2,1)} %fusion, pred[]{:T(512)S(6)} %eq.25), kind=kOutput, calls=%fused_computation.38 | convolution fusion | flops 1236271104 | bytes 8454145 | tf_op jit(solution)/shard_map/dot_general | solution.py:32
  254.5 7.4 %fusion.12 = f32[192,768]{1,0:T(8,128)S(1)} fusion(bf16[2048,768]{0,1:T(8,128)(2,1)} %collective-permute-done, bf16[2048,768]{0,1:T(8,128)(2,1)} %fusion.2, pred[]{:T(512)S(6)} %eq.25, bf16[192,4096]{1,0:T(8,128)(2,1)S(1)} %scatter_custom_fusion.4, f32[192]{0:T(256)S(1)} %convert_element_type.100), kind=kOutput, calls=%fused_computation.41 | convolution fusion | flops 1238630400 | bytes 8454913 | tf_op jit(solution)/shard_map/dot_general | solution.py:42
  261.9 36.4 %collective-permute-done.1 = bf16[2048,768]{0,1:T(8,128)(2,1)} collective-permute-done((bf16[2048,768]{0,1:T(8,128)(2,1)}, bf16[2048,768]{0,1:T(8,128)(2,1)}, u32[]{:S(2)}, u32[]{:S(2)}) %collective-permute-start.1) | collective-permute-done | bytes 3145760 | tf_op jit(solution)/shard_map/ppermute | solution.py:16
  298.3 8.0 %multiply_convert_fusion = (bf16[192,768]{1,0:T(8,128)(2,1)}, bf16[192,768]{1,0:T(8,128)(2,1)S(1)}, bf16[192,768]{1,0:T(8,128)(2,1)S(1)}) fusion(f32[192,768]{1,0:T(8,128)S(1)} %fusion.9, f32[192,768]{1,0:T(8,128)S(1)} %fusion.12, bf16[192,4096]{1,0:T(8,128)(2,1)S(1)} %scatter_custom_fusion.6, bf16[2048,768]{0,1:T(8,128)(2,1)} %collective-permute-done.1, ...), kind=kOutput, calls=%fused_computation.53 | convolution fusion | flops 1238482944 | bytes 9928705 | tf_op jit(solution)/shard_map/dot_general | solution.py:33
  315.3 7.7 %fusion.10 = f32[192,4096]{1,0:T(8,128)S(1)} fusion(bf16[192,768]{1,0:T(8,128)(2,1)S(1)} %get-tuple-element.24, bf16[2048,768]{0,1:T(8,128)(2,1)} %collective-permute-done.1, bf16[2048,768]{0,1:T(8,128)(2,1)} %fusion.1, pred[]{:T(512)S(6)} %eq.25), kind=kOutput, calls=%fused_computation.39 | convolution fusion | flops 1236271104 | bytes 9732097 | tf_op jit(solution)/shard_map/dot_general | solution.py:26
  323.0 7.9 %fusion.3 = bf16[192,4096]{1,0:T(8,128)(2,1)S(1)} fusion(f32[192,4096]{1,0:T(8,128)S(1)} %fusion.10, bf16[192,768]{1,0:T(8,128)(2,1)S(1)} %get-tuple-element.23, bf16[2048,768]{0,1:T(8,128)(2,1)} %collective-permute-done.2, bf16[2048,768]{0,1:T(8,128)(2,1)} %fusion, pred[]{:T(512)S(6)} %eq.25), kind=kOutput, calls=%fused_computation.30 | convolution fusion | flops 1237843968 | bytes 11304961 | tf_op jit(solution)/shard_map/dot_general | solution.py:26
  338.5 8.1 %fusion.8 = bf16[192]{0:T(256)(128)(2,1)S(1)} fusion(bf16[192,768]{1,0:T(8,128)(2,1)S(1)} %copy-done.4, bf16[192,4096]{1,0:T(8,128)(2,1)S(1)} %scatter_custom_fusion.4, bf16[2048,768]{0,1:T(8,128)(2,1)} %collective-permute-done, bf16[2048,768]{0,1:T(8,128)(2,1)} %fusion.2, pred[]{:T(512)S(6)} %eq.25), kind=kOutput, calls=%fused_computation.37 | convolution fusion | flops 1238630144 | bytes 8159617 | tf_op jit(solution)/shard_map/dot_general | solution.py:26
  349.6 10.0 %all-to-all-start.5 = ((bf16[128,1,2]{2,1,0:T(2,128)(2,1)}), bf16[128,1,2]{2,1,0:T(2,128)(2,1)S(1)}, u32[]{:S(2)}, u32[]{:S(2)}) async-start(bf16[128,1,2]{2,1,0:T(2,128)(2,1)} %copy.51), calls=%async_computation.5 | async-start | bytes 131072 | tf_op jit(solution)/shard_map/all_to_all | solution.py:166
  372.4 10.3 %all-to-all-start.4 = ((bf16[128,2,4096]{2,1,0:T(2,128)(2,1)}), bf16[128,2,4096]{2,1,0:T(2,128)(2,1)}, u32[]{:S(2)}, u32[]{:S(2)}) async-start(bf16[128,2,4096]{2,1,0:T(2,128)(2,1)} %broadcast_select_fusion), calls=%async_computation.4 | async-start | bytes 4194304 | tf_op jit(solution)/shard_map/all_to_all | solution.py:165
  391.9 139.3 %all-to-all-done.4 = bf16[128,2,4096]{2,1,0:T(2,128)(2,1)} async-done(((bf16[128,2,4096]{2,1,0:T(2,128)(2,1)}), bf16[128,2,4096]{2,1,0:T(2,128)(2,1)}, u32[]{:S(2)}, u32[]{:S(2)}) %all-to-all-start.4) | async-done | bytes 2097184 | tf_op jit(solution)/shard_map/all_to_all | solution.py:165
  536.6 5.4 fusion.5
  542.0 5.4 fusion.6
  547.5 43.0 %collective-permute-done.5 = bf16[2048,768]{1,0:T(8,128)(2,1)} collective-permute-done((bf16[2048,768]{1,0:T(8,128)(2,1)}, bf16[2048,768]{1,0:T(8,128)(2,1)}, u32[]{:S(2)}, u32[]{:S(2)}) %collective-permute-start.5) | collective-permute-done | bytes 3145760 | tf_op jit(solution)/shard_map/ppermute | solution.py:16
  (106 shorter events, 100.3 us)
Async XLA Ops:
  0.6 63.7 %copy-start = (bf16[16,4096]{1,0:T(8,128)(2,1)S(1)}, bf16[16,4096]{1,0:T(8,128)(2,1)}, u32[]{:S(2)}) copy-start(bf16[16,4096]{1,0:T(8,128)(2,1)} %param.15) | copy-start | bytes 393220
  6.1 20.4 %all-to-all-start.1 = ((bf16[128,1,2]{2,1,0:T(2,128)(2,1)}), bf16[128,1,2]{2,1,0:T(2,128)(2,1)S(1)}, u32[]{:S(2)}, u32[]{:S(2)}) async-start(bf16[128,1,2]{2,1,0:T(2,128)(2,1)} %all_to_all.33), calls=%async_computation.1 | async-start | bytes 131072 | tf_op jit(solution)/shard_map/all_to_all | solution.py:106
  26.5 14.3 %all-to-all-start = ((s32[128,1,2]{2,1,0:T(1,128)}), s32[128,1,2]{2,1,0:T(1,128)S(1)}, u32[]{:S(2)}, u32[]{:S(2)}) async-start(s32[128,1,2]{2,1,0:T(1,128)} %bitcast.2), calls=%async_computation | async-start | bytes 131072 | tf_op jit(solution)/shard_map/all_to_all | solution.py:107
  40.7 39.9 %all-to-all-start.3 = ((bf16[128,2,4096]{2,1,0:T(2,128)(2,1)}), bf16[128,2,4096]{2,1,0:T(2,128)(2,1)}, u32[]{:S(2)}, u32[]{:S(2)}) async-start(bf16[128,2,4096]{2,1,0:T(2,128)(2,1)} %reshape.391), calls=%async_computation.3 | async-start | bytes 4194304 | tf_op jit(solution)/shard_map/all_to_all | solution.py:104
  50.2 3.2 copy-start.5
  56.0 4.6 copy-start.6
  56.0 191.2 %collective-permute-start.2 = (bf16[2048,768]{0,1:T(8,128)(2,1)}, bf16[2048,768]{0,1:T(8,128)(2,1)}, u32[]{:S(2)}, u32[]{:S(2)}) collective-permute-start(bf16[2048,768]{0,1:T(8,128)(2,1)} %fusion), channel_id=1, source_target_pairs={{0,32},{32,0},{64,96},{96,64},{1,33},{33,1},{65,97},{97,65},{2,34}... | collective-permute-start | bytes 9437192 | tf_op jit(solution)/shard_map/ppermute | solution.py:16
  63.2 191.3 %collective-permute-start = (bf16[2048,768]{0,1:T(8,128)(2,1)}, bf16[2048,768]{0,1:T(8,128)(2,1)}, u32[]{:S(2)}, u32[]{:S(2)}) collective-permute-start(bf16[2048,768]{0,1:T(8,128)(2,1)} %fusion.2), channel_id=1, source_target_pairs={{0,32},{32,0},{64,96},{96,64},{1,33},{33,1},{65,97},{97,65},{2,34}... | collective-permute-start | bytes 9437192 | tf_op jit(solution)/shard_map/ppermute | solution.py:16
  80.7 157.3 %all-to-all-start.2 = ((bf16[128,2,4096]{2,1,0:T(2,128)(2,1)}), bf16[128,2,4096]{2,1,0:T(2,128)(2,1)}, u32[]{:S(2)}, u32[]{:S(2)}) async-start(bf16[128,2,4096]{2,1,0:T(2,128)(2,1)} %reshape.386), calls=%async_computation.2 | async-start | bytes 4194304 | tf_op jit(solution)/shard_map/all_to_all | solution.py:105
  86.4 3.2 copy-start.7
  92.2 206.0 %collective-permute-start.1 = (bf16[2048,768]{0,1:T(8,128)(2,1)}, bf16[2048,768]{0,1:T(8,128)(2,1)}, u32[]{:S(2)}, u32[]{:S(2)}) collective-permute-start(bf16[2048,768]{0,1:T(8,128)(2,1)} %fusion.1), channel_id=1, source_target_pairs={{0,32},{32,0},{64,96},{96,64},{1,33},{33,1},{65,97},{97,65},{2,34}... | collective-permute-start | bytes 9437192 | tf_op jit(solution)/shard_map/ppermute | solution.py:16
  334.1 4.4 copy-start.4
  349.6 22.8 %all-to-all-start.5 = ((bf16[128,1,2]{2,1,0:T(2,128)(2,1)}), bf16[128,1,2]{2,1,0:T(2,128)(2,1)S(1)}, u32[]{:S(2)}, u32[]{:S(2)}) async-start(bf16[128,1,2]{2,1,0:T(2,128)(2,1)} %copy.51), calls=%async_computation.5 | async-start | bytes 131072 | tf_op jit(solution)/shard_map/all_to_all | solution.py:166
  363.3 5.8 copy-start.3
  363.3 173.2 %collective-permute-start.3 = (bf16[2048,768]{1,0:T(8,128)(2,1)}, bf16[2048,768]{1,0:T(8,128)(2,1)}, u32[]{:S(2)}, u32[]{:S(2)}) collective-permute-start(bf16[2048,768]{1,0:T(8,128)(2,1)} %constant_dynamic-slice_fusion.2), channel_id=1, source_target_pairs={{0,32},{32,0},{64,96},{96,64},{1,33},{33,1},{65,97},{97,65},{2,34}... | collective-permute-start | bytes 9437192 | tf_op jit(solution)/shard_map/ppermute | solution.py:16
  368.1 173.9 %collective-permute-start.4 = (bf16[2048,768]{1,0:T(8,128)(2,1)}, bf16[2048,768]{1,0:T(8,128)(2,1)}, u32[]{:S(2)}, u32[]{:S(2)}) collective-permute-start(bf16[2048,768]{1,0:T(8,128)(2,1)} %constant_dynamic-slice_fusion.1), channel_id=1, source_target_pairs={{0,32},{32,0},{64,96},{96,64},{1,33},{33,1},{65,97},{97,65},{2,34}... | collective-permute-start | bytes 9437192 | tf_op jit(solution)/shard_map/ppermute | solution.py:16
  372.4 158.9 %all-to-all-start.4 = ((bf16[128,2,4096]{2,1,0:T(2,128)(2,1)}), bf16[128,2,4096]{2,1,0:T(2,128)(2,1)}, u32[]{:S(2)}, u32[]{:S(2)}) async-start(bf16[128,2,4096]{2,1,0:T(2,128)(2,1)} %broadcast_select_fusion), calls=%async_computation.4 | async-start | bytes 4194304 | tf_op jit(solution)/shard_map/all_to_all | solution.py:165
  384.6 3.8 copy-start.2
  388.4 202.0 %collective-permute-start.5 = (bf16[2048,768]{1,0:T(8,128)(2,1)}, bf16[2048,768]{1,0:T(8,128)(2,1)}, u32[]{:S(2)}, u32[]{:S(2)}) collective-permute-start(bf16[2048,768]{1,0:T(8,128)(2,1)} %constant_dynamic-slice_fusion), channel_id=1, source_target_pairs={{0,32},{32,0},{64,96},{96,64},{1,33},{33,1},{65,97},{97,65},{2,34}... | collective-permute-start | bytes 9437192 | tf_op jit(solution)/shard_map/ppermute | solution.py:16
  536.6 53.9 %slice-start = ((s8[6291456]{0:T(1024)(128)(4,1)}), s8[4194304]{0:T(1024)(128)(4,1)S(1)}, s32[]{:S(2)}) async-start(s8[6291456]{0:T(1024)(128)(4,1)} %bitcast.82), calls=%async_computation.6 | async-start | bytes 8388608
  542.0 48.4 %slice-start.1 = ((s8[6291456]{0:T(1024)(128)(4,1)}), s8[2097152]{0:T(1024)(128)(4,1)S(1)}, s32[]{:S(2)}) async-start(s8[6291456]{0:T(1024)(128)(4,1)} %bitcast.82), calls=%async_computation.7 | async-start | bytes 4194304
  542.0 52.9 %copy-start.1 = (bf16[16,4096]{1,0:T(8,128)(2,1)S(1)}, bf16[16,4096]{1,0:T(8,128)(2,1)}, u32[]{:S(2)}) copy-start(bf16[16,4096]{1,0:T(8,128)(2,1)} %param.15) | copy-start | bytes 393220
where the time goes:
time: 605 us; the launch traced here: 595 us
  waiting for transfers between devices  364 us (60%)
  local copies, waits for them, and re-layouts  84.6 us (14%)
  starting transfers between devices  57.9 us (10%)
  matrix products  57.3 us (9%)
  other arithmetic  30.1 us (5%)
    all_to_all x1, waiting for transfers between devices, shards(): lax.all_to_all(ret_x, ('group', 'local'), split_axis=0, concat_axis=0, ti...  139 us
    all_to_all x1, waiting for transfers between devices, shards(): lax.all_to_all(pack_dy, ('group', 'local'), split_axis=0, concat_axis=0,...  132 us
    ppermute x6, waiting for transfers between devices, partner(): return lax.ppermute(block, axis, route)  79.3 us
    dot_general x3, matrix products, contract_last(): lax.dot_general(left, right, (((1,), (1,)), ((), ())), preferred_element_...  23.6 us
    unnamed x37, local copies, waits for them, and re-layouts  15.2 us
  transfers between devices with their start and end apart: 12, of which 7 were waited for; matrix products, arithmetic and copies ran while one was open for 18% of the time, Pallas kernels for 0%

commit v1 on v0

v1 whole, which is shorter than its diff:
```python
import functools

import jax
import jax.numpy as jnp
from jax import lax
from jax.experimental import pallas as pl
from jax.experimental.pallas import tpu as pltpu
from jax.sharding import PartitionSpec as P

CAP = 192
META = 128
CODE, SLOT, GATE = 0, 8, 16
BF = jnp.bfloat16
F32 = jnp.float32
VMEM_LIMIT = 48 * 1024 * 1024

ROWS = (((0,), (0,)), ((), ()))
LAST = (((1,), (1,)), ((), ()))


def dot(left, right, dims=(((1,), (0,)), ((), ()))):
    return lax.dot_general(left, right, dims, preferred_element_type=F32)


def call(kernel, outs, args, flops=0, moved=0, **kw):
    return pl.pallas_call(
        kernel,
        out_shape=outs,
        compiler_params=pltpu.CompilerParams(vmem_limit_bytes=VMEM_LIMIT),
        cost_estimate=pl.CostEstimate(flops=flops, bytes_accessed=moved, transcendentals=0),
        **kw,
    )(*args)


SMEM = pl.BlockSpec(memory_space=pltpu.SMEM)
VMEM = pl.BlockSpec(memory_space=pltpu.VMEM)


def prepare_kernel(place_ref, xq_ref, xs_ref, dy_ref, meta_ref, same_x, other_x, same_dy, other_dy):
    half = xq_ref.shape[1] // 2
    blocks = half // 128
    first = lax.rem(place_ref[0], 2) == 0
    for c in range(blocks):
        low, high = c * 128, half + c * 128
        x_low = (xq_ref[:, low : low + 128].astype(F32) * xs_ref[:, c : c + 1]).astype(BF)
        x_high = (
            xq_ref[:, high : high + 128].astype(F32) * xs_ref[:, blocks + c : blocks + c + 1]
        ).astype(BF)
        same_x[:, low : low + 128] = jnp.where(first, x_low, x_high)
        other_x[:, low : low + 128] = jnp.where(first, x_high, x_low)
    same_x[:, half:] = meta_ref[...]
    other_x[:, half:] = meta_ref[...]
    dy_low, dy_high = dy_ref[:, :half], dy_ref[:, half:]
    same_dy[...] = jnp.where(first, dy_low, dy_high)
    other_dy[...] = jnp.where(first, dy_high, dy_low)


def matches(meta, k, base, count):
    lane = lax.broadcasted_iota(jnp.int32, (meta.shape[0], count), 1).astype(F32)
    code = meta[:, CODE + k : CODE + k + 1] - base
    return (code == lane) | (code - 64.0 == lane)


def owner_of_row(rows, count, per):
    row = lax.broadcasted_iota(jnp.int32, (rows, count), 0)
    lane = lax.broadcasted_iota(jnp.int32, (rows, count), 1)
    return lax.div(row, per) == lane


def pack_x_kernel(n_local, top, place_ref, b0, b1, b2, b3, out_ref, pick_ref, gated_ref, meta_out):
    half = b0.shape[1] - META
    tokens = jnp.concatenate([b[...] for b in (b0, b1, b2, b3)], axis=0)
    meta = tokens[:, half:].astype(F32)
    count = tokens.shape[0]
    base = (1 + lax.div(place_ref[0], 2) * n_local).astype(F32)
    named = jnp.zeros((count, n_local), F32)
    gate = jnp.zeros((count, n_local), F32)
    for k in range(top):
        hit = matches(meta, k, base, n_local) & (meta[:, SLOT + k : SLOT + k + 1] < CAP)
        named = jnp.where(hit, 1.0, named)
        gate = jnp.where(hit, meta[:, GATE + k : GATE + k + 1], gate)
    row = lax.broadcasted_iota(jnp.int32, (count, count), 0)
    col = lax.broadcasted_iota(jnp.int32, (count, count), 1)
    before = jnp.where(col < row, 1.0, 0.0).astype(BF)
    rank = jnp.where(named > 0.0, dot(before, named.astype(BF)), -1.0)
    rows = out_ref.shape[0]
    per = rows // n_local
    spread = jnp.where(owner_of_row(rows, n_local, per), 1.0, 0.0).astype(BF)
    rank_rows = dot(spread, rank.astype(BF), LAST)
    gate_rows = dot(spread, gate.astype(BF), LAST)
    position = lax.rem(lax.broadcasted_iota(jnp.int32, (rows, count), 0), per).astype(F32)
    hit = rank_rows == position
    pick = jnp.where(hit, 1.0, 0.0).astype(BF)
    pick_ref[...] = pick
    gated_ref[...] = jnp.where(hit, gate_rows, 0.0).astype(BF)
    meta_out[...] = meta.astype(BF)
    out_ref[...] = dot(pick, tokens).astype(BF)


def pack_dy_kernel(gated_ref, b0, b1, b2, b3, out_ref):
    tokens = jnp.concatenate([b[...] for b in (b0, b1, b2, b3)], axis=0)
    out_ref[...] = dot(gated_ref[...], tokens).astype(BF)


def forward_kernel(
    n_local, top, place_ref, x_ref, meta_ref, wg_ref, wu_ref, kept_ref, part_ref, send_ref, slot_ref
):
    step = pl.program_id(0)
    hidden = wg_ref.shape[1]

    @pl.when(step == 0)
    def _():
        meta = meta_ref[...].astype(F32)
        own = (1 + lax.div(place_ref[0], 2) * n_local + place_ref[1]).astype(F32)
        target = jnp.full((meta.shape[0], 1), -1.0, F32)
        for k in range(top):
            code = meta[:, CODE + k : CODE + k + 1]
            slot = meta[:, SLOT + k : SLOT + k + 1]
            target = jnp.where(code == own, slot, target)
            target = jnp.where(code == own + 64.0, slot + CAP, target)
        lane = lax.broadcasted_iota(jnp.int32, slot_ref.shape, 1).astype(F32)
        slot_ref[...] = jnp.where(lane == target, 1.0, 0.0).astype(BF)
        part_ref[...] = jnp.zeros_like(part_ref)

    kept = dot(slot_ref[...], x_ref[...], ROWS).astype(BF)
    kept_ref[...] = kept
    part_ref[:, :hidden] += dot(kept, wg_ref[...])
    part_ref[:, hidden:] += dot(kept, wu_ref[...])

    @pl.when(step == pl.num_programs(0) - 1)
    def _():
        send_ref[...] = part_ref[...].astype(BF)


def down_kernel(slot_ref, dy_ref, v_ref, kept_ref, part_ref, send_ref):
    step = pl.program_id(0)

    @pl.when(step == 0)
    def _():
        part_ref[...] = jnp.zeros_like(part_ref)

    kept = dot(slot_ref[...], dy_ref[...], ROWS).astype(BF)
    kept_ref[...] = kept
    part_ref[...] += dot(kept, v_ref[...])

    @pl.when(step == pl.num_programs(0) - 1)
    def _():
        send_ref[...] = part_ref[...].astype(BF)


def backward_kernel(
    ab_ref, ab_in, dh_ref, dh_in, slot_ref, wg_ref, wu_ref, da_out, db_out, hid_out, dx_ref, wide
):
    step = pl.program_id(0)
    hidden = wg_ref.shape[1]
    chunk = wg_ref.shape[0]
    width = dx_ref.shape[1] - META

    @pl.when(step == 0)
    def _():
        ab = ab_ref[...] + ab_in[...].astype(F32)
        d_hidden = dh_ref[...] + dh_in[...].astype(F32)
        act_a, act_b = ab[:, :hidden], ab[:, hidden:]
        sigma = jax.nn.sigmoid(act_a)
        silu_a = act_a * sigma
        hid = (silu_a * act_b).astype(BF)
        d_a = (d_hidden * act_b * sigma * (1.0 + act_a * (1.0 - sigma))).astype(BF)
        d_b = (d_hidden * silu_a).astype(BF)
        da_out[...] = d_a
        db_out[...] = d_b
        hid_out[...] = hid
        wide[:, :hidden] = dot(slot_ref[...], d_a).astype(BF)
        wide[:, hidden:] = dot(slot_ref[...], d_b).astype(BF)
        grad = jnp.sum(hid.astype(F32) * d_hidden, axis=1, keepdims=True)
        high = grad.astype(BF).astype(F32)
        lane = lax.broadcasted_iota(jnp.int32, (grad.shape[0], META), 1)
        both = jnp.where(lane == 0, high, jnp.where(lane == 1, grad - high, 0.0)).astype(BF)
        dx_ref[:, width:] = dot(slot_ref[...], both).astype(BF)

    dx = dot(wide[:, :hidden], wg_ref[...], LAST) + dot(wide[:, hidden:], wu_ref[...], LAST)
    dx_ref[:, pl.ds(pl.multiple_of(step * chunk, chunk), chunk)] = dx.astype(BF)


def combine_kernel(n_local, top, place_ref, ret_ref, pick_ref, meta_ref, *outs):
    width = ret_ref.shape[1] - META
    pick = pick_ref[...]
    meta = meta_ref[...].astype(F32)
    total = dot(pick, ret_ref[:, :width], ROWS).astype(BF)
    rows = ret_ref.shape[0]
    owner = owner_of_row(rows, n_local, rows // n_local)
    grads = ret_ref[:, width:].astype(F32)
    high = jnp.where(owner, grads[:, 0:1], 0.0).astype(BF)
    low = jnp.where(owner, grads[:, 1:2], 0.0).astype(BF)
    by_expert = dot(pick, high, ROWS) + dot(pick, low, ROWS)
    base = (1 + lax.div(place_ref[0], 2) * n_local).astype(F32)
    lane = lax.broadcasted_iota(jnp.int32, meta.shape, 1)
    tail = jnp.zeros(meta.shape, F32)
    for k in range(top):
        hit = matches(meta, k, base, n_local) & (meta[:, SLOT + k : SLOT + k + 1] < CAP)
        value = jnp.sum(jnp.where(hit, by_expert, 0.0), axis=1, keepdims=True)
        tail = jnp.where(lane == k, value / meta[:, GATE + k : GATE + k + 1], tail)
    tail = tail.astype(BF)
    block = outs[0].shape[0]
    for m, out in enumerate(outs):
        out[:, :width] = total[m * block : (m + 1) * block]
        out[:, width:] = tail[m * block : (m + 1) * block]


def finish_kernel(place_ref, b0, b1, b2, b3, tokens_ref, gates_ref):
    half = tokens_ref.shape[1] // 2
    first = lax.rem(place_ref[0], 2) == 0
    own = b0[...].astype(F32) + b2[...].astype(F32)
    other = b1[:, :half].astype(F32) + b3[:, :half].astype(F32)
    mine = own[:, :half]
    tokens_ref[:, :half] = jnp.where(first, mine, other).astype(BF)
    tokens_ref[:, half:] = jnp.where(first, other, mine).astype(BF)
    gates_ref[...] = own[:, half : half + gates_ref.shape[1]].astype(BF)


def dequant_half(quant, scales):
    scale = jnp.repeat(jnp.repeat(scales[:, 0, :], 128, axis=0), 128, axis=1)
    return (quant[:, 0, :].astype(F32) * scale).astype(BF)


def shape(*dims, dtype=BF):
    return jax.ShapeDtypeStruct(dims, dtype)


def shards(
    x_q,
    x_scale,
    cotangent,
    gates,
    experts,
    replicas,
    slots,
    w_gate_q,
    w_up_q,
    w_down_q,
    gate_scales,
    up_scales,
    down_scales,
):
    n_group = lax.axis_size("group")
    n_local = lax.axis_size("local")
    tok, width = x_q.shape
    top = experts.shape[1]
    half = width // 2
    hidden = w_gate_q.shape[2]
    column = n_group * tok
    rows = n_local * n_group * 4
    kept = 2 * CAP
    wide = half + META
    place = jnp.stack([lax.axis_index("group"), lax.axis_index("local")]).astype(jnp.int32)

    def across(block, apart):
        return lax.ppermute(block, "group", [(i, i ^ apart) for i in range(n_group)])

    def spread(block):
        return lax.all_to_all(block, "local", split_axis=0, concat_axis=0, tiled=True)

    meta = jnp.concatenate(
        [
            (1 + experts + 64 * replicas).astype(BF),
            slots.astype(BF),
            gates,
            jnp.zeros((tok, META - 3 * top), BF),
        ],
        axis=1,
    )
    same_x, other_x, same_dy, other_dy = call(
        prepare_kernel,
        (shape(tok, wide), shape(tok, wide), shape(tok, half), shape(tok, half)),
        (place, x_q, x_scale, cotangent, meta),
        moved=tok * width * 8,
        in_specs=[SMEM] + [VMEM] * 4,
        out_specs=[VMEM] * 4,
    )
    near_x = [same_x, across(other_x, 1), across(same_x, 2), across(other_x, 3)]
    near_dy = [same_dy, across(other_dy, 1), across(same_dy, 2), across(other_dy, 3)]
    packed_x, pick, gated, column_meta = call(
        functools.partial(pack_x_kernel, n_local, top),
        (shape(rows, wide), shape(rows, column), shape(rows, column), shape(column, META)),
        (place, *near_x),
        flops=2 * rows * column * wide,
        moved=2 * rows * wide,
        in_specs=[SMEM] + [VMEM] * 4,
        out_specs=[VMEM] * 4,
    )
    packed_dy = call(
        pack_dy_kernel,
        shape(rows, half),
        (gated, *near_dy),
        flops=2 * rows * column * half,
        moved=2 * rows * half,
        in_specs=[VMEM] * 5,
        out_specs=VMEM,
    )
    w_gate = dequant_half(w_gate_q, gate_scales)
    w_up = dequant_half(w_up_q, up_scales)
    w_down = dequant_half(w_down_q, down_scales)
    got_x = spread(packed_x)
    got_x, packed_dy = lax.optimization_barrier((got_x, packed_dy))
    got_dy = spread(packed_dy)

    chunk = 512
    steps = half // chunk
    whole = lambda *dims: pl.BlockSpec(dims, lambda i: (0,) * len(dims))
    rows_x, part_ab, send_ab, slot_of = call(
        functools.partial(forward_kernel, n_local, top),
        (
            shape(kept, half),
            shape(kept, 2 * hidden, dtype=F32),
            shape(kept, 2 * hidden),
            shape(rows, kept),
        ),
        (place, got_x, got_x, w_gate, w_up),
        flops=4 * kept * half * hidden,
        moved=4 * half * hidden + 4 * rows * half,
        grid=(steps,),
        in_specs=[
            SMEM,
            pl.BlockSpec((rows, chunk), lambda i: (0, i)),
            pl.BlockSpec((rows, META), lambda i: (0, half // META)),
            pl.BlockSpec((chunk, hidden), lambda i: (i, 0)),
            pl.BlockSpec((chunk, hidden), lambda i: (i, 0)),
        ],
        out_specs=[
            pl.BlockSpec((kept, chunk), lambda i: (0, i)),
            whole(kept, 2 * hidden),
            whole(kept, 2 * hidden),
            whole(rows, kept),
        ],
    )
    their_ab = across(send_ab, 1)
    rows_dy, part_dh, send_dh = call(
        down_kernel,
        (shape(kept, half), shape(kept, hidden, dtype=F32), shape(kept, hidden)),
        (slot_of, got_dy, w_down),
        flops=2 * kept * half * hidden,
        moved=2 * half * hidden + 4 * rows * half,
        grid=(steps,),
        in_specs=[
            whole(rows, kept),
            pl.BlockSpec((rows, chunk), lambda i: (0, i)),
            pl.BlockSpec((chunk, hidden), lambda i: (i, 0)),
        ],
        out_specs=[
            pl.BlockSpec((kept, chunk), lambda i: (0, i)),
            whole(kept, hidden),
            whole(kept, hidden),
        ],
    )
    their_dh = across(send_dh, 1)
    d_a, d_b, hid, dx = call(
        backward_kernel,
        (shape(kept, hidden), shape(kept, hidden), shape(kept, hidden), shape(rows, wide)),
        (part_ab, their_ab, part_dh, their_dh, slot_of, w_gate, w_up),
        flops=4 * rows * half * hidden,
        moved=4 * half * hidden + 2 * rows * half,
        grid=(steps,),
        in_specs=[
            whole(kept, 2 * hidden),
            whole(kept, 2 * hidden),
            whole(kept, hidden),
            whole(kept, hidden),
            whole(rows, kept),
            pl.BlockSpec((chunk, hidden), lambda i: (i, 0)),
            pl.BlockSpec((chunk, hidden), lambda i: (i, 0)),
        ],
        out_specs=[
            whole(kept, hidden),
            whole(kept, hidden),
            whole(kept, hidden),
            whole(rows, wide),
        ],
        scratch_shapes=[pltpu.VMEM((rows, 2 * hidden), BF)],
    )
    returned = spread(dx)
    grads = [
        dot(left, right, ROWS).astype(BF)
        for left, right in ((rows_x, d_a), (rows_x, d_b), (rows_dy, hid))
    ]
    blocks = call(
        functools.partial(combine_kernel, n_local, top),
        tuple(shape(tok, wide) for _ in range(n_group)),
        (place, returned, pick, column_meta),
        flops=2 * rows * column * half,
        moved=2 * rows * half,
        in_specs=[SMEM] + [VMEM] * 3,
        out_specs=[VMEM] * n_group,
    )
    back = [blocks[0]] + [across(blocks[m], m) for m in range(1, n_group)]
    grad_tokens, grad_gates = call(
        finish_kernel,
        (shape(tok, width), shape(tok, top)),
        (place, *back),
        moved=tok * width * 6,
        in_specs=[SMEM] + [VMEM] * 4,
        out_specs=[VMEM] * 2,
    )
    return (
        grad_tokens,
        grad_gates,
        grads[0][:, None, :],
        grads[1][:, None, :],
        grads[2][:, None, :],
    )


def solution(mesh):
    by_token = P(("group", "local"), None)
    by_expert = P("group", "local", None)
    return jax.shard_map(
        shards,
        mesh=mesh,
        in_specs=(by_token,) * 7 + (by_expert,) * 6,
        out_specs=(by_token,) * 2 + (by_expert,) * 3,
        check_vma=False,
    )
```

time: 605 us -> 198 us (0.33); the launches traced: 595 us -> 198 us
  waiting for transfers between devices: 364 us -> 57.3 us
  matrix products: 57.3 us -> 13.6 us
  local copies, waits for them, and re-layouts: 84.6 us -> 41.5 us
  Pallas kernels: 0 us -> 30.4 us
  starting transfers between devices: 57.9 us -> 37.1 us
  other arithmetic: 30.1 us -> 16.8 us
    all_to_all x6 -> x3, waiting for transfers between devices: 285 us -> 26.5 us  [spread(): lax.all_to_all(block, 'local', split_axis=0, concat_axis=0, tiled=True)]
    ppermute x6 -> x11, waiting for transfers between devices: 79.3 us -> 30.8 us  [across(): lax.ppermute(block, 'group', [(i, i ^ apart) for i in range(n_group)])]
    dot_general x9 -> x3, matrix products: 57.3 us -> 13.6 us  [dot(): return lax.dot_general(left, right, dims, preferred_element_type=F32)]
    pallas_call x0 -> x8, Pallas kernels: none -> 30.4 us  [call(): pl.pallas_call(kernel, out_shape=outs, compiler_params=pltpu.CompilerPara...]
    all_to_all x6 -> x3, starting transfers between devices: 51.7 us -> 23.1 us  [spread(): lax.all_to_all(block, 'local', split_axis=0, concat_axis=0, tiled=True)]
    scatter x7 -> x0, local copies, waits for them, and re-layouts: 26.1 us -> none  [the longest x1 5.77 us: shards(): jnp.zeros((arrivals, width), jnp.bfloat16).at[send_index].set(copy_x)]
    broadcast_in_dim x3 -> x0, other arithmetic: 15.4 us -> none  [the longest x1 5.45 us: shards(): grads[1][:, None, :]]
    gather x6 -> x0, local copies, waits for them, and re-layouts: 12.6 us -> none  [the longest x2 7.59 us: shards(): out_dx[pick]]
  transfers between devices with their start and end apart: 12 -> 14, of which waited for: 7 -> 6; matrix products, arithmetic and copies ran while one was open for 18% -> 30% of each run, Pallas kernels for 0% -> 8%
where the time goes in v1:
time: 198 us
  waiting for transfers between devices  57.3 us (29%)
  local copies, waits for them, and re-layouts  41.5 us (21%)
  starting transfers between devices  37.1 us (19%)
  Pallas kernels  30.4 us (15%)
  other arithmetic  16.8 us (8%)
  matrix products  13.6 us (7%)
    ppermute x11, waiting for transfers between devices, across(): lax.ppermute(block, 'group', [(i, i ^ apart) for i in range(n_group)])  30.8 us
    pallas_call x8, Pallas kernels, call(): pl.pallas_call(kernel, out_shape=outs, compiler_params=pltpu.CompilerPara...  30.4 us
    all_to_all x3, waiting for transfers between devices, spread(): lax.all_to_all(block, 'local', split_axis=0, concat_axis=0, tiled=True)  26.5 us
    all_to_all x3, starting transfers between devices, spread(): lax.all_to_all(block, 'local', split_axis=0, concat_axis=0, tiled=True)  23.1 us
    reshape x3, local copies, waits for them, and re-layouts, dequant_half(): scale = jnp.repeat(jnp.repeat(scales[:, 0, :], 128, axis=0), 128, axis=1)  19.8 us
    convert_element_type x2, other arithmetic, dequant_half(): return (quant[:, 0, :].astype(F32) * scale).astype(BF)  15.9 us
    ppermute x11, starting transfers between devices, across(): lax.ppermute(block, 'group', [(i, i ^ apart) for i in range(n_group)])  14 us
    dot_general x3, matrix products, dot(): return lax.dot_general(left, right, dims, preferred_element_type=F32)  13.6 us
  transfers between devices with their start and end apart: 14, of which 6 were waited for; matrix products, arithmetic and copies ran while one was open for 30% of the time, Pallas kernels for 8%

profile of v1, /device:TPU:0, one launch (start us, length us, event | category | flops | bytes accessed | tf_op | source)
XLA Modules:
  0.0 197.5 jit_solution(6503083308177528497)
XLA Ops:
  7.2 3.2 %collective-permute-start.1 = (bf16[16,2176]{1,0:T(8,128)(2,1)S(1)}, bf16[16,2176]{1,0:T(8,128)(2,1)S(1)}, u32[]{:S(2)}, u32[]{:S(2)}) collective-permute-start(bf16[16,2176]{1,0:T(8,128)(2,1)S(1)} %get-tuple-element.32.b0), channel_id=1, source_target_pairs={{0,64},{32,96},{64,0},{96,32},{1,65},{33,97},{65,1},{97,33},{2,66}... | collective-permute-start | bytes 208904 | tf_op jit(solution)/shard_map/ppermute | solution.py:257
  13.1 2.8 %collective-permute-done.2.b3 = bf16[16,2176]{1,0:T(8,128)(2,1)S(1)} collective-permute-done((bf16[16,2176]{1,0:T(8,128)(2,1)S(1)}, bf16[16,2176]{1,0:T(8,128)(2,1)S(1)}, u32[]{:S(2)}, u32[]{:S(2)}) %collective-permute-start.2) | collective-permute-done | bytes 69664 | tf_op jit(solution)/shard_map/ppermute | solution.py:257
  19.2 8.3 %all-to-all-start = ((bf16[32,16,2176]{2,1,0:T(8,128)(2,1)}), bf16[32,16,2176]{2,1,0:T(8,128)(2,1)S(1)}, u32[]{:S(2)}, u32[]{:S(2)}) async-start(bf16[32,16,2176]{2,1,0:T(8,128)(2,1)} %bitcast.66), calls=%async_computation | async-start | bytes 4456448 | tf_op jit(solution)/shard_map/all_to_all | solution.py:260
  32.7 3.4 %broadcast_in_dim.32 = f32[2048,6,128]{0,2,1:T(8,128)} broadcast(f32[2048,6]{0,1:T(8,128)S(1)} %bitcast.73), dimensions={0,1} | broadcast | bytes 6340608 | tf_op jit(solution)/shard_map/broadcast_in_dim | solution.py:221
  36.1 6.6 %copy.39 = f32[2048,768]{1,0:T(8,128)} copy(f32[2048,768]{0,1:T(8,128)} %bitcast.67) | data formatting | bytes 12582912 | tf_op jit(solution)/shard_map/reshape | solution.py:221
  42.7 3.4 %broadcast_in_dim.34 = f32[2048,6,128]{0,2,1:T(8,128)} broadcast(f32[2048,6]{0,1:T(8,128)S(1)} %bitcast.72), dimensions={0,1} | broadcast | bytes 6340608 | tf_op jit(solution)/shard_map/broadcast_in_dim | solution.py:221
  46.1 6.6 %copy.40 = f32[2048,768]{1,0:T(8,128)} copy(f32[2048,768]{0,1:T(8,128)} %bitcast.68) | data formatting | bytes 12582912 | tf_op jit(solution)/shard_map/reshape | solution.py:221
  52.7 3.4 %broadcast_in_dim.36 = f32[2048,6,128]{0,2,1:T(8,128)} broadcast(f32[2048,6]{0,1:T(8,128)S(1)} %bitcast.71), dimensions={0,1} | broadcast | bytes 6340608 | tf_op jit(solution)/shard_map/broadcast_in_dim | solution.py:221
  56.1 6.6 %copy.41 = f32[2048,768]{1,0:T(8,128)} copy(f32[2048,768]{0,1:T(8,128)} %bitcast.69) | data formatting | bytes 12582912 | tf_op jit(solution)/shard_map/reshape | solution.py:221
  64.8 7.5 %all-to-all-start.1 = ((bf16[32,16,2048]{2,1,0:T(8,128)(2,1)}), bf16[32,16,2048]{2,1,0:T(8,128)(2,1)}, u32[]{:S(2)}, u32[]{:S(2)}) async-start(bf16[32,16,2048]{2,1,0:T(8,128)(2,1)} %bitcast.65), calls=%async_computation.1 | async-start | bytes 4194304 | tf_op jit(solution)/shard_map/all_to_all | solution.py:260
  72.3 10.5 %fusion.1 = (bf16[2048,768]{1,0:T(8,128)(2,1)}, bf16[2048,768]{1,0:T(8,128)(2,1)}) fusion(f32[2048,768]{1,0:T(8,128)} %copy.40, bf16[2048,1,768]{2,0,1:T(8,128)(2,1)} %param.21, f32[2048,768]{1,0:T(8,128)} %copy.39, bf16[2048,1,768]{2,0,1:T(8,128)(2,1)} %param.20), kind=kLoop, calls=%fused_computation.3 | loop fusion | flops 9437184 | bytes 25165824 | tf_op jit(solution)/shard_map/convert_element_type | solution.py:222
  82.8 9.2 %shard_map.167 = (bf16[384,2048]{1,0:T(8,128)(2,1)S(1)}, f32[384,1536]{1,0:T(8,128)}, bf16[384,1536]{1,0:T(8,128)(2,1)}, bf16[512,384]{1,0:T(8,128)(2,1)S(1)}) custom-call(s32[2]{0:T(128)S(1)} %pad_add_fusion.place_ref, bf16[512,2176]{1,0:T(8,128)(2,1)S(1)} %bitcast.62, bf16[512,2176]{1,0:T(8,128)(2,1)S(1)} %bitcast.63, ...), custom_call_target="tpu_custom_call" | custom-call | flops 2415919104 | bytes 10485760 | tf_op jit(solution)/shard_map/pallas_call | solution.py:26
  93.3 5.4 %fusion.v_ref = bf16[2048,768]{1,0:T(8,128)(2,1)} fusion(f32[2048,768]{1,0:T(8,128)} %copy.41, bf16[2048,1,768]{2,0,1:T(8,128)(2,1)S(1)} %copy-done.11), kind=kLoop, calls=%fused_computation.1 | loop fusion | flops 4718592 | bytes 12582912 | tf_op jit(solution)/shard_map/convert_element_type | solution.py:222
  98.6 3.6 %all-to-all-done.1 = bf16[32,16,2048]{2,1,0:T(8,128)(2,1)} async-done(((bf16[32,16,2048]{2,1,0:T(8,128)(2,1)}), bf16[32,16,2048]{2,1,0:T(8,128)(2,1)}, u32[]{:S(2)}, u32[]{:S(2)}) %all-to-all-start.1) | async-done | bytes 2097184 | tf_op jit(solution)/shard_map/all_to_all | solution.py:260
  102.3 5.4 %shard_map.168 = (bf16[384,2048]{1,0:T(8,128)(2,1)S(1)}, f32[384,768]{1,0:T(8,128)S(1)}, bf16[384,768]{1,0:T(8,128)(2,1)S(1)}) custom-call(bf16[512,384]{1,0:T(8,128)(2,1)S(1)} %get-tuple-element.41.slot_ref, bf16[512,2048]{1,0:T(8,128)(2,1)} %bitcast.9.dy_ref, bf16[2048,768]{1,0:T(8,128)(2,1)} %fusion.v_ref), custom_call_target="tpu_custom_call" | custom-call | flops 1207959552 | bytes 7340032 | tf_op jit(solution)/shard_map/pallas_call | solution.py:26
  107.8 14.5 %collective-permute-done.6.ab_in = bf16[384,1536]{1,0:T(8,128)(2,1)S(1)} collective-permute-done((bf16[384,1536]{1,0:T(8,128)(2,1)}, bf16[384,1536]{1,0:T(8,128)(2,1)S(1)}, u32[]{:S(2)}, u32[]{:S(2)}) %collective-permute-start.6) | collective-permute-done | bytes 1179680 | tf_op jit(solution)/shard_map/ppermute | solution.py:257
  122.3 11.9 %collective-permute-done.7.dh_in = bf16[384,768]{1,0:T(8,128)(2,1)S(1)} collective-permute-done((bf16[384,768]{1,0:T(8,128)(2,1)S(1)}, bf16[384,768]{1,0:T(8,128)(2,1)S(1)}, u32[]{:S(2)}, u32[]{:S(2)}) %collective-permute-start.7) | collective-permute-done | bytes 589856 | tf_op jit(solution)/shard_map/ppermute | solution.py:257
  134.2 9.7 %shard_map.169 = (bf16[384,768]{1,0:T(8,128)(2,1)S(1)}, bf16[384,768]{1,0:T(8,128)(2,1)S(1)}, bf16[384,768]{1,0:T(8,128)(2,1)S(1)}, bf16[512,2176]{1,0:T(8,128)(2,1)}) custom-call(f32[384,1536]{1,0:T(8,128)} %get-tuple-element.39.ab_ref, bf16[384,1536]{1,0:T(8,128)(2,1)S(1)} %collective-permute-done.6.ab_in, f32[384,768]{1,0:T(8,128)S(1)} %get-tuple-element.43.dh_ref, ...), custom_call_target="tpu_custom_call" | custom-call | flops 3221225472 | bytes 8388608 | tf_op jit(solution)/shard_map/pallas_call | solution.py:26
  145.5 7.3 %all-to-all-start.2 = ((bf16[32,16,2176]{2,1,0:T(8,128)(2,1)}), bf16[32,16,2176]{2,1,0:T(8,128)(2,1)S(1)}, u32[]{:S(2)}, u32[]{:S(2)}) async-start(bf16[32,16,2176]{2,1,0:T(8,128)(2,1)} %bitcast.70), calls=%async_computation.2 | async-start | bytes 4456448 | tf_op jit(solution)/shard_map/all_to_all | solution.py:260
  152.8 5.2 %fusion.3 = bf16[2048,1,768]{2,0,1:T(8,128)(2,1)} fusion(bf16[384,2048]{1,0:T(8,128)(2,1)} %copy-done.6, bf16[384,768]{1,0:T(8,128)(2,1)} %copy-done.10), kind=kOutput, calls=%fused_computation.9 | convolution fusion | flops 1209532416 | bytes 5308416 | tf_op jit(solution)/shard_map/dot_general | solution.py:22
  158.0 3.5 %fusion.4 = bf16[2048,1,768]{2,0,1:T(8,128)(2,1)} fusion(bf16[384,2048]{1,0:T(8,128)(2,1)S(1)} %copy-done.7, bf16[384,768]{1,0:T(8,128)(2,1)S(1)} %copy-done.9), kind=kOutput, calls=%fused_computation.10 | convolution fusion | flops 1209532416 | bytes 5308416 | tf_op jit(solution)/shard_map/dot_general | solution.py:22
  161.5 22.8 %all-to-all-done.2 = bf16[32,16,2176]{2,1,0:T(8,128)(2,1)S(1)} async-done(((bf16[32,16,2176]{2,1,0:T(8,128)(2,1)}), bf16[32,16,2176]{2,1,0:T(8,128)(2,1)S(1)}, u32[]{:S(2)}, u32[]{:S(2)}) %all-to-all-start.2) | async-done | bytes 2228256 | tf_op jit(solution)/shard_map/all_to_all | solution.py:260
  186.3 3.2 %collective-permute-start.9 = (bf16[16,2176]{1,0:T(8,128)(2,1)S(1)}, bf16[16,2176]{1,0:T(8,128)(2,1)S(1)}, u32[]{:S(2)}, u32[]{:S(2)}) collective-permute-start(bf16[16,2176]{1,0:T(8,128)(2,1)S(1)} %get-tuple-element.50), channel_id=1, source_target_pairs={{0,64},{32,96},{64,0},{96,32},{1,65},{33,97},{65,1},{97,33},{2,66}... | collective-permute-start | bytes 208904 | tf_op jit(solution)/shard_map/ppermute | solution.py:257
  190.7 4.9 %fusion.5 = bf16[2048,1,768]{2,0,1:T(8,128)(2,1)} fusion(bf16[384,2048]{1,0:T(8,128)(2,1)} %copy-done.5, bf16[384,768]{1,0:T(8,128)(2,1)S(1)} %get-tuple-element.58), kind=kOutput, calls=%fused_computation.11 | convolution fusion | flops 1209532416 | bytes 5308416 | tf_op jit(solution)/shard_map/dot_general | solution.py:22
  (73 shorter events, 27.7 us)
Async XLA Ops:
  0.6 31.7 %copy-start.12 = (f32[16,1,6]{0,1,2:T(1,128)S(1)}, f32[16,1,6]{0,1,2:T(1,128)}, u32[]{:S(2)}) copy-start(f32[16,1,6]{0,1,2:T(1,128)} %param.23) | copy-start | bytes 1156
  0.6 31.7 %copy-start.13 = (f32[16,1,6]{0,1,2:T(1,128)S(1)}, f32[16,1,6]{0,1,2:T(1,128)}, u32[]{:S(2)}) copy-start(f32[16,1,6]{0,1,2:T(1,128)} %param.24) | copy-start | bytes 1156
  0.7 31.7 %copy-start.14 = (f32[16,1,6]{0,1,2:T(1,128)S(1)}, f32[16,1,6]{0,1,2:T(1,128)}, u32[]{:S(2)}) copy-start(f32[16,1,6]{0,1,2:T(1,128)} %param.25) | copy-start | bytes 1156
  7.2 5.9 %collective-permute-start.1 = (bf16[16,2176]{1,0:T(8,128)(2,1)S(1)}, bf16[16,2176]{1,0:T(8,128)(2,1)S(1)}, u32[]{:S(2)}, u32[]{:S(2)}) collective-permute-start(bf16[16,2176]{1,0:T(8,128)(2,1)S(1)} %get-tuple-element.32.b0), channel_id=1, source_target_pairs={{0,64},{32,96},{64,0},{96,32},{1,65},{33,97},{65,1},{97,33},{2,66}... | collective-permute-start | bytes 208904 | tf_op jit(solution)/shard_map/ppermute | solution.py:257
  10.4 5.5 %collective-permute-start.2 = (bf16[16,2176]{1,0:T(8,128)(2,1)S(1)}, bf16[16,2176]{1,0:T(8,128)(2,1)S(1)}, u32[]{:S(2)}, u32[]{:S(2)}) collective-permute-start(bf16[16,2176]{1,0:T(8,128)(2,1)S(1)} %get-tuple-element.33), channel_id=1, source_target_pairs={{0,96},{32,64},{64,32},{96,0},{1,97},{33,65},{65,33},{97,1},{2,98}... | collective-permute-start | bytes 208904 | tf_op jit(solution)/shard_map/ppermute | solution.py:257
  11.5 4.4 %collective-permute-start = (bf16[16,2176]{1,0:T(8,128)(2,1)S(1)}, bf16[16,2176]{1,0:T(8,128)(2,1)S(1)}, u32[]{:S(2)}, u32[]{:S(2)}) collective-permute-start(bf16[16,2176]{1,0:T(8,128)(2,1)S(1)} %get-tuple-element.33), channel_id=1, source_target_pairs={{0,32},{32,0},{64,96},{96,64},{1,33},{33,1},{65,97},{97,65},{2,34}... | collective-permute-start | bytes 208904 | tf_op jit(solution)/shard_map/ppermute | solution.py:257
  17.8 1.4 copy-start.1
  19.2 45.6 %all-to-all-start = ((bf16[32,16,2176]{2,1,0:T(8,128)(2,1)}), bf16[32,16,2176]{2,1,0:T(8,128)(2,1)S(1)}, u32[]{:S(2)}, u32[]{:S(2)}) async-start(bf16[32,16,2176]{2,1,0:T(8,128)(2,1)} %bitcast.66), calls=%async_computation | async-start | bytes 4456448 | tf_op jit(solution)/shard_map/all_to_all | solution.py:260
  27.5 35.2 %collective-permute-start.5 = (bf16[16,2048]{1,0:T(8,128)(2,1)S(1)}, bf16[16,2048]{1,0:T(8,128)(2,1)S(1)}, u32[]{:S(2)}, u32[]{:S(2)}) collective-permute-start(bf16[16,2048]{1,0:T(8,128)(2,1)S(1)} %get-tuple-element.37), channel_id=1, source_target_pairs={{0,96},{32,64},{64,32},{96,0},{1,97},{33,65},{65,33},{97,1},{2,98}... | collective-permute-start | bytes 196616 | tf_op jit(solution)/shard_map/ppermute | solution.py:257
  29.6 33.1 %collective-permute-start.3 = (bf16[16,2048]{1,0:T(8,128)(2,1)S(1)}, bf16[16,2048]{1,0:T(8,128)(2,1)S(1)}, u32[]{:S(2)}, u32[]{:S(2)}) collective-permute-start(bf16[16,2048]{1,0:T(8,128)(2,1)S(1)} %get-tuple-element.37), channel_id=1, source_target_pairs={{0,32},{32,0},{64,96},{96,64},{1,33},{33,1},{65,97},{97,65},{2,34}... | collective-permute-start | bytes 196616 | tf_op jit(solution)/shard_map/ppermute | solution.py:257
  29.7 33.0 %collective-permute-start.4 = (bf16[16,2048]{1,0:T(8,128)(2,1)S(1)}, bf16[16,2048]{1,0:T(8,128)(2,1)S(1)}, u32[]{:S(2)}, u32[]{:S(2)}) collective-permute-start(bf16[16,2048]{1,0:T(8,128)(2,1)S(1)} %get-tuple-element.36.b0), channel_id=1, source_target_pairs={{0,64},{32,96},{64,0},{96,32},{1,65},{33,97},{65,1},{97,33},{2,66}... | collective-permute-start | bytes 196616 | tf_op jit(solution)/shard_map/ppermute | solution.py:257
  63.4 1.4 copy-start
  64.8 37.5 %all-to-all-start.1 = ((bf16[32,16,2048]{2,1,0:T(8,128)(2,1)}), bf16[32,16,2048]{2,1,0:T(8,128)(2,1)}, u32[]{:S(2)}, u32[]{:S(2)}) async-start(bf16[32,16,2048]{2,1,0:T(8,128)(2,1)} %bitcast.65), calls=%async_computation.1 | async-start | bytes 4194304 | tf_op jit(solution)/shard_map/all_to_all | solution.py:260
  82.8 10.4 %copy-start.11 = (bf16[2048,1,768]{2,0,1:T(8,128)(2,1)S(1)}, bf16[2048,1,768]{2,0,1:T(8,128)(2,1)}, u32[]{:S(2)}) copy-start(bf16[2048,1,768]{2,0,1:T(8,128)(2,1)} %param.22) | copy-start | bytes 9437188
  92.0 1.2 copy-start.6
  93.3 29.0 %collective-permute-start.6 = (bf16[384,1536]{1,0:T(8,128)(2,1)}, bf16[384,1536]{1,0:T(8,128)(2,1)S(1)}, u32[]{:S(2)}, u32[]{:S(2)}) collective-permute-start(bf16[384,1536]{1,0:T(8,128)(2,1)} %get-tuple-element.40), channel_id=1, source_target_pairs={{0,32},{32,0},{64,96},{96,64},{1,33},{33,1},{65,97},{97,65},{2,34}... | collective-permute-start | bytes 3538952 | tf_op jit(solution)/shard_map/ppermute | solution.py:257
  107.7 36.2 %copy-start.5 = (bf16[384,2048]{1,0:T(8,128)(2,1)}, bf16[384,2048]{1,0:T(8,128)(2,1)S(1)}, u32[]{:S(2)}) copy-start(bf16[384,2048]{1,0:T(8,128)(2,1)S(1)} %get-tuple-element.57) | copy-start | bytes 4718596
  107.7 26.5 %collective-permute-start.7 = (bf16[384,768]{1,0:T(8,128)(2,1)S(1)}, bf16[384,768]{1,0:T(8,128)(2,1)S(1)}, u32[]{:S(2)}, u32[]{:S(2)}) collective-permute-start(bf16[384,768]{1,0:T(8,128)(2,1)S(1)} %get-tuple-element.44), channel_id=1, source_target_pairs={{0,32},{32,0},{64,96},{96,64},{1,33},{33,1},{65,97},{97,65},{2,34}... | collective-permute-start | bytes 1769480 | tf_op jit(solution)/shard_map/ppermute | solution.py:257
  145.5 38.8 %all-to-all-start.2 = ((bf16[32,16,2176]{2,1,0:T(8,128)(2,1)}), bf16[32,16,2176]{2,1,0:T(8,128)(2,1)S(1)}, u32[]{:S(2)}, u32[]{:S(2)}) async-start(bf16[32,16,2176]{2,1,0:T(8,128)(2,1)} %bitcast.70), calls=%async_computation.2 | async-start | bytes 4456448 | tf_op jit(solution)/shard_map/all_to_all | solution.py:260
  152.7 5.2 %copy-start.7 = (bf16[384,2048]{1,0:T(8,128)(2,1)S(1)}, bf16[384,2048]{1,0:T(8,128)(2,1)}, u32[]{:S(2)}) copy-start(bf16[384,2048]{1,0:T(8,128)(2,1)} %copy-done.6) | copy-start | bytes 4718596
  152.7 5.2 %copy-start.9 = (bf16[384,768]{1,0:T(8,128)(2,1)S(1)}, bf16[384,768]{1,0:T(8,128)(2,1)}, u32[]{:S(2)}) copy-start(bf16[384,768]{1,0:T(8,128)(2,1)} %copy-done.8) | copy-start | bytes 1769476
  185.9 9.7 %collective-permute-start.8 = (bf16[16,2176]{1,0:T(8,128)(2,1)S(1)}, bf16[16,2176]{1,0:T(8,128)(2,1)S(1)}, u32[]{:S(2)}, u32[]{:S(2)}) collective-permute-start(bf16[16,2176]{1,0:T(8,128)(2,1)S(1)} %get-tuple-element.49), channel_id=1, source_target_pairs={{0,32},{32,0},{64,96},{96,64},{1,33},{33,1},{65,97},{97,65},{2,34}... | collective-permute-start | bytes 208904 | tf_op jit(solution)/shard_map/ppermute | solution.py:257
  186.3 9.3 %collective-permute-start.9 = (bf16[16,2176]{1,0:T(8,128)(2,1)S(1)}, bf16[16,2176]{1,0:T(8,128)(2,1)S(1)}, u32[]{:S(2)}, u32[]{:S(2)}) collective-permute-start(bf16[16,2176]{1,0:T(8,128)(2,1)S(1)} %get-tuple-element.50), channel_id=1, source_target_pairs={{0,64},{32,96},{64,0},{96,32},{1,65},{33,97},{65,1},{97,33},{2,66}... | collective-permute-start | bytes 208904 | tf_op jit(solution)/shard_map/ppermute | solution.py:257
  189.5 6.2 %collective-permute-start.10 = (bf16[16,2176]{1,0:T(8,128)(2,1)S(1)}, bf16[16,2176]{1,0:T(8,128)(2,1)S(1)}, u32[]{:S(2)}, u32[]{:S(2)}) collective-permute-start(bf16[16,2176]{1,0:T(8,128)(2,1)S(1)} %get-tuple-element.51), channel_id=1, source_target_pairs={{0,96},{32,64},{64,32},{96,0},{1,97},{33,65},{65,33},{97,1},{2,98}... | collective-permute-start | bytes 208904 | tf_op jit(solution)/shard_map/ppermute | solution.py:257
  (5 other events, 4.1 us)

commit v2 on v1

v2 whole, which is shorter than its diff:
```python
import functools

import jax
import jax.numpy as jnp
from jax import lax
from jax.experimental import pallas as pl
from jax.experimental.pallas import tpu as pltpu
from jax.sharding import PartitionSpec as P

CAP = 192
META = 128
CODE, SLOT, GATE = 0, 8, 16
BF = jnp.bfloat16
F32 = jnp.float32
MIB = 1024 * 1024

ROWS = (((0,), (0,)), ((), ()))
LAST = (((1,), (1,)), ((), ()))


def dot(left, right, dims=(((1,), (0,)), ((), ()))):
    return lax.dot_general(left, right, dims, preferred_element_type=F32)


def call(kernel, outs, args, limit, flops=0, moved=0, **kw):
    return pl.pallas_call(
        kernel,
        out_shape=outs,
        compiler_params=pltpu.CompilerParams(vmem_limit_bytes=limit * MIB),
        cost_estimate=pl.CostEstimate(flops=flops, bytes_accessed=moved, transcendentals=0),
        **kw,
    )(*args)


SMEM = pl.BlockSpec(memory_space=pltpu.SMEM)


def whole(*dims):
    return pl.BlockSpec(dims, lambda i: (0,) * len(dims))


def placed(source, offset):
    lane = lax.broadcasted_iota(jnp.int32, (source.shape[0], META), 1)
    row = lax.broadcasted_iota(jnp.int32, (source.shape[0], META), 0)
    return dot(source.astype(BF), jnp.where(lane == row + offset, 1.0, 0.0).astype(BF), ROWS)


def prepare_kernel(
    place_ref, xq_ref, xs_ref, dy_ref, e_ref, r_ref, s_ref, g_ref, same_x, other_x, same_dy, other_dy
):
    half = xq_ref.shape[1] // 2
    blocks = half // 128
    first = lax.rem(place_ref[0], 2) == 0
    code = (1 + e_ref[...] + 64 * r_ref[...]).astype(F32)
    meta = placed(code, CODE) + placed(s_ref[...].astype(F32), SLOT) + placed(g_ref[...], GATE)
    same_x[:, half:] = meta.astype(BF)
    other_x[:, half:] = meta.astype(BF)
    for c in range(blocks):
        low, high = c * 128, half + c * 128
        x_low = (xq_ref[:, low : low + 128].astype(F32) * xs_ref[:, c : c + 1]).astype(BF)
        x_high = (
            xq_ref[:, high : high + 128].astype(F32) * xs_ref[:, blocks + c : blocks + c + 1]
        ).astype(BF)
        same_x[:, low : low + 128] = jnp.where(first, x_low, x_high)
        other_x[:, low : low + 128] = jnp.where(first, x_high, x_low)
    dy_low, dy_high = dy_ref[:, :half], dy_ref[:, half:]
    same_dy[...] = jnp.where(first, dy_low, dy_high)
    other_dy[...] = jnp.where(first, dy_high, dy_low)


def matches(meta, k, base, count):
    lane = lax.broadcasted_iota(jnp.int32, (meta.shape[0], count), 1).astype(F32)
    code = meta[:, CODE + k : CODE + k + 1] - base
    return (code == lane) | (code - 64.0 == lane)


def owner_of_row(rows, count, per, start=0):
    row = lax.broadcasted_iota(jnp.int32, (rows, count), 0) + start
    lane = lax.broadcasted_iota(jnp.int32, (rows, count), 1)
    return lax.div(row, per) == lane


def pack_x_kernel(
    n_local, top, per, place_ref, b0, b1, b2, b3, out_ref, pick_ref, gated_ref, meta_out, tokens, ranks, gates
):
    step = pl.program_id(0)
    half = b0.shape[1] - META
    count = tokens.shape[0]

    @pl.when(step == 0)
    def _():
        block = b0.shape[0]
        for m, b in enumerate((b0, b1, b2, b3)):
            tokens[m * block : (m + 1) * block] = b[...]
        meta_out[...] = tokens[:, half:]
        meta = tokens[:, half:].astype(F32)
        base = (1 + lax.div(place_ref[0], 2) * n_local).astype(F32)
        named = jnp.zeros((count, n_local), F32)
        gate = jnp.zeros((count, n_local), F32)
        for k in range(top):
            hit = matches(meta, k, base, n_local) & (meta[:, SLOT + k : SLOT + k + 1] < CAP)
            named = jnp.where(hit, 1.0, named)
            gate = jnp.where(hit, meta[:, GATE + k : GATE + k + 1], gate)
        row = lax.broadcasted_iota(jnp.int32, (count, count), 0)
        col = lax.broadcasted_iota(jnp.int32, (count, count), 1)
        before = jnp.where(col < row, 1.0, 0.0).astype(BF)
        ranks[...] = jnp.where(named > 0.0, dot(before, named.astype(BF)), -1.0).astype(BF)
        gates[...] = gate.astype(BF)

    rows = out_ref.shape[0]
    spread = jnp.where(owner_of_row(rows, n_local, per, step * rows), 1.0, 0.0).astype(BF)
    rank_rows = dot(spread, ranks[...], LAST)
    gate_rows = dot(spread, gates[...], LAST)
    position = lax.rem(lax.broadcasted_iota(jnp.int32, (rows, count), 0), per).astype(F32)
    hit = rank_rows == position
    pick = jnp.where(hit, 1.0, 0.0).astype(BF)
    pick_ref[...] = pick
    gated_ref[...] = jnp.where(hit, gate_rows, 0.0).astype(BF)
    out_ref[...] = dot(pick, tokens[...]).astype(BF)


def pack_dy_kernel(gated_ref, b0, b1, b2, b3, out_ref):
    tokens = jnp.concatenate([b[...] for b in (b0, b1, b2, b3)], axis=0)
    out_ref[...] = dot(gated_ref[...], tokens).astype(BF)


def dequant(quant_ref, scales_ref, out_ref, first_row, first_col, at_col=0):
    rows, cols = quant_ref.shape
    for c in range(cols // 128):
        for r in range(rows // 128):
            scale = scales_ref[first_col + c, first_row + r]
            factor = jnp.full((1, 16, 128), scale, F32).astype(BF)
            block = quant_ref[r * 128 : (r + 1) * 128, c * 128 : (c + 1) * 128]
            out_ref[r * 128 : (r + 1) * 128, at_col + c * 128 : at_col + (c + 1) * 128] = (
                block.reshape(8, 16, 128) * factor
            ).reshape(128, 128)


def forward_kernel(
    n_local, top, place_ref, sg_ref, su_ref, x_ref, wg_ref, wu_ref,
    kept_ref, a_ref, b_ref, send_ref, slot_ref, wg, wu,
):
    step = pl.program_id(0)
    half = kept_ref.shape[1]
    blocks = wg_ref.shape[1] // 128

    @pl.when(step == 0)
    def _():
        lane = lax.broadcasted_iota(jnp.int32, (2 * top, META), 1)
        row = lax.broadcasted_iota(jnp.int32, (2 * top, META), 0)
        turn = jnp.where(lane == row, 1.0, 0.0).astype(BF)
        meta = dot(turn, x_ref[:, half:], LAST)
        own = (1 + lax.div(place_ref[0], 2) * n_local + place_ref[1]).astype(F32)
        target = jnp.full((1, meta.shape[1]), -1.0, F32)
        for k in range(top):
            code = meta[CODE + k : CODE + k + 1]
            slot = meta[SLOT + k : SLOT + k + 1]
            target = jnp.where(code == own, slot, target)
            target = jnp.where(code == own + 64.0, slot + CAP, target)
        row = lax.broadcasted_iota(jnp.int32, slot_ref.shape, 0).astype(F32)
        slot_ref[...] = jnp.where(row == target, 1.0, 0.0).astype(BF)
        kept_ref[...] = dot(slot_ref[...], x_ref[:, :half]).astype(BF)

    dequant(wg_ref, sg_ref, wg, 0, step * blocks)
    dequant(wu_ref, su_ref, wu, 0, step * blocks)
    part_a = dot(kept_ref[...], wg[...])
    a_ref[...] = part_a
    send_ref[0] = part_a.astype(BF)
    part_b = dot(kept_ref[...], wu[...])
    b_ref[...] = part_b
    send_ref[1] = part_b.astype(BF)


def down_kernel(sv_ref, slot_ref, dy_ref, v_ref, kept_ref, part_ref, send_ref, v):
    step = pl.program_id(0)

    @pl.when(step == 0)
    def _():
        kept_ref[...] = dot(slot_ref[...], dy_ref[...]).astype(BF)

    dequant(v_ref, sv_ref, v, 0, step * (v_ref.shape[1] // 128))
    part = dot(kept_ref[...], v[...])
    part_ref[...] = part
    send_ref[...] = part.astype(BF)


def backward_kernel(
    sg_ref, su_ref, a_ref, b_ref, ab_in, dh_ref, dh_in, slot_ref, wg_ref, wu_ref,
    da_out, db_out, hid_out, dx_ref, wide, both, wcat,
):
    step = pl.program_id(0)
    hidden = wg_ref.shape[1]
    chunk = wg_ref.shape[0]
    width = dx_ref.shape[1] - META
    block = 64

    @pl.when(step == 0)
    def _():
        for r in range(0, a_ref.shape[0], block):
            at = slice(r, r + block)
            d_hidden = dh_ref[at] + dh_in[at].astype(F32)
            act_a = a_ref[at] + ab_in[0, at].astype(F32)
            act_b = b_ref[at] + ab_in[1, at].astype(F32)
            sigma = jax.nn.sigmoid(act_a)
            silu_a = act_a * sigma
            hid = (silu_a * act_b).astype(BF)
            hid_out[at] = hid
            d_a = d_hidden * act_b * sigma * (1.0 + act_a * (1.0 - sigma))
            da_out[at] = d_a.astype(BF)
            db_out[at] = (d_hidden * silu_a).astype(BF)
            grad = jnp.sum(hid.astype(F32) * d_hidden, axis=1, keepdims=True)
            high = grad.astype(BF).astype(F32)
            lane = lax.broadcasted_iota(jnp.int32, (block, META), 1)
            pair = jnp.where(lane == 0, high, jnp.where(lane == 1, grad - high, 0.0))
            both[at] = pair.astype(BF)
        wide[:, :hidden] = dot(slot_ref[...], da_out[...], ROWS).astype(BF)
        wide[:, hidden:] = dot(slot_ref[...], db_out[...], ROWS).astype(BF)
        dx_ref[:, width:] = dot(slot_ref[...], both[...], ROWS).astype(BF)

    rows = chunk // 128
    dequant(wg_ref, sg_ref, wcat, step * rows, 0)
    dequant(wu_ref, su_ref, wcat, step * rows, 0, hidden)
    dx = dot(wide[...], wcat[...], LAST)
    dx_ref[:, pl.ds(pl.multiple_of(step * chunk, chunk), chunk)] = dx.astype(BF)


def combine_kernel(n_local, top, place_ref, ret_ref, pick_ref, meta_ref, *outs):
    width = ret_ref.shape[1] - META
    pick = pick_ref[...]
    meta = meta_ref[...].astype(F32)
    total = dot(pick, ret_ref[:, :width], ROWS).astype(BF)
    rows = ret_ref.shape[0]
    owner = owner_of_row(rows, n_local, rows // n_local)
    grads = ret_ref[:, width:].astype(F32)
    high = jnp.where(owner, grads[:, 0:1], 0.0).astype(BF)
    low = jnp.where(owner, grads[:, 1:2], 0.0).astype(BF)
    by_expert = dot(pick, high, ROWS) + dot(pick, low, ROWS)
    base = (1 + lax.div(place_ref[0], 2) * n_local).astype(F32)
    lane = lax.broadcasted_iota(jnp.int32, meta.shape, 1)
    tail = jnp.zeros(meta.shape, F32)
    for k in range(top):
        hit = matches(meta, k, base, n_local) & (meta[:, SLOT + k : SLOT + k + 1] < CAP)
        value = jnp.sum(jnp.where(hit, by_expert, 0.0), axis=1, keepdims=True)
        tail = jnp.where(lane == k, value / meta[:, GATE + k : GATE + k + 1], tail)
    tail = tail.astype(BF)
    block = outs[0].shape[0]
    for m, out in enumerate(outs):
        out[:, :width] = total[m * block : (m + 1) * block]
        out[:, width:] = tail[m * block : (m + 1) * block]


def finish_kernel(place_ref, b0, b1, b2, b3, tokens_ref, gates_ref):
    half = tokens_ref.shape[1] // 2
    first = lax.rem(place_ref[0], 2) == 0
    own = b0[...].astype(F32) + b2[...].astype(F32)
    other = b1[:, :half].astype(F32) + b3[:, :half].astype(F32)
    mine = own[:, :half]
    tokens_ref[:, :half] = jnp.where(first, mine, other).astype(BF)
    tokens_ref[:, half:] = jnp.where(first, other, mine).astype(BF)
    lane = lax.broadcasted_iota(jnp.int32, (gates_ref.shape[0], META), 1)
    row = lax.broadcasted_iota(jnp.int32, (gates_ref.shape[0], META), 0)
    turn = jnp.where(lane == row, 1.0, 0.0).astype(BF)
    gates_ref[...] = dot(turn, own[:, half:].astype(BF), LAST).astype(BF)


def shape(*dims, dtype=BF):
    return jax.ShapeDtypeStruct(dims, dtype)


def shards(
    x_q,
    x_scale,
    cotangent,
    gates,
    experts,
    replicas,
    slots,
    w_gate_q,
    w_up_q,
    w_down_q,
    gate_scales,
    up_scales,
    down_scales,
):
    n_group = lax.axis_size("group")
    n_local = lax.axis_size("local")
    tok, width = x_q.shape
    top = experts.shape[1]
    half = width // 2
    hidden = w_gate_q.shape[2]
    column = n_group * tok
    rows = n_local * n_group * 4
    kept = 2 * CAP
    wide = half + META
    place = jnp.stack([lax.axis_index("group"), lax.axis_index("local")]).astype(jnp.int32)

    def across(block, apart):
        return lax.ppermute(block, "group", [(i, i ^ apart) for i in range(n_group)])

    def spread(block):
        return lax.all_to_all(block, "local", split_axis=0, concat_axis=0, tiled=True)

    same_x, other_x, same_dy, other_dy = call(
        prepare_kernel,
        (shape(tok, wide), shape(tok, wide), shape(tok, half), shape(tok, half)),
        (place, x_q, x_scale, cotangent, experts.T, replicas.T, slots.T, gates.T),
        limit=63,
        moved=tok * width * 8,
        grid=(1,),
        in_specs=[SMEM, whole(tok, width), whole(*x_scale.shape), whole(tok, width)]
        + [whole(top, tok)] * 4,
        out_specs=[whole(tok, wide)] * 2 + [whole(tok, half)] * 2,
    )
    near_x = [same_x, across(other_x, 1), across(same_x, 2), across(other_x, 3)]
    near_dy = [same_dy, across(other_dy, 1), across(same_dy, 2), across(other_dy, 3)]
    part = rows // 4
    by_row = lambda *dims: pl.BlockSpec(dims, lambda i: (i, 0))
    packed_x, pick, gated, column_meta = call(
        functools.partial(pack_x_kernel, n_local, top, rows // n_local),
        (shape(rows, wide), shape(rows, column), shape(rows, column), shape(column, META)),
        (place, *near_x),
        flops=2 * rows * column * wide,
        limit=24,
        moved=2 * rows * wide,
        grid=(4,),
        in_specs=[SMEM] + [whole(tok, wide)] * 4,
        out_specs=[by_row(part, wide), by_row(part, column), by_row(part, column), whole(column, META)],
        scratch_shapes=[
            pltpu.VMEM((column, wide), BF),
            pltpu.VMEM((column, n_local), BF),
            pltpu.VMEM((column, n_local), BF),
        ],
    )
    packed_dy = call(
        pack_dy_kernel,
        shape(rows, half),
        (gated, *near_dy),
        flops=2 * rows * column * half,
        limit=24,
        moved=2 * rows * half,
        grid=(4,),
        in_specs=[by_row(part, column)] + [whole(tok, half)] * 4,
        out_specs=by_row(part, half),
    )
    got_x = spread(packed_x)
    got_x, packed_dy = lax.optimization_barrier((got_x, packed_dy))
    got_dy = spread(packed_dy)

    weights = [w[:, 0, :] for w in (w_gate_q, w_up_q, w_down_q)]
    scales = [s[:, 0, :].T for s in (gate_scales, up_scales, down_scales)]
    cols = 256
    steps = hidden // cols
    by_col = lambda *dims: pl.BlockSpec(dims, lambda i: (0, i))
    rows_x, part_a, part_b, send_ab, slot_of = call(
        functools.partial(forward_kernel, n_local, top),
        (
            shape(kept, half),
            shape(kept, hidden, dtype=F32),
            shape(kept, hidden, dtype=F32),
            shape(2, kept, hidden),
            shape(kept, rows),
        ),
        (place, scales[0], scales[1], got_x, weights[0], weights[1]),
        flops=4 * kept * half * hidden,
        limit=63,
        moved=4 * half * hidden + 4 * rows * half,
        grid=(steps,),
        in_specs=[SMEM, SMEM, SMEM, whole(rows, wide), by_col(half, cols), by_col(half, cols)],
        out_specs=[
            whole(kept, half),
            by_col(kept, cols),
            by_col(kept, cols),
            pl.BlockSpec((2, kept, cols), lambda i: (0, 0, i)),
            whole(kept, rows),
        ],
        scratch_shapes=[pltpu.VMEM((half, cols), BF)] * 2,
    )
    their_ab = across(send_ab, 1)
    rows_dy, part_dh, send_dh = call(
        down_kernel,
        (shape(kept, half), shape(kept, hidden, dtype=F32), shape(kept, hidden)),
        (scales[2], slot_of, got_dy, weights[2]),
        flops=2 * kept * half * hidden,
        limit=63,
        moved=2 * half * hidden + 4 * rows * half,
        grid=(steps,),
        in_specs=[SMEM, whole(kept, rows), whole(rows, half), by_col(half, cols)],
        out_specs=[whole(kept, half), by_col(kept, cols), by_col(kept, cols)],
        scratch_shapes=[pltpu.VMEM((half, cols), BF)],
    )
    their_dh = across(send_dh, 1)
    chunk = 512
    d_a, d_b, hid, dx = call(
        backward_kernel,
        (shape(kept, hidden), shape(kept, hidden), shape(kept, hidden), shape(rows, wide)),
        (
            scales[0], scales[1], part_a, part_b, their_ab, part_dh, their_dh, slot_of,
            weights[0], weights[1],
        ),
        flops=4 * rows * half * hidden,
        limit=63,
        moved=4 * half * hidden + 2 * rows * half,
        grid=(half // chunk,),
        in_specs=[SMEM, SMEM]
        + [whole(kept, hidden), whole(kept, hidden), whole(2, kept, hidden)]
        + [whole(kept, hidden), whole(kept, hidden), whole(kept, rows)]
        + [by_row(chunk, hidden)] * 2,
        out_specs=[whole(kept, hidden)] * 3 + [whole(rows, wide)],
        scratch_shapes=[
            pltpu.VMEM((rows, 2 * hidden), BF),
            pltpu.VMEM((kept, META), BF),
            pltpu.VMEM((chunk, 2 * hidden), BF),
        ],
    )
    returned = spread(dx)
    grads = [
        dot(left, right, ROWS).astype(BF)
        for left, right in ((rows_x, d_a), (rows_x, d_b), (rows_dy, hid))
    ]
    blocks = call(
        functools.partial(combine_kernel, n_local, top),
        tuple(shape(tok, wide) for _ in range(n_group)),
        (place, returned, pick, column_meta),
        flops=2 * rows * column * half,
        limit=24,
        moved=2 * rows * half,
        grid=(1,),
        in_specs=[SMEM, whole(rows, wide), whole(rows, column), whole(column, META)],
        out_specs=[whole(tok, wide)] * n_group,
    )
    back = [blocks[0]] + [across(blocks[m], m) for m in range(1, n_group)]
    grad_tokens, grad_gates = call(
        finish_kernel,
        (shape(tok, width), shape(top, tok)),
        (place, *back),
        limit=24,
        moved=tok * width * 6,
        grid=(1,),
        in_specs=[SMEM] + [whole(tok, wide)] * 4,
        out_specs=[whole(tok, width), whole(top, tok)],
    )
    return (
        grad_tokens,
        grad_gates.T,
        grads[0][:, None, :],
        grads[1][:, None, :],
        grads[2][:, None, :],
    )


def solution(mesh):
    by_token = P(("group", "local"), None)
    by_expert = P("group", "local", None)
    return jax.shard_map(
        shards,
        mesh=mesh,
        in_specs=(by_token,) * 7 + (by_expert,) * 6,
        out_specs=(by_token,) * 2 + (by_expert,) * 3,
        check_vma=False,
    )
```

time: 198 us -> 178 us (0.90)
  local copies, waits for them, and re-layouts: 41.5 us -> 4.97 us
  waiting for transfers between devices: 57.3 us -> 87 us
  other arithmetic: 16.8 us -> 0.62 us
  Pallas kernels: 30.4 us -> 38.1 us
  starting transfers between devices: 37.1 us -> 33.6 us
    all_to_all x3, waiting for transfers between devices: 26.5 us -> 64.3 us  [spread(): lax.all_to_all(block, 'local', split_axis=0, concat_axis=0, tiled=True)]
    reshape x3 -> x0, local copies, waits for them, and re-layouts: 19.8 us -> none  [dequant_half(): scale = jnp.repeat(jnp.repeat(scales[:, 0, :], 128, axis=0), 128, axis=1)]
    convert_element_type x4 -> x0, other arithmetic: 16.6 us -> none  [the longest x2 15.9 us: dequant_half(): return (quant[:, 0, :].astype(F32) * scale).astype(BF)]
    broadcast_in_dim x4 -> x0, local copies, waits for them, and re-layouts: 10.3 us -> none  [the longest x3 10.3 us: dequant_half(): scale = jnp.repeat(jnp.repeat(scales[:, 0, :], 128, axis=0), 128, axis=1)]
    ppermute x11, waiting for transfers between devices: 30.8 us -> 22.7 us  [across(): lax.ppermute(block, 'group', [(i, i ^ apart) for i in range(n_group)])]
    pallas_call x8, Pallas kernels: 30.4 us -> 38.1 us  [call(): pl.pallas_call(kernel, out_shape=outs, compiler_params=pltpu.CompilerPara...]
    unnamed x43 -> x31, local copies, waits for them, and re-layouts: 11.3 us -> 4.36 us
    all_to_all x3, starting transfers between devices: 23.1 us -> 20.9 us  [spread(): lax.all_to_all(block, 'local', split_axis=0, concat_axis=0, tiled=True)]
  transfers between devices with their start and end apart: 14 -> 14, of which waited for: 6 -> 10; matrix products, arithmetic and copies ran while one was open for 30% -> 7% of each run, Pallas kernels for 8% -> 10%
where the time goes in v2:
time: 178 us; the launch traced here: 177 us
  waiting for transfers between devices  87 us (49%)
  Pallas kernels  38.1 us (21%)
  starting transfers between devices  33.6 us (19%)
  matrix products  12.1 us (7%)
  local copies, waits for them, and re-layouts  4.97 us (3%)
    all_to_all x3, waiting for transfers between devices, spread(): lax.all_to_all(block, 'local', split_axis=0, concat_axis=0, tiled=True)  64.3 us
    pallas_call x8, Pallas kernels, call(): pl.pallas_call(kernel, out_shape=outs, compiler_params=pltpu.CompilerPara...  38.1 us
    ppermute x11, waiting for transfers between devices, across(): lax.ppermute(block, 'group', [(i, i ^ apart) for i in range(n_group)])  22.7 us
    all_to_all x3, starting transfers between devices, spread(): lax.all_to_all(block, 'local', split_axis=0, concat_axis=0, tiled=True)  20.9 us
    ppermute x11, starting transfers between devices, across(): lax.ppermute(block, 'group', [(i, i ^ apart) for i in range(n_group)])  12.7 us
    dot_general x3, matrix products, dot(): return lax.dot_general(left, right, dims, preferred_element_type=F32)  12.1 us
    unnamed x31, local copies, waits for them, and re-layouts  4.36 us
  transfers between devices with their start and end apart: 14, of which 10 were waited for; matrix products, arithmetic and copies ran while one was open for 7% of the time, Pallas kernels for 10%

profile of v2, /device:TPU:0, one launch (start us, length us, event | category | flops | bytes accessed | tf_op | source)
XLA Modules:
  0.0 177.1 jit_solution(15375242105520918752)
XLA Ops:
  1.3 1.9 %shard_map.164 = (bf16[16,2176]{1,0:T(8,128)(2,1)}, bf16[16,2176]{1,0:T(8,128)(2,1)}, bf16[16,2048]{1,0:T(8,128)(2,1)}, bf16[16,2048]{1,0:T(8,128)(2,1)}) custom-call(s32[2]{0:T(128)} %pad_add_fusion.place_ref, bf16[16,4096]{1,0:T(8,128)(2,1)} %xq_ref.1, f32[16,32]{1,0:T(8,128)} %xs_ref.1, bf16[16,4096]{1,0:T(8,128)(2,1)} %dy_ref.1, s32[8,16]{1,0:T(8,128)} %bitcast.50, ...), custom_call_target="tpu_custom_call" | custom-call | bytes 524288 | tf_op jit(solution)/shard_map/pallas_call | solution.py:26
  3.1 3.1 %collective-permute-start.1 = (bf16[16,2176]{1,0:T(8,128)(2,1)}, bf16[16,2176]{1,0:T(8,128)(2,1)S(1)}, u32[]{:S(2)}, u32[]{:S(2)}) collective-permute-start(bf16[16,2176]{1,0:T(8,128)(2,1)} %get-tuple-element.33.b0), channel_id=1, source_target_pairs={{0,64},{32,96},{64,0},{96,32},{1,65},{33,97},{65,1},{97,33},{2,66}... | collective-permute-start | bytes 208904 | tf_op jit(solution)/shard_map/ppermute | solution.py:298
  7.4 1.8 %collective-permute-done.1.b2 = bf16[16,2176]{1,0:T(8,128)(2,1)S(1)} collective-permute-done((bf16[16,2176]{1,0:T(8,128)(2,1)}, bf16[16,2176]{1,0:T(8,128)(2,1)S(1)}, u32[]{:S(2)}, u32[]{:S(2)}) %collective-permute-start.1) | collective-permute-done | bytes 69664 | tf_op jit(solution)/shard_map/ppermute | solution.py:298
  9.2 2.8 %collective-permute-done.2.b3 = bf16[16,2176]{1,0:T(8,128)(2,1)S(1)} collective-permute-done((bf16[16,2176]{1,0:T(8,128)(2,1)}, bf16[16,2176]{1,0:T(8,128)(2,1)S(1)}, u32[]{:S(2)}, u32[]{:S(2)}) %collective-permute-start.2) | collective-permute-done | bytes 69664 | tf_op jit(solution)/shard_map/ppermute | solution.py:298
  13.5 3.9 %shard_map.165 = (bf16[512,2176]{1,0:T(8,128)(2,1)}, bf16[512,64]{1,0:T(8,128)(2,1)S(1)}, bf16[512,64]{1,0:T(8,128)(2,1)S(1)}, bf16[64,128]{1,0:T(8,128)(2,1)S(1)}) custom-call(s32[2]{0:T(128)S(1)} %copy-done.1, bf16[16,2176]{1,0:T(8,128)(2,1)S(1)} %copy-done.3, bf16[16,2176]{1,0:T(8,128)(2,1)S(1)} %collective-permute-done.b1, ...), custom_call_target="tpu_custom_call" | custom-call | flops 142606336 | bytes 2228224 | tf_op jit(solution)/shard_map/pallas_call | solution.py:26
  17.4 8.5 %all-to-all-start = ((bf16[32,16,2176]{2,1,0:T(8,128)(2,1)}), bf16[32,16,2176]{2,1,0:T(8,128)(2,1)S(1)}, u32[]{:S(2)}, u32[]{:S(2)}) async-start(bf16[32,16,2176]{2,1,0:T(8,128)(2,1)} %bitcast.8), calls=%async_computation | async-start | bytes 4456448 | tf_op jit(solution)/shard_map/all_to_all | solution.py:301
  25.9 1.6 collective-permute-start.4
  29.5 2.3 %collective-permute-done.4.b2 = bf16[16,2048]{1,0:T(8,128)(2,1)S(1)} collective-permute-done((bf16[16,2048]{1,0:T(8,128)(2,1)S(1)}, bf16[16,2048]{1,0:T(8,128)(2,1)S(1)}, u32[]{:S(2)}, u32[]{:S(2)}) %collective-permute-start.4) | collective-permute-done | bytes 65568 | tf_op jit(solution)/shard_map/ppermute | solution.py:298
  33.2 2.4 %shard_map.166 = bf16[512,2048]{1,0:T(8,128)(2,1)} custom-call(bf16[512,64]{1,0:T(8,128)(2,1)S(1)} %get-tuple-element.36.gated_ref, bf16[16,2048]{1,0:T(8,128)(2,1)S(1)} %copy-done, bf16[16,2048]{1,0:T(8,128)(2,1)S(1)} %collective-permute-done.3.b1, bf16[16,2048]{1,0:T(8,128)(2,1)S(1)} %collective-permute-done.4.b2, ...), custom_call_target="tpu_custom_call" | custom-call | flops 134217728 | bytes 2097152 | tf_op jit(solution)/shard_map/pallas_call | solution.py:26
  35.6 21.9 %all-to-all-done = bf16[32,16,2176]{2,1,0:T(8,128)(2,1)S(1)} async-done(((bf16[32,16,2176]{2,1,0:T(8,128)(2,1)}), bf16[32,16,2176]{2,1,0:T(8,128)(2,1)S(1)}, u32[]{:S(2)}, u32[]{:S(2)}) %all-to-all-start) | async-done | bytes 2228256 | tf_op jit(solution)/shard_map/all_to_all | solution.py:301
  57.5 1.4 copy-done.4
  58.8 4.8 %all-to-all-start.1 = ((bf16[32,16,2048]{2,1,0:T(8,128)(2,1)}), bf16[32,16,2048]{2,1,0:T(8,128)(2,1)}, u32[]{:S(2)}, u32[]{:S(2)}) async-start(bf16[32,16,2048]{2,1,0:T(8,128)(2,1)} %bitcast.13), calls=%async_computation.1 | async-start | bytes 4194304 | tf_op jit(solution)/shard_map/all_to_all | solution.py:301
  64.2 9.0 %shard_map.167 = (bf16[384,2048]{1,0:T(8,128)(2,1)}, f32[384,768]{1,0:T(8,128)}, f32[384,768]{1,0:T(8,128)}, bf16[2,384,768]{2,1,0:T(8,128)(2,1)}, bf16[384,512]{1,0:T(8,128)(2,1)}) custom-call(s32[2]{0:T(128)} %pad_add_fusion.place_ref, f32[6,16]{1,0:T(8,128)} %get-tuple-element.62.sg_ref, f32[6,16]{1,0:T(8,128)} %get-tuple-element.61.su_ref, ...), custom_call_target="tpu_custom_call" | custom-call | flops 2415919104 | bytes 10485760 | tf_op jit(solution)/shard_map/pallas_call | solution.py:26
  73.9 19.7 %all-to-all-done.1 = bf16[32,16,2048]{2,1,0:T(8,128)(2,1)} async-done(((bf16[32,16,2048]{2,1,0:T(8,128)(2,1)}), bf16[32,16,2048]{2,1,0:T(8,128)(2,1)}, u32[]{:S(2)}, u32[]{:S(2)}) %all-to-all-start.1) | async-done | bytes 2097184 | tf_op jit(solution)/shard_map/all_to_all | solution.py:301
  93.5 6.8 %shard_map.168 = (bf16[384,2048]{1,0:T(8,128)(2,1)}, f32[384,768]{1,0:T(8,128)}, bf16[384,768]{1,0:T(8,128)(2,1)}) custom-call(f32[6,16]{1,0:T(8,128)} %bitcast.49, bf16[384,512]{1,0:T(8,128)(2,1)} %get-tuple-element.43.slot_ref, bf16[512,2048]{1,0:T(8,128)(2,1)} %bitcast.14.dy_ref, bf16[2048,768]{1,0:T(8,128)(2,1)} %bitcast.42), custom_call_target="tpu_custom_call" | custom-call | flops 1207959552 | bytes 7340032 | tf_op jit(solution)/shard_map/pallas_call | solution.py:26
  101.6 12.5 %collective-permute-done.7.dh_in = bf16[384,768]{1,0:T(8,128)(2,1)S(1)} collective-permute-done((bf16[384,768]{1,0:T(8,128)(2,1)}, bf16[384,768]{1,0:T(8,128)(2,1)S(1)}, u32[]{:S(2)}, u32[]{:S(2)}) %collective-permute-start.7) | collective-permute-done | bytes 589856 | tf_op jit(solution)/shard_map/ppermute | solution.py:298
  114.9 11.1 %shard_map.169 = (bf16[384,768]{1,0:T(8,128)(2,1)}, bf16[384,768]{1,0:T(8,128)(2,1)}, bf16[384,768]{1,0:T(8,128)(2,1)}, bf16[512,2176]{1,0:T(8,128)(2,1)}) custom-call(f32[6,16]{1,0:T(8,128)} %get-tuple-element.62.sg_ref, f32[6,16]{1,0:T(8,128)} %get-tuple-element.61.su_ref, f32[384,768]{1,0:T(8,128)} %get-tuple-element.40.a_ref, ...), custom_call_target="tpu_custom_call" | custom-call | flops 3221225472 | bytes 8388608 | tf_op jit(solution)/shard_map/pallas_call | solution.py:26
  126.0 7.7 %all-to-all-start.2 = ((bf16[32,16,2176]{2,1,0:T(8,128)(2,1)}), bf16[32,16,2176]{2,1,0:T(8,128)(2,1)S(1)}, u32[]{:S(2)}, u32[]{:S(2)}) async-start(bf16[32,16,2176]{2,1,0:T(8,128)(2,1)} %bitcast.48), calls=%async_computation.2 | async-start | bytes 4456448 | tf_op jit(solution)/shard_map/all_to_all | solution.py:301
  133.8 5.1 %fusion = bf16[2048,1,768]{2,0,1:T(8,128)(2,1)} fusion(bf16[384,2048]{1,0:T(8,128)(2,1)} %get-tuple-element.56, bf16[384,768]{1,0:T(8,128)(2,1)S(1)} %copy-done.12), kind=kOutput, calls=%fused_computation.3 | convolution fusion | flops 1209532416 | bytes 5308416 | tf_op jit(solution)/shard_map/dot_general | solution.py:22
  138.8 3.5 %fusion.1 = bf16[2048,1,768]{2,0,1:T(8,128)(2,1)} fusion(bf16[384,2048]{1,0:T(8,128)(2,1)S(1)} %copy-done.14, bf16[384,768]{1,0:T(8,128)(2,1)S(1)} %copy-done.11), kind=kOutput, calls=%fused_computation.4 | convolution fusion | flops 1209532416 | bytes 5308416 | tf_op jit(solution)/shard_map/dot_general | solution.py:22
  142.3 22.8 %all-to-all-done.2 = bf16[32,16,2176]{2,1,0:T(8,128)(2,1)S(1)} async-done(((bf16[32,16,2176]{2,1,0:T(8,128)(2,1)}), bf16[32,16,2176]{2,1,0:T(8,128)(2,1)S(1)}, u32[]{:S(2)}, u32[]{:S(2)}) %all-to-all-start.2) | async-done | bytes 2228256 | tf_op jit(solution)/shard_map/all_to_all | solution.py:301
  165.1 1.6 shard_map.170
  167.1 3.2 %collective-permute-start.9 = (bf16[16,2176]{1,0:T(8,128)(2,1)S(1)}, bf16[16,2176]{1,0:T(8,128)(2,1)S(1)}, u32[]{:S(2)}, u32[]{:S(2)}) collective-permute-start(bf16[16,2176]{1,0:T(8,128)(2,1)S(1)} %get-tuple-element.52), channel_id=1, source_target_pairs={{0,64},{32,96},{64,0},{96,32},{1,65},{33,97},{65,1},{97,33},{2,66}... | collective-permute-start | bytes 208904 | tf_op jit(solution)/shard_map/ppermute | solution.py:298
  171.5 3.5 %fusion.2 = bf16[2048,1,768]{2,0,1:T(8,128)(2,1)} fusion(bf16[384,2048]{1,0:T(8,128)(2,1)S(1)} %copy-done.9, bf16[384,768]{1,0:T(8,128)(2,1)S(1)} %copy-done.10), kind=kOutput, calls=%fused_computation.5 | convolution fusion | flops 1209532416 | bytes 5308416 | tf_op jit(solution)/shard_map/dot_general | solution.py:22
  (48 shorter events, 13.5 us)
Async XLA Ops:
  3.1 6.0 %collective-permute-start.1 = (bf16[16,2176]{1,0:T(8,128)(2,1)}, bf16[16,2176]{1,0:T(8,128)(2,1)S(1)}, u32[]{:S(2)}, u32[]{:S(2)}) collective-permute-start(bf16[16,2176]{1,0:T(8,128)(2,1)} %get-tuple-element.33.b0), channel_id=1, source_target_pairs={{0,64},{32,96},{64,0},{96,32},{1,65},{33,97},{65,1},{97,33},{2,66}... | collective-permute-start | bytes 208904 | tf_op jit(solution)/shard_map/ppermute | solution.py:298
  6.3 5.7 %collective-permute-start.2 = (bf16[16,2176]{1,0:T(8,128)(2,1)}, bf16[16,2176]{1,0:T(8,128)(2,1)S(1)}, u32[]{:S(2)}, u32[]{:S(2)}) collective-permute-start(bf16[16,2176]{1,0:T(8,128)(2,1)} %get-tuple-element.34), channel_id=1, source_target_pairs={{0,96},{32,64},{64,32},{96,0},{1,97},{33,65},{65,33},{97,1},{2,98}... | collective-permute-start | bytes 208904 | tf_op jit(solution)/shard_map/ppermute | solution.py:298
  7.4 4.6 %collective-permute-start = (bf16[16,2176]{1,0:T(8,128)(2,1)}, bf16[16,2176]{1,0:T(8,128)(2,1)S(1)}, u32[]{:S(2)}, u32[]{:S(2)}) collective-permute-start(bf16[16,2176]{1,0:T(8,128)(2,1)} %get-tuple-element.34), channel_id=1, source_target_pairs={{0,32},{32,0},{64,96},{96,64},{1,33},{33,1},{65,97},{97,65},{2,34}... | collective-permute-start | bytes 208904 | tf_op jit(solution)/shard_map/ppermute | solution.py:298
  17.4 8.5 %copy-start = (bf16[16,2048]{1,0:T(8,128)(2,1)S(1)}, bf16[16,2048]{1,0:T(8,128)(2,1)}, u32[]{:S(2)}) copy-start(bf16[16,2048]{1,0:T(8,128)(2,1)} %get-tuple-element.37.b0) | copy-start | bytes 196612
  17.4 10.1 %copy-start.13 = (bf16[16,2048]{1,0:T(8,128)(2,1)S(1)}, bf16[16,2048]{1,0:T(8,128)(2,1)}, u32[]{:S(2)}) copy-start(bf16[16,2048]{1,0:T(8,128)(2,1)} %get-tuple-element.38) | copy-start | bytes 196612
  17.4 40.0 %all-to-all-start = ((bf16[32,16,2176]{2,1,0:T(8,128)(2,1)}), bf16[32,16,2176]{2,1,0:T(8,128)(2,1)S(1)}, u32[]{:S(2)}, u32[]{:S(2)}) async-start(bf16[32,16,2176]{2,1,0:T(8,128)(2,1)} %bitcast.8), calls=%async_computation | async-start | bytes 4456448 | tf_op jit(solution)/shard_map/all_to_all | solution.py:301
  25.9 5.9 %collective-permute-start.4 = (bf16[16,2048]{1,0:T(8,128)(2,1)S(1)}, bf16[16,2048]{1,0:T(8,128)(2,1)S(1)}, u32[]{:S(2)}, u32[]{:S(2)}) collective-permute-start(bf16[16,2048]{1,0:T(8,128)(2,1)S(1)} %copy-done), channel_id=1, source_target_pairs={{0,64},{32,96},{64,0},{96,32},{1,65},{33,97},{65,1},{97,33},{2,66}... | collective-permute-start | bytes 196616 | tf_op jit(solution)/shard_map/ppermute | solution.py:298
  27.5 5.7 %collective-permute-start.5 = (bf16[16,2048]{1,0:T(8,128)(2,1)S(1)}, bf16[16,2048]{1,0:T(8,128)(2,1)S(1)}, u32[]{:S(2)}, u32[]{:S(2)}) collective-permute-start(bf16[16,2048]{1,0:T(8,128)(2,1)S(1)} %copy-done.13), channel_id=1, source_target_pairs={{0,96},{32,64},{64,32},{96,0},{1,97},{33,65},{65,33},{97,1},{2,98}... | collective-permute-start | bytes 196616 | tf_op jit(solution)/shard_map/ppermute | solution.py:298
  28.7 4.5 %collective-permute-start.3 = (bf16[16,2048]{1,0:T(8,128)(2,1)S(1)}, bf16[16,2048]{1,0:T(8,128)(2,1)S(1)}, u32[]{:S(2)}, u32[]{:S(2)}) collective-permute-start(bf16[16,2048]{1,0:T(8,128)(2,1)S(1)} %copy-done.13), channel_id=1, source_target_pairs={{0,32},{32,0},{64,96},{96,64},{1,33},{33,1},{65,97},{97,65},{2,34}... | collective-permute-start | bytes 196616 | tf_op jit(solution)/shard_map/ppermute | solution.py:298
  57.5 6.1 %copy-start.6 = (f32[16,1,6]{0,1,2:T(1,128)S(1)}, f32[16,1,6]{0,1,2:T(1,128)}, u32[]{:S(2)}) copy-start(f32[16,1,6]{0,1,2:T(1,128)} %param.24) | copy-start | bytes 1156
  57.5 6.1 %copy-start.7 = (f32[16,1,6]{0,1,2:T(1,128)S(1)}, f32[16,1,6]{0,1,2:T(1,128)}, u32[]{:S(2)}) copy-start(f32[16,1,6]{0,1,2:T(1,128)} %param.23) | copy-start | bytes 1156
  58.8 34.7 %all-to-all-start.1 = ((bf16[32,16,2048]{2,1,0:T(8,128)(2,1)}), bf16[32,16,2048]{2,1,0:T(8,128)(2,1)}, u32[]{:S(2)}, u32[]{:S(2)}) async-start(bf16[32,16,2048]{2,1,0:T(8,128)(2,1)} %bitcast.13), calls=%async_computation.1 | async-start | bytes 4194304 | tf_op jit(solution)/shard_map/all_to_all | solution.py:301
  64.2 9.1 %copy-start.8 = (f32[16,1,6]{0,1,2:T(1,128)S(1)}, f32[16,1,6]{0,1,2:T(1,128)}, u32[]{:S(2)}) copy-start(f32[16,1,6]{0,1,2:T(1,128)} %param.25) | copy-start | bytes 1156
  73.2 28.3 %collective-permute-start.6 = (bf16[2,384,768]{2,1,0:T(8,128)(2,1)}, bf16[2,384,768]{2,1,0:T(8,128)(2,1)}, u32[]{:S(2)}, u32[]{:S(2)}) collective-permute-start(bf16[2,384,768]{2,1,0:T(8,128)(2,1)} %get-tuple-element.42), channel_id=1, source_target_pairs={{0,32},{32,0},{64,96},{96,64},{1,33},{33,1},{65,97},{97,65},{2,34}... | collective-permute-start | bytes 3538952 | tf_op jit(solution)/shard_map/ppermute | solution.py:298
  100.4 13.7 %collective-permute-start.7 = (bf16[384,768]{1,0:T(8,128)(2,1)}, bf16[384,768]{1,0:T(8,128)(2,1)S(1)}, u32[]{:S(2)}, u32[]{:S(2)}) collective-permute-start(bf16[384,768]{1,0:T(8,128)(2,1)} %get-tuple-element.46), channel_id=1, source_target_pairs={{0,32},{32,0},{64,96},{96,64},{1,33},{33,1},{65,97},{97,65},{2,34}... | collective-permute-start | bytes 1769480 | tf_op jit(solution)/shard_map/ppermute | solution.py:298
  126.0 7.7 %copy-start.12 = (bf16[384,768]{1,0:T(8,128)(2,1)S(1)}, bf16[384,768]{1,0:T(8,128)(2,1)}, u32[]{:S(2)}) copy-start(bf16[384,768]{1,0:T(8,128)(2,1)} %get-tuple-element.57) | copy-start | bytes 1769476
  126.0 39.1 %all-to-all-start.2 = ((bf16[32,16,2176]{2,1,0:T(8,128)(2,1)}), bf16[32,16,2176]{2,1,0:T(8,128)(2,1)S(1)}, u32[]{:S(2)}, u32[]{:S(2)}) async-start(bf16[32,16,2176]{2,1,0:T(8,128)(2,1)} %bitcast.48), calls=%async_computation.2 | async-start | bytes 4456448 | tf_op jit(solution)/shard_map/all_to_all | solution.py:301
  133.7 5.1 %copy-start.11 = (bf16[384,768]{1,0:T(8,128)(2,1)S(1)}, bf16[384,768]{1,0:T(8,128)(2,1)}, u32[]{:S(2)}) copy-start(bf16[384,768]{1,0:T(8,128)(2,1)} %get-tuple-element.58) | copy-start | bytes 1769476
  138.8 26.3 %copy-start.2 = (s32[2]{0:T(128)S(1)}, s32[2]{0:T(128)}, u32[]{:S(2)}) copy-start(s32[2]{0:T(128)} %pad_add_fusion.place_ref) | copy-start | bytes 28
  142.3 29.2 %copy-start.10 = (bf16[384,768]{1,0:T(8,128)(2,1)S(1)}, bf16[384,768]{1,0:T(8,128)(2,1)}, u32[]{:S(2)}) copy-start(bf16[384,768]{1,0:T(8,128)(2,1)} %get-tuple-element.60) | copy-start | bytes 1769476
  165.1 6.4 %copy-start.9 = (bf16[384,2048]{1,0:T(8,128)(2,1)S(1)}, bf16[384,2048]{1,0:T(8,128)(2,1)}, u32[]{:S(2)}) copy-start(bf16[384,2048]{1,0:T(8,128)(2,1)} %get-tuple-element.59) | copy-start | bytes 4718596
  166.8 8.3 %collective-permute-start.8 = (bf16[16,2176]{1,0:T(8,128)(2,1)S(1)}, bf16[16,2176]{1,0:T(8,128)(2,1)S(1)}, u32[]{:S(2)}, u32[]{:S(2)}) collective-permute-start(bf16[16,2176]{1,0:T(8,128)(2,1)S(1)} %get-tuple-element.51), channel_id=1, source_target_pairs={{0,32},{32,0},{64,96},{96,64},{1,33},{33,1},{65,97},{97,65},{2,34}... | collective-permute-start | bytes 208904 | tf_op jit(solution)/shard_map/ppermute | solution.py:298
  167.1 7.9 %collective-permute-start.9 = (bf16[16,2176]{1,0:T(8,128)(2,1)S(1)}, bf16[16,2176]{1,0:T(8,128)(2,1)S(1)}, u32[]{:S(2)}, u32[]{:S(2)}) collective-permute-start(bf16[16,2176]{1,0:T(8,128)(2,1)S(1)} %get-tuple-element.52), channel_id=1, source_target_pairs={{0,64},{32,96},{64,0},{96,32},{1,65},{33,97},{65,1},{97,33},{2,66}... | collective-permute-start | bytes 208904 | tf_op jit(solution)/shard_map/ppermute | solution.py:298
  170.3 5.5 %collective-permute-start.10 = (bf16[16,2176]{1,0:T(8,128)(2,1)S(1)}, bf16[16,2176]{1,0:T(8,128)(2,1)S(1)}, u32[]{:S(2)}, u32[]{:S(2)}) collective-permute-start(bf16[16,2176]{1,0:T(8,128)(2,1)S(1)} %get-tuple-element.53), channel_id=1, source_target_pairs={{0,96},{32,64},{64,32},{96,0},{1,97},{33,65},{65,33},{97,1},{2,98}... | collective-permute-start | bytes 208904 | tf_op jit(solution)/shard_map/ppermute | solution.py:298
  (5 other events, 8.8 us)

commit v3 on v2

v3 whole, which is shorter than its diff:
```python
import functools

import jax
import jax.numpy as jnp
from jax import lax
from jax.experimental import pallas as pl
from jax.experimental.pallas import tpu as pltpu
from jax.sharding import PartitionSpec as P

CAP = 192
META = 128
CODE, SLOT, GATE = 0, 8, 16
BF = jnp.bfloat16
F32 = jnp.float32
MIB = 1024 * 1024
LIMIT = 24
LIMIT_FORWARD = 50
LIMIT_DOWN = 50
LIMIT_BACKWARD = 50

ROWS = (((0,), (0,)), ((), ()))
LAST = (((1,), (1,)), ((), ()))


def dot(left, right, dims=(((1,), (0,)), ((), ()))):
    return lax.dot_general(left, right, dims, preferred_element_type=F32)


def call(kernel, outs, args, limit, flops=0, moved=0, **kw):
    return pl.pallas_call(
        kernel,
        out_shape=outs,
        compiler_params=pltpu.CompilerParams(vmem_limit_bytes=limit * MIB),
        cost_estimate=pl.CostEstimate(flops=flops, bytes_accessed=moved, transcendentals=0),
        **kw,
    )(*args)


SMEM = pl.BlockSpec(memory_space=pltpu.SMEM)
VMEM = pl.BlockSpec(memory_space=pltpu.VMEM)
HBM = pl.BlockSpec(memory_space=pltpu.HBM)
SEMS = pltpu.SemaphoreType.DMA


def whole(*dims):
    return pl.BlockSpec(dims, lambda i: (0,) * len(dims))


def placed(source, offset):
    lane = lax.broadcasted_iota(jnp.int32, (source.shape[0], META), 1)
    row = lax.broadcasted_iota(jnp.int32, (source.shape[0], META), 0)
    return dot(source.astype(BF), jnp.where(lane == row + offset, 1.0, 0.0).astype(BF), ROWS)


def prepare_kernel(
    xq_ref, xs_ref, dy_ref, e_ref, r_ref, s_ref, g_ref, same_x, other_x, same_dy, other_dy
):
    half = xq_ref.shape[1] // 2
    blocks = half // 128
    first = lax.rem(lax.axis_index("group"), 2) == 0
    code = (1 + e_ref[...] + 64 * r_ref[...]).astype(F32)
    meta = placed(code, CODE) + placed(s_ref[...].astype(F32), SLOT) + placed(g_ref[...], GATE)
    same_x[:, half:] = meta.astype(BF)
    other_x[:, half:] = meta.astype(BF)
    for c in range(blocks):
        low, high = c * 128, half + c * 128
        x_low = (xq_ref[:, low : low + 128].astype(F32) * xs_ref[:, c : c + 1]).astype(BF)
        x_high = (
            xq_ref[:, high : high + 128].astype(F32) * xs_ref[:, blocks + c : blocks + c + 1]
        ).astype(BF)
        same_x[:, low : low + 128] = jnp.where(first, x_low, x_high)
        other_x[:, low : low + 128] = jnp.where(first, x_high, x_low)
    dy_low, dy_high = dy_ref[:, :half], dy_ref[:, half:]
    same_dy[...] = jnp.where(first, dy_low, dy_high)
    other_dy[...] = jnp.where(first, dy_high, dy_low)


def matches(meta, k, base, count):
    lane = lax.broadcasted_iota(jnp.int32, (meta.shape[0], count), 1).astype(F32)
    code = meta[:, CODE + k : CODE + k + 1] - base
    return (code == lane) | (code - 64.0 == lane)


def owner_of_row(rows, count, per, start=0):
    row = lax.broadcasted_iota(jnp.int32, (rows, count), 0) + start
    lane = lax.broadcasted_iota(jnp.int32, (rows, count), 1)
    return lax.div(row, per) == lane


def pack_x_kernel(
    n_local, top, per, b0, b1, b2, b3, out_hbm, pick_ref, gated_ref, meta_out, tokens, out, sems
):
    half = b0.shape[1] - META
    count = tokens.shape[0]
    block = b0.shape[0]
    for m, b in enumerate((b0, b1, b2, b3)):
        tokens[m * block : (m + 1) * block] = b[...]
    meta_out[...] = tokens[:, half:]
    lane = lax.broadcasted_iota(jnp.int32, (4 * top, META), 1)
    row = lax.broadcasted_iota(jnp.int32, (4 * top, META), 0)
    turn = jnp.where(lane == row, 1.0, 0.0).astype(BF)
    meta = dot(turn, tokens[:, half:], LAST)
    base = (1 + lax.div(lax.axis_index("group"), 2) * n_local).astype(F32)
    expert = lax.broadcasted_iota(jnp.int32, (n_local, count), 0).astype(F32) + base
    named = jnp.zeros((n_local, count), F32)
    gate = jnp.zeros((n_local, count), F32)
    for k in range(top):
        code = meta[CODE + k : CODE + k + 1]
        kept = meta[SLOT + k : SLOT + k + 1] < CAP
        hit = ((code == expert) | (code - 64.0 == expert)) & kept
        named = jnp.where(hit, 1.0, named)
        gate = jnp.where(hit, meta[GATE + k : GATE + k + 1], gate)
    row = lax.broadcasted_iota(jnp.int32, (count, count), 0)
    col = lax.broadcasted_iota(jnp.int32, (count, count), 1)
    before = jnp.where(row < col, 1.0, 0.0).astype(BF)
    rank = jnp.where(named > 0.0, dot(named.astype(BF), before), -1.0)
    position = lax.broadcasted_iota(jnp.int32, (per, count), 0).astype(F32)
    part = out.shape[0] // sems.shape[0]
    copies = []
    for j in range(n_local):
        at = slice(j * per, (j + 1) * per)
        hit = rank[j : j + 1] == position
        pick_ref[at] = jnp.where(hit, 1.0, 0.0).astype(BF)
        gated_ref[at] = jnp.where(hit, gate[j : j + 1], 0.0).astype(BF)
        if (j + 1) * per % part == 0:
            at = slice((j + 1) * per - part, (j + 1) * per)
            out[at] = dot(pick_ref[at], tokens[...]).astype(BF)
            copies.append(
                pltpu.make_async_copy(out.at[at], out_hbm.at[at], sems.at[len(copies)])
            )
            copies[-1].start()
    for copy in copies:
        copy.wait()


def pack_dy_kernel(gated_ref, b0, b1, b2, b3, out_hbm, out, sems):
    tokens = jnp.concatenate([b[...] for b in (b0, b1, b2, b3)], axis=0)
    part = out.shape[0] // sems.shape[0]
    copies = []
    for i in range(sems.shape[0]):
        at = slice(i * part, (i + 1) * part)
        out[at] = dot(gated_ref[at], tokens).astype(BF)
        copies.append(pltpu.make_async_copy(out.at[at], out_hbm.at[at], sems.at[i]))
        copies[-1].start()
    for copy in copies:
        copy.wait()


def dequant(quant_ref, scales_ref, out_ref, row, col, rows, cols, at_col=0):
    for c in range(cols // 128):
        for r in range(rows // 128):
            top, left = row + r * 128, col + c * 128
            factor = jnp.full((1, 16, 128), scales_ref[left // 128, top // 128], F32).astype(BF)
            block = quant_ref[top : top + 128, left : left + 128].reshape(8, 16, 128) * factor
            out_ref[r * 128 : (r + 1) * 128, at_col + c * 128 : at_col + (c + 1) * 128] = (
                block.reshape(128, 128)
            )


def fetch(source, target, sems, pieces):
    copies = [
        pltpu.make_async_copy(source.at[piece], target.at[piece], sems.at[i])
        for i, piece in enumerate(pieces)
    ]
    for copy in copies:
        copy.start()
    return copies


def columns(count, size):
    return [(slice(None), slice(c, c + size)) for c in range(0, count, size)]


def forward_kernel(
    n_local, top, cols, sg_ref, su_ref, x_ref, wg_hbm, wu_hbm,
    kept_hbm, send_ref, slot_ref, kept, wg_raw, wu_raw, wg, wu, sems_g, sems_u, sem_k,
):
    half, hidden = wg_raw.shape
    ready_g = fetch(wg_hbm, wg_raw, sems_g, columns(hidden, cols))
    ready_u = fetch(wu_hbm, wu_raw, sems_u, columns(hidden, cols))
    lane = lax.broadcasted_iota(jnp.int32, (2 * top, META), 1)
    row = lax.broadcasted_iota(jnp.int32, (2 * top, META), 0)
    turn = jnp.where(lane == row, 1.0, 0.0).astype(BF)
    meta = dot(turn, x_ref[:, half:], LAST)
    own = (
        1 + lax.div(lax.axis_index("group"), 2) * n_local + lax.axis_index("local")
    ).astype(F32)
    target = jnp.full((1, meta.shape[1]), -1.0, F32)
    for k in range(top):
        code = meta[CODE + k : CODE + k + 1]
        slot = meta[SLOT + k : SLOT + k + 1]
        target = jnp.where(code == own, slot, target)
        target = jnp.where(code == own + 64.0, slot + CAP, target)
    row = lax.broadcasted_iota(jnp.int32, slot_ref.shape, 0).astype(F32)
    slot_ref[...] = jnp.where(row == target, 1.0, 0.0).astype(BF)
    for c in range(0, half, 512):
        kept[:, c : c + 512] = dot(slot_ref[...], x_ref[:, c : c + 512]).astype(BF)
    save = pltpu.make_async_copy(kept, kept_hbm, sem_k)
    save.start()
    for i, c in enumerate(range(0, hidden, cols)):
        at = slice(c, c + cols)
        ready_g[i].wait()
        dequant(wg_raw, sg_ref, wg, 0, c, half, cols)
        send_ref[0, :, at] = dot(kept[...], wg[...]).astype(BF)
        ready_u[i].wait()
        dequant(wu_raw, su_ref, wu, 0, c, half, cols)
        send_ref[1, :, at] = dot(kept[...], wu[...]).astype(BF)
    save.wait()


def down_kernel(
    cols, sv_ref, slot_ref, dy_ref, v_hbm, kept_hbm, send_ref, kept, v_raw, v, sems_v, sem_k
):
    half, hidden = v_raw.shape
    ready = fetch(v_hbm, v_raw, sems_v, columns(hidden, cols))
    for c in range(0, half, 512):
        kept[:, c : c + 512] = dot(slot_ref[...], dy_ref[:, c : c + 512]).astype(BF)
    save = pltpu.make_async_copy(kept, kept_hbm, sem_k)
    save.start()
    for i, c in enumerate(range(0, hidden, cols)):
        ready[i].wait()
        dequant(v_raw, sv_ref, v, 0, c, half, cols)
        send_ref[:, c : c + cols] = dot(kept[...], v[...]).astype(BF)
    save.wait()


def backward_kernel(
    chunk, sg_ref, su_ref, ab_ref, ab_in, dh_ref, dh_in, slot_ref, wg_hbm, wu_hbm,
    d_hbm, dx_hbm, d_all, wide, both, wg_raw, wu_raw, wcat, dx, sems_g, sems_u, sems_x, sem_d,
):
    half, hidden = wg_raw.shape
    pieces = [slice(c, c + chunk) for c in range(0, half, chunk)]
    ready_g = fetch(wg_hbm, wg_raw, sems_g, pieces)
    ready_u = fetch(wu_hbm, wu_raw, sems_u, pieces)
    block = 64
    for r in range(0, dh_ref.shape[0], block):
        at = slice(r, r + block)
        d_hidden = dh_ref[at].astype(F32) + dh_in[at].astype(F32)
        act_a = ab_ref[0, at].astype(F32) + ab_in[0, at].astype(F32)
        act_b = ab_ref[1, at].astype(F32) + ab_in[1, at].astype(F32)
        sigma = jax.nn.sigmoid(act_a)
        silu_a = act_a * sigma
        hid = (silu_a * act_b).astype(BF)
        d_a = d_hidden * act_b * sigma * (1.0 + act_a * (1.0 - sigma))
        d_all[0, at] = d_a.astype(BF)
        d_all[1, at] = (d_hidden * silu_a).astype(BF)
        d_all[2, at] = hid
        grad = jnp.sum(hid.astype(F32) * d_hidden, axis=1, keepdims=True)
        high = grad.astype(BF).astype(F32)
        lane = lax.broadcasted_iota(jnp.int32, (block, META), 1)
        pair = jnp.where(lane == 0, high, jnp.where(lane == 1, grad - high, 0.0))
        both[at] = pair.astype(BF)
    save = pltpu.make_async_copy(d_all, d_hbm, sem_d)
    save.start()
    wide[:, :hidden] = dot(slot_ref[...], d_all[0], ROWS).astype(BF)
    wide[:, hidden:] = dot(slot_ref[...], d_all[1], ROWS).astype(BF)
    dx[:, half:] = dot(slot_ref[...], both[...], ROWS).astype(BF)
    copies = []
    for i, c in enumerate(range(0, half, chunk)):
        ready_g[i].wait()
        ready_u[i].wait()
        dequant(wg_raw, sg_ref, wcat, c, 0, chunk, hidden, 0)
        dequant(wu_raw, su_ref, wcat, c, 0, chunk, hidden, hidden)
        dx[:, c : c + chunk] = dot(wide[...], wcat[...], LAST).astype(BF)
        stop = c + chunk if c + chunk < half else half + META
        copies.append(
            pltpu.make_async_copy(dx.at[:, c:stop], dx_hbm.at[:, c:stop], sems_x.at[i])
        )
        copies[-1].start()
    for copy in copies:
        copy.wait()
    save.wait()


def combine_kernel(n_local, top, ret_ref, pick_ref, meta_ref, *outs):
    width = ret_ref.shape[1] - META
    pick = pick_ref[...]
    meta = meta_ref[...].astype(F32)
    total = dot(pick, ret_ref[:, :width], ROWS).astype(BF)
    rows = ret_ref.shape[0]
    owner = owner_of_row(rows, n_local, rows // n_local)
    grads = ret_ref[:, width:].astype(F32)
    high = jnp.where(owner, grads[:, 0:1], 0.0).astype(BF)
    low = jnp.where(owner, grads[:, 1:2], 0.0).astype(BF)
    by_expert = dot(pick, high, ROWS) + dot(pick, low, ROWS)
    base = (1 + lax.div(lax.axis_index("group"), 2) * n_local).astype(F32)
    lane = lax.broadcasted_iota(jnp.int32, meta.shape, 1)
    tail = jnp.zeros(meta.shape, F32)
    for k in range(top):
        hit = matches(meta, k, base, n_local) & (meta[:, SLOT + k : SLOT + k + 1] < CAP)
        value = jnp.sum(jnp.where(hit, by_expert, 0.0), axis=1, keepdims=True)
        tail = jnp.where(lane == k, value / meta[:, GATE + k : GATE + k + 1], tail)
    tail = tail.astype(BF)
    block = outs[0].shape[0]
    for m, out in enumerate(outs):
        out[:, :width] = total[m * block : (m + 1) * block]
        out[:, width:] = tail[m * block : (m + 1) * block]


def finish_kernel(b0, b1, b2, b3, tokens_ref, gates_ref):
    half = tokens_ref.shape[1] // 2
    first = lax.rem(lax.axis_index("group"), 2) == 0
    own = b0[...].astype(F32) + b2[...].astype(F32)
    other = b1[:, :half].astype(F32) + b3[:, :half].astype(F32)
    mine = own[:, :half]
    tokens_ref[:, :half] = jnp.where(first, mine, other).astype(BF)
    tokens_ref[:, half:] = jnp.where(first, other, mine).astype(BF)
    lane = lax.broadcasted_iota(jnp.int32, (gates_ref.shape[0], META), 1)
    row = lax.broadcasted_iota(jnp.int32, (gates_ref.shape[0], META), 0)
    turn = jnp.where(lane == row, 1.0, 0.0).astype(BF)
    gates_ref[...] = dot(turn, own[:, half:].astype(BF), LAST).astype(BF)


def shape(*dims, dtype=BF):
    return jax.ShapeDtypeStruct(dims, dtype)


def shards(
    x_q,
    x_scale,
    cotangent,
    gates,
    experts,
    replicas,
    slots,
    w_gate_q,
    w_up_q,
    w_down_q,
    gate_scales,
    up_scales,
    down_scales,
):
    n_group = lax.axis_size("group")
    n_local = lax.axis_size("local")
    tok, width = x_q.shape
    top = experts.shape[1]
    half = width // 2
    hidden = w_gate_q.shape[2]
    column = n_group * tok
    rows = n_local * n_group * 4
    kept = 2 * CAP
    wide = half + META

    def across(block, apart):
        return lax.ppermute(block, "group", [(i, i ^ apart) for i in range(n_group)])

    def spread(block):
        return lax.all_to_all(block, "local", split_axis=0, concat_axis=0, tiled=True)

    same_x, other_x, same_dy, other_dy = call(
        prepare_kernel,
        (shape(tok, wide), shape(tok, wide), shape(tok, half), shape(tok, half)),
        (x_q, x_scale, cotangent, experts.T, replicas.T, slots.T, gates.T),
        limit=63,
        moved=tok * width * 8,
        grid=(1,),
        in_specs=[whole(tok, width), whole(*x_scale.shape), whole(tok, width)]
        + [whole(top, tok)] * 4,
        out_specs=[whole(tok, wide)] * 2 + [whole(tok, half)] * 2,
    )
    near_x = [same_x, across(other_x, 1), across(same_x, 2), across(other_x, 3)]
    near_dy = [same_dy, across(other_dy, 1), across(same_dy, 2), across(other_dy, 3)]
    packed_x, pick, gated, column_meta = call(
        functools.partial(pack_x_kernel, n_local, top, rows // n_local),
        (shape(rows, wide), shape(rows, column), shape(rows, column), shape(column, META)),
        tuple(near_x),
        limit=LIMIT,
        flops=2 * rows * column * wide,
        moved=2 * rows * wide,
        in_specs=[VMEM] * 4,
        out_specs=[HBM] + [VMEM] * 3,
        scratch_shapes=[pltpu.VMEM((column, wide), BF), pltpu.VMEM((rows, wide), BF), SEMS((4,))],
    )
    packed_dy = call(
        pack_dy_kernel,
        shape(rows, half),
        (gated, *near_dy),
        limit=LIMIT,
        flops=2 * rows * column * half,
        moved=2 * rows * half,
        in_specs=[VMEM] * 5,
        out_specs=HBM,
        scratch_shapes=[pltpu.VMEM((rows, half), BF), SEMS((4,))],
    )
    got_x = spread(packed_x)
    got_x, packed_dy = lax.optimization_barrier((got_x, packed_dy))
    got_dy = spread(packed_dy)

    weights = [w[:, 0, :] for w in (w_gate_q, w_up_q, w_down_q)]
    scales = [s[:, 0, :].T for s in (gate_scales, up_scales, down_scales)]
    cols = 256
    steps = hidden // cols
    raw = pltpu.VMEM((half, hidden), BF)
    rows_x, send_ab, slot_of = call(
        functools.partial(forward_kernel, n_local, top, cols),
        (shape(kept, half), shape(2, kept, hidden), shape(kept, rows)),
        (scales[0], scales[1], got_x, weights[0], weights[1]),
        limit=LIMIT_FORWARD,
        flops=4 * kept * half * hidden,
        moved=4 * half * hidden + 4 * rows * half,
        in_specs=[SMEM, SMEM, VMEM, HBM, HBM],
        out_specs=[HBM, VMEM, VMEM],
        scratch_shapes=[pltpu.VMEM((kept, half), BF), raw, raw]
        + [pltpu.VMEM((half, cols), BF)] * 2
        + [SEMS((steps,)), SEMS((steps,)), SEMS],
    )
    their_ab = across(send_ab, 1)
    rows_dy, send_dh = call(
        functools.partial(down_kernel, cols),
        (shape(kept, half), shape(kept, hidden)),
        (scales[2], slot_of, got_dy, weights[2]),
        limit=LIMIT_DOWN,
        flops=2 * kept * half * hidden,
        moved=2 * half * hidden + 4 * rows * half,
        in_specs=[SMEM, VMEM, VMEM, HBM],
        out_specs=[HBM, VMEM],
        scratch_shapes=[
            pltpu.VMEM((kept, half), BF), raw, pltpu.VMEM((half, cols), BF), SEMS((steps,)), SEMS,
        ],
    )
    their_dh = across(send_dh, 1)
    chunk = 512
    parts = half // chunk
    d_all, dx = call(
        functools.partial(backward_kernel, chunk),
        (shape(3, kept, hidden), shape(rows, wide)),
        (
            scales[0], scales[1], send_ab, their_ab, send_dh, their_dh, slot_of,
            weights[0], weights[1],
        ),
        limit=LIMIT_BACKWARD,
        flops=4 * rows * half * hidden,
        moved=4 * half * hidden + 2 * rows * half,
        in_specs=[SMEM, SMEM] + [VMEM] * 5 + [HBM, HBM],
        out_specs=[HBM, HBM],
        scratch_shapes=[
            pltpu.VMEM((3, kept, hidden), BF),
            pltpu.VMEM((rows, 2 * hidden), BF),
            pltpu.VMEM((kept, META), BF),
            raw,
            raw,
            pltpu.VMEM((chunk, 2 * hidden), BF),
            pltpu.VMEM((rows, wide), BF),
            SEMS((parts,)),
            SEMS((parts,)),
            SEMS((parts,)),
            SEMS,
        ],
    )
    returned = spread(dx)
    grads = [
        dot(left, right, ROWS).astype(BF)
        for left, right in ((rows_x, d_all[0]), (rows_x, d_all[1]), (rows_dy, d_all[2]))
    ]
    blocks = call(
        functools.partial(combine_kernel, n_local, top),
        tuple(shape(tok, wide) for _ in range(n_group)),
        (returned, pick, column_meta),
        flops=2 * rows * column * half,
        limit=24,
        moved=2 * rows * half,
        in_specs=[VMEM] * 3,
        out_specs=[VMEM] * n_group,
    )
    back = [blocks[0]] + [across(blocks[m], m) for m in range(1, n_group)]
    grad_tokens, grad_gates = call(
        finish_kernel,
        (shape(tok, width), shape(top, tok)),
        tuple(back),
        limit=24,
        moved=tok * width * 6,
        grid=(1,),
        in_specs=[whole(tok, wide)] * 4,
        out_specs=[whole(tok, width), whole(top, tok)],
    )
    return (
        grad_tokens,
        grad_gates.T,
        grads[0][:, None, :],
        grads[1][:, None, :],
        grads[2][:, None, :],
    )


def solution(mesh):
    by_token = P(("group", "local"), None)
    by_expert = P("group", "local", None)
    return jax.shard_map(
        shards,
        mesh=mesh,
        in_specs=(by_token,) * 7 + (by_expert,) * 6,
        out_specs=(by_token,) * 2 + (by_expert,) * 3,
        check_vma=False,
    )
```

time: 178 us -> 173 us (0.972)
  Pallas kernels: 38.1 us -> 34.2 us
  matrix products: 12.1 us -> 14.3 us
    pallas_call x8, Pallas kernels: 38.1 us -> 34.2 us  [call(): pl.pallas_call(kernel, out_shape=outs, compiler_params=pltpu.CompilerPara...]
    dot_general x3, matrix products: 12.1 us -> 14.3 us  [dot(): return lax.dot_general(left, right, dims, preferred_element_type=F32)]
    unnamed x31 -> x23, local copies, waits for them, and re-layouts: 4.36 us -> 3.42 us
  transfers between devices with their start and end apart: 14 -> 14, of which waited for: 10 -> 9; matrix products, arithmetic and copies ran while one was open for 7% -> 8% of each run, Pallas kernels for 10% -> 11%
where the time goes in v3:
time: 173 us; the launch traced here: 172 us
  waiting for transfers between devices  85.8 us (50%)
  Pallas kernels  34.2 us (20%)
  starting transfers between devices  33.6 us (19%)
  matrix products  14.3 us (8%)
  local copies, waits for them, and re-layouts  3.42 us (2%)
    all_to_all x3, waiting for transfers between devices, spread(): lax.all_to_all(block, 'local', split_axis=0, concat_axis=0, tiled=True)  62.8 us
    pallas_call x8, Pallas kernels, call(): pl.pallas_call(kernel, out_shape=outs, compiler_params=pltpu.CompilerPara...  34.2 us
    ppermute x11, waiting for transfers between devices, across(): lax.ppermute(block, 'group', [(i, i ^ apart) for i in range(n_group)])  23.1 us
    all_to_all x3, starting transfers between devices, spread(): lax.all_to_all(block, 'local', split_axis=0, concat_axis=0, tiled=True)  20.8 us
    dot_general x3, matrix products, dot(): return lax.dot_general(left, right, dims, preferred_element_type=F32)  14.3 us
    ppermute x11, starting transfers between devices, across(): lax.ppermute(block, 'group', [(i, i ^ apart) for i in range(n_group)])  12.7 us
  transfers between devices with their start and end apart: 14, of which 9 were waited for; matrix products, arithmetic and copies ran while one was open for 8% of the time, Pallas kernels for 11%

profile of v3, /device:TPU:0, one launch (start us, length us, event | category | flops | bytes accessed | tf_op | source)
XLA Modules:
  0.0 172.2 jit_solution(2591948573927644590)
XLA Ops:
  0.6 1.9 %shard_map.164 = (bf16[16,2176]{1,0:T(8,128)(2,1)}, bf16[16,2176]{1,0:T(8,128)(2,1)}, bf16[16,2048]{1,0:T(8,128)(2,1)}, bf16[16,2048]{1,0:T(8,128)(2,1)}) custom-call(bf16[16,4096]{1,0:T(8,128)(2,1)} %xq_ref.1, f32[16,32]{1,0:T(8,128)} %xs_ref.1, bf16[16,4096]{1,0:T(8,128)(2,1)} %dy_ref.1, s32[8,16]{1,0:T(8,128)} %bitcast.50, s32[8,16]{1,0:T(8,128)} %bitcast.51, ...), custom_call_target="tpu_custom_call" | custom-call | bytes 524288 | tf_op jit(solution)/shard_map/pallas_call | solution.py:30
  2.5 3.1 %collective-permute-start.1 = (bf16[16,2176]{1,0:T(8,128)(2,1)}, bf16[16,2176]{1,0:T(8,128)(2,1)S(1)}, u32[]{:S(2)}, u32[]{:S(2)}) collective-permute-start(bf16[16,2176]{1,0:T(8,128)(2,1)} %get-tuple-element.28.b0), channel_id=1, source_target_pairs={{0,64},{32,96},{64,0},{96,32},{1,65},{33,97},{65,1},{97,33},{2,66}... | collective-permute-start | bytes 208904 | tf_op jit(solution)/shard_map/ppermute | solution.py:345
  6.8 1.8 %collective-permute-done.1.b2 = bf16[16,2176]{1,0:T(8,128)(2,1)S(1)} collective-permute-done((bf16[16,2176]{1,0:T(8,128)(2,1)}, bf16[16,2176]{1,0:T(8,128)(2,1)S(1)}, u32[]{:S(2)}, u32[]{:S(2)}) %collective-permute-start.1) | collective-permute-done | bytes 69664 | tf_op jit(solution)/shard_map/ppermute | solution.py:345
  8.5 2.8 %collective-permute-done.2.b3 = bf16[16,2176]{1,0:T(8,128)(2,1)S(1)} collective-permute-done((bf16[16,2176]{1,0:T(8,128)(2,1)}, bf16[16,2176]{1,0:T(8,128)(2,1)S(1)}, u32[]{:S(2)}, u32[]{:S(2)}) %collective-permute-start.2) | collective-permute-done | bytes 69664 | tf_op jit(solution)/shard_map/ppermute | solution.py:345
  12.2 2.0 %shard_map.165 = (bf16[512,2176]{1,0:T(8,128)(2,1)}, bf16[512,64]{1,0:T(8,128)(2,1)S(1)}, bf16[512,64]{1,0:T(8,128)(2,1)S(1)}, bf16[64,128]{1,0:T(8,128)(2,1)S(1)}) custom-call(bf16[16,2176]{1,0:T(8,128)(2,1)S(1)} %copy-done.3, bf16[16,2176]{1,0:T(8,128)(2,1)S(1)} %collective-permute-done.b1, bf16[16,2176]{1,0:T(8,128)(2,1)S(1)} %collective-permute-done.1.b2, ...), custom_call_target="tpu_custom_call" | custom-call | flops 142606336 | bytes 2228224 | tf_op jit(solution)/shard_map/pallas_call | solution.py:30
  14.3 8.5 %all-to-all-start = ((bf16[32,16,2176]{2,1,0:T(8,128)(2,1)}), bf16[32,16,2176]{2,1,0:T(8,128)(2,1)S(1)}, u32[]{:S(2)}, u32[]{:S(2)}) async-start(bf16[32,16,2176]{2,1,0:T(8,128)(2,1)} %bitcast.6), calls=%async_computation | async-start | bytes 4456448 | tf_op jit(solution)/shard_map/all_to_all | solution.py:348
  22.8 1.6 collective-permute-start.4
  26.3 2.3 %collective-permute-done.4.b2 = bf16[16,2048]{1,0:T(8,128)(2,1)S(1)} collective-permute-done((bf16[16,2048]{1,0:T(8,128)(2,1)S(1)}, bf16[16,2048]{1,0:T(8,128)(2,1)S(1)}, u32[]{:S(2)}, u32[]{:S(2)}) %collective-permute-start.4) | collective-permute-done | bytes 65568 | tf_op jit(solution)/shard_map/ppermute | solution.py:345
  30.0 1.6 shard_map.166
  31.7 22.7 %all-to-all-done = bf16[32,16,2176]{2,1,0:T(8,128)(2,1)S(1)} async-done(((bf16[32,16,2176]{2,1,0:T(8,128)(2,1)}), bf16[32,16,2176]{2,1,0:T(8,128)(2,1)S(1)}, u32[]{:S(2)}, u32[]{:S(2)}) %all-to-all-start) | async-done | bytes 2228256 | tf_op jit(solution)/shard_map/all_to_all | solution.py:348
  54.3 1.4 copy-done.6
  55.7 4.8 %all-to-all-start.1 = ((bf16[32,16,2048]{2,1,0:T(8,128)(2,1)}), bf16[32,16,2048]{2,1,0:T(8,128)(2,1)}, u32[]{:S(2)}, u32[]{:S(2)}) async-start(bf16[32,16,2048]{2,1,0:T(8,128)(2,1)} %bitcast.11), calls=%async_computation.1 | async-start | bytes 4194304 | tf_op jit(solution)/shard_map/all_to_all | solution.py:348
  60.5 10.2 %shard_map.167 = (bf16[384,2048]{1,0:T(8,128)(2,1)S(1)}, bf16[2,384,768]{2,1,0:T(8,128)(2,1)S(1)}, bf16[384,512]{1,0:T(8,128)(2,1)S(1)}) custom-call(f32[6,16]{1,0:T(8,128)S(1)} %get-tuple-element.52.sg_ref, f32[6,16]{1,0:T(8,128)S(1)} %get-tuple-element.51.su_ref, bf16[512,2176]{1,0:T(8,128)(2,1)} %bitcast.48, bf16[2048,768]{1,0:T(8,128)(2,1)} %bitcast.54, ...), custom_call_target="tpu_custom_call" | custom-call | flops 2415919104 | bytes 10485760 | tf_op jit(solution)/shard_map/pallas_call | solution.py:30
  71.9 18.5 %all-to-all-done.1 = bf16[32,16,2048]{2,1,0:T(8,128)(2,1)} async-done(((bf16[32,16,2048]{2,1,0:T(8,128)(2,1)}), bf16[32,16,2048]{2,1,0:T(8,128)(2,1)}, u32[]{:S(2)}, u32[]{:S(2)}) %all-to-all-start.1) | async-done | bytes 2097184 | tf_op jit(solution)/shard_map/all_to_all | solution.py:348
  90.4 7.1 %shard_map.168 = (bf16[384,2048]{1,0:T(8,128)(2,1)S(1)}, bf16[384,768]{1,0:T(8,128)(2,1)S(1)}) custom-call(f32[6,16]{1,0:T(8,128)S(1)} %bitcast.46, bf16[384,512]{1,0:T(8,128)(2,1)S(1)} %get-tuple-element.36.slot_ref, bf16[512,2048]{1,0:T(8,128)(2,1)} %bitcast.12.dy_ref, bf16[2048,768]{1,0:T(8,128)(2,1)} %bitcast.47), custom_call_target="tpu_custom_call" | custom-call | flops 1207959552 | bytes 7340032 | tf_op jit(solution)/shard_map/pallas_call | solution.py:30
  97.7 3.1 %collective-permute-done.6.ab_in = bf16[2,384,768]{2,1,0:T(8,128)(2,1)} collective-permute-done((bf16[2,384,768]{2,1,0:T(8,128)(2,1)S(1)}, bf16[2,384,768]{2,1,0:T(8,128)(2,1)}, u32[]{:S(2)}, u32[]{:S(2)}) %collective-permute-start.6) | collective-permute-done | bytes 1179680 | tf_op jit(solution)/shard_map/ppermute | solution.py:345
  100.8 11.7 %collective-permute-done.7.dh_in = bf16[384,768]{1,0:T(8,128)(2,1)S(1)} collective-permute-done((bf16[384,768]{1,0:T(8,128)(2,1)S(1)}, bf16[384,768]{1,0:T(8,128)(2,1)S(1)}, u32[]{:S(2)}, u32[]{:S(2)}) %collective-permute-start.7) | collective-permute-done | bytes 589856 | tf_op jit(solution)/shard_map/ppermute | solution.py:345
  112.5 9.6 %shard_map.169 = (bf16[3,384,768]{2,1,0:T(8,128)(2,1)}, bf16[512,2176]{1,0:T(8,128)(2,1)}) custom-call(f32[6,16]{1,0:T(8,128)S(1)} %get-tuple-element.52.sg_ref, f32[6,16]{1,0:T(8,128)S(1)} %get-tuple-element.51.su_ref, bf16[2,384,768]{2,1,0:T(8,128)(2,1)S(1)} %get-tuple-element.35.ab_ref, bf16[2,384,768]{2,1,0:T(8,128)(2,1)} %collective-permute-done.6.ab_in, ...), custom_call_target="tpu_custom_call" | custom-call | flops 3221225472 | bytes 8388608 | tf_op jit(solution)/shard_map/pallas_call | solution.py:30
  122.0 7.6 %all-to-all-start.2 = ((bf16[32,16,2176]{2,1,0:T(8,128)(2,1)}), bf16[32,16,2176]{2,1,0:T(8,128)(2,1)S(1)}, u32[]{:S(2)}, u32[]{:S(2)}) async-start(bf16[32,16,2176]{2,1,0:T(8,128)(2,1)} %bitcast.49), calls=%async_computation.2 | async-start | bytes 4456448 | tf_op jit(solution)/shard_map/all_to_all | solution.py:348
  129.7 5.2 %fusion.1 = bf16[2048,1,768]{2,0,1:T(8,128)(2,1)} fusion(bf16[384,2048]{1,0:T(8,128)(2,1)} %copy-done.4, bf16[3,384,768]{2,1,0:T(8,128)(2,1)} %get-tuple-element.49), kind=kOutput, calls=%fused_computation.4 | convolution fusion | flops 1209532416 | bytes 5308416 | tf_op jit(solution)/shard_map/dot_general | solution.py:26
  134.8 4.6 %fusion = bf16[2048,1,768]{2,0,1:T(8,128)(2,1)} fusion(bf16[384,2048]{1,0:T(8,128)(2,1)S(1)} %copy-done.5, bf16[3,384,768]{2,1,0:T(8,128)(2,1)} %get-tuple-element.49), kind=kOutput, calls=%fused_computation.3 | convolution fusion | flops 1209532416 | bytes 5308416 | tf_op jit(solution)/shard_map/dot_general | solution.py:26
  139.4 21.6 %all-to-all-done.2 = bf16[32,16,2176]{2,1,0:T(8,128)(2,1)S(1)} async-done(((bf16[32,16,2176]{2,1,0:T(8,128)(2,1)}), bf16[32,16,2176]{2,1,0:T(8,128)(2,1)S(1)}, u32[]{:S(2)}, u32[]{:S(2)}) %all-to-all-start.2) | async-done | bytes 2228256 | tf_op jit(solution)/shard_map/all_to_all | solution.py:348
  162.4 3.2 %collective-permute-start.9 = (bf16[16,2176]{1,0:T(8,128)(2,1)S(1)}, bf16[16,2176]{1,0:T(8,128)(2,1)S(1)}, u32[]{:S(2)}, u32[]{:S(2)}) collective-permute-start(bf16[16,2176]{1,0:T(8,128)(2,1)S(1)} %get-tuple-element.44), channel_id=1, source_target_pairs={{0,64},{32,96},{64,0},{96,32},{1,65},{33,97},{65,1},{97,33},{2,66}... | collective-permute-start | bytes 208904 | tf_op jit(solution)/shard_map/ppermute | solution.py:345
  166.9 4.6 %fusion.2 = bf16[2048,1,768]{2,0,1:T(8,128)(2,1)} fusion(bf16[384,2048]{1,0:T(8,128)(2,1)S(1)} %copy-done.2, bf16[3,384,768]{2,1,0:T(8,128)(2,1)} %get-tuple-element.49), kind=kOutput, calls=%fused_computation.5 | convolution fusion | flops 1209532416 | bytes 5308416 | tf_op jit(solution)/shard_map/dot_general | solution.py:26
  (39 shorter events, 10.1 us)
Async XLA Ops:
  2.5 6.0 %collective-permute-start.1 = (bf16[16,2176]{1,0:T(8,128)(2,1)}, bf16[16,2176]{1,0:T(8,128)(2,1)S(1)}, u32[]{:S(2)}, u32[]{:S(2)}) collective-permute-start(bf16[16,2176]{1,0:T(8,128)(2,1)} %get-tuple-element.28.b0), channel_id=1, source_target_pairs={{0,64},{32,96},{64,0},{96,32},{1,65},{33,97},{65,1},{97,33},{2,66}... | collective-permute-start | bytes 208904 | tf_op jit(solution)/shard_map/ppermute | solution.py:345
  5.6 5.7 %collective-permute-start.2 = (bf16[16,2176]{1,0:T(8,128)(2,1)}, bf16[16,2176]{1,0:T(8,128)(2,1)S(1)}, u32[]{:S(2)}, u32[]{:S(2)}) collective-permute-start(bf16[16,2176]{1,0:T(8,128)(2,1)} %get-tuple-element.29), channel_id=1, source_target_pairs={{0,96},{32,64},{64,32},{96,0},{1,97},{33,65},{65,33},{97,1},{2,98}... | collective-permute-start | bytes 208904 | tf_op jit(solution)/shard_map/ppermute | solution.py:345
  6.8 4.6 %collective-permute-start = (bf16[16,2176]{1,0:T(8,128)(2,1)}, bf16[16,2176]{1,0:T(8,128)(2,1)S(1)}, u32[]{:S(2)}, u32[]{:S(2)}) collective-permute-start(bf16[16,2176]{1,0:T(8,128)(2,1)} %get-tuple-element.29), channel_id=1, source_target_pairs={{0,32},{32,0},{64,96},{96,64},{1,33},{33,1},{65,97},{97,65},{2,34}... | collective-permute-start | bytes 208904 | tf_op jit(solution)/shard_map/ppermute | solution.py:345
  14.3 8.5 %copy-start = (bf16[16,2048]{1,0:T(8,128)(2,1)S(1)}, bf16[16,2048]{1,0:T(8,128)(2,1)}, u32[]{:S(2)}) copy-start(bf16[16,2048]{1,0:T(8,128)(2,1)} %get-tuple-element.32.b0) | copy-start | bytes 196612
  14.3 10.1 %copy-start.10 = (bf16[16,2048]{1,0:T(8,128)(2,1)S(1)}, bf16[16,2048]{1,0:T(8,128)(2,1)}, u32[]{:S(2)}) copy-start(bf16[16,2048]{1,0:T(8,128)(2,1)} %get-tuple-element.33) | copy-start | bytes 196612
  14.3 40.0 %all-to-all-start = ((bf16[32,16,2176]{2,1,0:T(8,128)(2,1)}), bf16[32,16,2176]{2,1,0:T(8,128)(2,1)S(1)}, u32[]{:S(2)}, u32[]{:S(2)}) async-start(bf16[32,16,2176]{2,1,0:T(8,128)(2,1)} %bitcast.6), calls=%async_computation | async-start | bytes 4456448 | tf_op jit(solution)/shard_map/all_to_all | solution.py:348
  22.8 5.9 %collective-permute-start.4 = (bf16[16,2048]{1,0:T(8,128)(2,1)S(1)}, bf16[16,2048]{1,0:T(8,128)(2,1)S(1)}, u32[]{:S(2)}, u32[]{:S(2)}) collective-permute-start(bf16[16,2048]{1,0:T(8,128)(2,1)S(1)} %copy-done), channel_id=1, source_target_pairs={{0,64},{32,96},{64,0},{96,32},{1,65},{33,97},{65,1},{97,33},{2,66}... | collective-permute-start | bytes 196616 | tf_op jit(solution)/shard_map/ppermute | solution.py:345
  24.3 5.7 %collective-permute-start.5 = (bf16[16,2048]{1,0:T(8,128)(2,1)S(1)}, bf16[16,2048]{1,0:T(8,128)(2,1)S(1)}, u32[]{:S(2)}, u32[]{:S(2)}) collective-permute-start(bf16[16,2048]{1,0:T(8,128)(2,1)S(1)} %copy-done.10), channel_id=1, source_target_pairs={{0,96},{32,64},{64,32},{96,0},{1,97},{33,65},{65,33},{97,1},{2,98}... | collective-permute-start | bytes 196616 | tf_op jit(solution)/shard_map/ppermute | solution.py:345
  25.6 4.5 %collective-permute-start.3 = (bf16[16,2048]{1,0:T(8,128)(2,1)S(1)}, bf16[16,2048]{1,0:T(8,128)(2,1)S(1)}, u32[]{:S(2)}, u32[]{:S(2)}) collective-permute-start(bf16[16,2048]{1,0:T(8,128)(2,1)S(1)} %copy-done.10), channel_id=1, source_target_pairs={{0,32},{32,0},{64,96},{96,64},{1,33},{33,1},{65,97},{97,65},{2,34}... | collective-permute-start | bytes 196616 | tf_op jit(solution)/shard_map/ppermute | solution.py:345
  54.3 1.4 copy-start.6
  54.3 6.1 %copy-start.7 = (f32[16,1,6]{0,1,2:T(1,128)S(1)}, f32[16,1,6]{0,1,2:T(1,128)}, u32[]{:S(2)}) copy-start(f32[16,1,6]{0,1,2:T(1,128)} %param.24) | copy-start | bytes 1156
  54.3 6.1 %copy-start.8 = (f32[16,1,6]{0,1,2:T(1,128)S(1)}, f32[16,1,6]{0,1,2:T(1,128)}, u32[]{:S(2)}) copy-start(f32[16,1,6]{0,1,2:T(1,128)} %param.23) | copy-start | bytes 1156
  55.7 34.7 %all-to-all-start.1 = ((bf16[32,16,2048]{2,1,0:T(8,128)(2,1)}), bf16[32,16,2048]{2,1,0:T(8,128)(2,1)}, u32[]{:S(2)}, u32[]{:S(2)}) async-start(bf16[32,16,2048]{2,1,0:T(8,128)(2,1)} %bitcast.11), calls=%async_computation.1 | async-start | bytes 4194304 | tf_op jit(solution)/shard_map/all_to_all | solution.py:348
  60.5 11.4 %copy-start.9 = (f32[16,1,6]{0,1,2:T(1,128)S(1)}, f32[16,1,6]{0,1,2:T(1,128)}, u32[]{:S(2)}) copy-start(f32[16,1,6]{0,1,2:T(1,128)} %param.25) | copy-start | bytes 1156
  70.7 1.1 copy-start.4
  71.8 28.9 %collective-permute-start.6 = (bf16[2,384,768]{2,1,0:T(8,128)(2,1)S(1)}, bf16[2,384,768]{2,1,0:T(8,128)(2,1)}, u32[]{:S(2)}, u32[]{:S(2)}) collective-permute-start(bf16[2,384,768]{2,1,0:T(8,128)(2,1)S(1)} %get-tuple-element.35.ab_ref), channel_id=1, source_target_pairs={{0,32},{32,0},{64,96},{96,64},{1,33},{33,1},{65,97},{97,65},{2,34}... | collective-permute-start | bytes 3538952 | tf_op jit(solution)/shard_map/ppermute | solution.py:345
  97.6 24.5 %copy-start.1 = (bf16[384,2048]{1,0:T(8,128)(2,1)}, bf16[384,2048]{1,0:T(8,128)(2,1)S(1)}, u32[]{:S(2)}) copy-start(bf16[384,2048]{1,0:T(8,128)(2,1)S(1)} %get-tuple-element.50) | copy-start | bytes 4718596
  97.6 14.9 %collective-permute-start.7 = (bf16[384,768]{1,0:T(8,128)(2,1)S(1)}, bf16[384,768]{1,0:T(8,128)(2,1)S(1)}, u32[]{:S(2)}, u32[]{:S(2)}) collective-permute-start(bf16[384,768]{1,0:T(8,128)(2,1)S(1)} %get-tuple-element.38.dh_ref), channel_id=1, source_target_pairs={{0,32},{32,0},{64,96},{96,64},{1,33},{33,1},{65,97},{97,65},{2,34}... | collective-permute-start | bytes 1769480 | tf_op jit(solution)/shard_map/ppermute | solution.py:345
  122.0 39.0 %all-to-all-start.2 = ((bf16[32,16,2176]{2,1,0:T(8,128)(2,1)}), bf16[32,16,2176]{2,1,0:T(8,128)(2,1)S(1)}, u32[]{:S(2)}, u32[]{:S(2)}) async-start(bf16[32,16,2176]{2,1,0:T(8,128)(2,1)} %bitcast.49), calls=%async_computation.2 | async-start | bytes 4456448 | tf_op jit(solution)/shard_map/all_to_all | solution.py:348
  129.6 5.2 %copy-start.5 = (bf16[384,2048]{1,0:T(8,128)(2,1)S(1)}, bf16[384,2048]{1,0:T(8,128)(2,1)}, u32[]{:S(2)}) copy-start(bf16[384,2048]{1,0:T(8,128)(2,1)} %copy-done.4) | copy-start | bytes 4718596
  161.0 5.9 %copy-start.2 = (bf16[384,2048]{1,0:T(8,128)(2,1)S(1)}, bf16[384,2048]{1,0:T(8,128)(2,1)}, u32[]{:S(2)}) copy-start(bf16[384,2048]{1,0:T(8,128)(2,1)} %copy-done.1) | copy-start | bytes 4718596
  162.1 9.4 %collective-permute-start.8 = (bf16[16,2176]{1,0:T(8,128)(2,1)S(1)}, bf16[16,2176]{1,0:T(8,128)(2,1)S(1)}, u32[]{:S(2)}, u32[]{:S(2)}) collective-permute-start(bf16[16,2176]{1,0:T(8,128)(2,1)S(1)} %get-tuple-element.43), channel_id=1, source_target_pairs={{0,32},{32,0},{64,96},{96,64},{1,33},{33,1},{65,97},{97,65},{2,34}... | collective-permute-start | bytes 208904 | tf_op jit(solution)/shard_map/ppermute | solution.py:345
  162.4 9.0 %collective-permute-start.9 = (bf16[16,2176]{1,0:T(8,128)(2,1)S(1)}, bf16[16,2176]{1,0:T(8,128)(2,1)S(1)}, u32[]{:S(2)}, u32[]{:S(2)}) collective-permute-start(bf16[16,2176]{1,0:T(8,128)(2,1)S(1)} %get-tuple-element.44), channel_id=1, source_target_pairs={{0,64},{32,96},{64,0},{96,32},{1,65},{33,97},{65,1},{97,33},{2,66}... | collective-permute-start | bytes 208904 | tf_op jit(solution)/shard_map/ppermute | solution.py:345
  165.6 5.8 %collective-permute-start.10 = (bf16[16,2176]{1,0:T(8,128)(2,1)S(1)}, bf16[16,2176]{1,0:T(8,128)(2,1)S(1)}, u32[]{:S(2)}, u32[]{:S(2)}) collective-permute-start(bf16[16,2176]{1,0:T(8,128)(2,1)S(1)} %get-tuple-element.45), channel_id=1, source_target_pairs={{0,96},{32,64},{64,32},{96,0},{1,97},{33,65},{65,33},{97,1},{2,98}... | collective-permute-start | bytes 208904 | tf_op jit(solution)/shard_map/ppermute | solution.py:345
  (1 other events, 0.9 us)

commit v4 on v3

--- a/solution.py
+++ b/solution.py
@@ -14,6 +14,7 @@
 F32 = jnp.float32
 MIB = 1024 * 1024
 LIMIT = 24
+LIMIT_DEQUANT = 16
 LIMIT_FORWARD = 50
 LIMIT_DOWN = 50
 LIMIT_BACKWARD = 50
@@ -115,60 +116,65 @@
     before = jnp.where(row < col, 1.0, 0.0).astype(BF)
     rank = jnp.where(named > 0.0, dot(named.astype(BF), before), -1.0)
     position = lax.broadcasted_iota(jnp.int32, (per, count), 0).astype(F32)
-    part = out.shape[0] // sems.shape[0]
-    copies = []
     for j in range(n_local):
         at = slice(j * per, (j + 1) * per)
         hit = rank[j : j + 1] == position
         pick_ref[at] = jnp.where(hit, 1.0, 0.0).astype(BF)
         gated_ref[at] = jnp.where(hit, gate[j : j + 1], 0.0).astype(BF)
-        if (j + 1) * per % part == 0:
-            at = slice((j + 1) * per - part, (j + 1) * per)
-            out[at] = dot(pick_ref[at], tokens[...]).astype(BF)
-            copies.append(
-                pltpu.make_async_copy(out.at[at], out_hbm.at[at], sems.at[len(copies)])
-            )
-            copies[-1].start()
-    for copy in copies:
-        copy.wait()
-
-
-def pack_dy_kernel(gated_ref, b0, b1, b2, b3, out_hbm, out, sems):
-    tokens = jnp.concatenate([b[...] for b in (b0, b1, b2, b3)], axis=0)
-    part = out.shape[0] // sems.shape[0]
-    copies = []
-    for i in range(sems.shape[0]):
-        at = slice(i * part, (i + 1) * part)
-        out[at] = dot(gated_ref[at], tokens).astype(BF)
-        copies.append(pltpu.make_async_copy(out.at[at], out_hbm.at[at], sems.at[i]))
-        copies[-1].start()
-    for copy in copies:
-        copy.wait()
-
-
-def dequant(quant_ref, scales_ref, out_ref, row, col, rows, cols, at_col=0):
+    multiply_out(pick_ref, tokens, out, out_hbm, sems)
+
+
+def multiply_out(left, right, out, out_hbm, sems):
+    parts = sems.shape[0]
+    size = out.shape[0] // parts
+
+    def copy(i):
+        at = pl.ds(pl.multiple_of(i * size, size), size)
+        return pltpu.make_async_copy(out.at[at], out_hbm.at[at], sems.at[i])
+
+    def step(i, carry):
+        at = pl.ds(pl.multiple_of(i * size, size), size)
+        out[at] = dot(left[at], right[...]).astype(BF)
+        copy(i).start()
+        return carry
+
+    lax.fori_loop(0, parts, step, 0)
+    for i in range(parts):
+        copy(i).wait()
+
+
+def pack_dy_kernel(gated_ref, b0, b1, b2, b3, out_hbm, tokens, out, sems):
+    block = b0.shape[0]
+    for m, b in enumerate((b0, b1, b2, b3)):
+        tokens[m * block : (m + 1) * block] = b[...]
+    multiply_out(gated_ref, tokens, out, out_hbm, sems)
+
+
+def dequant(quant_ref, scales_ref, out_ref, row, col):
+    rows, cols = quant_ref.shape
     for c in range(cols // 128):
         for r in range(rows // 128):
-            top, left = row + r * 128, col + c * 128
-            factor = jnp.full((1, 16, 128), scales_ref[left // 128, top // 128], F32).astype(BF)
-            block = quant_ref[top : top + 128, left : left + 128].reshape(8, 16, 128) * factor
-            out_ref[r * 128 : (r + 1) * 128, at_col + c * 128 : at_col + (c + 1) * 128] = (
-                block.reshape(128, 128)
-            )
-
-
-def fetch(source, target, sems, pieces):
-    copies = [
-        pltpu.make_async_copy(source.at[piece], target.at[piece], sems.at[i])
-        for i, piece in enumerate(pieces)
-    ]
-    for copy in copies:
-        copy.start()
-    return copies
-
-
-def columns(count, size):
-    return [(slice(None), slice(c, c + size)) for c in range(0, count, size)]
+            at = (slice(r * 128, (r + 1) * 128), slice(c * 128, (c + 1) * 128))
+            factor = jnp.full((1, 16, 128), scales_ref[col + c, row + r], F32).astype(BF)
+            out_ref[at] = (quant_ref[at].reshape(8, 16, 128) * factor).reshape(128, 128)
+
+
+def columns(i, size):
+    return (slice(None), pl.ds(pl.multiple_of(i * size, size), size))
+
+
+def fetch(source, target, sems, i, size):
+    at = columns(i, size)
+    return pltpu.make_async_copy(source.at[at], target.at[at], sems.at[i])
+
+
+def compact(slot_ref, rows_ref, kept, size=512):
+    def step(i, carry):
+        at = columns(i, size)
+        kept[at] = dot(slot_ref[...], rows_ref[at]).astype(BF)
+        return carry
+
+    lax.fori_loop(0, kept.shape[1] // size, step, 0)
 
 
 def forward_kernel(
@@ -176,8 +182,10 @@
     kept_hbm, send_ref, slot_ref, kept, wg_raw, wu_raw, wg, wu, sems_g, sems_u, sem_k,
 ):
     half, hidden = wg_raw.shape
-    ready_g = fetch(wg_hbm, wg_raw, sems_g, columns(hidden, cols))
-    ready_u = fetch(wu_hbm, wu_raw, sems_u, columns(hidden, cols))
+    steps = hidden // cols
+    for i in range(steps):
+        fetch(wg_hbm, wg_raw, sems_g, i, cols).start()
+        fetch(wu_hbm, wu_raw, sems_u, i, cols).start()
     lane = lax.broadcasted_iota(jnp.int32, (2 * top, META), 1)
     row = lax.broadcasted_iota(jnp.int32, (2 * top, META), 0)
     turn = jnp.where(lane == row, 1.0, 0.0).astype(BF)
@@ -193,18 +201,21 @@
         target = jnp.where(code == own + 64.0, slot + CAP, target)
     row = lax.broadcasted_iota(jnp.int32, slot_ref.shape, 0).astype(F32)
     slot_ref[...] = jnp.where(row == target, 1.0, 0.0).astype(BF)
-    for c in range(0, half, 512):
-        kept[:, c : c + 512] = dot(slot_ref[...], x_ref[:, c : c + 512]).astype(BF)
+    compact(slot_ref, x_ref, kept)
     save = pltpu.make_async_copy(kept, kept_hbm, sem_k)
     save.start()
-    for i, c in enumerate(range(0, hidden, cols)):
-        at = slice(c, c + cols)
-        ready_g[i].wait()
-        dequant(wg_raw, sg_ref, wg, 0, c, half, cols)
-        send_ref[0, :, at] = dot(kept[...], wg[...]).astype(BF)
-        ready_u[i].wait()
-        dequant(wu_raw, su_ref, wu, 0, c, half, cols)
-        send_ref[1, :, at] = dot(kept[...], wu[...]).astype(BF)
+
+    def step(i, carry):
+        at = columns(i, cols)
+        fetch(wg_hbm, wg_raw, sems_g, i, cols).wait()
+        fetch(wu_hbm, wu_raw, sems_u, i, cols).wait()
+        dequant(wg_raw.at[at], sg_ref, wg, 0, i * (cols // 128))
+        dequant(wu_raw.at[at], su_ref, wu, 0, i * (cols // 128))
+        send_ref[(0, *at)] = dot(kept[...], wg[...]).astype(BF)
+        send_ref[(1, *at)] = dot(kept[...], wu[...]).astype(BF)
+        return carry
+
+    lax.fori_loop(0, steps, step, 0)
     save.wait()
 
 
@@ -212,29 +223,42 @@
     cols, sv_ref, slot_ref, dy_ref, v_hbm, kept_hbm, send_ref, kept, v_raw, v, sems_v, sem_k
 ):
     half, hidden = v_raw.shape
-    ready = fetch(v_hbm, v_raw, sems_v, columns(hidden, cols))
-    for c in range(0, half, 512):
-        kept[:, c : c + 512] = dot(slot_ref[...], dy_ref[:, c : c + 512]).astype(BF)
+    steps = hidden // cols
+    for i in range(steps):
+        fetch(v_hbm, v_raw, sems_v, i, cols).start()
+    compact(slot_ref, dy_ref, kept)
     save = pltpu.make_async_copy(kept, kept_hbm, sem_k)
     save.start()
-    for i, c in enumerate(range(0, hidden, cols)):
-        ready[i].wait()
-        dequant(v_raw, sv_ref, v, 0, c, half, cols)
-        send_ref[:, c : c + cols] = dot(kept[...], v[...]).astype(BF)
+
+    def step(i, carry):
+        at = columns(i, cols)
+        fetch(v_hbm, v_raw, sems_v, i, cols).wait()
+        dequant(v_raw.at[at], sv_ref, v, 0, i * (cols // 128))
+        send_ref[at] = dot(kept[...], v[...]).astype(BF)
+        return carry
+
+    lax.fori_loop(0, steps, step, 0)
     save.wait()
 
 
 def backward_kernel(
     chunk, sg_ref, su_ref, ab_ref, ab_in, dh_ref, dh_in, slot_ref, wg_hbm, wu_hbm,
-    d_hbm, dx_hbm, d_all, wide, both, wg_raw, wu_raw, wcat, dx, sems_g, sems_u, sems_x, sem_d,
+    d_hbm, dx_hbm, d_all, wide, both, wg_raw, wu_raw, wcat, dx, sems_g, sems_u, sems_x, sem_d, sem_m,
 ):
     half, hidden = wg_raw.shape
-    pieces = [slice(c, c + chunk) for c in range(0, half, chunk)]
-    ready_g = fetch(wg_hbm, wg_raw, sems_g, pieces)
-    ready_u = fetch(wu_hbm, wu_raw, sems_u, pieces)
+    parts = half // chunk
     block = 64
-    for r in range(0, dh_ref.shape[0], block):
-        at = slice(r, r + block)
+
+    def load(source, target, sems, i):
+        at = pl.ds(pl.multiple_of(i * chunk, chunk), chunk)
+        return pltpu.make_async_copy(source.at[at], target.at[at], sems.at[i])
+
+    for i in range(parts):
+        load(wg_hbm, wg_raw, sems_g, i).start()
+        load(wu_hbm, wu_raw, sems_u, i).start()
+
+    def activate(i, carry):
+        at = pl.ds(pl.multiple_of(i * block, block), block)
         d_hidden = dh_ref[at].astype(F32) + dh_in[at].astype(F32)
         act_a = ab_ref[0, at].astype(F32) + ab_in[0, at].astype(F32)
         act_b = ab_ref[1, at].astype(F32) + ab_in[1, at].astype(F32)
@@ -250,25 +274,31 @@
         lane = lax.broadcasted_iota(jnp.int32, (block, META), 1)
         pair = jnp.where(lane == 0, high, jnp.where(lane == 1, grad - high, 0.0))
         both[at] = pair.astype(BF)
+        return carry
+
+    lax.fori_loop(0, dh_ref.shape[0] // block, activate, 0)
     save = pltpu.make_async_copy(d_all, d_hbm, sem_d)
     save.start()
     wide[:, :hidden] = dot(slot_ref[...], d_all[0], ROWS).astype(BF)
     wide[:, hidden:] = dot(slot_ref[...], d_all[1], ROWS).astype(BF)
     dx[:, half:] = dot(slot_ref[...], both[...], ROWS).astype(BF)
-    copies = []
-    for i, c in enumerate(range(0, half, chunk)):
-        ready_g[i].wait()
-        ready_u[i].wait()
-        dequant(wg_raw, sg_ref, wcat, c, 0, chunk, hidden, 0)
-        dequant(wu_raw, su_ref, wcat, c, 0, chunk, hidden, hidden)
-        dx[:, c : c + chunk] = dot(wide[...], wcat[...], LAST).astype(BF)
-        stop = c + chunk if c + chunk < half else half + META
-        copies.append(
-            pltpu.make_async_copy(dx.at[:, c:stop], dx_hbm.at[:, c:stop], sems_x.at[i])
-        )
-        copies[-1].start()
-    for copy in copies:
-        copy.wait()
+    tail = pltpu.make_async_copy(dx.at[:, half:], dx_hbm.at[:, half:], sem_m)
+    tail.start()
+
+    def step(i, carry):
+        at = pl.ds(pl.multiple_of(i * chunk, chunk), chunk)
+        load(wg_hbm, wg_raw, sems_g, i).wait()
+        load(wu_hbm, wu_raw, sems_u, i).wait()
+        dequant(wg_raw.at[at], sg_ref, wcat.at[:, :hidden], i * (chunk // 128), 0)
+        dequant(wu_raw.at[at], su_ref, wcat.at[:, hidden:], i * (chunk // 128), 0)
+        dx[columns(i, chunk)] = dot(wide[...], wcat[...], LAST).astype(BF)
+        fetch(dx, dx_hbm, sems_x, i, chunk).start()
+        return carry
+
+    lax.fori_loop(0, parts, step, 0)
+    for i in range(parts):
+        fetch(dx, dx_hbm, sems_x, i, chunk).wait()
+    tail.wait()
     save.wait()
 
 
@@ -380,7 +410,7 @@
         moved=2 * rows * half,
         in_specs=[VMEM] * 5,
         out_specs=HBM,
-        scratch_shapes=[pltpu.VMEM((rows, half), BF), SEMS((4,))],
+        scratch_shapes=[pltpu.VMEM((column, half), BF), pltpu.VMEM((rows, half), BF), SEMS((4,))],
     )
     got_x = spread(packed_x)
     got_x, packed_dy = lax.optimization_barrier((got_x, packed_dy))
@@ -445,6 +475,7 @@
             SEMS((parts,)),
             SEMS((parts,)),
             SEMS,
+            SEMS,
         ],
     )
     returned = spread(dx)

time: 173 us -> 169 us (0.977)
  Pallas kernels: 34.2 us -> 29.2 us
    pallas_call x8, Pallas kernels: 34.2 us -> 29.2 us  [call(): pl.pallas_call(kernel, out_shape=outs, compiler_params=pltpu.CompilerPara...]
    all_to_all x3, waiting for transfers between devices: 62.8 us -> 65.7 us  [spread(): lax.all_to_all(block, 'local', split_axis=0, concat_axis=0, tiled=True)]
  transfers between devices with their start and end apart: 14 -> 14, of which waited for: 9 -> 9; matrix products, arithmetic and copies ran while one was open for 8% -> 8% of each run, Pallas kernels for 11% -> 8%
where the time goes in v4:
time: 169 us
  waiting for transfers between devices  87.4 us (52%)
  starting transfers between devices  33.6 us (20%)
  Pallas kernels  29.2 us (17%)
  matrix products  14.3 us (8%)
  local copies, waits for them, and re-layouts  3.42 us (2%)
    all_to_all x3, waiting for transfers between devices, spread(): lax.all_to_all(block, 'local', split_axis=0, concat_axis=0, tiled=True)  65.7 us
    pallas_call x8, Pallas kernels, call(): pl.pallas_call(kernel, out_shape=outs, compiler_params=pltpu.CompilerPara...  29.2 us
    ppermute x11, waiting for transfers between devices, across(): lax.ppermute(block, 'group', [(i, i ^ apart) for i in range(n_group)])  21.7 us
    all_to_all x3, starting transfers between devices, spread(): lax.all_to_all(block, 'local', split_axis=0, concat_axis=0, tiled=True)  20.8 us
    dot_general x3, matrix products, dot(): return lax.dot_general(left, right, dims, preferred_element_type=F32)  14.3 us
    ppermute x11, starting transfers between devices, across(): lax.ppermute(block, 'group', [(i, i ^ apart) for i in range(n_group)])  12.7 us
    unnamed x23, local copies, waits for them, and re-layouts  3.42 us
  transfers between devices with their start and end apart: 14, of which 9 were waited for; matrix products, arithmetic and copies ran while one was open for 8% of the time, Pallas kernels for 8%

profile of v4, /device:TPU:0, one launch (start us, length us, event | category | flops | bytes accessed | tf_op | source)
XLA Modules:
  0.0 168.7 jit_solution(2025874229859387572)
XLA Ops:
  0.6 1.9 %shard_map.164 = (bf16[16,2176]{1,0:T(8,128)(2,1)}, bf16[16,2176]{1,0:T(8,128)(2,1)}, bf16[16,2048]{1,0:T(8,128)(2,1)}, bf16[16,2048]{1,0:T(8,128)(2,1)}) custom-call(bf16[16,4096]{1,0:T(8,128)(2,1)} %xq_ref.1, f32[16,32]{1,0:T(8,128)} %xs_ref.1, bf16[16,4096]{1,0:T(8,128)(2,1)} %dy_ref.1, s32[8,16]{1,0:T(8,128)} %bitcast.50, s32[8,16]{1,0:T(8,128)} %bitcast.51, ...), custom_call_target="tpu_custom_call" | custom-call | bytes 524288 | tf_op jit(solution)/shard_map/pallas_call | solution.py:31
  2.5 3.1 %collective-permute-start.1 = (bf16[16,2176]{1,0:T(8,128)(2,1)}, bf16[16,2176]{1,0:T(8,128)(2,1)S(1)}, u32[]{:S(2)}, u32[]{:S(2)}) collective-permute-start(bf16[16,2176]{1,0:T(8,128)(2,1)} %get-tuple-element.28.b0), channel_id=1, source_target_pairs={{0,64},{32,96},{64,0},{96,32},{1,65},{33,97},{65,1},{97,33},{2,66}... | collective-permute-start | bytes 208904 | tf_op jit(solution)/shard_map/ppermute | solution.py:375
  6.8 1.8 %collective-permute-done.1.b2 = bf16[16,2176]{1,0:T(8,128)(2,1)S(1)} collective-permute-done((bf16[16,2176]{1,0:T(8,128)(2,1)}, bf16[16,2176]{1,0:T(8,128)(2,1)S(1)}, u32[]{:S(2)}, u32[]{:S(2)}) %collective-permute-start.1) | collective-permute-done | bytes 69664 | tf_op jit(solution)/shard_map/ppermute | solution.py:375
  8.5 2.8 %collective-permute-done.2.b3 = bf16[16,2176]{1,0:T(8,128)(2,1)S(1)} collective-permute-done((bf16[16,2176]{1,0:T(8,128)(2,1)}, bf16[16,2176]{1,0:T(8,128)(2,1)S(1)}, u32[]{:S(2)}, u32[]{:S(2)}) %collective-permute-start.2) | collective-permute-done | bytes 69664 | tf_op jit(solution)/shard_map/ppermute | solution.py:375
  12.2 2.3 %shard_map.165 = (bf16[512,2176]{1,0:T(8,128)(2,1)}, bf16[512,64]{1,0:T(8,128)(2,1)S(1)}, bf16[512,64]{1,0:T(8,128)(2,1)S(1)}, bf16[64,128]{1,0:T(8,128)(2,1)S(1)}) custom-call(bf16[16,2176]{1,0:T(8,128)(2,1)S(1)} %copy-done.3, bf16[16,2176]{1,0:T(8,128)(2,1)S(1)} %collective-permute-done.b1, bf16[16,2176]{1,0:T(8,128)(2,1)S(1)} %collective-permute-done.1.b2, ...), custom_call_target="tpu_custom_call" | custom-call | flops 142606336 | bytes 2228224 | tf_op jit(solution)/shard_map/pallas_call | solution.py:31
  14.6 8.5 %all-to-all-start = ((bf16[32,16,2176]{2,1,0:T(8,128)(2,1)}), bf16[32,16,2176]{2,1,0:T(8,128)(2,1)S(1)}, u32[]{:S(2)}, u32[]{:S(2)}) async-start(bf16[32,16,2176]{2,1,0:T(8,128)(2,1)} %bitcast.6), calls=%async_computation | async-start | bytes 4456448 | tf_op jit(solution)/shard_map/all_to_all | solution.py:378
  23.1 1.6 collective-permute-start.4
  26.7 2.3 %collective-permute-done.4.b2 = bf16[16,2048]{1,0:T(8,128)(2,1)S(1)} collective-permute-done((bf16[16,2048]{1,0:T(8,128)(2,1)S(1)}, bf16[16,2048]{1,0:T(8,128)(2,1)S(1)}, u32[]{:S(2)}, u32[]{:S(2)}) %collective-permute-start.4) | collective-permute-done | bytes 65568 | tf_op jit(solution)/shard_map/ppermute | solution.py:375
  29.0 1.4 collective-permute-done.5.b3
  30.4 1.9 %shard_map.166 = bf16[512,2048]{1,0:T(8,128)(2,1)} custom-call(bf16[512,64]{1,0:T(8,128)(2,1)S(1)} %get-tuple-element.31.gated_ref, bf16[16,2048]{1,0:T(8,128)(2,1)S(1)} %copy-done, bf16[16,2048]{1,0:T(8,128)(2,1)S(1)} %collective-permute-done.3.b1, bf16[16,2048]{1,0:T(8,128)(2,1)S(1)} %collective-permute-done.4.b2, ...), custom_call_target="tpu_custom_call" | custom-call | flops 134217728 | bytes 2097152 | tf_op jit(solution)/shard_map/pallas_call | solution.py:31
  32.3 22.3 %all-to-all-done = bf16[32,16,2176]{2,1,0:T(8,128)(2,1)S(1)} async-done(((bf16[32,16,2176]{2,1,0:T(8,128)(2,1)}), bf16[32,16,2176]{2,1,0:T(8,128)(2,1)S(1)}, u32[]{:S(2)}, u32[]{:S(2)}) %all-to-all-start) | async-done | bytes 2228256 | tf_op jit(solution)/shard_map/all_to_all | solution.py:378
  54.7 1.4 copy-done.6
  56.0 4.8 %all-to-all-start.1 = ((bf16[32,16,2048]{2,1,0:T(8,128)(2,1)}), bf16[32,16,2048]{2,1,0:T(8,128)(2,1)}, u32[]{:S(2)}, u32[]{:S(2)}) async-start(bf16[32,16,2048]{2,1,0:T(8,128)(2,1)} %bitcast.11), calls=%async_computation.1 | async-start | bytes 4194304 | tf_op jit(solution)/shard_map/all_to_all | solution.py:378
  60.8 6.9 %shard_map.167 = (bf16[384,2048]{1,0:T(8,128)(2,1)S(1)}, bf16[2,384,768]{2,1,0:T(8,128)(2,1)S(1)}, bf16[384,512]{1,0:T(8,128)(2,1)S(1)}) custom-call(f32[6,16]{1,0:T(8,128)S(1)} %get-tuple-element.52.sg_ref, f32[6,16]{1,0:T(8,128)S(1)} %get-tuple-element.51.su_ref, bf16[512,2176]{1,0:T(8,128)(2,1)} %bitcast.48, bf16[2048,768]{1,0:T(8,128)(2,1)} %bitcast.54, ...), custom_call_target="tpu_custom_call" | custom-call | flops 2415919104 | bytes 10485760 | tf_op jit(solution)/shard_map/pallas_call | solution.py:31
  68.9 21.8 %all-to-all-done.1 = bf16[32,16,2048]{2,1,0:T(8,128)(2,1)} async-done(((bf16[32,16,2048]{2,1,0:T(8,128)(2,1)}), bf16[32,16,2048]{2,1,0:T(8,128)(2,1)}, u32[]{:S(2)}, u32[]{:S(2)}) %all-to-all-start.1) | async-done | bytes 2097184 | tf_op jit(solution)/shard_map/all_to_all | solution.py:378
  90.7 5.2 %shard_map.168 = (bf16[384,2048]{1,0:T(8,128)(2,1)S(1)}, bf16[384,768]{1,0:T(8,128)(2,1)S(1)}) custom-call(f32[6,16]{1,0:T(8,128)S(1)} %bitcast.46, bf16[384,512]{1,0:T(8,128)(2,1)S(1)} %get-tuple-element.36.slot_ref, bf16[512,2048]{1,0:T(8,128)(2,1)} %bitcast.12.dy_ref, bf16[2048,768]{1,0:T(8,128)(2,1)} %bitcast.47), custom_call_target="tpu_custom_call" | custom-call | flops 1207959552 | bytes 7340032 | tf_op jit(solution)/shard_map/pallas_call | solution.py:31
  97.0 12.5 %collective-permute-done.7.dh_in = bf16[384,768]{1,0:T(8,128)(2,1)S(1)} collective-permute-done((bf16[384,768]{1,0:T(8,128)(2,1)S(1)}, bf16[384,768]{1,0:T(8,128)(2,1)S(1)}, u32[]{:S(2)}, u32[]{:S(2)}) %collective-permute-start.7) | collective-permute-done | bytes 589856 | tf_op jit(solution)/shard_map/ppermute | solution.py:375
  109.5 9.1 %shard_map.169 = (bf16[3,384,768]{2,1,0:T(8,128)(2,1)}, bf16[512,2176]{1,0:T(8,128)(2,1)}) custom-call(f32[6,16]{1,0:T(8,128)S(1)} %get-tuple-element.52.sg_ref, f32[6,16]{1,0:T(8,128)S(1)} %get-tuple-element.51.su_ref, bf16[2,384,768]{2,1,0:T(8,128)(2,1)S(1)} %get-tuple-element.35.ab_ref, bf16[2,384,768]{2,1,0:T(8,128)(2,1)} %collective-permute-done.6.ab_in, ...), custom_call_target="tpu_custom_call" | custom-call | flops 3221225472 | bytes 8388608 | tf_op jit(solution)/shard_map/pallas_call | solution.py:31
  118.6 7.6 %all-to-all-start.2 = ((bf16[32,16,2176]{2,1,0:T(8,128)(2,1)}), bf16[32,16,2176]{2,1,0:T(8,128)(2,1)S(1)}, u32[]{:S(2)}, u32[]{:S(2)}) async-start(bf16[32,16,2176]{2,1,0:T(8,128)(2,1)} %bitcast.49), calls=%async_computation.2 | async-start | bytes 4456448 | tf_op jit(solution)/shard_map/all_to_all | solution.py:378
  126.2 5.2 %fusion.1 = bf16[2048,1,768]{2,0,1:T(8,128)(2,1)} fusion(bf16[384,2048]{1,0:T(8,128)(2,1)} %copy-done.4, bf16[3,384,768]{2,1,0:T(8,128)(2,1)} %get-tuple-element.49), kind=kOutput, calls=%fused_computation.4 | convolution fusion | flops 1209532416 | bytes 5308416 | tf_op jit(solution)/shard_map/dot_general | solution.py:27
  131.4 4.6 %fusion = bf16[2048,1,768]{2,0,1:T(8,128)(2,1)} fusion(bf16[384,2048]{1,0:T(8,128)(2,1)S(1)} %copy-done.5, bf16[3,384,768]{2,1,0:T(8,128)(2,1)} %get-tuple-element.49), kind=kOutput, calls=%fused_computation.3 | convolution fusion | flops 1209532416 | bytes 5308416 | tf_op jit(solution)/shard_map/dot_general | solution.py:27
  135.9 21.6 %all-to-all-done.2 = bf16[32,16,2176]{2,1,0:T(8,128)(2,1)S(1)} async-done(((bf16[32,16,2176]{2,1,0:T(8,128)(2,1)}), bf16[32,16,2176]{2,1,0:T(8,128)(2,1)S(1)}, u32[]{:S(2)}, u32[]{:S(2)}) %all-to-all-start.2) | async-done | bytes 2228256 | tf_op jit(solution)/shard_map/all_to_all | solution.py:378
  159.0 3.2 %collective-permute-start.9 = (bf16[16,2176]{1,0:T(8,128)(2,1)S(1)}, bf16[16,2176]{1,0:T(8,128)(2,1)S(1)}, u32[]{:S(2)}, u32[]{:S(2)}) collective-permute-start(bf16[16,2176]{1,0:T(8,128)(2,1)S(1)} %get-tuple-element.44), channel_id=1, source_target_pairs={{0,64},{32,96},{64,0},{96,32},{1,65},{33,97},{65,1},{97,33},{2,66}... | collective-permute-start | bytes 208904 | tf_op jit(solution)/shard_map/ppermute | solution.py:375
  163.4 4.6 %fusion.2 = bf16[2048,1,768]{2,0,1:T(8,128)(2,1)} fusion(bf16[384,2048]{1,0:T(8,128)(2,1)S(1)} %copy-done.2, bf16[3,384,768]{2,1,0:T(8,128)(2,1)} %get-tuple-element.49), kind=kOutput, calls=%fused_computation.5 | convolution fusion | flops 1209532416 | bytes 5308416 | tf_op jit(solution)/shard_map/dot_general | solution.py:27
  (39 shorter events, 9.6 us)
Async XLA Ops:
  2.5 6.0 %collective-permute-start.1 = (bf16[16,2176]{1,0:T(8,128)(2,1)}, bf16[16,2176]{1,0:T(8,128)(2,1)S(1)}, u32[]{:S(2)}, u32[]{:S(2)}) collective-permute-start(bf16[16,2176]{1,0:T(8,128)(2,1)} %get-tuple-element.28.b0), channel_id=1, source_target_pairs={{0,64},{32,96},{64,0},{96,32},{1,65},{33,97},{65,1},{97,33},{2,66}... | collective-permute-start | bytes 208904 | tf_op jit(solution)/shard_map/ppermute | solution.py:375
  5.6 5.7 %collective-permute-start.2 = (bf16[16,2176]{1,0:T(8,128)(2,1)}, bf16[16,2176]{1,0:T(8,128)(2,1)S(1)}, u32[]{:S(2)}, u32[]{:S(2)}) collective-permute-start(bf16[16,2176]{1,0:T(8,128)(2,1)} %get-tuple-element.29), channel_id=1, source_target_pairs={{0,96},{32,64},{64,32},{96,0},{1,97},{33,65},{65,33},{97,1},{2,98}... | collective-permute-start | bytes 208904 | tf_op jit(solution)/shard_map/ppermute | solution.py:375
  6.8 4.6 %collective-permute-start = (bf16[16,2176]{1,0:T(8,128)(2,1)}, bf16[16,2176]{1,0:T(8,128)(2,1)S(1)}, u32[]{:S(2)}, u32[]{:S(2)}) collective-permute-start(bf16[16,2176]{1,0:T(8,128)(2,1)} %get-tuple-element.29), channel_id=1, source_target_pairs={{0,32},{32,0},{64,96},{96,64},{1,33},{33,1},{65,97},{97,65},{2,34}... | collective-permute-start | bytes 208904 | tf_op jit(solution)/shard_map/ppermute | solution.py:375
  14.6 8.5 %copy-start = (bf16[16,2048]{1,0:T(8,128)(2,1)S(1)}, bf16[16,2048]{1,0:T(8,128)(2,1)}, u32[]{:S(2)}) copy-start(bf16[16,2048]{1,0:T(8,128)(2,1)} %get-tuple-element.32.b0) | copy-start | bytes 196612
  14.6 10.1 %copy-start.10 = (bf16[16,2048]{1,0:T(8,128)(2,1)S(1)}, bf16[16,2048]{1,0:T(8,128)(2,1)}, u32[]{:S(2)}) copy-start(bf16[16,2048]{1,0:T(8,128)(2,1)} %get-tuple-element.33) | copy-start | bytes 196612
  14.6 40.0 %all-to-all-start = ((bf16[32,16,2176]{2,1,0:T(8,128)(2,1)}), bf16[32,16,2176]{2,1,0:T(8,128)(2,1)S(1)}, u32[]{:S(2)}, u32[]{:S(2)}) async-start(bf16[32,16,2176]{2,1,0:T(8,128)(2,1)} %bitcast.6), calls=%async_computation | async-start | bytes 4456448 | tf_op jit(solution)/shard_map/all_to_all | solution.py:378
  23.1 5.9 %collective-permute-start.4 = (bf16[16,2048]{1,0:T(8,128)(2,1)S(1)}, bf16[16,2048]{1,0:T(8,128)(2,1)S(1)}, u32[]{:S(2)}, u32[]{:S(2)}) collective-permute-start(bf16[16,2048]{1,0:T(8,128)(2,1)S(1)} %copy-done), channel_id=1, source_target_pairs={{0,64},{32,96},{64,0},{96,32},{1,65},{33,97},{65,1},{97,33},{2,66}... | collective-permute-start | bytes 196616 | tf_op jit(solution)/shard_map/ppermute | solution.py:375
  24.7 5.7 %collective-permute-start.5 = (bf16[16,2048]{1,0:T(8,128)(2,1)S(1)}, bf16[16,2048]{1,0:T(8,128)(2,1)S(1)}, u32[]{:S(2)}, u32[]{:S(2)}) collective-permute-start(bf16[16,2048]{1,0:T(8,128)(2,1)S(1)} %copy-done.10), channel_id=1, source_target_pairs={{0,96},{32,64},{64,32},{96,0},{1,97},{33,65},{65,33},{97,1},{2,98}... | collective-permute-start | bytes 196616 | tf_op jit(solution)/shard_map/ppermute | solution.py:375
  25.9 4.5 %collective-permute-start.3 = (bf16[16,2048]{1,0:T(8,128)(2,1)S(1)}, bf16[16,2048]{1,0:T(8,128)(2,1)S(1)}, u32[]{:S(2)}, u32[]{:S(2)}) collective-permute-start(bf16[16,2048]{1,0:T(8,128)(2,1)S(1)} %copy-done.10), channel_id=1, source_target_pairs={{0,32},{32,0},{64,96},{96,64},{1,33},{33,1},{65,97},{97,65},{2,34}... | collective-permute-start | bytes 196616 | tf_op jit(solution)/shard_map/ppermute | solution.py:375
  54.7 1.4 copy-start.6
  54.7 6.1 %copy-start.7 = (f32[16,1,6]{0,1,2:T(1,128)S(1)}, f32[16,1,6]{0,1,2:T(1,128)}, u32[]{:S(2)}) copy-start(f32[16,1,6]{0,1,2:T(1,128)} %param.24) | copy-start | bytes 1156
  54.7 6.1 %copy-start.8 = (f32[16,1,6]{0,1,2:T(1,128)S(1)}, f32[16,1,6]{0,1,2:T(1,128)}, u32[]{:S(2)}) copy-start(f32[16,1,6]{0,1,2:T(1,128)} %param.23) | copy-start | bytes 1156
  56.0 34.7 %all-to-all-start.1 = ((bf16[32,16,2048]{2,1,0:T(8,128)(2,1)}), bf16[32,16,2048]{2,1,0:T(8,128)(2,1)}, u32[]{:S(2)}, u32[]{:S(2)}) async-start(bf16[32,16,2048]{2,1,0:T(8,128)(2,1)} %bitcast.11), calls=%async_computation.1 | async-start | bytes 4194304 | tf_op jit(solution)/shard_map/all_to_all | solution.py:378
  60.8 8.1 %copy-start.9 = (f32[16,1,6]{0,1,2:T(1,128)S(1)}, f32[16,1,6]{0,1,2:T(1,128)}, u32[]{:S(2)}) copy-start(f32[16,1,6]{0,1,2:T(1,128)} %param.25) | copy-start | bytes 1156
  67.8 1.1 copy-start.4
  68.9 28.1 %collective-permute-start.6 = (bf16[2,384,768]{2,1,0:T(8,128)(2,1)S(1)}, bf16[2,384,768]{2,1,0:T(8,128)(2,1)}, u32[]{:S(2)}, u32[]{:S(2)}) collective-permute-start(bf16[2,384,768]{2,1,0:T(8,128)(2,1)S(1)} %get-tuple-element.35.ab_ref), channel_id=1, source_target_pairs={{0,32},{32,0},{64,96},{96,64},{1,33},{33,1},{65,97},{97,65},{2,34}... | collective-permute-start | bytes 3538952 | tf_op jit(solution)/shard_map/ppermute | solution.py:375
  96.0 22.6 %copy-start.1 = (bf16[384,2048]{1,0:T(8,128)(2,1)}, bf16[384,2048]{1,0:T(8,128)(2,1)S(1)}, u32[]{:S(2)}) copy-start(bf16[384,2048]{1,0:T(8,128)(2,1)S(1)} %get-tuple-element.50) | copy-start | bytes 4718596
  96.0 13.5 %collective-permute-start.7 = (bf16[384,768]{1,0:T(8,128)(2,1)S(1)}, bf16[384,768]{1,0:T(8,128)(2,1)S(1)}, u32[]{:S(2)}, u32[]{:S(2)}) collective-permute-start(bf16[384,768]{1,0:T(8,128)(2,1)S(1)} %get-tuple-element.38.dh_ref), channel_id=1, source_target_pairs={{0,32},{32,0},{64,96},{96,64},{1,33},{33,1},{65,97},{97,65},{2,34}... | collective-permute-start | bytes 1769480 | tf_op jit(solution)/shard_map/ppermute | solution.py:375
  118.6 39.0 %all-to-all-start.2 = ((bf16[32,16,2176]{2,1,0:T(8,128)(2,1)}), bf16[32,16,2176]{2,1,0:T(8,128)(2,1)S(1)}, u32[]{:S(2)}, u32[]{:S(2)}) async-start(bf16[32,16,2176]{2,1,0:T(8,128)(2,1)} %bitcast.49), calls=%async_computation.2 | async-start | bytes 4456448 | tf_op jit(solution)/shard_map/all_to_all | solution.py:378
  126.2 5.2 %copy-start.5 = (bf16[384,2048]{1,0:T(8,128)(2,1)S(1)}, bf16[384,2048]{1,0:T(8,128)(2,1)}, u32[]{:S(2)}) copy-start(bf16[384,2048]{1,0:T(8,128)(2,1)} %copy-done.4) | copy-start | bytes 4718596
  157.6 5.9 %copy-start.2 = (bf16[384,2048]{1,0:T(8,128)(2,1)S(1)}, bf16[384,2048]{1,0:T(8,128)(2,1)}, u32[]{:S(2)}) copy-start(bf16[384,2048]{1,0:T(8,128)(2,1)} %copy-done.1) | copy-start | bytes 4718596
  158.6 9.4 %collective-permute-start.8 = (bf16[16,2176]{1,0:T(8,128)(2,1)S(1)}, bf16[16,2176]{1,0:T(8,128)(2,1)S(1)}, u32[]{:S(2)}, u32[]{:S(2)}) collective-permute-start(bf16[16,2176]{1,0:T(8,128)(2,1)S(1)} %get-tuple-element.43), channel_id=1, source_target_pairs={{0,32},{32,0},{64,96},{96,64},{1,33},{33,1},{65,97},{97,65},{2,34}... | collective-permute-start | bytes 208904 | tf_op jit(solution)/shard_map/ppermute | solution.py:375
  159.0 9.0 %collective-permute-start.9 = (bf16[16,2176]{1,0:T(8,128)(2,1)S(1)}, bf16[16,2176]{1,0:T(8,128)(2,1)S(1)}, u32[]{:S(2)}, u32[]{:S(2)}) collective-permute-start(bf16[16,2176]{1,0:T(8,128)(2,1)S(1)} %get-tuple-element.44), channel_id=1, source_target_pairs={{0,64},{32,96},{64,0},{96,32},{1,65},{33,97},{65,1},{97,33},{2,66}... | collective-permute-start | bytes 208904 | tf_op jit(solution)/shard_map/ppermute | solution.py:375
  162.2 5.8 %collective-permute-start.10 = (bf16[16,2176]{1,0:T(8,128)(2,1)S(1)}, bf16[16,2176]{1,0:T(8,128)(2,1)S(1)}, u32[]{:S(2)}, u32[]{:S(2)}) collective-permute-start(bf16[16,2176]{1,0:T(8,128)(2,1)S(1)} %get-tuple-element.45), channel_id=1, source_target_pairs={{0,96},{32,64},{64,32},{96,0},{1,97},{33,65},{65,33},{97,1},{2,98}... | collective-permute-start | bytes 208904 | tf_op jit(solution)/shard_map/ppermute | solution.py:375
  (1 other events, 0.9 us)

commit v5 on v4

--- a/solution.py
+++ b/solution.py
@@ -14,10 +14,10 @@
 F32 = jnp.float32
 MIB = 1024 * 1024
 LIMIT = 24
-LIMIT_DEQUANT = 16
+LIMIT_FACTOR = 50
 LIMIT_FORWARD = 50
 LIMIT_DOWN = 50
-LIMIT_BACKWARD = 50
+LIMIT_BACKWARD = 51
 
 ROWS = (((0,), (0,)), ((), ()))
 LAST = (((1,), (1,)), ((), ()))
@@ -241,9 +241,9 @@
     save.wait()
 
 
-def backward_kernel(
-    chunk, sg_ref, su_ref, ab_ref, ab_in, dh_ref, dh_in, slot_ref, wg_hbm, wu_hbm,
-    d_hbm, dx_hbm, d_all, wide, both, wg_raw, wu_raw, wcat, dx, sems_g, sems_u, sems_x, sem_d, sem_m,
+def factor_kernel(
+    chunk, sg_ref, su_ref, ab_ref, ab_in, wg_hbm, wu_hbm,
+    factor_ref, hid_ref, both_w, wg_raw, wu_raw, sems_g, sems_u,
 ):
     half, hidden = wg_raw.shape
     parts = half // chunk
@@ -259,39 +259,73 @@
 
     def activate(i, carry):
         at = pl.ds(pl.multiple_of(i * block, block), block)
-        d_hidden = dh_ref[at].astype(F32) + dh_in[at].astype(F32)
         act_a = ab_ref[0, at].astype(F32) + ab_in[0, at].astype(F32)
         act_b = ab_ref[1, at].astype(F32) + ab_in[1, at].astype(F32)
         sigma = jax.nn.sigmoid(act_a)
         silu_a = act_a * sigma
-        hid = (silu_a * act_b).astype(BF)
-        d_a = d_hidden * act_b * sigma * (1.0 + act_a * (1.0 - sigma))
-        d_all[0, at] = d_a.astype(BF)
-        d_all[1, at] = (d_hidden * silu_a).astype(BF)
-        d_all[2, at] = hid
-        grad = jnp.sum(hid.astype(F32) * d_hidden, axis=1, keepdims=True)
-        high = grad.astype(BF).astype(F32)
-        lane = lax.broadcasted_iota(jnp.int32, (block, META), 1)
-        pair = jnp.where(lane == 0, high, jnp.where(lane == 1, grad - high, 0.0))
-        both[at] = pair.astype(BF)
-        return carry
-
-    lax.fori_loop(0, dh_ref.shape[0] // block, activate, 0)
-    save = pltpu.make_async_copy(d_all, d_hbm, sem_d)
-    save.start()
-    wide[:, :hidden] = dot(slot_ref[...], d_all[0], ROWS).astype(BF)
-    wide[:, hidden:] = dot(slot_ref[...], d_all[1], ROWS).astype(BF)
-    dx[:, half:] = dot(slot_ref[...], both[...], ROWS).astype(BF)
-    tail = pltpu.make_async_copy(dx.at[:, half:], dx_hbm.at[:, half:], sem_m)
-    tail.start()
+        hid_ref[at] = (silu_a * act_b).astype(BF)
+        factor_ref[0, at] = act_b * sigma * (1.0 + act_a * (1.0 - sigma))
+        factor_ref[1, at] = silu_a
+        return carry
+
+    lax.fori_loop(0, hid_ref.shape[0] // block, activate, 0)
 
     def step(i, carry):
         at = pl.ds(pl.multiple_of(i * chunk, chunk), chunk)
         load(wg_hbm, wg_raw, sems_g, i).wait()
         load(wu_hbm, wu_raw, sems_u, i).wait()
-        dequant(wg_raw.at[at], sg_ref, wcat.at[:, :hidden], i * (chunk // 128), 0)
-        dequant(wu_raw.at[at], su_ref, wcat.at[:, hidden:], i * (chunk // 128), 0)
-        dx[columns(i, chunk)] = dot(wide[...], wcat[...], LAST).astype(BF)
+        dequant(wg_raw.at[at], sg_ref, both_w.at[at, :hidden], i * (chunk // 128), 0)
+        dequant(wu_raw.at[at], su_ref, both_w.at[at, hidden:], i * (chunk // 128), 0)
+        return carry
+
+    lax.fori_loop(0, parts, step, 0)
+
+
+def backward_kernel(
+    chunk, factor_ref, hid_ref, dh_ref, dh_in, slot_ref, w_hbm,
+    d_hbm, dx_hbm, d_ab, wide, pairs, both_w, dx, sems_w, sems_x, sem_d, sem_m,
+):
+    kept, hidden = hid_ref.shape
+    half = both_w.shape[0]
+    parts = half // chunk
+    block = 64
+
+    def load(i):
+        at = pl.ds(pl.multiple_of(i * chunk, chunk), chunk)
+        return pltpu.make_async_copy(w_hbm.at[at], both_w.at[at], sems_w.at[i])
+
+    for i in range(parts):
+        load(i).start()
+
+    def activate(i, carry):
+        at = pl.ds(pl.multiple_of(i * block, block), block)
+        d_hidden = dh_ref[at].astype(F32) + dh_in[at].astype(F32)
+        d_ab[0, at] = (d_hidden * factor_ref[0, at]).astype(BF)
+        d_ab[1, at] = (d_hidden * factor_ref[1, at]).astype(BF)
+        grad = jnp.sum(hid_ref[at].astype(F32) * d_hidden, axis=1, keepdims=True)
+        high = grad.astype(BF).astype(F32)
+        lane = lax.broadcasted_iota(jnp.int32, (block, META), 1)
+        pair = jnp.where(lane == 0, high, jnp.where(lane == 1, grad - high, 0.0))
+        pairs[at] = pair.astype(BF)
+        return carry
+
+    lax.fori_loop(0, kept // block, activate, 0)
+    save = pltpu.make_async_copy(d_ab, d_hbm, sem_d)
+    save.start()
+
+    def widen(i, carry):
+        wide[columns(i, hidden)] = dot(slot_ref[...], d_ab[i], ROWS).astype(BF)
+        return carry
+
+    lax.fori_loop(0, 2, widen, 0)
+    dx[:, half:] = dot(slot_ref[...], pairs[...], ROWS).astype(BF)
+    tail = pltpu.make_async_copy(dx.at[:, half:], dx_hbm.at[:, half:], sem_m)
+    tail.start()
+
+    def step(i, carry):
+        at = pl.ds(pl.multiple_of(i * chunk, chunk), chunk)
+        load(i).wait()
+        dx[columns(i, chunk)] = dot(wide[...], both_w[at], LAST).astype(BF)
         fetch(dx, dx_hbm, sems_x, i, chunk).start()
         return carry
 
@@ -451,27 +485,32 @@
     their_dh = across(send_dh, 1)
     chunk = 512
     parts = half // chunk
-    d_all, dx = call(
+    factor, hid, both_w = call(
+        functools.partial(factor_kernel, chunk),
+        (shape(2, kept, hidden, dtype=F32), shape(kept, hidden), shape(half, 2 * hidden)),
+        (scales[0], scales[1], send_ab, their_ab, weights[0], weights[1]),
+        limit=LIMIT_FACTOR,
+        flops=16 * kept * hidden,
+        moved=8 * half * hidden,
+        in_specs=[SMEM, SMEM, VMEM, VMEM, HBM, HBM],
+        out_specs=[VMEM] * 3,
+        scratch_shapes=[raw, raw, SEMS((parts,)), SEMS((parts,))],
+    )
+    d_ab, dx = call(
         functools.partial(backward_kernel, chunk),
-        (shape(3, kept, hidden), shape(rows, wide)),
-        (
-            scales[0], scales[1], send_ab, their_ab, send_dh, their_dh, slot_of,
-            weights[0], weights[1],
-        ),
+        (shape(2, kept, hidden), shape(rows, wide)),
+        (factor, hid, send_dh, their_dh, slot_of, both_w),
         limit=LIMIT_BACKWARD,
         flops=4 * rows * half * hidden,
         moved=4 * half * hidden + 2 * rows * half,
-        in_specs=[SMEM, SMEM] + [VMEM] * 5 + [HBM, HBM],
+        in_specs=[VMEM] * 5 + [HBM],
         out_specs=[HBM, HBM],
         scratch_shapes=[
-            pltpu.VMEM((3, kept, hidden), BF),
+            pltpu.VMEM((2, kept, hidden), BF),
             pltpu.VMEM((rows, 2 * hidden), BF),
             pltpu.VMEM((kept, META), BF),
-            raw,
-            raw,
-            pltpu.VMEM((chunk, 2 * hidden), BF),
+            pltpu.VMEM((half, 2 * hidden), BF),
             pltpu.VMEM((rows, wide), BF),
-            SEMS((parts,)),
             SEMS((parts,)),
             SEMS((parts,)),
             SEMS,
@@ -481,8 +520,9 @@
     returned = spread(dx)
     grads = [
         dot(left, right, ROWS).astype(BF)
-        for left, right in ((rows_x, d_all[0]), (rows_x, d_all[1]), (rows_dy, d_all[2]))
+        for left, right in ((rows_x, d_ab[0]), (rows_x, d_ab[1]), (rows_dy, hid))
     ]
+    returned, *grads = lax.optimization_barrier((returned, *grads))
     blocks = call(
         functools.partial(combine_kernel, n_local, top),
         tuple(shape(tok, wide) for _ in range(n_group)),

time: 169 us -> 169 us (level)
  Pallas kernels: 29.2 us -> 36.4 us
  waiting for transfers between devices: 87.4 us -> 82 us
  matrix products: 14.3 us -> 12.1 us
    pallas_call x8 -> x9, Pallas kernels: 29.2 us -> 36.4 us  [call(): pl.pallas_call(kernel, out_shape=outs, compiler_params=pltpu.CompilerPara...]
    ppermute x11, waiting for transfers between devices: 21.7 us -> 18.7 us  [across(): lax.ppermute(block, 'group', [(i, i ^ apart) for i in range(n_group)])]
    all_to_all x3, waiting for transfers between devices: 65.7 us -> 63.4 us  [spread(): lax.all_to_all(block, 'local', split_axis=0, concat_axis=0, tiled=True)]
    dot_general x3, matrix products: 14.3 us -> 12.1 us  [dot(): return lax.dot_general(left, right, dims, preferred_element_type=F32)]
  transfers between devices with their start and end apart: 14 -> 14, of which waited for: 9 -> 10; matrix products, arithmetic and copies ran while one was open for 8% -> 7% of each run, Pallas kernels for 8% -> 13%
where the time goes in v5:
time: 169 us; the launch traced here: 168 us
  waiting for transfers between devices  82 us (49%)
  Pallas kernels  36.4 us (22%)
  starting transfers between devices  32.5 us (19%)
  matrix products  12.1 us (7%)
  local copies, waits for them, and re-layouts  4.56 us (3%)
    all_to_all x3, waiting for transfers between devices, spread(): lax.all_to_all(block, 'local', split_axis=0, concat_axis=0, tiled=True)  63.4 us
    pallas_call x9, Pallas kernels, call(): pl.pallas_call(kernel, out_shape=outs, compiler_params=pltpu.CompilerPara...  36.4 us
    all_to_all x3, starting transfers between devices, spread(): lax.all_to_all(block, 'local', split_axis=0, concat_axis=0, tiled=True)  19.8 us
    ppermute x11, waiting for transfers between devices, across(): lax.ppermute(block, 'group', [(i, i ^ apart) for i in range(n_group)])  18.7 us
    ppermute x11, starting transfers between devices, across(): lax.ppermute(block, 'group', [(i, i ^ apart) for i in range(n_group)])  12.7 us
    dot_general x3, matrix products, dot(): return lax.dot_general(left, right, dims, preferred_element_type=F32)  12.1 us
    unnamed x23, local copies, waits for them, and re-layouts  4.55 us
  transfers between devices with their start and end apart: 14, of which 10 were waited for; matrix products, arithmetic and copies ran while one was open for 7% of the time, Pallas kernels for 13%

profile of v5, /device:TPU:0, one launch (start us, length us, event | category | flops | bytes accessed | tf_op | source)
XLA Modules:
  0.0 168.4 jit_solution(16109805629507058482)
XLA Ops:
  0.6 1.9 %shard_map.164 = (bf16[16,2176]{1,0:T(8,128)(2,1)}, bf16[16,2176]{1,0:T(8,128)(2,1)}, bf16[16,2048]{1,0:T(8,128)(2,1)}, bf16[16,2048]{1,0:T(8,128)(2,1)}) custom-call(bf16[16,4096]{1,0:T(8,128)(2,1)} %xq_ref.1, f32[16,32]{1,0:T(8,128)} %xs_ref.1, bf16[16,4096]{1,0:T(8,128)(2,1)} %dy_ref.1, s32[8,16]{1,0:T(8,128)} %bitcast.49, s32[8,16]{1,0:T(8,128)} %bitcast.50, ...), custom_call_target="tpu_custom_call" | custom-call | bytes 524288 | tf_op jit(solution)/shard_map/pallas_call | solution.py:31
  2.5 3.1 %collective-permute-start.1 = (bf16[16,2176]{1,0:T(8,128)(2,1)}, bf16[16,2176]{1,0:T(8,128)(2,1)S(1)}, u32[]{:S(2)}, u32[]{:S(2)}) collective-permute-start(bf16[16,2176]{1,0:T(8,128)(2,1)} %get-tuple-element.35.b0), channel_id=1, source_target_pairs={{0,64},{32,96},{64,0},{96,32},{1,65},{33,97},{65,1},{97,33},{2,66}... | collective-permute-start | bytes 208904 | tf_op jit(solution)/shard_map/ppermute | solution.py:409
  6.8 1.8 %collective-permute-done.1.b2 = bf16[16,2176]{1,0:T(8,128)(2,1)S(1)} collective-permute-done((bf16[16,2176]{1,0:T(8,128)(2,1)}, bf16[16,2176]{1,0:T(8,128)(2,1)S(1)}, u32[]{:S(2)}, u32[]{:S(2)}) %collective-permute-start.1) | collective-permute-done | bytes 69664 | tf_op jit(solution)/shard_map/ppermute | solution.py:409
  8.5 2.8 %collective-permute-done.2.b3 = bf16[16,2176]{1,0:T(8,128)(2,1)S(1)} collective-permute-done((bf16[16,2176]{1,0:T(8,128)(2,1)}, bf16[16,2176]{1,0:T(8,128)(2,1)S(1)}, u32[]{:S(2)}, u32[]{:S(2)}) %collective-permute-start.2) | collective-permute-done | bytes 69664 | tf_op jit(solution)/shard_map/ppermute | solution.py:409
  12.2 2.3 %shard_map.165 = (bf16[512,2176]{1,0:T(8,128)(2,1)}, bf16[512,64]{1,0:T(8,128)(2,1)S(1)}, bf16[512,64]{1,0:T(8,128)(2,1)S(1)}, bf16[64,128]{1,0:T(8,128)(2,1)S(1)}) custom-call(bf16[16,2176]{1,0:T(8,128)(2,1)S(1)} %copy-done.2, bf16[16,2176]{1,0:T(8,128)(2,1)S(1)} %collective-permute-done.b1, bf16[16,2176]{1,0:T(8,128)(2,1)S(1)} %collective-permute-done.1.b2, ...), custom_call_target="tpu_custom_call" | custom-call | flops 142606336 | bytes 2228224 | tf_op jit(solution)/shard_map/pallas_call | solution.py:31
  14.6 8.5 %all-to-all-start = ((bf16[32,16,2176]{2,1,0:T(8,128)(2,1)}), bf16[32,16,2176]{2,1,0:T(8,128)(2,1)S(1)}, u32[]{:S(2)}, u32[]{:S(2)}) async-start(bf16[32,16,2176]{2,1,0:T(8,128)(2,1)} %bitcast.6), calls=%async_computation | async-start | bytes 4456448 | tf_op jit(solution)/shard_map/all_to_all | solution.py:412
  26.7 2.3 %collective-permute-done.4.b2 = bf16[16,2048]{1,0:T(8,128)(2,1)S(1)} collective-permute-done((bf16[16,2048]{1,0:T(8,128)(2,1)S(1)}, bf16[16,2048]{1,0:T(8,128)(2,1)S(1)}, u32[]{:S(2)}, u32[]{:S(2)}) %collective-permute-start.4) | collective-permute-done | bytes 65568 | tf_op jit(solution)/shard_map/ppermute | solution.py:409
  30.4 2.0 %shard_map.166 = bf16[512,2048]{1,0:T(8,128)(2,1)} custom-call(bf16[512,64]{1,0:T(8,128)(2,1)S(1)} %get-tuple-element.38.gated_ref, bf16[16,2048]{1,0:T(8,128)(2,1)S(1)} %copy-done, bf16[16,2048]{1,0:T(8,128)(2,1)S(1)} %collective-permute-done.3.b1, bf16[16,2048]{1,0:T(8,128)(2,1)S(1)} %collective-permute-done.4.b2, ...), custom_call_target="tpu_custom_call" | custom-call | flops 134217728 | bytes 2097152 | tf_op jit(solution)/shard_map/pallas_call | solution.py:31
  32.3 22.3 %all-to-all-done = bf16[32,16,2176]{2,1,0:T(8,128)(2,1)S(1)} async-done(((bf16[32,16,2176]{2,1,0:T(8,128)(2,1)}), bf16[32,16,2176]{2,1,0:T(8,128)(2,1)S(1)}, u32[]{:S(2)}, u32[]{:S(2)}) %all-to-all-start) | async-done | bytes 2228256 | tf_op jit(solution)/shard_map/all_to_all | solution.py:412
  56.0 4.8 %all-to-all-start.1 = ((bf16[32,16,2048]{2,1,0:T(8,128)(2,1)}), bf16[32,16,2048]{2,1,0:T(8,128)(2,1)}, u32[]{:S(2)}, u32[]{:S(2)}) async-start(bf16[32,16,2048]{2,1,0:T(8,128)(2,1)} %bitcast.11), calls=%async_computation.1 | async-start | bytes 4194304 | tf_op jit(solution)/shard_map/all_to_all | solution.py:412
  60.8 6.9 %shard_map.167 = (bf16[384,2048]{1,0:T(8,128)(2,1)S(1)}, bf16[2,384,768]{2,1,0:T(8,128)(2,1)S(1)}, bf16[384,512]{1,0:T(8,128)(2,1)S(1)}) custom-call(f32[6,16]{1,0:T(8,128)S(1)} %get-tuple-element.66.sg_ref, f32[6,16]{1,0:T(8,128)S(1)} %get-tuple-element.65.su_ref, bf16[512,2176]{1,0:T(8,128)(2,1)} %bitcast.47, bf16[2048,768]{1,0:T(8,128)(2,1)} %bitcast.42, ...), custom_call_target="tpu_custom_call" | custom-call | flops 2415919104 | bytes 10485760 | tf_op jit(solution)/shard_map/pallas_call | solution.py:31
  69.0 21.8 %all-to-all-done.1 = bf16[32,16,2048]{2,1,0:T(8,128)(2,1)} async-done(((bf16[32,16,2048]{2,1,0:T(8,128)(2,1)}), bf16[32,16,2048]{2,1,0:T(8,128)(2,1)}, u32[]{:S(2)}, u32[]{:S(2)}) %all-to-all-start.1) | async-done | bytes 2097184 | tf_op jit(solution)/shard_map/all_to_all | solution.py:412
  90.8 5.2 %shard_map.169 = (bf16[384,2048]{1,0:T(8,128)(2,1)S(1)}, bf16[384,768]{1,0:T(8,128)(2,1)S(1)}) custom-call(f32[6,16]{1,0:T(8,128)S(1)} %bitcast.41, bf16[384,512]{1,0:T(8,128)(2,1)S(1)} %get-tuple-element.45.slot_ref, bf16[512,2048]{1,0:T(8,128)(2,1)} %bitcast.12.dy_ref, bf16[2048,768]{1,0:T(8,128)(2,1)} %bitcast.46), custom_call_target="tpu_custom_call" | custom-call | flops 1207959552 | bytes 7340032 | tf_op jit(solution)/shard_map/pallas_call | solution.py:31
  97.2 7.2 %shard_map.168 = (f32[2,384,768]{2,1,0:T(8,128)}, bf16[384,768]{1,0:T(8,128)(2,1)S(1)}, bf16[2048,1536]{1,0:T(8,128)(2,1)}) custom-call(f32[6,16]{1,0:T(8,128)S(1)} %get-tuple-element.66.sg_ref, f32[6,16]{1,0:T(8,128)S(1)} %get-tuple-element.65.su_ref, bf16[2,384,768]{2,1,0:T(8,128)(2,1)S(1)} %get-tuple-element.42.ab_ref, ...), custom_call_target="tpu_custom_call" | custom-call | flops 4718592 | bytes 12582912 | tf_op jit(solution)/shard_map/pallas_call | solution.py:31
  104.4 6.1 %collective-permute-done.7.dh_in = bf16[384,768]{1,0:T(8,128)(2,1)S(1)} collective-permute-done((bf16[384,768]{1,0:T(8,128)(2,1)S(1)}, bf16[384,768]{1,0:T(8,128)(2,1)S(1)}, u32[]{:S(2)}, u32[]{:S(2)}) %collective-permute-start.7) | collective-permute-done | bytes 589856 | tf_op jit(solution)/shard_map/ppermute | solution.py:409
  110.5 9.0 %shard_map.170 = (bf16[2,384,768]{2,1,0:T(8,128)(2,1)}, bf16[512,2176]{1,0:T(8,128)(2,1)}) custom-call(f32[2,384,768]{2,1,0:T(8,128)} %get-tuple-element.43.factor_ref, bf16[384,768]{1,0:T(8,128)(2,1)S(1)} %get-tuple-element.44.hid_ref, bf16[384,768]{1,0:T(8,128)(2,1)S(1)} %get-tuple-element.47.dh_ref, bf16[384,768]{1,0:T(8,128)(2,1)S(1)} %collective-permute-done.7.dh_in, ...), custom_call_target="tpu_custom_call" | custom-call | flops 3221225472 | bytes 8388608 | tf_op jit(solution)/shard_map/pallas_call | solution.py:31
  119.5 6.6 %all-to-all-start.2 = ((bf16[32,16,2176]{2,1,0:T(8,128)(2,1)}), bf16[32,16,2176]{2,1,0:T(8,128)(2,1)S(1)}, u32[]{:S(2)}, u32[]{:S(2)}) async-start(bf16[32,16,2176]{2,1,0:T(8,128)(2,1)} %bitcast.48), calls=%async_computation.2 | async-start | bytes 4456448 | tf_op jit(solution)/shard_map/all_to_all | solution.py:412
  126.1 5.1 %convolution_convert_fusion = bf16[2048,768]{1,0:T(8,128)(2,1)} fusion(bf16[384,2048]{1,0:T(8,128)(2,1)} %copy-done.1, bf16[384,768]{1,0:T(8,128)(2,1)S(1)} %get-tuple-element.44.hid_ref), kind=kOutput, calls=%fused_computation | convolution fusion | flops 1209532416 | bytes 5308416 | tf_op jit(solution)/shard_map/dot_general | solution.py:27
  131.2 3.5 %convolution_convert_fusion.1 = bf16[2048,768]{1,0:T(8,128)(2,1)} fusion(bf16[384,2048]{1,0:T(8,128)(2,1)S(1)} %copy-done.4, bf16[2,384,768]{2,1,0:T(8,128)(2,1)S(1)} %copy-done.10), kind=kOutput, calls=%fused_computation.1 | convolution fusion | flops 1209532416 | bytes 5308416 | tf_op jit(solution)/shard_map/dot_general | solution.py:27
  134.7 3.5 %convolution_convert_fusion.2 = bf16[2048,768]{1,0:T(8,128)(2,1)} fusion(bf16[384,2048]{1,0:T(8,128)(2,1)S(1)} %copy-done.4, bf16[2,384,768]{2,1,0:T(8,128)(2,1)S(1)} %copy-done.10), kind=kOutput, calls=%fused_computation.2 | convolution fusion | flops 1209532416 | bytes 5308416 | tf_op jit(solution)/shard_map/dot_general | solution.py:27
  138.3 19.3 %all-to-all-done.2 = bf16[32,16,2176]{2,1,0:T(8,128)(2,1)S(1)} async-done(((bf16[32,16,2176]{2,1,0:T(8,128)(2,1)}), bf16[32,16,2176]{2,1,0:T(8,128)(2,1)S(1)}, u32[]{:S(2)}, u32[]{:S(2)}) %all-to-all-start.2) | async-done | bytes 2228256 | tf_op jit(solution)/shard_map/all_to_all | solution.py:412
  158.9 3.2 %collective-permute-start.9 = (bf16[16,2176]{1,0:T(8,128)(2,1)S(1)}, bf16[16,2176]{1,0:T(8,128)(2,1)S(1)}, u32[]{:S(2)}, u32[]{:S(2)}) collective-permute-start(bf16[16,2176]{1,0:T(8,128)(2,1)S(1)} %get-tuple-element.58), channel_id=1, source_target_pairs={{0,64},{32,96},{64,0},{96,32},{1,65},{33,97},{65,1},{97,33},{2,66}... | collective-permute-start | bytes 208904 | tf_op jit(solution)/shard_map/ppermute | solution.py:409
  163.4 1.8 %collective-permute-done.9.b2 = bf16[16,2176]{1,0:T(8,128)(2,1)S(1)} collective-permute-done((bf16[16,2176]{1,0:T(8,128)(2,1)S(1)}, bf16[16,2176]{1,0:T(8,128)(2,1)S(1)}, u32[]{:S(2)}, u32[]{:S(2)}) %collective-permute-start.9) | collective-permute-done | bytes 69664 | tf_op jit(solution)/shard_map/ppermute | solution.py:409
  165.2 2.5 %collective-permute-done.10.b3 = bf16[16,2176]{1,0:T(8,128)(2,1)S(1)} collective-permute-done((bf16[16,2176]{1,0:T(8,128)(2,1)S(1)}, bf16[16,2176]{1,0:T(8,128)(2,1)S(1)}, u32[]{:S(2)}, u32[]{:S(2)}) %collective-permute-start.10) | collective-permute-done | bytes 69664 | tf_op jit(solution)/shard_map/ppermute | solution.py:409
  (40 shorter events, 14.1 us)
Async XLA Ops:
  2.5 6.0 %collective-permute-start.1 = (bf16[16,2176]{1,0:T(8,128)(2,1)}, bf16[16,2176]{1,0:T(8,128)(2,1)S(1)}, u32[]{:S(2)}, u32[]{:S(2)}) collective-permute-start(bf16[16,2176]{1,0:T(8,128)(2,1)} %get-tuple-element.35.b0), channel_id=1, source_target_pairs={{0,64},{32,96},{64,0},{96,32},{1,65},{33,97},{65,1},{97,33},{2,66}... | collective-permute-start | bytes 208904 | tf_op jit(solution)/shard_map/ppermute | solution.py:409
  5.6 5.7 %collective-permute-start.2 = (bf16[16,2176]{1,0:T(8,128)(2,1)}, bf16[16,2176]{1,0:T(8,128)(2,1)S(1)}, u32[]{:S(2)}, u32[]{:S(2)}) collective-permute-start(bf16[16,2176]{1,0:T(8,128)(2,1)} %get-tuple-element.36), channel_id=1, source_target_pairs={{0,96},{32,64},{64,32},{96,0},{1,97},{33,65},{65,33},{97,1},{2,98}... | collective-permute-start | bytes 208904 | tf_op jit(solution)/shard_map/ppermute | solution.py:409
  6.8 4.6 %collective-permute-start = (bf16[16,2176]{1,0:T(8,128)(2,1)}, bf16[16,2176]{1,0:T(8,128)(2,1)S(1)}, u32[]{:S(2)}, u32[]{:S(2)}) collective-permute-start(bf16[16,2176]{1,0:T(8,128)(2,1)} %get-tuple-element.36), channel_id=1, source_target_pairs={{0,32},{32,0},{64,96},{96,64},{1,33},{33,1},{65,97},{97,65},{2,34}... | collective-permute-start | bytes 208904 | tf_op jit(solution)/shard_map/ppermute | solution.py:409
  14.6 8.5 %copy-start = (bf16[16,2048]{1,0:T(8,128)(2,1)S(1)}, bf16[16,2048]{1,0:T(8,128)(2,1)}, u32[]{:S(2)}) copy-start(bf16[16,2048]{1,0:T(8,128)(2,1)} %get-tuple-element.39.b0) | copy-start | bytes 196612
  14.6 10.1 %copy-start.9 = (bf16[16,2048]{1,0:T(8,128)(2,1)S(1)}, bf16[16,2048]{1,0:T(8,128)(2,1)}, u32[]{:S(2)}) copy-start(bf16[16,2048]{1,0:T(8,128)(2,1)} %get-tuple-element.40) | copy-start | bytes 196612
  14.6 40.0 %all-to-all-start = ((bf16[32,16,2176]{2,1,0:T(8,128)(2,1)}), bf16[32,16,2176]{2,1,0:T(8,128)(2,1)S(1)}, u32[]{:S(2)}, u32[]{:S(2)}) async-start(bf16[32,16,2176]{2,1,0:T(8,128)(2,1)} %bitcast.6), calls=%async_computation | async-start | bytes 4456448 | tf_op jit(solution)/shard_map/all_to_all | solution.py:412
  23.1 5.9 %collective-permute-start.4 = (bf16[16,2048]{1,0:T(8,128)(2,1)S(1)}, bf16[16,2048]{1,0:T(8,128)(2,1)S(1)}, u32[]{:S(2)}, u32[]{:S(2)}) collective-permute-start(bf16[16,2048]{1,0:T(8,128)(2,1)S(1)} %copy-done), channel_id=1, source_target_pairs={{0,64},{32,96},{64,0},{96,32},{1,65},{33,97},{65,1},{97,33},{2,66}... | collective-permute-start | bytes 196616 | tf_op jit(solution)/shard_map/ppermute | solution.py:409
  24.7 5.7 %collective-permute-start.5 = (bf16[16,2048]{1,0:T(8,128)(2,1)S(1)}, bf16[16,2048]{1,0:T(8,128)(2,1)S(1)}, u32[]{:S(2)}, u32[]{:S(2)}) collective-permute-start(bf16[16,2048]{1,0:T(8,128)(2,1)S(1)} %copy-done.9), channel_id=1, source_target_pairs={{0,96},{32,64},{64,32},{96,0},{1,97},{33,65},{65,33},{97,1},{2,98}... | collective-permute-start | bytes 196616 | tf_op jit(solution)/shard_map/ppermute | solution.py:409
  25.9 4.5 %collective-permute-start.3 = (bf16[16,2048]{1,0:T(8,128)(2,1)S(1)}, bf16[16,2048]{1,0:T(8,128)(2,1)S(1)}, u32[]{:S(2)}, u32[]{:S(2)}) collective-permute-start(bf16[16,2048]{1,0:T(8,128)(2,1)S(1)} %copy-done.9), channel_id=1, source_target_pairs={{0,32},{32,0},{64,96},{96,64},{1,33},{33,1},{65,97},{97,65},{2,34}... | collective-permute-start | bytes 196616 | tf_op jit(solution)/shard_map/ppermute | solution.py:409
  54.7 1.4 copy-start.5
  54.7 6.1 %copy-start.6 = (f32[16,1,6]{0,1,2:T(1,128)S(1)}, f32[16,1,6]{0,1,2:T(1,128)}, u32[]{:S(2)}) copy-start(f32[16,1,6]{0,1,2:T(1,128)} %param.24) | copy-start | bytes 1156
  54.7 6.2 %copy-start.7 = (f32[16,1,6]{0,1,2:T(1,128)S(1)}, f32[16,1,6]{0,1,2:T(1,128)}, u32[]{:S(2)}) copy-start(f32[16,1,6]{0,1,2:T(1,128)} %param.23) | copy-start | bytes 1156
  56.0 34.7 %all-to-all-start.1 = ((bf16[32,16,2048]{2,1,0:T(8,128)(2,1)}), bf16[32,16,2048]{2,1,0:T(8,128)(2,1)}, u32[]{:S(2)}, u32[]{:S(2)}) async-start(bf16[32,16,2048]{2,1,0:T(8,128)(2,1)} %bitcast.11), calls=%async_computation.1 | async-start | bytes 4194304 | tf_op jit(solution)/shard_map/all_to_all | solution.py:412
  60.8 8.1 %copy-start.8 = (f32[16,1,6]{0,1,2:T(1,128)S(1)}, f32[16,1,6]{0,1,2:T(1,128)}, u32[]{:S(2)}) copy-start(f32[16,1,6]{0,1,2:T(1,128)} %param.25) | copy-start | bytes 1156
  67.8 1.1 copy-start.3
  68.9 28.3 %collective-permute-start.6 = (bf16[2,384,768]{2,1,0:T(8,128)(2,1)S(1)}, bf16[2,384,768]{2,1,0:T(8,128)(2,1)S(1)}, u32[]{:S(2)}, u32[]{:S(2)}) collective-permute-start(bf16[2,384,768]{2,1,0:T(8,128)(2,1)S(1)} %get-tuple-element.42.ab_ref), channel_id=1, source_target_pairs={{0,32},{32,0},{64,96},{96,64},{1,33},{33,1},{65,97},{97,65},{2,34}... | collective-permute-start | bytes 3538952 | tf_op jit(solution)/shard_map/ppermute | solution.py:409
  96.0 1.1 copy-start.1
  97.2 13.3 %collective-permute-start.7 = (bf16[384,768]{1,0:T(8,128)(2,1)S(1)}, bf16[384,768]{1,0:T(8,128)(2,1)S(1)}, u32[]{:S(2)}, u32[]{:S(2)}) collective-permute-start(bf16[384,768]{1,0:T(8,128)(2,1)S(1)} %get-tuple-element.47.dh_ref), channel_id=1, source_target_pairs={{0,32},{32,0},{64,96},{96,64},{1,33},{33,1},{65,97},{97,65},{2,34}... | collective-permute-start | bytes 1769480 | tf_op jit(solution)/shard_map/ppermute | solution.py:409
  119.5 38.0 %all-to-all-start.2 = ((bf16[32,16,2176]{2,1,0:T(8,128)(2,1)}), bf16[32,16,2176]{2,1,0:T(8,128)(2,1)S(1)}, u32[]{:S(2)}, u32[]{:S(2)}) async-start(bf16[32,16,2176]{2,1,0:T(8,128)(2,1)} %bitcast.48), calls=%async_computation.2 | async-start | bytes 4456448 | tf_op jit(solution)/shard_map/all_to_all | solution.py:412
  126.1 5.1 %copy-start.4 = (bf16[384,2048]{1,0:T(8,128)(2,1)S(1)}, bf16[384,2048]{1,0:T(8,128)(2,1)}, u32[]{:S(2)}) copy-start(bf16[384,2048]{1,0:T(8,128)(2,1)} %copy-done.3) | copy-start | bytes 4718596
  126.1 5.1 %copy-start.10 = (bf16[2,384,768]{2,1,0:T(8,128)(2,1)S(1)}, bf16[2,384,768]{2,1,0:T(8,128)(2,1)}, u32[]{:S(2)}) copy-start(bf16[2,384,768]{2,1,0:T(8,128)(2,1)} %get-tuple-element.51) | copy-start | bytes 3538948
  158.6 4.8 %collective-permute-start.8 = (bf16[16,2176]{1,0:T(8,128)(2,1)S(1)}, bf16[16,2176]{1,0:T(8,128)(2,1)S(1)}, u32[]{:S(2)}, u32[]{:S(2)}) collective-permute-start(bf16[16,2176]{1,0:T(8,128)(2,1)S(1)} %get-tuple-element.57), channel_id=1, source_target_pairs={{0,32},{32,0},{64,96},{96,64},{1,33},{33,1},{65,97},{97,65},{2,34}... | collective-permute-start | bytes 208904 | tf_op jit(solution)/shard_map/ppermute | solution.py:409
  158.9 6.2 %collective-permute-start.9 = (bf16[16,2176]{1,0:T(8,128)(2,1)S(1)}, bf16[16,2176]{1,0:T(8,128)(2,1)S(1)}, u32[]{:S(2)}, u32[]{:S(2)}) collective-permute-start(bf16[16,2176]{1,0:T(8,128)(2,1)S(1)} %get-tuple-element.58), channel_id=1, source_target_pairs={{0,64},{32,96},{64,0},{96,32},{1,65},{33,97},{65,1},{97,33},{2,66}... | collective-permute-start | bytes 208904 | tf_op jit(solution)/shard_map/ppermute | solution.py:409
  162.1 5.5 %collective-permute-start.10 = (bf16[16,2176]{1,0:T(8,128)(2,1)S(1)}, bf16[16,2176]{1,0:T(8,128)(2,1)S(1)}, u32[]{:S(2)}, u32[]{:S(2)}) collective-permute-start(bf16[16,2176]{1,0:T(8,128)(2,1)S(1)} %get-tuple-element.59), channel_id=1, source_target_pairs={{0,96},{32,64},{64,32},{96,0},{1,97},{33,65},{65,33},{97,1},{2,98}... | collective-permute-start | bytes 208904 | tf_op jit(solution)/shard_map/ppermute | solution.py:409
  (1 other events, 0.9 us)

commit v6 on v5

--- a/solution.py
+++ b/solution.py
@@ -14,9 +14,9 @@
 F32 = jnp.float32
 MIB = 1024 * 1024
 LIMIT = 24
-LIMIT_FACTOR = 50
-LIMIT_FORWARD = 50
-LIMIT_DOWN = 50
+LIMIT_FACTOR = 52
+LIMIT_FORWARD = 52
+LIMIT_DOWN = 52
 LIMIT_BACKWARD = 51
 
 ROWS = (((0,), (0,)), ((), ()))
@@ -168,9 +168,17 @@
     return pltpu.make_async_copy(source.at[at], target.at[at], sems.at[i])
 
 
-def compact(slot_ref, rows_ref, kept, size=512):
+def start_all(source, target, sems):
+    for i in range(sems.shape[0]):
+        fetch(source, target, sems, i, target.shape[1] // sems.shape[0]).start()
+
+
+def compact(slot_ref, rows_hbm, rows_ref, sems, kept):
+    size = kept.shape[1] // sems.shape[0]
+
     def step(i, carry):
         at = columns(i, size)
+        fetch(rows_hbm, rows_ref, sems, i, size).wait()
         kept[at] = dot(slot_ref[...], rows_ref[at]).astype(BF)
         return carry
 
@@ -178,18 +186,23 @@
 
 
 def forward_kernel(
-    n_local, top, cols, sg_ref, su_ref, x_ref, wg_hbm, wu_hbm,
-    kept_hbm, send_ref, slot_ref, kept, wg_raw, wu_raw, wg, wu, sems_g, sems_u, sem_k,
+    n_local, top, cols, sg_ref, su_ref, x_hbm, wg_hbm, wu_hbm,
+    kept_hbm, send_ref, slot_ref, x_ref, meta_ref, kept, wg_raw, wu_raw, wg, wu,
+    sems_x, sems_g, sems_u, sem_m, sem_k,
 ):
     half, hidden = wg_raw.shape
     steps = hidden // cols
+    tail = pltpu.make_async_copy(x_hbm.at[:, half:], meta_ref, sem_m)
+    tail.start()
+    start_all(x_hbm, x_ref, sems_x)
     for i in range(steps):
         fetch(wg_hbm, wg_raw, sems_g, i, cols).start()
         fetch(wu_hbm, wu_raw, sems_u, i, cols).start()
     lane = lax.broadcasted_iota(jnp.int32, (2 * top, META), 1)
     row = lax.broadcasted_iota(jnp.int32, (2 * top, META), 0)
     turn = jnp.where(lane == row, 1.0, 0.0).astype(BF)
-    meta = dot(turn, x_ref[:, half:], LAST)
+    tail.wait()
+    meta = dot(turn, meta_ref[...], LAST)
     own = (
         1 + lax.div(lax.axis_index("group"), 2) * n_local + lax.axis_index("local")
     ).astype(F32)
@@ -201,7 +214,7 @@
         target = jnp.where(code == own + 64.0, slot + CAP, target)
     row = lax.broadcasted_iota(jnp.int32, slot_ref.shape, 0).astype(F32)
     slot_ref[...] = jnp.where(row == target, 1.0, 0.0).astype(BF)
-    compact(slot_ref, x_ref, kept)
+    compact(slot_ref, x_hbm, x_ref, sems_x, kept)
     save = pltpu.make_async_copy(kept, kept_hbm, sem_k)
     save.start()
 
@@ -220,13 +233,15 @@
 
 
 def down_kernel(
-    cols, sv_ref, slot_ref, dy_ref, v_hbm, kept_hbm, send_ref, kept, v_raw, v, sems_v, sem_k
+    cols, sv_ref, slot_ref, dy_hbm, v_hbm, kept_hbm, send_ref,
+    dy_ref, kept, v_raw, v, sems_y, sems_v, sem_k,
 ):
     half, hidden = v_raw.shape
     steps = hidden // cols
+    start_all(dy_hbm, dy_ref, sems_y)
     for i in range(steps):
         fetch(v_hbm, v_raw, sems_v, i, cols).start()
-    compact(slot_ref, dy_ref, kept)
+    compact(slot_ref, dy_hbm, dy_ref, sems_y, kept)
     save = pltpu.make_async_copy(kept, kept_hbm, sem_k)
     save.start()
 
@@ -282,13 +297,20 @@
 
 
 def backward_kernel(
-    chunk, factor_ref, hid_ref, dh_ref, dh_in, slot_ref, w_hbm,
-    d_hbm, dx_hbm, d_ab, wide, pairs, both_w, dx, sems_w, sems_x, sem_d, sem_m,
+    chunk, factor_hbm, hid_ref, dh_ref, dh_in, slot_ref, w_hbm,
+    d_hbm, dx_hbm, factor_ref, d_ab, wide, pairs, both_w, dx, sems_f, sems_w, sems_x, sem_d, sem_m,
 ):
     kept, hidden = hid_ref.shape
     half = both_w.shape[0]
     parts = half // chunk
-    block = 64
+    block = kept // sems_f.shape[0]
+
+    def factors(i):
+        at = (slice(None), pl.ds(pl.multiple_of(i * block, block), block))
+        return pltpu.make_async_copy(factor_hbm.at[at], factor_ref.at[at], sems_f.at[i])
+
+    for i in range(kept // block):
+        factors(i).start()
 
     def load(i):
         at = pl.ds(pl.multiple_of(i * chunk, chunk), chunk)
@@ -300,6 +322,7 @@
     def activate(i, carry):
         at = pl.ds(pl.multiple_of(i * block, block), block)
         d_hidden = dh_ref[at].astype(F32) + dh_in[at].astype(F32)
+        factors(i).wait()
         d_ab[0, at] = (d_hidden * factor_ref[0, at]).astype(BF)
         d_ab[1, at] = (d_hidden * factor_ref[1, at]).astype(BF)
         grad = jnp.sum(hid_ref[at].astype(F32) * d_hidden, axis=1, keepdims=True)
@@ -462,11 +485,12 @@
         limit=LIMIT_FORWARD,
         flops=4 * kept * half * hidden,
         moved=4 * half * hidden + 4 * rows * half,
-        in_specs=[SMEM, SMEM, VMEM, HBM, HBM],
+        in_specs=[SMEM, SMEM, HBM, HBM, HBM],
         out_specs=[HBM, VMEM, VMEM],
-        scratch_shapes=[pltpu.VMEM((kept, half), BF), raw, raw]
+        scratch_shapes=[pltpu.VMEM((rows, half), BF), pltpu.VMEM((rows, META), BF)]
+        + [pltpu.VMEM((kept, half), BF), raw, raw]
         + [pltpu.VMEM((half, cols), BF)] * 2
-        + [SEMS((steps,)), SEMS((steps,)), SEMS],
+        + [SEMS((4,)), SEMS((steps,)), SEMS((steps,)), SEMS, SEMS],
     )
     their_ab = across(send_ab, 1)
     rows_dy, send_dh = call(
@@ -476,10 +500,11 @@
         limit=LIMIT_DOWN,
         flops=2 * kept * half * hidden,
         moved=2 * half * hidden + 4 * rows * half,
-        in_specs=[SMEM, VMEM, VMEM, HBM],
+        in_specs=[SMEM, VMEM, HBM, HBM],
         out_specs=[HBM, VMEM],
         scratch_shapes=[
-            pltpu.VMEM((kept, half), BF), raw, pltpu.VMEM((half, cols), BF), SEMS((steps,)), SEMS,
+            pltpu.VMEM((rows, half), BF), pltpu.VMEM((kept, half), BF), raw,
+            pltpu.VMEM((half, cols), BF), SEMS((4,)), SEMS((steps,)), SEMS,
         ],
     )
     their_dh = across(send_dh, 1)
@@ -503,14 +528,16 @@
         limit=LIMIT_BACKWARD,
         flops=4 * rows * half * hidden,
         moved=4 * half * hidden + 2 * rows * half,
-        in_specs=[VMEM] * 5 + [HBM],
+        in_specs=[HBM] + [VMEM] * 4 + [HBM],
         out_specs=[HBM, HBM],
         scratch_shapes=[
+            pltpu.VMEM((2, kept, hidden), F32),
             pltpu.VMEM((2, kept, hidden), BF),
             pltpu.VMEM((rows, 2 * hidden), BF),
             pltpu.VMEM((kept, META), BF),
             pltpu.VMEM((half, 2 * hidden), BF),
             pltpu.VMEM((rows, wide), BF),
+            SEMS((4,)),
             SEMS((parts,)),
             SEMS((parts,)),
             SEMS,

time: 169 us -> 169 us (level)
  local copies, waits for them, and re-layouts: 4.56 us -> 0.93 us
  Pallas kernels: 36.4 us -> 39.2 us
    unnamed x23 -> x17, local copies, waits for them, and re-layouts: 4.55 us -> 0.92 us
    pallas_call x9, Pallas kernels: 36.4 us -> 39.2 us  [call(): pl.pallas_call(kernel, out_shape=outs, compiler_params=pltpu.CompilerPara...]
  transfers between devices with their start and end apart: 14 -> 14, of which waited for: 10 -> 11; matrix products, arithmetic and copies ran while one was open for 7% -> 7% of each run, Pallas kernels for 13% -> 14%
where the time goes in v6:
time: 169 us; the launch traced here: 168 us
  waiting for transfers between devices  81.6 us (48%)
  Pallas kernels  39.2 us (23%)
  starting transfers between devices  33.9 us (20%)
  matrix products  12.1 us (7%)
    all_to_all x3, waiting for transfers between devices, spread(): lax.all_to_all(block, 'local', split_axis=0, concat_axis=0, tiled=True)  62.8 us
    pallas_call x9, Pallas kernels, call(): pl.pallas_call(kernel, out_shape=outs, compiler_params=pltpu.CompilerPara...  39.2 us
    all_to_all x3, starting transfers between devices, spread(): lax.all_to_all(block, 'local', split_axis=0, concat_axis=0, tiled=True)  21.1 us
    ppermute x11, waiting for transfers between devices, across(): lax.ppermute(block, 'group', [(i, i ^ apart) for i in range(n_group)])  18.7 us
    ppermute x11, starting transfers between devices, across(): lax.ppermute(block, 'group', [(i, i ^ apart) for i in range(n_group)])  12.8 us
    dot_general x3, matrix products, dot(): return lax.dot_general(left, right, dims, preferred_element_type=F32)  12.1 us
  transfers between devices with their start and end apart: 14, of which 11 were waited for; matrix products, arithmetic and copies ran while one was open for 7% of the time, Pallas kernels for 14%

profile of v6, /device:TPU:0, one launch (start us, length us, event | category | flops | bytes accessed | tf_op | source)
XLA Modules:
  0.0 168.5 jit_solution(17952321133742678471)
XLA Ops:
  0.6 1.9 %shard_map.164 = (bf16[16,2176]{1,0:T(8,128)(2,1)}, bf16[16,2176]{1,0:T(8,128)(2,1)}, bf16[16,2048]{1,0:T(8,128)(2,1)}, bf16[16,2048]{1,0:T(8,128)(2,1)}) custom-call(bf16[16,4096]{1,0:T(8,128)(2,1)} %xq_ref.1, f32[16,32]{1,0:T(8,128)} %xs_ref.1, bf16[16,4096]{1,0:T(8,128)(2,1)} %dy_ref.1, s32[8,16]{1,0:T(8,128)} %bitcast.48, s32[8,16]{1,0:T(8,128)} %bitcast.49, ...), custom_call_target="tpu_custom_call" | custom-call | bytes 524288 | tf_op jit(solution)/shard_map/pallas_call | solution.py:31
  2.5 3.1 %collective-permute-start.1 = (bf16[16,2176]{1,0:T(8,128)(2,1)}, bf16[16,2176]{1,0:T(8,128)(2,1)S(1)}, u32[]{:S(2)}, u32[]{:S(2)}) collective-permute-start(bf16[16,2176]{1,0:T(8,128)(2,1)} %get-tuple-element.35.b0), channel_id=1, source_target_pairs={{0,64},{32,96},{64,0},{96,32},{1,65},{33,97},{65,1},{97,33},{2,66}... | collective-permute-start | bytes 208904 | tf_op jit(solution)/shard_map/ppermute | solution.py:432
  8.5 2.8 %collective-permute-done.2.b3 = bf16[16,2176]{1,0:T(8,128)(2,1)S(1)} collective-permute-done((bf16[16,2176]{1,0:T(8,128)(2,1)}, bf16[16,2176]{1,0:T(8,128)(2,1)S(1)}, u32[]{:S(2)}, u32[]{:S(2)}) %collective-permute-start.2) | collective-permute-done | bytes 69664 | tf_op jit(solution)/shard_map/ppermute | solution.py:432
  12.2 2.3 %shard_map.165 = (bf16[512,2176]{1,0:T(8,128)(2,1)}, bf16[512,64]{1,0:T(8,128)(2,1)S(1)}, bf16[512,64]{1,0:T(8,128)(2,1)S(1)}, bf16[64,128]{1,0:T(8,128)(2,1)S(1)}) custom-call(bf16[16,2176]{1,0:T(8,128)(2,1)S(1)} %copy-done.1, bf16[16,2176]{1,0:T(8,128)(2,1)S(1)} %collective-permute-done.b1, bf16[16,2176]{1,0:T(8,128)(2,1)S(1)} %collective-permute-done.1.b2, ...), custom_call_target="tpu_custom_call" | custom-call | flops 142606336 | bytes 2228224 | tf_op jit(solution)/shard_map/pallas_call | solution.py:31
  14.6 8.6 %all-to-all-start = ((bf16[32,16,2176]{2,1,0:T(8,128)(2,1)}), bf16[32,16,2176]{2,1,0:T(8,128)(2,1)}, u32[]{:S(2)}, u32[]{:S(2)}) async-start(bf16[32,16,2176]{2,1,0:T(8,128)(2,1)} %bitcast.6), calls=%async_computation | async-start | bytes 4456448 | tf_op jit(solution)/shard_map/all_to_all | solution.py:435
  26.8 2.3 %collective-permute-done.4.b2 = bf16[16,2048]{1,0:T(8,128)(2,1)S(1)} collective-permute-done((bf16[16,2048]{1,0:T(8,128)(2,1)S(1)}, bf16[16,2048]{1,0:T(8,128)(2,1)S(1)}, u32[]{:S(2)}, u32[]{:S(2)}) %collective-permute-start.4) | collective-permute-done | bytes 65568 | tf_op jit(solution)/shard_map/ppermute | solution.py:432
  30.5 1.9 %shard_map.166 = bf16[512,2048]{1,0:T(8,128)(2,1)} custom-call(bf16[512,64]{1,0:T(8,128)(2,1)S(1)} %get-tuple-element.38.gated_ref, bf16[16,2048]{1,0:T(8,128)(2,1)S(1)} %copy-done, bf16[16,2048]{1,0:T(8,128)(2,1)S(1)} %collective-permute-done.3.b1, bf16[16,2048]{1,0:T(8,128)(2,1)S(1)} %collective-permute-done.4.b2, ...), custom_call_target="tpu_custom_call" | custom-call | flops 134217728 | bytes 2097152 | tf_op jit(solution)/shard_map/pallas_call | solution.py:31
  32.4 22.3 %all-to-all-done = bf16[32,16,2176]{2,1,0:T(8,128)(2,1)} async-done(((bf16[32,16,2176]{2,1,0:T(8,128)(2,1)}), bf16[32,16,2176]{2,1,0:T(8,128)(2,1)}, u32[]{:S(2)}, u32[]{:S(2)}) %all-to-all-start) | async-done | bytes 2228256 | tf_op jit(solution)/shard_map/all_to_all | solution.py:435
  54.8 4.9 %all-to-all-start.1 = ((bf16[32,16,2048]{2,1,0:T(8,128)(2,1)}), bf16[32,16,2048]{2,1,0:T(8,128)(2,1)}, u32[]{:S(2)}, u32[]{:S(2)}) async-start(bf16[32,16,2048]{2,1,0:T(8,128)(2,1)} %bitcast.11), calls=%async_computation.1 | async-start | bytes 4194304 | tf_op jit(solution)/shard_map/all_to_all | solution.py:435
  59.7 8.6 %shard_map.167 = (bf16[384,2048]{1,0:T(8,128)(2,1)}, bf16[2,384,768]{2,1,0:T(8,128)(2,1)S(1)}, bf16[384,512]{1,0:T(8,128)(2,1)S(1)}) custom-call(f32[6,16]{1,0:T(8,128)S(1)} %get-tuple-element.66.sg_ref, f32[6,16]{1,0:T(8,128)S(1)} %get-tuple-element.65.su_ref, bf16[512,2176]{1,0:T(8,128)(2,1)} %bitcast.7.x_hbm, bf16[2048,768]{1,0:T(8,128)(2,1)} %bitcast.42, ...), custom_call_target="tpu_custom_call" | custom-call | flops 2415919104 | bytes 10485760 | tf_op jit(solution)/shard_map/pallas_call | solution.py:31
  68.4 21.2 %all-to-all-done.1 = bf16[32,16,2048]{2,1,0:T(8,128)(2,1)} async-done(((bf16[32,16,2048]{2,1,0:T(8,128)(2,1)}), bf16[32,16,2048]{2,1,0:T(8,128)(2,1)}, u32[]{:S(2)}, u32[]{:S(2)}) %all-to-all-start.1) | async-done | bytes 2097184 | tf_op jit(solution)/shard_map/all_to_all | solution.py:435
  89.6 5.2 %shard_map.169 = (bf16[384,2048]{1,0:T(8,128)(2,1)}, bf16[384,768]{1,0:T(8,128)(2,1)S(1)}) custom-call(f32[6,16]{1,0:T(8,128)S(1)} %bitcast.41, bf16[384,512]{1,0:T(8,128)(2,1)S(1)} %get-tuple-element.45.slot_ref, bf16[512,2048]{1,0:T(8,128)(2,1)} %bitcast.12.dy_hbm, bf16[2048,768]{1,0:T(8,128)(2,1)} %bitcast.46), custom_call_target="tpu_custom_call" | custom-call | flops 1207959552 | bytes 7340032 | tf_op jit(solution)/shard_map/pallas_call | solution.py:31
  95.0 2.1 %collective-permute-done.6.ab_in = bf16[2,384,768]{2,1,0:T(8,128)(2,1)} collective-permute-done((bf16[2,384,768]{2,1,0:T(8,128)(2,1)S(1)}, bf16[2,384,768]{2,1,0:T(8,128)(2,1)}, u32[]{:S(2)}, u32[]{:S(2)}) %collective-permute-start.6) | collective-permute-done | bytes 1179680 | tf_op jit(solution)/shard_map/ppermute | solution.py:432
  97.1 7.8 %shard_map.168 = (f32[2,384,768]{2,1,0:T(8,128)}, bf16[384,768]{1,0:T(8,128)(2,1)S(1)}, bf16[2048,1536]{1,0:T(8,128)(2,1)}) custom-call(f32[6,16]{1,0:T(8,128)S(1)} %get-tuple-element.66.sg_ref, f32[6,16]{1,0:T(8,128)S(1)} %get-tuple-element.65.su_ref, bf16[2,384,768]{2,1,0:T(8,128)(2,1)S(1)} %get-tuple-element.42.ab_ref, ...), custom_call_target="tpu_custom_call" | custom-call | flops 4718592 | bytes 12582912 | tf_op jit(solution)/shard_map/pallas_call | solution.py:31
  104.9 4.1 %collective-permute-done.7.dh_in = bf16[384,768]{1,0:T(8,128)(2,1)S(1)} collective-permute-done((bf16[384,768]{1,0:T(8,128)(2,1)S(1)}, bf16[384,768]{1,0:T(8,128)(2,1)S(1)}, u32[]{:S(2)}, u32[]{:S(2)}) %collective-permute-start.7) | collective-permute-done | bytes 589856 | tf_op jit(solution)/shard_map/ppermute | solution.py:432
  109.0 9.7 %shard_map.170 = (bf16[2,384,768]{2,1,0:T(8,128)(2,1)}, bf16[512,2176]{1,0:T(8,128)(2,1)}) custom-call(f32[2,384,768]{2,1,0:T(8,128)} %get-tuple-element.43.factor_hbm, bf16[384,768]{1,0:T(8,128)(2,1)S(1)} %get-tuple-element.44.hid_ref, bf16[384,768]{1,0:T(8,128)(2,1)S(1)} %get-tuple-element.47.dh_ref, bf16[384,768]{1,0:T(8,128)(2,1)S(1)} %collective-permute-done.7.dh_in, ...), custom_call_target="tpu_custom_call" | custom-call | flops 3221225472 | bytes 8388608 | tf_op jit(solution)/shard_map/pallas_call | solution.py:31
  118.7 7.6 %all-to-all-start.2 = ((bf16[32,16,2176]{2,1,0:T(8,128)(2,1)}), bf16[32,16,2176]{2,1,0:T(8,128)(2,1)S(1)}, u32[]{:S(2)}, u32[]{:S(2)}) async-start(bf16[32,16,2176]{2,1,0:T(8,128)(2,1)} %bitcast.47), calls=%async_computation.2 | async-start | bytes 4456448 | tf_op jit(solution)/shard_map/all_to_all | solution.py:435
  126.3 5.1 %convolution_convert_fusion = bf16[2048,768]{1,0:T(8,128)(2,1)} fusion(bf16[384,2048]{1,0:T(8,128)(2,1)} %get-tuple-element.52, bf16[384,768]{1,0:T(8,128)(2,1)S(1)} %get-tuple-element.44.hid_ref), kind=kOutput, calls=%fused_computation | convolution fusion | flops 1209532416 | bytes 5308416 | tf_op jit(solution)/shard_map/dot_general | solution.py:27
  131.3 3.5 %convolution_convert_fusion.1 = bf16[2048,768]{1,0:T(8,128)(2,1)} fusion(bf16[384,2048]{1,0:T(8,128)(2,1)S(1)} %copy-done.6, bf16[2,384,768]{2,1,0:T(8,128)(2,1)S(1)} %copy-done.7), kind=kOutput, calls=%fused_computation.1 | convolution fusion | flops 1209532416 | bytes 5308416 | tf_op jit(solution)/shard_map/dot_general | solution.py:27
  134.8 3.5 %convolution_convert_fusion.2 = bf16[2048,768]{1,0:T(8,128)(2,1)} fusion(bf16[384,2048]{1,0:T(8,128)(2,1)S(1)} %copy-done.6, bf16[2,384,768]{2,1,0:T(8,128)(2,1)S(1)} %copy-done.7), kind=kOutput, calls=%fused_computation.2 | convolution fusion | flops 1209532416 | bytes 5308416 | tf_op jit(solution)/shard_map/dot_general | solution.py:27
  138.3 19.3 %all-to-all-done.2 = bf16[32,16,2176]{2,1,0:T(8,128)(2,1)S(1)} async-done(((bf16[32,16,2176]{2,1,0:T(8,128)(2,1)}), bf16[32,16,2176]{2,1,0:T(8,128)(2,1)S(1)}, u32[]{:S(2)}, u32[]{:S(2)}) %all-to-all-start.2) | async-done | bytes 2228256 | tf_op jit(solution)/shard_map/all_to_all | solution.py:435
  159.1 3.2 %collective-permute-start.9 = (bf16[16,2176]{1,0:T(8,128)(2,1)S(1)}, bf16[16,2176]{1,0:T(8,128)(2,1)S(1)}, u32[]{:S(2)}, u32[]{:S(2)}) collective-permute-start(bf16[16,2176]{1,0:T(8,128)(2,1)S(1)} %get-tuple-element.58), channel_id=1, source_target_pairs={{0,64},{32,96},{64,0},{96,32},{1,65},{33,97},{65,1},{97,33},{2,66}... | collective-permute-start | bytes 208904 | tf_op jit(solution)/shard_map/ppermute | solution.py:432
  163.5 1.8 %collective-permute-done.9.b2 = bf16[16,2176]{1,0:T(8,128)(2,1)S(1)} collective-permute-done((bf16[16,2176]{1,0:T(8,128)(2,1)S(1)}, bf16[16,2176]{1,0:T(8,128)(2,1)S(1)}, u32[]{:S(2)}, u32[]{:S(2)}) %collective-permute-start.9) | collective-permute-done | bytes 69664 | tf_op jit(solution)/shard_map/ppermute | solution.py:432
  165.3 2.5 %collective-permute-done.10.b3 = bf16[16,2176]{1,0:T(8,128)(2,1)S(1)} collective-permute-done((bf16[16,2176]{1,0:T(8,128)(2,1)S(1)}, bf16[16,2176]{1,0:T(8,128)(2,1)S(1)}, u32[]{:S(2)}, u32[]{:S(2)}) %collective-permute-start.10) | collective-permute-done | bytes 69664 | tf_op jit(solution)/shard_map/ppermute | solution.py:432
  (34 shorter events, 12.4 us)
Async XLA Ops:
  2.5 6.0 %collective-permute-start.1 = (bf16[16,2176]{1,0:T(8,128)(2,1)}, bf16[16,2176]{1,0:T(8,128)(2,1)S(1)}, u32[]{:S(2)}, u32[]{:S(2)}) collective-permute-start(bf16[16,2176]{1,0:T(8,128)(2,1)} %get-tuple-element.35.b0), channel_id=1, source_target_pairs={{0,64},{32,96},{64,0},{96,32},{1,65},{33,97},{65,1},{97,33},{2,66}... | collective-permute-start | bytes 208904 | tf_op jit(solution)/shard_map/ppermute | solution.py:432
  5.6 5.7 %collective-permute-start.2 = (bf16[16,2176]{1,0:T(8,128)(2,1)}, bf16[16,2176]{1,0:T(8,128)(2,1)S(1)}, u32[]{:S(2)}, u32[]{:S(2)}) collective-permute-start(bf16[16,2176]{1,0:T(8,128)(2,1)} %get-tuple-element.36), channel_id=1, source_target_pairs={{0,96},{32,64},{64,32},{96,0},{1,97},{33,65},{65,33},{97,1},{2,98}... | collective-permute-start | bytes 208904 | tf_op jit(solution)/shard_map/ppermute | solution.py:432
  6.8 4.6 %collective-permute-start = (bf16[16,2176]{1,0:T(8,128)(2,1)}, bf16[16,2176]{1,0:T(8,128)(2,1)S(1)}, u32[]{:S(2)}, u32[]{:S(2)}) collective-permute-start(bf16[16,2176]{1,0:T(8,128)(2,1)} %get-tuple-element.36), channel_id=1, source_target_pairs={{0,32},{32,0},{64,96},{96,64},{1,33},{33,1},{65,97},{97,65},{2,34}... | collective-permute-start | bytes 208904 | tf_op jit(solution)/shard_map/ppermute | solution.py:432
  11.4 0.9 copy-start.1
  14.6 8.6 %copy-start = (bf16[16,2048]{1,0:T(8,128)(2,1)S(1)}, bf16[16,2048]{1,0:T(8,128)(2,1)}, u32[]{:S(2)}) copy-start(bf16[16,2048]{1,0:T(8,128)(2,1)} %get-tuple-element.39.b0) | copy-start | bytes 196612
  14.6 10.2 %copy-start.5 = (bf16[16,2048]{1,0:T(8,128)(2,1)S(1)}, bf16[16,2048]{1,0:T(8,128)(2,1)}, u32[]{:S(2)}) copy-start(bf16[16,2048]{1,0:T(8,128)(2,1)} %get-tuple-element.40) | copy-start | bytes 196612
  14.6 40.2 %all-to-all-start = ((bf16[32,16,2176]{2,1,0:T(8,128)(2,1)}), bf16[32,16,2176]{2,1,0:T(8,128)(2,1)}, u32[]{:S(2)}, u32[]{:S(2)}) async-start(bf16[32,16,2176]{2,1,0:T(8,128)(2,1)} %bitcast.6), calls=%async_computation | async-start | bytes 4456448 | tf_op jit(solution)/shard_map/all_to_all | solution.py:435
  23.2 5.9 %collective-permute-start.4 = (bf16[16,2048]{1,0:T(8,128)(2,1)S(1)}, bf16[16,2048]{1,0:T(8,128)(2,1)S(1)}, u32[]{:S(2)}, u32[]{:S(2)}) collective-permute-start(bf16[16,2048]{1,0:T(8,128)(2,1)S(1)} %copy-done), channel_id=1, source_target_pairs={{0,64},{32,96},{64,0},{96,32},{1,65},{33,97},{65,1},{97,33},{2,66}... | collective-permute-start | bytes 196616 | tf_op jit(solution)/shard_map/ppermute | solution.py:432
  24.8 5.7 %collective-permute-start.5 = (bf16[16,2048]{1,0:T(8,128)(2,1)S(1)}, bf16[16,2048]{1,0:T(8,128)(2,1)S(1)}, u32[]{:S(2)}, u32[]{:S(2)}) collective-permute-start(bf16[16,2048]{1,0:T(8,128)(2,1)S(1)} %copy-done.5), channel_id=1, source_target_pairs={{0,96},{32,64},{64,32},{96,0},{1,97},{33,65},{65,33},{97,1},{2,98}... | collective-permute-start | bytes 196616 | tf_op jit(solution)/shard_map/ppermute | solution.py:432
  26.0 4.5 %collective-permute-start.3 = (bf16[16,2048]{1,0:T(8,128)(2,1)S(1)}, bf16[16,2048]{1,0:T(8,128)(2,1)S(1)}, u32[]{:S(2)}, u32[]{:S(2)}) collective-permute-start(bf16[16,2048]{1,0:T(8,128)(2,1)S(1)} %copy-done.5), channel_id=1, source_target_pairs={{0,32},{32,0},{64,96},{96,64},{1,33},{33,1},{65,97},{97,65},{2,34}... | collective-permute-start | bytes 196616 | tf_op jit(solution)/shard_map/ppermute | solution.py:432
  54.8 4.9 %copy-start.2 = (f32[16,1,6]{0,1,2:T(1,128)S(1)}, f32[16,1,6]{0,1,2:T(1,128)}, u32[]{:S(2)}) copy-start(f32[16,1,6]{0,1,2:T(1,128)} %param.24) | copy-start | bytes 1156
  54.8 4.9 %copy-start.3 = (f32[16,1,6]{0,1,2:T(1,128)S(1)}, f32[16,1,6]{0,1,2:T(1,128)}, u32[]{:S(2)}) copy-start(f32[16,1,6]{0,1,2:T(1,128)} %param.23) | copy-start | bytes 1156
  54.8 34.9 %all-to-all-start.1 = ((bf16[32,16,2048]{2,1,0:T(8,128)(2,1)}), bf16[32,16,2048]{2,1,0:T(8,128)(2,1)}, u32[]{:S(2)}, u32[]{:S(2)}) async-start(bf16[32,16,2048]{2,1,0:T(8,128)(2,1)} %bitcast.11), calls=%async_computation.1 | async-start | bytes 4194304 | tf_op jit(solution)/shard_map/all_to_all | solution.py:435
  59.7 8.7 %copy-start.4 = (f32[16,1,6]{0,1,2:T(1,128)S(1)}, f32[16,1,6]{0,1,2:T(1,128)}, u32[]{:S(2)}) copy-start(f32[16,1,6]{0,1,2:T(1,128)} %param.25) | copy-start | bytes 1156
  68.3 28.8 %collective-permute-start.6 = (bf16[2,384,768]{2,1,0:T(8,128)(2,1)S(1)}, bf16[2,384,768]{2,1,0:T(8,128)(2,1)}, u32[]{:S(2)}, u32[]{:S(2)}) collective-permute-start(bf16[2,384,768]{2,1,0:T(8,128)(2,1)S(1)} %get-tuple-element.42.ab_ref), channel_id=1, source_target_pairs={{0,32},{32,0},{64,96},{96,64},{1,33},{33,1},{65,97},{97,65},{2,34}... | collective-permute-start | bytes 3538952 | tf_op jit(solution)/shard_map/ppermute | solution.py:432
  94.9 14.1 %collective-permute-start.7 = (bf16[384,768]{1,0:T(8,128)(2,1)S(1)}, bf16[384,768]{1,0:T(8,128)(2,1)S(1)}, u32[]{:S(2)}, u32[]{:S(2)}) collective-permute-start(bf16[384,768]{1,0:T(8,128)(2,1)S(1)} %get-tuple-element.47.dh_ref), channel_id=1, source_target_pairs={{0,32},{32,0},{64,96},{96,64},{1,33},{33,1},{65,97},{97,65},{2,34}... | collective-permute-start | bytes 1769480 | tf_op jit(solution)/shard_map/ppermute | solution.py:432
  118.7 38.9 %all-to-all-start.2 = ((bf16[32,16,2176]{2,1,0:T(8,128)(2,1)}), bf16[32,16,2176]{2,1,0:T(8,128)(2,1)S(1)}, u32[]{:S(2)}, u32[]{:S(2)}) async-start(bf16[32,16,2176]{2,1,0:T(8,128)(2,1)} %bitcast.47), calls=%async_computation.2 | async-start | bytes 4456448 | tf_op jit(solution)/shard_map/all_to_all | solution.py:435
  126.2 5.1 %copy-start.6 = (bf16[384,2048]{1,0:T(8,128)(2,1)S(1)}, bf16[384,2048]{1,0:T(8,128)(2,1)}, u32[]{:S(2)}) copy-start(bf16[384,2048]{1,0:T(8,128)(2,1)} %get-tuple-element.50) | copy-start | bytes 4718596
  126.2 5.1 %copy-start.7 = (bf16[2,384,768]{2,1,0:T(8,128)(2,1)S(1)}, bf16[2,384,768]{2,1,0:T(8,128)(2,1)}, u32[]{:S(2)}) copy-start(bf16[2,384,768]{2,1,0:T(8,128)(2,1)} %get-tuple-element.51) | copy-start | bytes 3538948
  158.7 4.8 %collective-permute-start.8 = (bf16[16,2176]{1,0:T(8,128)(2,1)S(1)}, bf16[16,2176]{1,0:T(8,128)(2,1)S(1)}, u32[]{:S(2)}, u32[]{:S(2)}) collective-permute-start(bf16[16,2176]{1,0:T(8,128)(2,1)S(1)} %get-tuple-element.57), channel_id=1, source_target_pairs={{0,32},{32,0},{64,96},{96,64},{1,33},{33,1},{65,97},{97,65},{2,34}... | collective-permute-start | bytes 208904 | tf_op jit(solution)/shard_map/ppermute | solution.py:432
  159.1 6.2 %collective-permute-start.9 = (bf16[16,2176]{1,0:T(8,128)(2,1)S(1)}, bf16[16,2176]{1,0:T(8,128)(2,1)S(1)}, u32[]{:S(2)}, u32[]{:S(2)}) collective-permute-start(bf16[16,2176]{1,0:T(8,128)(2,1)S(1)} %get-tuple-element.58), channel_id=1, source_target_pairs={{0,64},{32,96},{64,0},{96,32},{1,65},{33,97},{65,1},{97,33},{2,66}... | collective-permute-start | bytes 208904 | tf_op jit(solution)/shard_map/ppermute | solution.py:432
  162.3 5.5 %collective-permute-start.10 = (bf16[16,2176]{1,0:T(8,128)(2,1)S(1)}, bf16[16,2176]{1,0:T(8,128)(2,1)S(1)}, u32[]{:S(2)}, u32[]{:S(2)}) collective-permute-start(bf16[16,2176]{1,0:T(8,128)(2,1)S(1)} %get-tuple-element.59), channel_id=1, source_target_pairs={{0,96},{32,64},{64,32},{96,0},{1,97},{33,65},{65,33},{97,1},{2,98}... | collective-permute-start | bytes 208904 | tf_op jit(solution)/shard_map/ppermute | solution.py:432

commit v7 on v6

--- a/solution.py
+++ b/solution.py
@@ -186,9 +186,9 @@
 
 
 def forward_kernel(
-    n_local, top, cols, sg_ref, su_ref, x_hbm, wg_hbm, wu_hbm,
-    kept_hbm, send_ref, slot_ref, x_ref, meta_ref, kept, wg_raw, wu_raw, wg, wu,
-    sems_x, sems_g, sems_u, sem_m, sem_k,
+    n_local, top, cols, sg_ref, x_hbm, wg_hbm,
+    kept_hbm, send_ref, slot_ref, x_ref, meta_ref, kept, wg_raw, wg,
+    sems_x, sems_g, sem_m, sem_k,
 ):
     half, hidden = wg_raw.shape
     steps = hidden // cols
@@ -197,7 +197,6 @@
     start_all(x_hbm, x_ref, sems_x)
     for i in range(steps):
         fetch(wg_hbm, wg_raw, sems_g, i, cols).start()
-        fetch(wu_hbm, wu_raw, sems_u, i, cols).start()
     lane = lax.broadcasted_iota(jnp.int32, (2 * top, META), 1)
     row = lax.broadcasted_iota(jnp.int32, (2 * top, META), 0)
     turn = jnp.where(lane == row, 1.0, 0.0).astype(BF)
@@ -218,18 +217,26 @@
     save = pltpu.make_async_copy(kept, kept_hbm, sem_k)
     save.start()
 
+    project(kept, wg_hbm, wg_raw, wg, sg_ref, sems_g, send_ref)
+    save.wait()
+
+
+def project(kept, w_hbm, w_raw, w, scales_ref, sems, send_ref):
+    cols = w.shape[1]
+
     def step(i, carry):
         at = columns(i, cols)
-        fetch(wg_hbm, wg_raw, sems_g, i, cols).wait()
-        fetch(wu_hbm, wu_raw, sems_u, i, cols).wait()
-        dequant(wg_raw.at[at], sg_ref, wg, 0, i * (cols // 128))
-        dequant(wu_raw.at[at], su_ref, wu, 0, i * (cols // 128))
-        send_ref[(0, *at)] = dot(kept[...], wg[...]).astype(BF)
-        send_ref[(1, *at)] = dot(kept[...], wu[...]).astype(BF)
-        return carry
-
-    lax.fori_loop(0, steps, step, 0)
-    save.wait()
+        fetch(w_hbm, w_raw, sems, i, cols).wait()
+        dequant(w_raw.at[at], scales_ref, w, 0, i * (cols // 128))
+        send_ref[at] = dot(kept[...], w[...]).astype(BF)
+        return carry
+
+    lax.fori_loop(0, sems.shape[0], step, 0)
+
+
+def up_kernel(s_ref, kept_ref, w_hbm, send_ref, w_raw, w, sems):
+    start_all(w_hbm, w_raw, sems)
+    project(kept_ref, w_hbm, w_raw, w, s_ref, sems, send_ref)
 
 
 def down_kernel(
@@ -245,19 +252,12 @@
     save = pltpu.make_async_copy(kept, kept_hbm, sem_k)
     save.start()
 
-    def step(i, carry):
-        at = columns(i, cols)
-        fetch(v_hbm, v_raw, sems_v, i, cols).wait()
-        dequant(v_raw.at[at], sv_ref, v, 0, i * (cols // 128))
-        send_ref[at] = dot(kept[...], v[...]).astype(BF)
-        return carry
-
-    lax.fori_loop(0, steps, step, 0)
+    project(kept, v_hbm, v_raw, v, sv_ref, sems_v, send_ref)
     save.wait()
 
 
 def factor_kernel(
-    chunk, sg_ref, su_ref, ab_ref, ab_in, wg_hbm, wu_hbm,
+    chunk, sg_ref, su_ref, a_ref, b_ref, a_in, b_in, wg_hbm, wu_hbm,
     factor_ref, hid_ref, both_w, wg_raw, wu_raw, sems_g, sems_u,
 ):
     half, hidden = wg_raw.shape
@@ -274,8 +274,8 @@
 
     def activate(i, carry):
         at = pl.ds(pl.multiple_of(i * block, block), block)
-        act_a = ab_ref[0, at].astype(F32) + ab_in[0, at].astype(F32)
-        act_b = ab_ref[1, at].astype(F32) + ab_in[1, at].astype(F32)
+        act_a = a_ref[at].astype(F32) + a_in[at].astype(F32)
+        act_b = b_ref[at].astype(F32) + b_in[at].astype(F32)
         sigma = jax.nn.sigmoid(act_a)
         silu_a = act_a * sigma
         hid_ref[at] = (silu_a * act_b).astype(BF)
@@ -478,21 +478,33 @@
     cols = 256
     steps = hidden // cols
     raw = pltpu.VMEM((half, hidden), BF)
-    rows_x, send_ab, slot_of = call(
+    rows_x, send_a, slot_of = call(
         functools.partial(forward_kernel, n_local, top, cols),
-        (shape(kept, half), shape(2, kept, hidden), shape(kept, rows)),
-        (scales[0], scales[1], got_x, weights[0], weights[1]),
+        (shape(kept, half), shape(kept, hidden), shape(kept, rows)),
+        (scales[0], got_x, weights[0]),
         limit=LIMIT_FORWARD,
-        flops=4 * kept * half * hidden,
-        moved=4 * half * hidden + 4 * rows * half,
-        in_specs=[SMEM, SMEM, HBM, HBM, HBM],
+        flops=2 * kept * half * hidden,
+        moved=2 * half * hidden + 4 * rows * half,
+        in_specs=[SMEM, HBM, HBM],
         out_specs=[HBM, VMEM, VMEM],
         scratch_shapes=[pltpu.VMEM((rows, half), BF), pltpu.VMEM((rows, META), BF)]
-        + [pltpu.VMEM((kept, half), BF), raw, raw]
-        + [pltpu.VMEM((half, cols), BF)] * 2
-        + [SEMS((4,)), SEMS((steps,)), SEMS((steps,)), SEMS, SEMS],
-    )
-    their_ab = across(send_ab, 1)
+        + [pltpu.VMEM((kept, half), BF), raw, pltpu.VMEM((half, cols), BF)]
+        + [SEMS((4,)), SEMS((steps,)), SEMS, SEMS],
+    )
+    their_a = across(send_a, 1)
+    send_b = call(
+        up_kernel,
+        shape(kept, hidden),
+        (scales[1], rows_x, weights[1]),
+        limit=LIMIT_FORWARD,
+        flops=2 * kept * half * hidden,
+        moved=2 * half * hidden + 2 * kept * half,
+        in_specs=[SMEM, VMEM, HBM],
+        out_specs=VMEM,
+        scratch_shapes=[raw, pltpu.VMEM((half, cols), BF), SEMS((steps,))],
+    )
+    their_a, send_b = lax.optimization_barrier((their_a, send_b))
+    their_b = across(send_b, 1)
     rows_dy, send_dh = call(
         functools.partial(down_kernel, cols),
         (shape(kept, half), shape(kept, hidden)),
@@ -513,11 +525,11 @@
     factor, hid, both_w = call(
         functools.partial(factor_kernel, chunk),
         (shape(2, kept, hidden, dtype=F32), shape(kept, hidden), shape(half, 2 * hidden)),
-        (scales[0], scales[1], send_ab, their_ab, weights[0], weights[1]),
+        (scales[0], scales[1], send_a, send_b, their_a, their_b, weights[0], weights[1]),
         limit=LIMIT_FACTOR,
         flops=16 * kept * hidden,
         moved=8 * half * hidden,
-        in_specs=[SMEM, SMEM, VMEM, VMEM, HBM, HBM],
+        in_specs=[SMEM, SMEM] + [VMEM] * 4 + [HBM, HBM],
         out_specs=[VMEM] * 3,
         scratch_shapes=[raw, raw, SEMS((parts,)), SEMS((parts,))],
     )

time: 169 us -> 169 us (level)
  waiting for transfers between devices: 81.6 us -> 78.6 us
  Pallas kernels: 39.2 us -> 41.8 us
    all_to_all x3, waiting for transfers between devices: 62.8 us -> 49.3 us  [spread(): lax.all_to_all(block, 'local', split_axis=0, concat_axis=0, tiled=True)]
    ppermute x11 -> x12, waiting for transfers between devices: 18.7 us -> 29.2 us  [across(): lax.ppermute(block, 'group', [(i, i ^ apart) for i in range(n_group)])]
    pallas_call x9 -> x10, Pallas kernels: 39.2 us -> 41.8 us  [call(): pl.pallas_call(kernel, out_shape=outs, compiler_params=pltpu.CompilerPara...]
    ppermute x11 -> x12, starting transfers between devices: 12.8 us -> 13.1 us  [across(): lax.ppermute(block, 'group', [(i, i ^ apart) for i in range(n_group)])]
  transfers between devices with their start and end apart: 14 -> 15, of which waited for: 11 -> 12; matrix products, arithmetic and copies ran while one was open for 7% -> 7% of each run, Pallas kernels for 14% -> 15%
where the time goes in v7:
time: 169 us; the launch traced here: 168 us
  waiting for transfers between devices  78.6 us (47%)
  Pallas kernels  41.8 us (25%)
  starting transfers between devices  34.1 us (20%)
  matrix products  12.1 us (7%)
    all_to_all x3, waiting for transfers between devices, spread(): lax.all_to_all(block, 'local', split_axis=0, concat_axis=0, tiled=True)  49.3 us
    pallas_call x10, Pallas kernels, call(): pl.pallas_call(kernel, out_shape=outs, compiler_params=pltpu.CompilerPara...  41.8 us
    ppermute x12, waiting for transfers between devices, across(): lax.ppermute(block, 'group', [(i, i ^ apart) for i in range(n_group)])  29.2 us
    all_to_all x3, starting transfers between devices, spread(): lax.all_to_all(block, 'local', split_axis=0, concat_axis=0, tiled=True)  21 us
    ppermute x12, starting transfers between devices, across(): lax.ppermute(block, 'group', [(i, i ^ apart) for i in range(n_group)])  13.1 us
    dot_general x3, matrix products, dot(): return lax.dot_general(left, right, dims, preferred_element_type=F32)  12.1 us
  transfers between devices with their start and end apart: 15, of which 12 were waited for; matrix products, arithmetic and copies ran while one was open for 7% of the time, Pallas kernels for 15%

profile of v7, /device:TPU:0, one launch (start us, length us, event | category | flops | bytes accessed | tf_op | source)
XLA Modules:
  0.0 168.3 jit_solution(325813602159697036)
XLA Ops:
  0.6 1.9 %shard_map.164 = (bf16[16,2176]{1,0:T(8,128)(2,1)}, bf16[16,2176]{1,0:T(8,128)(2,1)}, bf16[16,2048]{1,0:T(8,128)(2,1)}, bf16[16,2048]{1,0:T(8,128)(2,1)}) custom-call(bf16[16,4096]{1,0:T(8,128)(2,1)} %xq_ref.1, f32[16,32]{1,0:T(8,128)} %xs_ref.1, bf16[16,4096]{1,0:T(8,128)(2,1)} %dy_ref.1, s32[8,16]{1,0:T(8,128)} %bitcast.54, s32[8,16]{1,0:T(8,128)} %bitcast.55, ...), custom_call_target="tpu_custom_call" | custom-call | bytes 524288 | tf_op jit(solution)/shard_map/pallas_call | solution.py:31
  2.5 3.1 %collective-permute-start.1 = (bf16[16,2176]{1,0:T(8,128)(2,1)}, bf16[16,2176]{1,0:T(8,128)(2,1)S(1)}, u32[]{:S(2)}, u32[]{:S(2)}) collective-permute-start(bf16[16,2176]{1,0:T(8,128)(2,1)} %get-tuple-element.37.b0), channel_id=1, source_target_pairs={{0,64},{32,96},{64,0},{96,32},{1,65},{33,97},{65,1},{97,33},{2,66}... | collective-permute-start | bytes 208904 | tf_op jit(solution)/shard_map/ppermute | solution.py:432
  8.5 2.8 %collective-permute-done.2.b3 = bf16[16,2176]{1,0:T(8,128)(2,1)S(1)} collective-permute-done((bf16[16,2176]{1,0:T(8,128)(2,1)}, bf16[16,2176]{1,0:T(8,128)(2,1)S(1)}, u32[]{:S(2)}, u32[]{:S(2)}) %collective-permute-start.2) | collective-permute-done | bytes 69664 | tf_op jit(solution)/shard_map/ppermute | solution.py:432
  12.2 2.3 %shard_map.165 = (bf16[512,2176]{1,0:T(8,128)(2,1)}, bf16[512,64]{1,0:T(8,128)(2,1)S(1)}, bf16[512,64]{1,0:T(8,128)(2,1)S(1)}, bf16[64,128]{1,0:T(8,128)(2,1)S(1)}) custom-call(bf16[16,2176]{1,0:T(8,128)(2,1)S(1)} %copy-done.1, bf16[16,2176]{1,0:T(8,128)(2,1)S(1)} %collective-permute-done.b1, bf16[16,2176]{1,0:T(8,128)(2,1)S(1)} %collective-permute-done.1.b2, ...), custom_call_target="tpu_custom_call" | custom-call | flops 142606336 | bytes 2228224 | tf_op jit(solution)/shard_map/pallas_call | solution.py:31
  14.6 8.6 %all-to-all-start = ((bf16[32,16,2176]{2,1,0:T(8,128)(2,1)}), bf16[32,16,2176]{2,1,0:T(8,128)(2,1)}, u32[]{:S(2)}, u32[]{:S(2)}) async-start(bf16[32,16,2176]{2,1,0:T(8,128)(2,1)} %bitcast.6), calls=%async_computation | async-start | bytes 4456448 | tf_op jit(solution)/shard_map/all_to_all | solution.py:435
  26.8 2.3 %collective-permute-done.4.b2 = bf16[16,2048]{1,0:T(8,128)(2,1)S(1)} collective-permute-done((bf16[16,2048]{1,0:T(8,128)(2,1)S(1)}, bf16[16,2048]{1,0:T(8,128)(2,1)S(1)}, u32[]{:S(2)}, u32[]{:S(2)}) %collective-permute-start.4) | collective-permute-done | bytes 65568 | tf_op jit(solution)/shard_map/ppermute | solution.py:432
  30.5 1.9 %shard_map.166 = bf16[512,2048]{1,0:T(8,128)(2,1)} custom-call(bf16[512,64]{1,0:T(8,128)(2,1)S(1)} %get-tuple-element.40.gated_ref, bf16[16,2048]{1,0:T(8,128)(2,1)S(1)} %copy-done, bf16[16,2048]{1,0:T(8,128)(2,1)S(1)} %collective-permute-done.3.b1, bf16[16,2048]{1,0:T(8,128)(2,1)S(1)} %collective-permute-done.4.b2, ...), custom_call_target="tpu_custom_call" | custom-call | flops 134217728 | bytes 2097152 | tf_op jit(solution)/shard_map/pallas_call | solution.py:31
  32.4 22.3 %all-to-all-done = bf16[32,16,2176]{2,1,0:T(8,128)(2,1)} async-done(((bf16[32,16,2176]{2,1,0:T(8,128)(2,1)}), bf16[32,16,2176]{2,1,0:T(8,128)(2,1)}, u32[]{:S(2)}, u32[]{:S(2)}) %all-to-all-start) | async-done | bytes 2228256 | tf_op jit(solution)/shard_map/all_to_all | solution.py:435
  54.8 4.8 %all-to-all-start.1 = ((bf16[32,16,2048]{2,1,0:T(8,128)(2,1)}), bf16[32,16,2048]{2,1,0:T(8,128)(2,1)}, u32[]{:S(2)}, u32[]{:S(2)}) async-start(bf16[32,16,2048]{2,1,0:T(8,128)(2,1)} %bitcast.11), calls=%async_computation.1 | async-start | bytes 4194304 | tf_op jit(solution)/shard_map/all_to_all | solution.py:435
  59.6 6.5 %shard_map.167 = (bf16[384,2048]{1,0:T(8,128)(2,1)}, bf16[384,768]{1,0:T(8,128)(2,1)S(1)}, bf16[384,512]{1,0:T(8,128)(2,1)S(1)}) custom-call(f32[6,16]{1,0:T(8,128)S(1)} %bitcast.43, bf16[512,2176]{1,0:T(8,128)(2,1)} %bitcast.7.x_hbm, bf16[2048,768]{1,0:T(8,128)(2,1)} %bitcast.48), custom_call_target="tpu_custom_call" | custom-call | flops 1207959552 | bytes 7340032 | tf_op jit(solution)/shard_map/pallas_call | solution.py:31
  66.2 4.7 %shard_map.168.b_ref = bf16[384,768]{1,0:T(8,128)(2,1)S(1)} custom-call(f32[6,16]{1,0:T(8,128)S(1)} %bitcast.45, bf16[384,2048]{1,0:T(8,128)(2,1)} %get-tuple-element.45.kept_ref, bf16[2048,768]{1,0:T(8,128)(2,1)} %bitcast.50), custom_call_target="tpu_custom_call" | custom-call | flops 1207959552 | bytes 4718592 | tf_op jit(solution)/shard_map/pallas_call | solution.py:31
  70.9 10.6 %collective-permute-done.6.a_in = bf16[384,768]{1,0:T(8,128)(2,1)S(1)} collective-permute-done((bf16[384,768]{1,0:T(8,128)(2,1)S(1)}, bf16[384,768]{1,0:T(8,128)(2,1)S(1)}, u32[]{:S(2)}, u32[]{:S(2)}) %collective-permute-start.6) | collective-permute-done | bytes 589856 | tf_op jit(solution)/shard_map/ppermute | solution.py:432
  81.8 7.7 %all-to-all-done.1 = bf16[32,16,2048]{2,1,0:T(8,128)(2,1)} async-done(((bf16[32,16,2048]{2,1,0:T(8,128)(2,1)}), bf16[32,16,2048]{2,1,0:T(8,128)(2,1)}, u32[]{:S(2)}, u32[]{:S(2)}) %all-to-all-start.1) | async-done | bytes 2097184 | tf_op jit(solution)/shard_map/all_to_all | solution.py:435
  89.5 5.2 %shard_map.170 = (bf16[384,2048]{1,0:T(8,128)(2,1)}, bf16[384,768]{1,0:T(8,128)(2,1)S(1)}) custom-call(f32[6,16]{1,0:T(8,128)S(1)} %bitcast.47, bf16[384,512]{1,0:T(8,128)(2,1)S(1)} %get-tuple-element.50.slot_ref, bf16[512,2048]{1,0:T(8,128)(2,1)} %bitcast.12.dy_hbm, bf16[2048,768]{1,0:T(8,128)(2,1)} %bitcast.52), custom_call_target="tpu_custom_call" | custom-call | flops 1207959552 | bytes 7340032 | tf_op jit(solution)/shard_map/pallas_call | solution.py:31
  96.6 7.8 %shard_map.169 = (f32[2,384,768]{2,1,0:T(8,128)}, bf16[384,768]{1,0:T(8,128)(2,1)S(1)}, bf16[2048,1536]{1,0:T(8,128)(2,1)}) custom-call(f32[6,16]{1,0:T(8,128)S(1)} %bitcast.44, f32[6,16]{1,0:T(8,128)S(1)} %bitcast.46, bf16[384,768]{1,0:T(8,128)(2,1)S(1)} %get-tuple-element.44.a_ref, bf16[384,768]{1,0:T(8,128)(2,1)S(1)} %shard_map.168.b_ref, ...), custom_call_target="tpu_custom_call" | custom-call | flops 4718592 | bytes 12582912 | tf_op jit(solution)/shard_map/pallas_call | solution.py:31
  104.4 4.3 %collective-permute-done.8.dh_in = bf16[384,768]{1,0:T(8,128)(2,1)S(1)} collective-permute-done((bf16[384,768]{1,0:T(8,128)(2,1)S(1)}, bf16[384,768]{1,0:T(8,128)(2,1)S(1)}, u32[]{:S(2)}, u32[]{:S(2)}) %collective-permute-start.8) | collective-permute-done | bytes 589856 | tf_op jit(solution)/shard_map/ppermute | solution.py:432
  108.7 9.7 %shard_map.171 = (bf16[2,384,768]{2,1,0:T(8,128)(2,1)}, bf16[512,2176]{1,0:T(8,128)(2,1)}) custom-call(f32[2,384,768]{2,1,0:T(8,128)} %get-tuple-element.48.factor_hbm, bf16[384,768]{1,0:T(8,128)(2,1)S(1)} %get-tuple-element.49.hid_ref, bf16[384,768]{1,0:T(8,128)(2,1)S(1)} %get-tuple-element.52.dh_ref, bf16[384,768]{1,0:T(8,128)(2,1)S(1)} %collective-permute-done.8.dh_in, ...), custom_call_target="tpu_custom_call" | custom-call | flops 3221225472 | bytes 8388608 | tf_op jit(solution)/shard_map/pallas_call | solution.py:31
  118.4 7.6 %all-to-all-start.2 = ((bf16[32,16,2176]{2,1,0:T(8,128)(2,1)}), bf16[32,16,2176]{2,1,0:T(8,128)(2,1)S(1)}, u32[]{:S(2)}, u32[]{:S(2)}) async-start(bf16[32,16,2176]{2,1,0:T(8,128)(2,1)} %bitcast.53), calls=%async_computation.2 | async-start | bytes 4456448 | tf_op jit(solution)/shard_map/all_to_all | solution.py:435
  126.1 5.1 %convolution_convert_fusion = bf16[2048,768]{1,0:T(8,128)(2,1)} fusion(bf16[384,2048]{1,0:T(8,128)(2,1)} %get-tuple-element.56, bf16[384,768]{1,0:T(8,128)(2,1)S(1)} %get-tuple-element.49.hid_ref), kind=kOutput, calls=%fused_computation | convolution fusion | flops 1209532416 | bytes 5308416 | tf_op jit(solution)/shard_map/dot_general | solution.py:27
  131.1 3.5 %convolution_convert_fusion.1 = bf16[2048,768]{1,0:T(8,128)(2,1)} fusion(bf16[384,2048]{1,0:T(8,128)(2,1)S(1)} %copy-done.2, bf16[2,384,768]{2,1,0:T(8,128)(2,1)S(1)} %copy-done.8), kind=kOutput, calls=%fused_computation.1 | convolution fusion | flops 1209532416 | bytes 5308416 | tf_op jit(solution)/shard_map/dot_general | solution.py:27
  134.6 3.5 %convolution_convert_fusion.2 = bf16[2048,768]{1,0:T(8,128)(2,1)} fusion(bf16[384,2048]{1,0:T(8,128)(2,1)S(1)} %copy-done.2, bf16[2,384,768]{2,1,0:T(8,128)(2,1)S(1)} %copy-done.8), kind=kOutput, calls=%fused_computation.2 | convolution fusion | flops 1209532416 | bytes 5308416 | tf_op jit(solution)/shard_map/dot_general | solution.py:27
  138.2 19.3 %all-to-all-done.2 = bf16[32,16,2176]{2,1,0:T(8,128)(2,1)S(1)} async-done(((bf16[32,16,2176]{2,1,0:T(8,128)(2,1)}), bf16[32,16,2176]{2,1,0:T(8,128)(2,1)S(1)}, u32[]{:S(2)}, u32[]{:S(2)}) %all-to-all-start.2) | async-done | bytes 2228256 | tf_op jit(solution)/shard_map/all_to_all | solution.py:435
  159.1 2.9 %collective-permute-start.10 = (bf16[16,2176]{1,0:T(8,128)(2,1)S(1)}, bf16[16,2176]{1,0:T(8,128)(2,1)S(1)}, u32[]{:S(2)}, u32[]{:S(2)}) collective-permute-start(bf16[16,2176]{1,0:T(8,128)(2,1)S(1)} %get-tuple-element.62), channel_id=1, source_target_pairs={{0,64},{32,96},{64,0},{96,32},{1,65},{33,97},{65,1},{97,33},{2,66}... | collective-permute-start | bytes 208904 | tf_op jit(solution)/shard_map/ppermute | solution.py:432
  165.1 2.5 %collective-permute-done.11.b3 = bf16[16,2176]{1,0:T(8,128)(2,1)S(1)} collective-permute-done((bf16[16,2176]{1,0:T(8,128)(2,1)S(1)}, bf16[16,2176]{1,0:T(8,128)(2,1)S(1)}, u32[]{:S(2)}, u32[]{:S(2)}) %collective-permute-start.11) | collective-permute-done | bytes 69664 | tf_op jit(solution)/shard_map/ppermute | solution.py:432
  (40 shorter events, 16.5 us)
Async XLA Ops:
  2.5 6.0 %collective-permute-start.1 = (bf16[16,2176]{1,0:T(8,128)(2,1)}, bf16[16,2176]{1,0:T(8,128)(2,1)S(1)}, u32[]{:S(2)}, u32[]{:S(2)}) collective-permute-start(bf16[16,2176]{1,0:T(8,128)(2,1)} %get-tuple-element.37.b0), channel_id=1, source_target_pairs={{0,64},{32,96},{64,0},{96,32},{1,65},{33,97},{65,1},{97,33},{2,66}... | collective-permute-start | bytes 208904 | tf_op jit(solution)/shard_map/ppermute | solution.py:432
  5.6 5.7 %collective-permute-start.2 = (bf16[16,2176]{1,0:T(8,128)(2,1)}, bf16[16,2176]{1,0:T(8,128)(2,1)S(1)}, u32[]{:S(2)}, u32[]{:S(2)}) collective-permute-start(bf16[16,2176]{1,0:T(8,128)(2,1)} %get-tuple-element.38), channel_id=1, source_target_pairs={{0,96},{32,64},{64,32},{96,0},{1,97},{33,65},{65,33},{97,1},{2,98}... | collective-permute-start | bytes 208904 | tf_op jit(solution)/shard_map/ppermute | solution.py:432
  6.8 4.6 %collective-permute-start = (bf16[16,2176]{1,0:T(8,128)(2,1)}, bf16[16,2176]{1,0:T(8,128)(2,1)S(1)}, u32[]{:S(2)}, u32[]{:S(2)}) collective-permute-start(bf16[16,2176]{1,0:T(8,128)(2,1)} %get-tuple-element.38), channel_id=1, source_target_pairs={{0,32},{32,0},{64,96},{96,64},{1,33},{33,1},{65,97},{97,65},{2,34}... | collective-permute-start | bytes 208904 | tf_op jit(solution)/shard_map/ppermute | solution.py:432
  11.4 0.9 copy-start.1
  14.6 8.6 %copy-start = (bf16[16,2048]{1,0:T(8,128)(2,1)S(1)}, bf16[16,2048]{1,0:T(8,128)(2,1)}, u32[]{:S(2)}) copy-start(bf16[16,2048]{1,0:T(8,128)(2,1)} %get-tuple-element.41.b0) | copy-start | bytes 196612
  14.6 10.2 %copy-start.7 = (bf16[16,2048]{1,0:T(8,128)(2,1)S(1)}, bf16[16,2048]{1,0:T(8,128)(2,1)}, u32[]{:S(2)}) copy-start(bf16[16,2048]{1,0:T(8,128)(2,1)} %get-tuple-element.42) | copy-start | bytes 196612
  14.6 40.2 %all-to-all-start = ((bf16[32,16,2176]{2,1,0:T(8,128)(2,1)}), bf16[32,16,2176]{2,1,0:T(8,128)(2,1)}, u32[]{:S(2)}, u32[]{:S(2)}) async-start(bf16[32,16,2176]{2,1,0:T(8,128)(2,1)} %bitcast.6), calls=%async_computation | async-start | bytes 4456448 | tf_op jit(solution)/shard_map/all_to_all | solution.py:435
  23.2 5.9 %collective-permute-start.4 = (bf16[16,2048]{1,0:T(8,128)(2,1)S(1)}, bf16[16,2048]{1,0:T(8,128)(2,1)S(1)}, u32[]{:S(2)}, u32[]{:S(2)}) collective-permute-start(bf16[16,2048]{1,0:T(8,128)(2,1)S(1)} %copy-done), channel_id=1, source_target_pairs={{0,64},{32,96},{64,0},{96,32},{1,65},{33,97},{65,1},{97,33},{2,66}... | collective-permute-start | bytes 196616 | tf_op jit(solution)/shard_map/ppermute | solution.py:432
  24.8 5.7 %collective-permute-start.5 = (bf16[16,2048]{1,0:T(8,128)(2,1)S(1)}, bf16[16,2048]{1,0:T(8,128)(2,1)S(1)}, u32[]{:S(2)}, u32[]{:S(2)}) collective-permute-start(bf16[16,2048]{1,0:T(8,128)(2,1)S(1)} %copy-done.7), channel_id=1, source_target_pairs={{0,96},{32,64},{64,32},{96,0},{1,97},{33,65},{65,33},{97,1},{2,98}... | collective-permute-start | bytes 196616 | tf_op jit(solution)/shard_map/ppermute | solution.py:432
  26.0 4.5 %collective-permute-start.3 = (bf16[16,2048]{1,0:T(8,128)(2,1)S(1)}, bf16[16,2048]{1,0:T(8,128)(2,1)S(1)}, u32[]{:S(2)}, u32[]{:S(2)}) collective-permute-start(bf16[16,2048]{1,0:T(8,128)(2,1)S(1)} %copy-done.7), channel_id=1, source_target_pairs={{0,32},{32,0},{64,96},{96,64},{1,33},{33,1},{65,97},{97,65},{2,34}... | collective-permute-start | bytes 196616 | tf_op jit(solution)/shard_map/ppermute | solution.py:432
  32.4 27.1 %copy-start.4 = (f32[16,1,6]{0,1,2:T(1,128)S(1)}, f32[16,1,6]{0,1,2:T(1,128)}, u32[]{:S(2)}) copy-start(f32[16,1,6]{0,1,2:T(1,128)} %param.23) | copy-start | bytes 1156
  54.8 34.7 %all-to-all-start.1 = ((bf16[32,16,2048]{2,1,0:T(8,128)(2,1)}), bf16[32,16,2048]{2,1,0:T(8,128)(2,1)}, u32[]{:S(2)}, u32[]{:S(2)}) async-start(bf16[32,16,2048]{2,1,0:T(8,128)(2,1)} %bitcast.11), calls=%async_computation.1 | async-start | bytes 4194304 | tf_op jit(solution)/shard_map/all_to_all | solution.py:435
  59.6 6.6 %copy-start.5 = (f32[16,1,6]{0,1,2:T(1,128)S(1)}, f32[16,1,6]{0,1,2:T(1,128)}, u32[]{:S(2)}) copy-start(f32[16,1,6]{0,1,2:T(1,128)} %param.24) | copy-start | bytes 1156
  59.6 6.6 %copy-start.6 = (f32[16,1,6]{0,1,2:T(1,128)S(1)}, f32[16,1,6]{0,1,2:T(1,128)}, u32[]{:S(2)}) copy-start(f32[16,1,6]{0,1,2:T(1,128)} %param.25) | copy-start | bytes 1156
  66.1 15.4 %collective-permute-start.6 = (bf16[384,768]{1,0:T(8,128)(2,1)S(1)}, bf16[384,768]{1,0:T(8,128)(2,1)S(1)}, u32[]{:S(2)}, u32[]{:S(2)}) collective-permute-start(bf16[384,768]{1,0:T(8,128)(2,1)S(1)} %get-tuple-element.44.a_ref), channel_id=1, source_target_pairs={{0,32},{32,0},{64,96},{96,64},{1,33},{33,1},{65,97},{97,65},{2,34}... | collective-permute-start | bytes 1769480 | tf_op jit(solution)/shard_map/ppermute | solution.py:432
  81.5 13.3 %copy-start.3 = (bf16[384,768]{1,0:T(8,128)(2,1)}, bf16[384,768]{1,0:T(8,128)(2,1)S(1)}, u32[]{:S(2)}) copy-start(bf16[384,768]{1,0:T(8,128)(2,1)S(1)} %collective-permute-done.6.a_in) | copy-start | bytes 1769476
  81.5 15.1 %collective-permute-start.7 = (bf16[384,768]{1,0:T(8,128)(2,1)S(1)}, bf16[384,768]{1,0:T(8,128)(2,1)}, u32[]{:S(2)}, u32[]{:S(2)}) collective-permute-start(bf16[384,768]{1,0:T(8,128)(2,1)S(1)} %shard_map.168.b_ref), channel_id=1, source_target_pairs={{0,32},{32,0},{64,96},{96,64},{1,33},{33,1},{65,97},{97,65},{2,34}... | collective-permute-start | bytes 1769480 | tf_op jit(solution)/shard_map/ppermute | solution.py:432
  94.8 14.0 %collective-permute-start.8 = (bf16[384,768]{1,0:T(8,128)(2,1)S(1)}, bf16[384,768]{1,0:T(8,128)(2,1)S(1)}, u32[]{:S(2)}, u32[]{:S(2)}) collective-permute-start(bf16[384,768]{1,0:T(8,128)(2,1)S(1)} %get-tuple-element.52.dh_ref), channel_id=1, source_target_pairs={{0,32},{32,0},{64,96},{96,64},{1,33},{33,1},{65,97},{97,65},{2,34}... | collective-permute-start | bytes 1769480 | tf_op jit(solution)/shard_map/ppermute | solution.py:432
  118.4 39.0 %all-to-all-start.2 = ((bf16[32,16,2176]{2,1,0:T(8,128)(2,1)}), bf16[32,16,2176]{2,1,0:T(8,128)(2,1)S(1)}, u32[]{:S(2)}, u32[]{:S(2)}) async-start(bf16[32,16,2176]{2,1,0:T(8,128)(2,1)} %bitcast.53), calls=%async_computation.2 | async-start | bytes 4456448 | tf_op jit(solution)/shard_map/all_to_all | solution.py:435
  126.0 5.1 %copy-start.2 = (bf16[384,2048]{1,0:T(8,128)(2,1)S(1)}, bf16[384,2048]{1,0:T(8,128)(2,1)}, u32[]{:S(2)}) copy-start(bf16[384,2048]{1,0:T(8,128)(2,1)} %get-tuple-element.45.kept_ref) | copy-start | bytes 4718596
  126.0 5.1 %copy-start.8 = (bf16[2,384,768]{2,1,0:T(8,128)(2,1)S(1)}, bf16[2,384,768]{2,1,0:T(8,128)(2,1)}, u32[]{:S(2)}) copy-start(bf16[2,384,768]{2,1,0:T(8,128)(2,1)} %get-tuple-element.55) | copy-start | bytes 3538948
  158.5 4.8 %collective-permute-start.9 = (bf16[16,2176]{1,0:T(8,128)(2,1)S(1)}, bf16[16,2176]{1,0:T(8,128)(2,1)S(1)}, u32[]{:S(2)}, u32[]{:S(2)}) collective-permute-start(bf16[16,2176]{1,0:T(8,128)(2,1)S(1)} %get-tuple-element.61), channel_id=1, source_target_pairs={{0,32},{32,0},{64,96},{96,64},{1,33},{33,1},{65,97},{97,65},{2,34}... | collective-permute-start | bytes 208904 | tf_op jit(solution)/shard_map/ppermute | solution.py:432
  159.1 6.0 %collective-permute-start.10 = (bf16[16,2176]{1,0:T(8,128)(2,1)S(1)}, bf16[16,2176]{1,0:T(8,128)(2,1)S(1)}, u32[]{:S(2)}, u32[]{:S(2)}) collective-permute-start(bf16[16,2176]{1,0:T(8,128)(2,1)S(1)} %get-tuple-element.62), channel_id=1, source_target_pairs={{0,64},{32,96},{64,0},{96,32},{1,65},{33,97},{65,1},{97,33},{2,66}... | collective-permute-start | bytes 208904 | tf_op jit(solution)/shard_map/ppermute | solution.py:432
  162.1 5.5 %collective-permute-start.11 = (bf16[16,2176]{1,0:T(8,128)(2,1)S(1)}, bf16[16,2176]{1,0:T(8,128)(2,1)S(1)}, u32[]{:S(2)}, u32[]{:S(2)}) collective-permute-start(bf16[16,2176]{1,0:T(8,128)(2,1)S(1)} %get-tuple-element.63), channel_id=1, source_target_pairs={{0,96},{32,64},{64,32},{96,0},{1,97},{33,65},{65,33},{97,1},{2,98}... | collective-permute-start | bytes 208904 | tf_op jit(solution)/shard_map/ppermute | solution.py:432

commit v8 on v7

--- a/solution.py
+++ b/solution.py
@@ -187,8 +187,7 @@
 
 def forward_kernel(
     n_local, top, cols, sg_ref, x_hbm, wg_hbm,
-    kept_hbm, send_ref, slot_ref, x_ref, meta_ref, kept, wg_raw, wg,
-    sems_x, sems_g, sem_m, sem_k,
+    send_ref, slot_ref, x_ref, meta_ref, kept, wg_raw, wg, sems_x, sems_g, sem_m,
 ):
     half, hidden = wg_raw.shape
     steps = hidden // cols
@@ -214,11 +213,7 @@
     row = lax.broadcasted_iota(jnp.int32, slot_ref.shape, 0).astype(F32)
     slot_ref[...] = jnp.where(row == target, 1.0, 0.0).astype(BF)
     compact(slot_ref, x_hbm, x_ref, sems_x, kept)
-    save = pltpu.make_async_copy(kept, kept_hbm, sem_k)
-    save.start()
-
     project(kept, wg_hbm, wg_raw, wg, sg_ref, sems_g, send_ref)
-    save.wait()
 
 
 def project(kept, w_hbm, w_raw, w, scales_ref, sems, send_ref):
@@ -234,12 +229,7 @@
     lax.fori_loop(0, sems.shape[0], step, 0)
 
 
-def up_kernel(s_ref, kept_ref, w_hbm, send_ref, w_raw, w, sems):
-    start_all(w_hbm, w_raw, sems)
-    project(kept_ref, w_hbm, w_raw, w, s_ref, sems, send_ref)
-
-
-def down_kernel(
+def project_kernel(
     cols, sv_ref, slot_ref, dy_hbm, v_hbm, kept_hbm, send_ref,
     dy_ref, kept, v_raw, v, sems_y, sems_v, sem_k,
 ):
@@ -279,8 +269,8 @@
         sigma = jax.nn.sigmoid(act_a)
         silu_a = act_a * sigma
         hid_ref[at] = (silu_a * act_b).astype(BF)
-        factor_ref[0, at] = act_b * sigma * (1.0 + act_a * (1.0 - sigma))
-        factor_ref[1, at] = silu_a
+        factor_ref[0, at] = (act_b * sigma * (1.0 + act_a * (1.0 - sigma))).astype(BF)
+        factor_ref[1, at] = silu_a.astype(BF)
         return carry
 
     lax.fori_loop(0, hid_ref.shape[0] // block, activate, 0)
@@ -323,8 +313,8 @@
         at = pl.ds(pl.multiple_of(i * block, block), block)
         d_hidden = dh_ref[at].astype(F32) + dh_in[at].astype(F32)
         factors(i).wait()
-        d_ab[0, at] = (d_hidden * factor_ref[0, at]).astype(BF)
-        d_ab[1, at] = (d_hidden * factor_ref[1, at]).astype(BF)
+        d_ab[0, at] = (d_hidden * factor_ref[0, at].astype(F32)).astype(BF)
+        d_ab[1, at] = (d_hidden * factor_ref[1, at].astype(F32)).astype(BF)
         grad = jnp.sum(hid_ref[at].astype(F32) * d_hidden, axis=1, keepdims=True)
         high = grad.astype(BF).astype(F32)
         lane = lax.broadcasted_iota(jnp.int32, (block, META), 1)
@@ -478,35 +468,38 @@
     cols = 256
     steps = hidden // cols
     raw = pltpu.VMEM((half, hidden), BF)
-    rows_x, send_a, slot_of = call(
+    send_a, slot_of = call(
         functools.partial(forward_kernel, n_local, top, cols),
-        (shape(kept, half), shape(kept, hidden), shape(kept, rows)),
+        (shape(kept, hidden), shape(kept, rows)),
         (scales[0], got_x, weights[0]),
         limit=LIMIT_FORWARD,
         flops=2 * kept * half * hidden,
         moved=2 * half * hidden + 4 * rows * half,
         in_specs=[SMEM, HBM, HBM],
-        out_specs=[HBM, VMEM, VMEM],
+        out_specs=[VMEM, VMEM],
         scratch_shapes=[pltpu.VMEM((rows, half), BF), pltpu.VMEM((rows, META), BF)]
         + [pltpu.VMEM((kept, half), BF), raw, pltpu.VMEM((half, cols), BF)]
-        + [SEMS((4,)), SEMS((steps,)), SEMS, SEMS],
+        + [SEMS((4,)), SEMS((steps,)), SEMS],
     )
     their_a = across(send_a, 1)
-    send_b = call(
-        up_kernel,
-        shape(kept, hidden),
-        (scales[1], rows_x, weights[1]),
-        limit=LIMIT_FORWARD,
+    rows_x, send_b = call(
+        functools.partial(project_kernel, cols),
+        (shape(kept, half), shape(kept, hidden)),
+        (scales[1], slot_of, got_x, weights[1]),
+        limit=LIMIT_DOWN,
         flops=2 * kept * half * hidden,
-        moved=2 * half * hidden + 2 * kept * half,
-        in_specs=[SMEM, VMEM, HBM],
-        out_specs=VMEM,
-        scratch_shapes=[raw, pltpu.VMEM((half, cols), BF), SEMS((steps,))],
+        moved=2 * half * hidden + 4 * rows * half,
+        in_specs=[SMEM, VMEM, HBM, HBM],
+        out_specs=[HBM, VMEM],
+        scratch_shapes=[
+            pltpu.VMEM((rows, half), BF), pltpu.VMEM((kept, half), BF), raw,
+            pltpu.VMEM((half, cols), BF), SEMS((4,)), SEMS((steps,)), SEMS,
+        ],
     )
     their_a, send_b = lax.optimization_barrier((their_a, send_b))
     their_b = across(send_b, 1)
     rows_dy, send_dh = call(
-        functools.partial(down_kernel, cols),
+        functools.partial(project_kernel, cols),
         (shape(kept, half), shape(kept, hidden)),
         (scales[2], slot_of, got_dy, weights[2]),
         limit=LIMIT_DOWN,
@@ -524,7 +517,7 @@
     parts = half // chunk
     factor, hid, both_w = call(
         functools.partial(factor_kernel, chunk),
-        (shape(2, kept, hidden, dtype=F32), shape(kept, hidden), shape(half, 2 * hidden)),
+        (shape(2, kept, hidden), shape(kept, hidden), shape(half, 2 * hidden)),
         (scales[0], scales[1], send_a, send_b, their_a, their_b, weights[0], weights[1]),
         limit=LIMIT_FACTOR,
         flops=16 * kept * hidden,
@@ -543,7 +536,7 @@
         in_specs=[HBM] + [VMEM] * 4 + [HBM],
         out_specs=[HBM, HBM],
         scratch_shapes=[
-            pltpu.VMEM((2, kept, hidden), F32),
+            pltpu.VMEM((2, kept, hidden), BF),
             pltpu.VMEM((2, kept, hidden), BF),
             pltpu.VMEM((rows, 2 * hidden), BF),
             pltpu.VMEM((kept, META), BF),

time: 169 us -> 169 us (level)
  transfers between devices with their start and end apart: 15 -> 15, of which waited for: 12 -> 12; matrix products, arithmetic and copies ran while one was open for 7% -> 7% of each run, Pallas kernels for 15% -> 16%
where the time goes in v8:
time: 169 us; the launch traced here: 168 us
  waiting for transfers between devices  78.4 us (46%)
  Pallas kernels  41.6 us (25%)
  starting transfers between devices  34.2 us (20%)
  matrix products  12.1 us (7%)
    all_to_all x3, waiting for transfers between devices, spread(): lax.all_to_all(block, 'local', split_axis=0, concat_axis=0, tiled=True)  49.4 us
    pallas_call x10, Pallas kernels, call(): pl.pallas_call(kernel, out_shape=outs, compiler_params=pltpu.CompilerPara...  41.6 us
    ppermute x12, waiting for transfers between devices, across(): lax.ppermute(block, 'group', [(i, i ^ apart) for i in range(n_group)])  29 us
    all_to_all x3, starting transfers between devices, spread(): lax.all_to_all(block, 'local', split_axis=0, concat_axis=0, tiled=True)  21.1 us
    ppermute x12, starting transfers between devices, across(): lax.ppermute(block, 'group', [(i, i ^ apart) for i in range(n_group)])  13.1 us
    dot_general x3, matrix products, dot(): return lax.dot_general(left, right, dims, preferred_element_type=F32)  12.1 us
  transfers between devices with their start and end apart: 15, of which 12 were waited for; matrix products, arithmetic and copies ran while one was open for 7% of the time, Pallas kernels for 16%

profile of v8, /device:TPU:0, one launch (start us, length us, event | category | flops | bytes accessed | tf_op | source)
XLA Modules:
  0.0 168.0 jit_solution(15973724720737688733)
XLA Ops:
  0.6 1.9 %shard_map.164 = (bf16[16,2176]{1,0:T(8,128)(2,1)}, bf16[16,2176]{1,0:T(8,128)(2,1)}, bf16[16,2048]{1,0:T(8,128)(2,1)}, bf16[16,2048]{1,0:T(8,128)(2,1)}) custom-call(bf16[16,4096]{1,0:T(8,128)(2,1)} %xq_ref.1, f32[16,32]{1,0:T(8,128)} %xs_ref.1, bf16[16,4096]{1,0:T(8,128)(2,1)} %dy_ref.1, s32[8,16]{1,0:T(8,128)} %bitcast.48, s32[8,16]{1,0:T(8,128)} %bitcast.49, ...), custom_call_target="tpu_custom_call" | custom-call | bytes 524288 | tf_op jit(solution)/shard_map/pallas_call | solution.py:31
  2.5 3.1 %collective-permute-start.1 = (bf16[16,2176]{1,0:T(8,128)(2,1)}, bf16[16,2176]{1,0:T(8,128)(2,1)S(1)}, u32[]{:S(2)}, u32[]{:S(2)}) collective-permute-start(bf16[16,2176]{1,0:T(8,128)(2,1)} %get-tuple-element.38.b0), channel_id=1, source_target_pairs={{0,64},{32,96},{64,0},{96,32},{1,65},{33,97},{65,1},{97,33},{2,66}... | collective-permute-start | bytes 208904 | tf_op jit(solution)/shard_map/ppermute | solution.py:422
  8.5 2.8 %collective-permute-done.2.b3 = bf16[16,2176]{1,0:T(8,128)(2,1)S(1)} collective-permute-done((bf16[16,2176]{1,0:T(8,128)(2,1)}, bf16[16,2176]{1,0:T(8,128)(2,1)S(1)}, u32[]{:S(2)}, u32[]{:S(2)}) %collective-permute-start.2) | collective-permute-done | bytes 69664 | tf_op jit(solution)/shard_map/ppermute | solution.py:422
  12.2 2.3 %shard_map.165 = (bf16[512,2176]{1,0:T(8,128)(2,1)}, bf16[512,64]{1,0:T(8,128)(2,1)S(1)}, bf16[512,64]{1,0:T(8,128)(2,1)S(1)}, bf16[64,128]{1,0:T(8,128)(2,1)S(1)}) custom-call(bf16[16,2176]{1,0:T(8,128)(2,1)S(1)} %copy-done.1, bf16[16,2176]{1,0:T(8,128)(2,1)S(1)} %collective-permute-done.b1, bf16[16,2176]{1,0:T(8,128)(2,1)S(1)} %collective-permute-done.1.b2, ...), custom_call_target="tpu_custom_call" | custom-call | flops 142606336 | bytes 2228224 | tf_op jit(solution)/shard_map/pallas_call | solution.py:31
  14.6 8.6 %all-to-all-start = ((bf16[32,16,2176]{2,1,0:T(8,128)(2,1)}), bf16[32,16,2176]{2,1,0:T(8,128)(2,1)}, u32[]{:S(2)}, u32[]{:S(2)}) async-start(bf16[32,16,2176]{2,1,0:T(8,128)(2,1)} %bitcast.6), calls=%async_computation | async-start | bytes 4456448 | tf_op jit(solution)/shard_map/all_to_all | solution.py:425
  26.8 2.3 %collective-permute-done.4.b2 = bf16[16,2048]{1,0:T(8,128)(2,1)S(1)} collective-permute-done((bf16[16,2048]{1,0:T(8,128)(2,1)S(1)}, bf16[16,2048]{1,0:T(8,128)(2,1)S(1)}, u32[]{:S(2)}, u32[]{:S(2)}) %collective-permute-start.4) | collective-permute-done | bytes 65568 | tf_op jit(solution)/shard_map/ppermute | solution.py:422
  30.5 1.9 %shard_map.166 = bf16[512,2048]{1,0:T(8,128)(2,1)} custom-call(bf16[512,64]{1,0:T(8,128)(2,1)S(1)} %get-tuple-element.41.gated_ref, bf16[16,2048]{1,0:T(8,128)(2,1)S(1)} %copy-done, bf16[16,2048]{1,0:T(8,128)(2,1)S(1)} %collective-permute-done.3.b1, bf16[16,2048]{1,0:T(8,128)(2,1)S(1)} %collective-permute-done.4.b2, ...), custom_call_target="tpu_custom_call" | custom-call | flops 134217728 | bytes 2097152 | tf_op jit(solution)/shard_map/pallas_call | solution.py:31
  32.4 22.3 %all-to-all-done = bf16[32,16,2176]{2,1,0:T(8,128)(2,1)} async-done(((bf16[32,16,2176]{2,1,0:T(8,128)(2,1)}), bf16[32,16,2176]{2,1,0:T(8,128)(2,1)}, u32[]{:S(2)}, u32[]{:S(2)}) %all-to-all-start) | async-done | bytes 2228256 | tf_op jit(solution)/shard_map/all_to_all | solution.py:425
  54.8 4.9 %all-to-all-start.1 = ((bf16[32,16,2048]{2,1,0:T(8,128)(2,1)}), bf16[32,16,2048]{2,1,0:T(8,128)(2,1)}, u32[]{:S(2)}, u32[]{:S(2)}) async-start(bf16[32,16,2048]{2,1,0:T(8,128)(2,1)} %bitcast.11), calls=%async_computation.1 | async-start | bytes 4194304 | tf_op jit(solution)/shard_map/all_to_all | solution.py:425
  59.7 6.5 %shard_map.167 = (bf16[384,768]{1,0:T(8,128)(2,1)S(1)}, bf16[384,512]{1,0:T(8,128)(2,1)S(1)}) custom-call(f32[6,16]{1,0:T(8,128)S(1)} %get-tuple-element.72.sg_ref, bf16[512,2176]{1,0:T(8,128)(2,1)} %bitcast.7.x_hbm.dy_hbm, bf16[2048,768]{1,0:T(8,128)(2,1)} %bitcast.42), custom_call_target="tpu_custom_call" | custom-call | flops 1207959552 | bytes 7340032 | tf_op jit(solution)/shard_map/pallas_call | solution.py:31
  66.3 5.2 %shard_map.168 = (bf16[384,2048]{1,0:T(8,128)(2,1)}, bf16[384,768]{1,0:T(8,128)(2,1)S(1)}) custom-call(f32[6,16]{1,0:T(8,128)S(1)} %get-tuple-element.71.sv_ref.su_ref, bf16[384,512]{1,0:T(8,128)(2,1)S(1)} %get-tuple-element.46.slot_ref, bf16[512,2176]{1,0:T(8,128)(2,1)} %bitcast.7.x_hbm.dy_hbm, bf16[2048,768]{1,0:T(8,128)(2,1)} %bitcast.44), custom_call_target="tpu_custom_call" | custom-call | flops 1207959552 | bytes 7340032 | tf_op jit(solution)/shard_map/pallas_call | solution.py:31
  71.5 10.1 %collective-permute-done.6.a_in = bf16[384,768]{1,0:T(8,128)(2,1)S(1)} collective-permute-done((bf16[384,768]{1,0:T(8,128)(2,1)S(1)}, bf16[384,768]{1,0:T(8,128)(2,1)S(1)}, u32[]{:S(2)}, u32[]{:S(2)}) %collective-permute-start.6) | collective-permute-done | bytes 589856 | tf_op jit(solution)/shard_map/ppermute | solution.py:422
  81.9 7.8 %all-to-all-done.1 = bf16[32,16,2048]{2,1,0:T(8,128)(2,1)} async-done(((bf16[32,16,2048]{2,1,0:T(8,128)(2,1)}), bf16[32,16,2048]{2,1,0:T(8,128)(2,1)}, u32[]{:S(2)}, u32[]{:S(2)}) %all-to-all-start.1) | async-done | bytes 2097184 | tf_op jit(solution)/shard_map/all_to_all | solution.py:425
  89.6 5.2 %shard_map.170 = (bf16[384,2048]{1,0:T(8,128)(2,1)}, bf16[384,768]{1,0:T(8,128)(2,1)S(1)}) custom-call(f32[6,16]{1,0:T(8,128)S(1)} %bitcast.41, bf16[384,512]{1,0:T(8,128)(2,1)S(1)} %get-tuple-element.46.slot_ref, bf16[512,2048]{1,0:T(8,128)(2,1)} %bitcast.12.dy_hbm, bf16[2048,768]{1,0:T(8,128)(2,1)} %bitcast.46), custom_call_target="tpu_custom_call" | custom-call | flops 1207959552 | bytes 7340032 | tf_op jit(solution)/shard_map/pallas_call | solution.py:31
  96.7 7.4 %shard_map.169 = (bf16[2,384,768]{2,1,0:T(8,128)(2,1)}, bf16[384,768]{1,0:T(8,128)(2,1)S(1)}, bf16[2048,1536]{1,0:T(8,128)(2,1)}) custom-call(f32[6,16]{1,0:T(8,128)S(1)} %get-tuple-element.72.sg_ref, f32[6,16]{1,0:T(8,128)S(1)} %get-tuple-element.71.sv_ref.su_ref, bf16[384,768]{1,0:T(8,128)(2,1)S(1)} %get-tuple-element.45.a_ref, ...), custom_call_target="tpu_custom_call" | custom-call | flops 4718592 | bytes 12582912 | tf_op jit(solution)/shard_map/pallas_call | solution.py:31
  104.1 4.7 %collective-permute-done.8.dh_in = bf16[384,768]{1,0:T(8,128)(2,1)S(1)} collective-permute-done((bf16[384,768]{1,0:T(8,128)(2,1)S(1)}, bf16[384,768]{1,0:T(8,128)(2,1)S(1)}, u32[]{:S(2)}, u32[]{:S(2)}) %collective-permute-start.8) | collective-permute-done | bytes 589856 | tf_op jit(solution)/shard_map/ppermute | solution.py:422
  108.8 9.3 %shard_map.171 = (bf16[2,384,768]{2,1,0:T(8,128)(2,1)}, bf16[512,2176]{1,0:T(8,128)(2,1)}) custom-call(bf16[2,384,768]{2,1,0:T(8,128)(2,1)} %get-tuple-element.50.factor_hbm, bf16[384,768]{1,0:T(8,128)(2,1)S(1)} %get-tuple-element.51.hid_ref, bf16[384,768]{1,0:T(8,128)(2,1)S(1)} %get-tuple-element.53.dh_ref, ...), custom_call_target="tpu_custom_call" | custom-call | flops 3221225472 | bytes 8388608 | tf_op jit(solution)/shard_map/pallas_call | solution.py:31
  118.1 7.6 %all-to-all-start.2 = ((bf16[32,16,2176]{2,1,0:T(8,128)(2,1)}), bf16[32,16,2176]{2,1,0:T(8,128)(2,1)S(1)}, u32[]{:S(2)}, u32[]{:S(2)}) async-start(bf16[32,16,2176]{2,1,0:T(8,128)(2,1)} %bitcast.47), calls=%async_computation.2 | async-start | bytes 4456448 | tf_op jit(solution)/shard_map/all_to_all | solution.py:425
  125.8 5.1 %convolution_convert_fusion = bf16[2048,768]{1,0:T(8,128)(2,1)} fusion(bf16[384,2048]{1,0:T(8,128)(2,1)} %get-tuple-element.58, bf16[384,768]{1,0:T(8,128)(2,1)S(1)} %get-tuple-element.51.hid_ref), kind=kOutput, calls=%fused_computation | convolution fusion | flops 1209532416 | bytes 5308416 | tf_op jit(solution)/shard_map/dot_general | solution.py:27
  130.9 3.5 %convolution_convert_fusion.1 = bf16[2048,768]{1,0:T(8,128)(2,1)} fusion(bf16[384,2048]{1,0:T(8,128)(2,1)S(1)} %copy-done.6, bf16[2,384,768]{2,1,0:T(8,128)(2,1)S(1)} %copy-done.8), kind=kOutput, calls=%fused_computation.1 | convolution fusion | flops 1209532416 | bytes 5308416 | tf_op jit(solution)/shard_map/dot_general | solution.py:27
  134.4 3.5 %convolution_convert_fusion.2 = bf16[2048,768]{1,0:T(8,128)(2,1)} fusion(bf16[384,2048]{1,0:T(8,128)(2,1)S(1)} %copy-done.6, bf16[2,384,768]{2,1,0:T(8,128)(2,1)S(1)} %copy-done.8), kind=kOutput, calls=%fused_computation.2 | convolution fusion | flops 1209532416 | bytes 5308416 | tf_op jit(solution)/shard_map/dot_general | solution.py:27
  137.9 19.3 %all-to-all-done.2 = bf16[32,16,2176]{2,1,0:T(8,128)(2,1)S(1)} async-done(((bf16[32,16,2176]{2,1,0:T(8,128)(2,1)}), bf16[32,16,2176]{2,1,0:T(8,128)(2,1)S(1)}, u32[]{:S(2)}, u32[]{:S(2)}) %all-to-all-start.2) | async-done | bytes 2228256 | tf_op jit(solution)/shard_map/all_to_all | solution.py:425
  158.9 2.9 %collective-permute-start.10 = (bf16[16,2176]{1,0:T(8,128)(2,1)S(1)}, bf16[16,2176]{1,0:T(8,128)(2,1)S(1)}, u32[]{:S(2)}, u32[]{:S(2)}) collective-permute-start(bf16[16,2176]{1,0:T(8,128)(2,1)S(1)} %get-tuple-element.64), channel_id=1, source_target_pairs={{0,64},{32,96},{64,0},{96,32},{1,65},{33,97},{65,1},{97,33},{2,66}... | collective-permute-start | bytes 208904 | tf_op jit(solution)/shard_map/ppermute | solution.py:422
  164.8 2.5 %collective-permute-done.11.b3 = bf16[16,2176]{1,0:T(8,128)(2,1)S(1)} collective-permute-done((bf16[16,2176]{1,0:T(8,128)(2,1)S(1)}, bf16[16,2176]{1,0:T(8,128)(2,1)S(1)}, u32[]{:S(2)}, u32[]{:S(2)}) %collective-permute-start.11) | collective-permute-done | bytes 69664 | tf_op jit(solution)/shard_map/ppermute | solution.py:422
  (39 shorter events, 16.5 us)
Async XLA Ops:
  2.5 6.0 %collective-permute-start.1 = (bf16[16,2176]{1,0:T(8,128)(2,1)}, bf16[16,2176]{1,0:T(8,128)(2,1)S(1)}, u32[]{:S(2)}, u32[]{:S(2)}) collective-permute-start(bf16[16,2176]{1,0:T(8,128)(2,1)} %get-tuple-element.38.b0), channel_id=1, source_target_pairs={{0,64},{32,96},{64,0},{96,32},{1,65},{33,97},{65,1},{97,33},{2,66}... | collective-permute-start | bytes 208904 | tf_op jit(solution)/shard_map/ppermute | solution.py:422
  5.6 5.7 %collective-permute-start.2 = (bf16[16,2176]{1,0:T(8,128)(2,1)}, bf16[16,2176]{1,0:T(8,128)(2,1)S(1)}, u32[]{:S(2)}, u32[]{:S(2)}) collective-permute-start(bf16[16,2176]{1,0:T(8,128)(2,1)} %get-tuple-element.39), channel_id=1, source_target_pairs={{0,96},{32,64},{64,32},{96,0},{1,97},{33,65},{65,33},{97,1},{2,98}... | collective-permute-start | bytes 208904 | tf_op jit(solution)/shard_map/ppermute | solution.py:422
  6.8 4.6 %collective-permute-start = (bf16[16,2176]{1,0:T(8,128)(2,1)}, bf16[16,2176]{1,0:T(8,128)(2,1)S(1)}, u32[]{:S(2)}, u32[]{:S(2)}) collective-permute-start(bf16[16,2176]{1,0:T(8,128)(2,1)} %get-tuple-element.39), channel_id=1, source_target_pairs={{0,32},{32,0},{64,96},{96,64},{1,33},{33,1},{65,97},{97,65},{2,34}... | collective-permute-start | bytes 208904 | tf_op jit(solution)/shard_map/ppermute | solution.py:422
  11.4 0.9 copy-start.1
  14.6 8.6 %copy-start = (bf16[16,2048]{1,0:T(8,128)(2,1)S(1)}, bf16[16,2048]{1,0:T(8,128)(2,1)}, u32[]{:S(2)}) copy-start(bf16[16,2048]{1,0:T(8,128)(2,1)} %get-tuple-element.42.b0) | copy-start | bytes 196612
  14.6 10.2 %copy-start.7 = (bf16[16,2048]{1,0:T(8,128)(2,1)S(1)}, bf16[16,2048]{1,0:T(8,128)(2,1)}, u32[]{:S(2)}) copy-start(bf16[16,2048]{1,0:T(8,128)(2,1)} %get-tuple-element.43) | copy-start | bytes 196612
  14.6 40.2 %all-to-all-start = ((bf16[32,16,2176]{2,1,0:T(8,128)(2,1)}), bf16[32,16,2176]{2,1,0:T(8,128)(2,1)}, u32[]{:S(2)}, u32[]{:S(2)}) async-start(bf16[32,16,2176]{2,1,0:T(8,128)(2,1)} %bitcast.6), calls=%async_computation | async-start | bytes 4456448 | tf_op jit(solution)/shard_map/all_to_all | solution.py:425
  23.2 5.9 %collective-permute-start.4 = (bf16[16,2048]{1,0:T(8,128)(2,1)S(1)}, bf16[16,2048]{1,0:T(8,128)(2,1)S(1)}, u32[]{:S(2)}, u32[]{:S(2)}) collective-permute-start(bf16[16,2048]{1,0:T(8,128)(2,1)S(1)} %copy-done), channel_id=1, source_target_pairs={{0,64},{32,96},{64,0},{96,32},{1,65},{33,97},{65,1},{97,33},{2,66}... | collective-permute-start | bytes 196616 | tf_op jit(solution)/shard_map/ppermute | solution.py:422
  24.8 5.7 %collective-permute-start.5 = (bf16[16,2048]{1,0:T(8,128)(2,1)S(1)}, bf16[16,2048]{1,0:T(8,128)(2,1)S(1)}, u32[]{:S(2)}, u32[]{:S(2)}) collective-permute-start(bf16[16,2048]{1,0:T(8,128)(2,1)S(1)} %copy-done.7), channel_id=1, source_target_pairs={{0,96},{32,64},{64,32},{96,0},{1,97},{33,65},{65,33},{97,1},{2,98}... | collective-permute-start | bytes 196616 | tf_op jit(solution)/shard_map/ppermute | solution.py:422
  26.0 4.5 %collective-permute-start.3 = (bf16[16,2048]{1,0:T(8,128)(2,1)S(1)}, bf16[16,2048]{1,0:T(8,128)(2,1)S(1)}, u32[]{:S(2)}, u32[]{:S(2)}) collective-permute-start(bf16[16,2048]{1,0:T(8,128)(2,1)S(1)} %copy-done.7), channel_id=1, source_target_pairs={{0,32},{32,0},{64,96},{96,64},{1,33},{33,1},{65,97},{97,65},{2,34}... | collective-permute-start | bytes 196616 | tf_op jit(solution)/shard_map/ppermute | solution.py:422
  54.8 4.9 %copy-start.3 = (f32[16,1,6]{0,1,2:T(1,128)S(1)}, f32[16,1,6]{0,1,2:T(1,128)}, u32[]{:S(2)}) copy-start(f32[16,1,6]{0,1,2:T(1,128)} %param.24) | copy-start | bytes 1156
  54.8 4.9 %copy-start.4 = (f32[16,1,6]{0,1,2:T(1,128)S(1)}, f32[16,1,6]{0,1,2:T(1,128)}, u32[]{:S(2)}) copy-start(f32[16,1,6]{0,1,2:T(1,128)} %param.23) | copy-start | bytes 1156
  54.8 34.9 %all-to-all-start.1 = ((bf16[32,16,2048]{2,1,0:T(8,128)(2,1)}), bf16[32,16,2048]{2,1,0:T(8,128)(2,1)}, u32[]{:S(2)}, u32[]{:S(2)}) async-start(bf16[32,16,2048]{2,1,0:T(8,128)(2,1)} %bitcast.11), calls=%async_computation.1 | async-start | bytes 4194304 | tf_op jit(solution)/shard_map/all_to_all | solution.py:425
  59.7 6.6 %copy-start.5 = (f32[16,1,6]{0,1,2:T(1,128)S(1)}, f32[16,1,6]{0,1,2:T(1,128)}, u32[]{:S(2)}) copy-start(f32[16,1,6]{0,1,2:T(1,128)} %param.25) | copy-start | bytes 1156
  66.2 15.4 %collective-permute-start.6 = (bf16[384,768]{1,0:T(8,128)(2,1)S(1)}, bf16[384,768]{1,0:T(8,128)(2,1)S(1)}, u32[]{:S(2)}, u32[]{:S(2)}) collective-permute-start(bf16[384,768]{1,0:T(8,128)(2,1)S(1)} %get-tuple-element.45.a_ref), channel_id=1, source_target_pairs={{0,32},{32,0},{64,96},{96,64},{1,33},{33,1},{65,97},{97,65},{2,34}... | collective-permute-start | bytes 1769480 | tf_op jit(solution)/shard_map/ppermute | solution.py:422
  81.6 13.3 %copy-start.2 = (bf16[384,768]{1,0:T(8,128)(2,1)}, bf16[384,768]{1,0:T(8,128)(2,1)S(1)}, u32[]{:S(2)}) copy-start(bf16[384,768]{1,0:T(8,128)(2,1)S(1)} %collective-permute-done.6.a_in) | copy-start | bytes 1769476
  81.6 15.1 %collective-permute-start.7 = (bf16[384,768]{1,0:T(8,128)(2,1)S(1)}, bf16[384,768]{1,0:T(8,128)(2,1)}, u32[]{:S(2)}, u32[]{:S(2)}) collective-permute-start(bf16[384,768]{1,0:T(8,128)(2,1)S(1)} %get-tuple-element.48.b_ref), channel_id=1, source_target_pairs={{0,32},{32,0},{64,96},{96,64},{1,33},{33,1},{65,97},{97,65},{2,34}... | collective-permute-start | bytes 1769480 | tf_op jit(solution)/shard_map/ppermute | solution.py:422
  94.9 13.9 %collective-permute-start.8 = (bf16[384,768]{1,0:T(8,128)(2,1)S(1)}, bf16[384,768]{1,0:T(8,128)(2,1)S(1)}, u32[]{:S(2)}, u32[]{:S(2)}) collective-permute-start(bf16[384,768]{1,0:T(8,128)(2,1)S(1)} %get-tuple-element.53.dh_ref), channel_id=1, source_target_pairs={{0,32},{32,0},{64,96},{96,64},{1,33},{33,1},{65,97},{97,65},{2,34}... | collective-permute-start | bytes 1769480 | tf_op jit(solution)/shard_map/ppermute | solution.py:422
  118.1 39.0 %all-to-all-start.2 = ((bf16[32,16,2176]{2,1,0:T(8,128)(2,1)}), bf16[32,16,2176]{2,1,0:T(8,128)(2,1)S(1)}, u32[]{:S(2)}, u32[]{:S(2)}) async-start(bf16[32,16,2176]{2,1,0:T(8,128)(2,1)} %bitcast.47), calls=%async_computation.2 | async-start | bytes 4456448 | tf_op jit(solution)/shard_map/all_to_all | solution.py:425
  125.8 5.1 %copy-start.6 = (bf16[384,2048]{1,0:T(8,128)(2,1)S(1)}, bf16[384,2048]{1,0:T(8,128)(2,1)}, u32[]{:S(2)}) copy-start(bf16[384,2048]{1,0:T(8,128)(2,1)} %get-tuple-element.56) | copy-start | bytes 4718596
  125.8 5.1 %copy-start.8 = (bf16[2,384,768]{2,1,0:T(8,128)(2,1)S(1)}, bf16[2,384,768]{2,1,0:T(8,128)(2,1)}, u32[]{:S(2)}) copy-start(bf16[2,384,768]{2,1,0:T(8,128)(2,1)} %get-tuple-element.57) | copy-start | bytes 3538948
  158.2 4.8 %collective-permute-start.9 = (bf16[16,2176]{1,0:T(8,128)(2,1)S(1)}, bf16[16,2176]{1,0:T(8,128)(2,1)S(1)}, u32[]{:S(2)}, u32[]{:S(2)}) collective-permute-start(bf16[16,2176]{1,0:T(8,128)(2,1)S(1)} %get-tuple-element.63), channel_id=1, source_target_pairs={{0,32},{32,0},{64,96},{96,64},{1,33},{33,1},{65,97},{97,65},{2,34}... | collective-permute-start | bytes 208904 | tf_op jit(solution)/shard_map/ppermute | solution.py:422
  158.9 6.0 %collective-permute-start.10 = (bf16[16,2176]{1,0:T(8,128)(2,1)S(1)}, bf16[16,2176]{1,0:T(8,128)(2,1)S(1)}, u32[]{:S(2)}, u32[]{:S(2)}) collective-permute-start(bf16[16,2176]{1,0:T(8,128)(2,1)S(1)} %get-tuple-element.64), channel_id=1, source_target_pairs={{0,64},{32,96},{64,0},{96,32},{1,65},{33,97},{65,1},{97,33},{2,66}... | collective-permute-start | bytes 208904 | tf_op jit(solution)/shard_map/ppermute | solution.py:422
  161.8 5.5 %collective-permute-start.11 = (bf16[16,2176]{1,0:T(8,128)(2,1)S(1)}, bf16[16,2176]{1,0:T(8,128)(2,1)S(1)}, u32[]{:S(2)}, u32[]{:S(2)}) collective-permute-start(bf16[16,2176]{1,0:T(8,128)(2,1)S(1)} %get-tuple-element.65), channel_id=1, source_target_pairs={{0,96},{32,64},{64,32},{96,0},{1,97},{33,65},{65,33},{97,1},{2,98}... | collective-permute-start | bytes 208904 | tf_op jit(solution)/shard_map/ppermute | solution.py:422

commit v9 on v8

--- a/solution.py
+++ b/solution.py
@@ -287,20 +287,13 @@
 
 
 def backward_kernel(
-    chunk, factor_hbm, hid_ref, dh_ref, dh_in, slot_ref, w_hbm,
-    d_hbm, dx_hbm, factor_ref, d_ab, wide, pairs, both_w, dx, sems_f, sems_w, sems_x, sem_d, sem_m,
+    chunk, factor_ref, hid_ref, dh_ref, dh_in, slot_ref, w_hbm,
+    d_hbm, dx_hbm, d_ab, wide, pairs, both_w, dx, sems_w, sems_x, sem_d, sem_m,
 ):
     kept, hidden = hid_ref.shape
     half = both_w.shape[0]
     parts = half // chunk
-    block = kept // sems_f.shape[0]
-
-    def factors(i):
-        at = (slice(None), pl.ds(pl.multiple_of(i * block, block), block))
-        return pltpu.make_async_copy(factor_hbm.at[at], factor_ref.at[at], sems_f.at[i])
-
-    for i in range(kept // block):
-        factors(i).start()
+    block = 64
 
     def load(i):
         at = pl.ds(pl.multiple_of(i * chunk, chunk), chunk)
@@ -312,7 +305,6 @@
     def activate(i, carry):
         at = pl.ds(pl.multiple_of(i * block, block), block)
         d_hidden = dh_ref[at].astype(F32) + dh_in[at].astype(F32)
-        factors(i).wait()
         d_ab[0, at] = (d_hidden * factor_ref[0, at].astype(F32)).astype(BF)
         d_ab[1, at] = (d_hidden * factor_ref[1, at].astype(F32)).astype(BF)
         grad = jnp.sum(hid_ref[at].astype(F32) * d_hidden, axis=1, keepdims=True)
@@ -533,16 +525,14 @@
         limit=LIMIT_BACKWARD,
         flops=4 * rows * half * hidden,
         moved=4 * half * hidden + 2 * rows * half,
-        in_specs=[HBM] + [VMEM] * 4 + [HBM],
+        in_specs=[VMEM] * 5 + [HBM],
         out_specs=[HBM, HBM],
         scratch_shapes=[
-            pltpu.VMEM((2, kept, hidden), BF),
             pltpu.VMEM((2, kept, hidden), BF),
             pltpu.VMEM((rows, 2 * hidden), BF),
             pltpu.VMEM((kept, META), BF),
             pltpu.VMEM((half, 2 * hidden), BF),
             pltpu.VMEM((rows, wide), BF),
-            SEMS((4,)),
             SEMS((parts,)),
             SEMS((parts,)),
             SEMS,

time: 169 us -> 168 us (level)
  no operation moved by 1% of the time
where the time goes in v9:
time: 168 us; the launch traced here: 167 us
  waiting for transfers between devices  78.4 us (47%)
  Pallas kernels  40.9 us (24%)
  starting transfers between devices  34.3 us (20%)
  matrix products  12.1 us (7%)
    all_to_all x3, waiting for transfers between devices, spread(): lax.all_to_all(block, 'local', split_axis=0, concat_axis=0, tiled=True)  49.4 us
    pallas_call x10, Pallas kernels, call(): pl.pallas_call(kernel, out_shape=outs, compiler_params=pltpu.CompilerPara...  40.9 us
    ppermute x12, waiting for transfers between devices, across(): lax.ppermute(block, 'group', [(i, i ^ apart) for i in range(n_group)])  29 us
    all_to_all x3, starting transfers between devices, spread(): lax.all_to_all(block, 'local', split_axis=0, concat_axis=0, tiled=True)  21.1 us
    ppermute x12, starting transfers between devices, across(): lax.ppermute(block, 'group', [(i, i ^ apart) for i in range(n_group)])  13.1 us
    dot_general x3, matrix products, dot(): return lax.dot_general(left, right, dims, preferred_element_type=F32)  12.1 us
  transfers between devices with their start and end apart: 15, of which 12 were waited for; matrix products, arithmetic and copies ran while one was open for 7% of the time, Pallas kernels for 16%

profile of v9, /device:TPU:0, one launch (start us, length us, event | category | flops | bytes accessed | tf_op | source)
XLA Modules:
  0.0 167.4 jit_solution(1670098221275461486)
XLA Ops:
  0.6 1.9 %shard_map.164 = (bf16[16,2176]{1,0:T(8,128)(2,1)}, bf16[16,2176]{1,0:T(8,128)(2,1)}, bf16[16,2048]{1,0:T(8,128)(2,1)}, bf16[16,2048]{1,0:T(8,128)(2,1)}) custom-call(bf16[16,4096]{1,0:T(8,128)(2,1)} %xq_ref.1, f32[16,32]{1,0:T(8,128)} %xs_ref.1, bf16[16,4096]{1,0:T(8,128)(2,1)} %dy_ref.1, s32[8,16]{1,0:T(8,128)} %bitcast.48, s32[8,16]{1,0:T(8,128)} %bitcast.49, ...), custom_call_target="tpu_custom_call" | custom-call | bytes 524288 | tf_op jit(solution)/shard_map/pallas_call | solution.py:31
  2.5 3.1 %collective-permute-start.1 = (bf16[16,2176]{1,0:T(8,128)(2,1)}, bf16[16,2176]{1,0:T(8,128)(2,1)S(1)}, u32[]{:S(2)}, u32[]{:S(2)}) collective-permute-start(bf16[16,2176]{1,0:T(8,128)(2,1)} %get-tuple-element.38.b0), channel_id=1, source_target_pairs={{0,64},{32,96},{64,0},{96,32},{1,65},{33,97},{65,1},{97,33},{2,66}... | collective-permute-start | bytes 208904 | tf_op jit(solution)/shard_map/ppermute | solution.py:414
  8.5 2.8 %collective-permute-done.2.b3 = bf16[16,2176]{1,0:T(8,128)(2,1)S(1)} collective-permute-done((bf16[16,2176]{1,0:T(8,128)(2,1)}, bf16[16,2176]{1,0:T(8,128)(2,1)S(1)}, u32[]{:S(2)}, u32[]{:S(2)}) %collective-permute-start.2) | collective-permute-done | bytes 69664 | tf_op jit(solution)/shard_map/ppermute | solution.py:414
  12.2 2.3 %shard_map.165 = (bf16[512,2176]{1,0:T(8,128)(2,1)}, bf16[512,64]{1,0:T(8,128)(2,1)S(1)}, bf16[512,64]{1,0:T(8,128)(2,1)S(1)}, bf16[64,128]{1,0:T(8,128)(2,1)S(1)}) custom-call(bf16[16,2176]{1,0:T(8,128)(2,1)S(1)} %copy-done.1, bf16[16,2176]{1,0:T(8,128)(2,1)S(1)} %collective-permute-done.b1, bf16[16,2176]{1,0:T(8,128)(2,1)S(1)} %collective-permute-done.1.b2, ...), custom_call_target="tpu_custom_call" | custom-call | flops 142606336 | bytes 2228224 | tf_op jit(solution)/shard_map/pallas_call | solution.py:31
  14.6 8.6 %all-to-all-start = ((bf16[32,16,2176]{2,1,0:T(8,128)(2,1)}), bf16[32,16,2176]{2,1,0:T(8,128)(2,1)}, u32[]{:S(2)}, u32[]{:S(2)}) async-start(bf16[32,16,2176]{2,1,0:T(8,128)(2,1)} %bitcast.6), calls=%async_computation | async-start | bytes 4456448 | tf_op jit(solution)/shard_map/all_to_all | solution.py:417
  26.8 2.3 %collective-permute-done.4.b2 = bf16[16,2048]{1,0:T(8,128)(2,1)S(1)} collective-permute-done((bf16[16,2048]{1,0:T(8,128)(2,1)S(1)}, bf16[16,2048]{1,0:T(8,128)(2,1)S(1)}, u32[]{:S(2)}, u32[]{:S(2)}) %collective-permute-start.4) | collective-permute-done | bytes 65568 | tf_op jit(solution)/shard_map/ppermute | solution.py:414
  30.5 1.9 %shard_map.166 = bf16[512,2048]{1,0:T(8,128)(2,1)} custom-call(bf16[512,64]{1,0:T(8,128)(2,1)S(1)} %get-tuple-element.41.gated_ref, bf16[16,2048]{1,0:T(8,128)(2,1)S(1)} %copy-done, bf16[16,2048]{1,0:T(8,128)(2,1)S(1)} %collective-permute-done.3.b1, bf16[16,2048]{1,0:T(8,128)(2,1)S(1)} %collective-permute-done.4.b2, ...), custom_call_target="tpu_custom_call" | custom-call | flops 134217728 | bytes 2097152 | tf_op jit(solution)/shard_map/pallas_call | solution.py:31
  32.4 22.3 %all-to-all-done = bf16[32,16,2176]{2,1,0:T(8,128)(2,1)} async-done(((bf16[32,16,2176]{2,1,0:T(8,128)(2,1)}), bf16[32,16,2176]{2,1,0:T(8,128)(2,1)}, u32[]{:S(2)}, u32[]{:S(2)}) %all-to-all-start) | async-done | bytes 2228256 | tf_op jit(solution)/shard_map/all_to_all | solution.py:417
  54.8 4.9 %all-to-all-start.1 = ((bf16[32,16,2048]{2,1,0:T(8,128)(2,1)}), bf16[32,16,2048]{2,1,0:T(8,128)(2,1)}, u32[]{:S(2)}, u32[]{:S(2)}) async-start(bf16[32,16,2048]{2,1,0:T(8,128)(2,1)} %bitcast.11), calls=%async_computation.1 | async-start | bytes 4194304 | tf_op jit(solution)/shard_map/all_to_all | solution.py:417
  59.7 6.5 %shard_map.167 = (bf16[384,768]{1,0:T(8,128)(2,1)S(1)}, bf16[384,512]{1,0:T(8,128)(2,1)S(1)}) custom-call(f32[6,16]{1,0:T(8,128)S(1)} %get-tuple-element.72.sg_ref, bf16[512,2176]{1,0:T(8,128)(2,1)} %bitcast.7.x_hbm.dy_hbm, bf16[2048,768]{1,0:T(8,128)(2,1)} %bitcast.42), custom_call_target="tpu_custom_call" | custom-call | flops 1207959552 | bytes 7340032 | tf_op jit(solution)/shard_map/pallas_call | solution.py:31
  66.3 5.2 %shard_map.168 = (bf16[384,2048]{1,0:T(8,128)(2,1)}, bf16[384,768]{1,0:T(8,128)(2,1)S(1)}) custom-call(f32[6,16]{1,0:T(8,128)S(1)} %get-tuple-element.71.sv_ref.su_ref, bf16[384,512]{1,0:T(8,128)(2,1)S(1)} %get-tuple-element.46.slot_ref, bf16[512,2176]{1,0:T(8,128)(2,1)} %bitcast.7.x_hbm.dy_hbm, bf16[2048,768]{1,0:T(8,128)(2,1)} %bitcast.44), custom_call_target="tpu_custom_call" | custom-call | flops 1207959552 | bytes 7340032 | tf_op jit(solution)/shard_map/pallas_call | solution.py:31
  71.5 10.1 %collective-permute-done.6.a_in = bf16[384,768]{1,0:T(8,128)(2,1)S(1)} collective-permute-done((bf16[384,768]{1,0:T(8,128)(2,1)S(1)}, bf16[384,768]{1,0:T(8,128)(2,1)S(1)}, u32[]{:S(2)}, u32[]{:S(2)}) %collective-permute-start.6) | collective-permute-done | bytes 589856 | tf_op jit(solution)/shard_map/ppermute | solution.py:414
  81.9 7.8 %all-to-all-done.1 = bf16[32,16,2048]{2,1,0:T(8,128)(2,1)} async-done(((bf16[32,16,2048]{2,1,0:T(8,128)(2,1)}), bf16[32,16,2048]{2,1,0:T(8,128)(2,1)}, u32[]{:S(2)}, u32[]{:S(2)}) %all-to-all-start.1) | async-done | bytes 2097184 | tf_op jit(solution)/shard_map/all_to_all | solution.py:417
  89.6 5.2 %shard_map.170 = (bf16[384,2048]{1,0:T(8,128)(2,1)}, bf16[384,768]{1,0:T(8,128)(2,1)S(1)}) custom-call(f32[6,16]{1,0:T(8,128)S(1)} %bitcast.41, bf16[384,512]{1,0:T(8,128)(2,1)S(1)} %get-tuple-element.46.slot_ref, bf16[512,2048]{1,0:T(8,128)(2,1)} %bitcast.12.dy_hbm, bf16[2048,768]{1,0:T(8,128)(2,1)} %bitcast.46), custom_call_target="tpu_custom_call" | custom-call | flops 1207959552 | bytes 7340032 | tf_op jit(solution)/shard_map/pallas_call | solution.py:31
  96.7 7.4 %shard_map.169 = (bf16[2,384,768]{2,1,0:T(8,128)(2,1)}, bf16[384,768]{1,0:T(8,128)(2,1)S(1)}, bf16[2048,1536]{1,0:T(8,128)(2,1)}) custom-call(f32[6,16]{1,0:T(8,128)S(1)} %get-tuple-element.72.sg_ref, f32[6,16]{1,0:T(8,128)S(1)} %get-tuple-element.71.sv_ref.su_ref, bf16[384,768]{1,0:T(8,128)(2,1)S(1)} %get-tuple-element.45.a_ref, ...), custom_call_target="tpu_custom_call" | custom-call | flops 4718592 | bytes 12582912 | tf_op jit(solution)/shard_map/pallas_call | solution.py:31
  104.1 4.7 %collective-permute-done.8.dh_in = bf16[384,768]{1,0:T(8,128)(2,1)S(1)} collective-permute-done((bf16[384,768]{1,0:T(8,128)(2,1)S(1)}, bf16[384,768]{1,0:T(8,128)(2,1)S(1)}, u32[]{:S(2)}, u32[]{:S(2)}) %collective-permute-start.8) | collective-permute-done | bytes 589856 | tf_op jit(solution)/shard_map/ppermute | solution.py:414
  108.8 8.7 %shard_map.171 = (bf16[2,384,768]{2,1,0:T(8,128)(2,1)}, bf16[512,2176]{1,0:T(8,128)(2,1)}) custom-call(bf16[2,384,768]{2,1,0:T(8,128)(2,1)} %get-tuple-element.50.factor_ref, bf16[384,768]{1,0:T(8,128)(2,1)S(1)} %get-tuple-element.51.hid_ref, bf16[384,768]{1,0:T(8,128)(2,1)S(1)} %get-tuple-element.53.dh_ref, ...), custom_call_target="tpu_custom_call" | custom-call | flops 3221225472 | bytes 8388608 | tf_op jit(solution)/shard_map/pallas_call | solution.py:31
  117.5 7.6 %all-to-all-start.2 = ((bf16[32,16,2176]{2,1,0:T(8,128)(2,1)}), bf16[32,16,2176]{2,1,0:T(8,128)(2,1)S(1)}, u32[]{:S(2)}, u32[]{:S(2)}) async-start(bf16[32,16,2176]{2,1,0:T(8,128)(2,1)} %bitcast.47), calls=%async_computation.2 | async-start | bytes 4456448 | tf_op jit(solution)/shard_map/all_to_all | solution.py:417
  125.2 5.1 %convolution_convert_fusion = bf16[2048,768]{1,0:T(8,128)(2,1)} fusion(bf16[384,2048]{1,0:T(8,128)(2,1)} %get-tuple-element.58, bf16[384,768]{1,0:T(8,128)(2,1)S(1)} %get-tuple-element.51.hid_ref), kind=kOutput, calls=%fused_computation | convolution fusion | flops 1209532416 | bytes 5308416 | tf_op jit(solution)/shard_map/dot_general | solution.py:27
  130.2 3.5 %convolution_convert_fusion.1 = bf16[2048,768]{1,0:T(8,128)(2,1)} fusion(bf16[384,2048]{1,0:T(8,128)(2,1)S(1)} %copy-done.6, bf16[2,384,768]{2,1,0:T(8,128)(2,1)S(1)} %copy-done.8), kind=kOutput, calls=%fused_computation.1 | convolution fusion | flops 1209532416 | bytes 5308416 | tf_op jit(solution)/shard_map/dot_general | solution.py:27
  133.8 3.5 %convolution_convert_fusion.2 = bf16[2048,768]{1,0:T(8,128)(2,1)} fusion(bf16[384,2048]{1,0:T(8,128)(2,1)S(1)} %copy-done.6, bf16[2,384,768]{2,1,0:T(8,128)(2,1)S(1)} %copy-done.8), kind=kOutput, calls=%fused_computation.2 | convolution fusion | flops 1209532416 | bytes 5308416 | tf_op jit(solution)/shard_map/dot_general | solution.py:27
  137.3 19.3 %all-to-all-done.2 = bf16[32,16,2176]{2,1,0:T(8,128)(2,1)S(1)} async-done(((bf16[32,16,2176]{2,1,0:T(8,128)(2,1)}), bf16[32,16,2176]{2,1,0:T(8,128)(2,1)S(1)}, u32[]{:S(2)}, u32[]{:S(2)}) %all-to-all-start.2) | async-done | bytes 2228256 | tf_op jit(solution)/shard_map/all_to_all | solution.py:417
  158.3 2.9 %collective-permute-start.10 = (bf16[16,2176]{1,0:T(8,128)(2,1)S(1)}, bf16[16,2176]{1,0:T(8,128)(2,1)S(1)}, u32[]{:S(2)}, u32[]{:S(2)}) collective-permute-start(bf16[16,2176]{1,0:T(8,128)(2,1)S(1)} %get-tuple-element.64), channel_id=1, source_target_pairs={{0,64},{32,96},{64,0},{96,32},{1,65},{33,97},{65,1},{97,33},{2,66}... | collective-permute-start | bytes 208904 | tf_op jit(solution)/shard_map/ppermute | solution.py:414
  164.2 2.5 %collective-permute-done.11.b3 = bf16[16,2176]{1,0:T(8,128)(2,1)S(1)} collective-permute-done((bf16[16,2176]{1,0:T(8,128)(2,1)S(1)}, bf16[16,2176]{1,0:T(8,128)(2,1)S(1)}, u32[]{:S(2)}, u32[]{:S(2)}) %collective-permute-start.11) | collective-permute-done | bytes 69664 | tf_op jit(solution)/shard_map/ppermute | solution.py:414
  (39 shorter events, 16.5 us)
Async XLA Ops:
  2.5 6.0 %collective-permute-start.1 = (bf16[16,2176]{1,0:T(8,128)(2,1)}, bf16[16,2176]{1,0:T(8,128)(2,1)S(1)}, u32[]{:S(2)}, u32[]{:S(2)}) collective-permute-start(bf16[16,2176]{1,0:T(8,128)(2,1)} %get-tuple-element.38.b0), channel_id=1, source_target_pairs={{0,64},{32,96},{64,0},{96,32},{1,65},{33,97},{65,1},{97,33},{2,66}... | collective-permute-start | bytes 208904 | tf_op jit(solution)/shard_map/ppermute | solution.py:414
  5.6 5.7 %collective-permute-start.2 = (bf16[16,2176]{1,0:T(8,128)(2,1)}, bf16[16,2176]{1,0:T(8,128)(2,1)S(1)}, u32[]{:S(2)}, u32[]{:S(2)}) collective-permute-start(bf16[16,2176]{1,0:T(8,128)(2,1)} %get-tuple-element.39), channel_id=1, source_target_pairs={{0,96},{32,64},{64,32},{96,0},{1,97},{33,65},{65,33},{97,1},{2,98}... | collective-permute-start | bytes 208904 | tf_op jit(solution)/shard_map/ppermute | solution.py:414
  6.8 4.6 %collective-permute-start = (bf16[16,2176]{1,0:T(8,128)(2,1)}, bf16[16,2176]{1,0:T(8,128)(2,1)S(1)}, u32[]{:S(2)}, u32[]{:S(2)}) collective-permute-start(bf16[16,2176]{1,0:T(8,128)(2,1)} %get-tuple-element.39), channel_id=1, source_target_pairs={{0,32},{32,0},{64,96},{96,64},{1,33},{33,1},{65,97},{97,65},{2,34}... | collective-permute-start | bytes 208904 | tf_op jit(solution)/shard_map/ppermute | solution.py:414
  11.4 0.9 copy-start.1
  14.6 8.6 %copy-start = (bf16[16,2048]{1,0:T(8,128)(2,1)S(1)}, bf16[16,2048]{1,0:T(8,128)(2,1)}, u32[]{:S(2)}) copy-start(bf16[16,2048]{1,0:T(8,128)(2,1)} %get-tuple-element.42.b0) | copy-start | bytes 196612
  14.6 10.2 %copy-start.7 = (bf16[16,2048]{1,0:T(8,128)(2,1)S(1)}, bf16[16,2048]{1,0:T(8,128)(2,1)}, u32[]{:S(2)}) copy-start(bf16[16,2048]{1,0:T(8,128)(2,1)} %get-tuple-element.43) | copy-start | bytes 196612
  14.6 40.2 %all-to-all-start = ((bf16[32,16,2176]{2,1,0:T(8,128)(2,1)}), bf16[32,16,2176]{2,1,0:T(8,128)(2,1)}, u32[]{:S(2)}, u32[]{:S(2)}) async-start(bf16[32,16,2176]{2,1,0:T(8,128)(2,1)} %bitcast.6), calls=%async_computation | async-start | bytes 4456448 | tf_op jit(solution)/shard_map/all_to_all | solution.py:417
  23.2 5.9 %collective-permute-start.4 = (bf16[16,2048]{1,0:T(8,128)(2,1)S(1)}, bf16[16,2048]{1,0:T(8,128)(2,1)S(1)}, u32[]{:S(2)}, u32[]{:S(2)}) collective-permute-start(bf16[16,2048]{1,0:T(8,128)(2,1)S(1)} %copy-done), channel_id=1, source_target_pairs={{0,64},{32,96},{64,0},{96,32},{1,65},{33,97},{65,1},{97,33},{2,66}... | collective-permute-start | bytes 196616 | tf_op jit(solution)/shard_map/ppermute | solution.py:414
  24.8 5.7 %collective-permute-start.5 = (bf16[16,2048]{1,0:T(8,128)(2,1)S(1)}, bf16[16,2048]{1,0:T(8,128)(2,1)S(1)}, u32[]{:S(2)}, u32[]{:S(2)}) collective-permute-start(bf16[16,2048]{1,0:T(8,128)(2,1)S(1)} %copy-done.7), channel_id=1, source_target_pairs={{0,96},{32,64},{64,32},{96,0},{1,97},{33,65},{65,33},{97,1},{2,98}... | collective-permute-start | bytes 196616 | tf_op jit(solution)/shard_map/ppermute | solution.py:414
  26.0 4.5 %collective-permute-start.3 = (bf16[16,2048]{1,0:T(8,128)(2,1)S(1)}, bf16[16,2048]{1,0:T(8,128)(2,1)S(1)}, u32[]{:S(2)}, u32[]{:S(2)}) collective-permute-start(bf16[16,2048]{1,0:T(8,128)(2,1)S(1)} %copy-done.7), channel_id=1, source_target_pairs={{0,32},{32,0},{64,96},{96,64},{1,33},{33,1},{65,97},{97,65},{2,34}... | collective-permute-start | bytes 196616 | tf_op jit(solution)/shard_map/ppermute | solution.py:414
  54.8 4.9 %copy-start.3 = (f32[16,1,6]{0,1,2:T(1,128)S(1)}, f32[16,1,6]{0,1,2:T(1,128)}, u32[]{:S(2)}) copy-start(f32[16,1,6]{0,1,2:T(1,128)} %param.24) | copy-start | bytes 1156
  54.8 4.9 %copy-start.4 = (f32[16,1,6]{0,1,2:T(1,128)S(1)}, f32[16,1,6]{0,1,2:T(1,128)}, u32[]{:S(2)}) copy-start(f32[16,1,6]{0,1,2:T(1,128)} %param.23) | copy-start | bytes 1156
  54.8 34.9 %all-to-all-start.1 = ((bf16[32,16,2048]{2,1,0:T(8,128)(2,1)}), bf16[32,16,2048]{2,1,0:T(8,128)(2,1)}, u32[]{:S(2)}, u32[]{:S(2)}) async-start(bf16[32,16,2048]{2,1,0:T(8,128)(2,1)} %bitcast.11), calls=%async_computation.1 | async-start | bytes 4194304 | tf_op jit(solution)/shard_map/all_to_all | solution.py:417
  59.7 6.6 %copy-start.5 = (f32[16,1,6]{0,1,2:T(1,128)S(1)}, f32[16,1,6]{0,1,2:T(1,128)}, u32[]{:S(2)}) copy-start(f32[16,1,6]{0,1,2:T(1,128)} %param.25) | copy-start | bytes 1156
  66.2 15.4 %collective-permute-start.6 = (bf16[384,768]{1,0:T(8,128)(2,1)S(1)}, bf16[384,768]{1,0:T(8,128)(2,1)S(1)}, u32[]{:S(2)}, u32[]{:S(2)}) collective-permute-start(bf16[384,768]{1,0:T(8,128)(2,1)S(1)} %get-tuple-element.45.a_ref), channel_id=1, source_target_pairs={{0,32},{32,0},{64,96},{96,64},{1,33},{33,1},{65,97},{97,65},{2,34}... | collective-permute-start | bytes 1769480 | tf_op jit(solution)/shard_map/ppermute | solution.py:414
  81.6 13.3 %copy-start.2 = (bf16[384,768]{1,0:T(8,128)(2,1)}, bf16[384,768]{1,0:T(8,128)(2,1)S(1)}, u32[]{:S(2)}) copy-start(bf16[384,768]{1,0:T(8,128)(2,1)S(1)} %collective-permute-done.6.a_in) | copy-start | bytes 1769476
  81.6 15.1 %collective-permute-start.7 = (bf16[384,768]{1,0:T(8,128)(2,1)S(1)}, bf16[384,768]{1,0:T(8,128)(2,1)}, u32[]{:S(2)}, u32[]{:S(2)}) collective-permute-start(bf16[384,768]{1,0:T(8,128)(2,1)S(1)} %get-tuple-element.48.b_ref), channel_id=1, source_target_pairs={{0,32},{32,0},{64,96},{96,64},{1,33},{33,1},{65,97},{97,65},{2,34}... | collective-permute-start | bytes 1769480 | tf_op jit(solution)/shard_map/ppermute | solution.py:414
  94.9 13.9 %collective-permute-start.8 = (bf16[384,768]{1,0:T(8,128)(2,1)S(1)}, bf16[384,768]{1,0:T(8,128)(2,1)S(1)}, u32[]{:S(2)}, u32[]{:S(2)}) collective-permute-start(bf16[384,768]{1,0:T(8,128)(2,1)S(1)} %get-tuple-element.53.dh_ref), channel_id=1, source_target_pairs={{0,32},{32,0},{64,96},{96,64},{1,33},{33,1},{65,97},{97,65},{2,34}... | collective-permute-start | bytes 1769480 | tf_op jit(solution)/shard_map/ppermute | solution.py:414
  117.5 39.0 %all-to-all-start.2 = ((bf16[32,16,2176]{2,1,0:T(8,128)(2,1)}), bf16[32,16,2176]{2,1,0:T(8,128)(2,1)S(1)}, u32[]{:S(2)}, u32[]{:S(2)}) async-start(bf16[32,16,2176]{2,1,0:T(8,128)(2,1)} %bitcast.47), calls=%async_computation.2 | async-start | bytes 4456448 | tf_op jit(solution)/shard_map/all_to_all | solution.py:417
  125.2 5.1 %copy-start.6 = (bf16[384,2048]{1,0:T(8,128)(2,1)S(1)}, bf16[384,2048]{1,0:T(8,128)(2,1)}, u32[]{:S(2)}) copy-start(bf16[384,2048]{1,0:T(8,128)(2,1)} %get-tuple-element.56) | copy-start | bytes 4718596
  125.2 5.1 %copy-start.8 = (bf16[2,384,768]{2,1,0:T(8,128)(2,1)S(1)}, bf16[2,384,768]{2,1,0:T(8,128)(2,1)}, u32[]{:S(2)}) copy-start(bf16[2,384,768]{2,1,0:T(8,128)(2,1)} %get-tuple-element.57) | copy-start | bytes 3538948
  157.6 4.8 %collective-permute-start.9 = (bf16[16,2176]{1,0:T(8,128)(2,1)S(1)}, bf16[16,2176]{1,0:T(8,128)(2,1)S(1)}, u32[]{:S(2)}, u32[]{:S(2)}) collective-permute-start(bf16[16,2176]{1,0:T(8,128)(2,1)S(1)} %get-tuple-element.63), channel_id=1, source_target_pairs={{0,32},{32,0},{64,96},{96,64},{1,33},{33,1},{65,97},{97,65},{2,34}... | collective-permute-start | bytes 208904 | tf_op jit(solution)/shard_map/ppermute | solution.py:414
  158.3 6.0 %collective-permute-start.10 = (bf16[16,2176]{1,0:T(8,128)(2,1)S(1)}, bf16[16,2176]{1,0:T(8,128)(2,1)S(1)}, u32[]{:S(2)}, u32[]{:S(2)}) collective-permute-start(bf16[16,2176]{1,0:T(8,128)(2,1)S(1)} %get-tuple-element.64), channel_id=1, source_target_pairs={{0,64},{32,96},{64,0},{96,32},{1,65},{33,97},{65,1},{97,33},{2,66}... | collective-permute-start | bytes 208904 | tf_op jit(solution)/shard_map/ppermute | solution.py:414
  161.2 5.5 %collective-permute-start.11 = (bf16[16,2176]{1,0:T(8,128)(2,1)S(1)}, bf16[16,2176]{1,0:T(8,128)(2,1)S(1)}, u32[]{:S(2)}, u32[]{:S(2)}) collective-permute-start(bf16[16,2176]{1,0:T(8,128)(2,1)S(1)} %get-tuple-element.65), channel_id=1, source_target_pairs={{0,96},{32,64},{64,32},{96,0},{1,97},{33,65},{65,33},{97,1},{2,98}... | collective-permute-start | bytes 208904 | tf_op jit(solution)/shard_map/ppermute | solution.py:414

commit v10 on v9

--- a/solution.py
+++ b/solution.py
@@ -505,7 +505,7 @@
         ],
     )
     their_dh = across(send_dh, 1)
-    chunk = 512
+    chunk = 1024
     parts = half // chunk
     factor, hid, both_w = call(
         functools.partial(factor_kernel, chunk),

time: 168 us -> 168 us (level)
  no operation moved by 1% of the time
where the time goes in v10:
time: 168 us; the launch traced here: 167 us
  waiting for transfers between devices  78.1 us (46%)
  Pallas kernels  41 us (24%)
  starting transfers between devices  34.2 us (20%)
  matrix products  12.1 us (7%)
    all_to_all x3, waiting for transfers between devices, spread(): lax.all_to_all(block, 'local', split_axis=0, concat_axis=0, tiled=True)  49.4 us
    pallas_call x10, Pallas kernels, call(): pl.pallas_call(kernel, out_shape=outs, compiler_params=pltpu.CompilerPara...  41 us
    ppermute x12, waiting for transfers between devices, across(): lax.ppermute(block, 'group', [(i, i ^ apart) for i in range(n_group)])  28.7 us
    all_to_all x3, starting transfers between devices, spread(): lax.all_to_all(block, 'local', split_axis=0, concat_axis=0, tiled=True)  21.1 us
    ppermute x12, starting transfers between devices, across(): lax.ppermute(block, 'group', [(i, i ^ apart) for i in range(n_group)])  13.1 us
    dot_general x3, matrix products, dot(): return lax.dot_general(left, right, dims, preferred_element_type=F32)  12.1 us
  transfers between devices with their start and end apart: 15, of which 12 were waited for; matrix products, arithmetic and copies ran while one was open for 7% of the time, Pallas kernels for 16%

profile of v10, /device:TPU:0, one launch (start us, length us, event | category | flops | bytes accessed | tf_op | source)
XLA Modules:
  0.0 167.1 jit_solution(1976825294392498462)
XLA Ops:
  0.6 1.9 %shard_map.164 = (bf16[16,2176]{1,0:T(8,128)(2,1)}, bf16[16,2176]{1,0:T(8,128)(2,1)}, bf16[16,2048]{1,0:T(8,128)(2,1)}, bf16[16,2048]{1,0:T(8,128)(2,1)}) custom-call(bf16[16,4096]{1,0:T(8,128)(2,1)} %xq_ref.1, f32[16,32]{1,0:T(8,128)} %xs_ref.1, bf16[16,4096]{1,0:T(8,128)(2,1)} %dy_ref.1, s32[8,16]{1,0:T(8,128)} %bitcast.48, s32[8,16]{1,0:T(8,128)} %bitcast.49, ...), custom_call_target="tpu_custom_call" | custom-call | bytes 524288 | tf_op jit(solution)/shard_map/pallas_call | solution.py:31
  2.5 3.1 %collective-permute-start.1 = (bf16[16,2176]{1,0:T(8,128)(2,1)}, bf16[16,2176]{1,0:T(8,128)(2,1)S(1)}, u32[]{:S(2)}, u32[]{:S(2)}) collective-permute-start(bf16[16,2176]{1,0:T(8,128)(2,1)} %get-tuple-element.38.b0), channel_id=1, source_target_pairs={{0,64},{32,96},{64,0},{96,32},{1,65},{33,97},{65,1},{97,33},{2,66}... | collective-permute-start | bytes 208904 | tf_op jit(solution)/shard_map/ppermute | solution.py:414
  8.5 2.8 %collective-permute-done.2.b3 = bf16[16,2176]{1,0:T(8,128)(2,1)S(1)} collective-permute-done((bf16[16,2176]{1,0:T(8,128)(2,1)}, bf16[16,2176]{1,0:T(8,128)(2,1)S(1)}, u32[]{:S(2)}, u32[]{:S(2)}) %collective-permute-start.2) | collective-permute-done | bytes 69664 | tf_op jit(solution)/shard_map/ppermute | solution.py:414
  12.2 2.3 %shard_map.165 = (bf16[512,2176]{1,0:T(8,128)(2,1)}, bf16[512,64]{1,0:T(8,128)(2,1)S(1)}, bf16[512,64]{1,0:T(8,128)(2,1)S(1)}, bf16[64,128]{1,0:T(8,128)(2,1)S(1)}) custom-call(bf16[16,2176]{1,0:T(8,128)(2,1)S(1)} %copy-done.1, bf16[16,2176]{1,0:T(8,128)(2,1)S(1)} %collective-permute-done.b1, bf16[16,2176]{1,0:T(8,128)(2,1)S(1)} %collective-permute-done.1.b2, ...), custom_call_target="tpu_custom_call" | custom-call | flops 142606336 | bytes 2228224 | tf_op jit(solution)/shard_map/pallas_call | solution.py:31
  14.6 8.6 %all-to-all-start = ((bf16[32,16,2176]{2,1,0:T(8,128)(2,1)}), bf16[32,16,2176]{2,1,0:T(8,128)(2,1)}, u32[]{:S(2)}, u32[]{:S(2)}) async-start(bf16[32,16,2176]{2,1,0:T(8,128)(2,1)} %bitcast.6), calls=%async_computation | async-start | bytes 4456448 | tf_op jit(solution)/shard_map/all_to_all | solution.py:417
  26.8 2.3 %collective-permute-done.4.b2 = bf16[16,2048]{1,0:T(8,128)(2,1)S(1)} collective-permute-done((bf16[16,2048]{1,0:T(8,128)(2,1)S(1)}, bf16[16,2048]{1,0:T(8,128)(2,1)S(1)}, u32[]{:S(2)}, u32[]{:S(2)}) %collective-permute-start.4) | collective-permute-done | bytes 65568 | tf_op jit(solution)/shard_map/ppermute | solution.py:414
  30.5 1.9 %shard_map.166 = bf16[512,2048]{1,0:T(8,128)(2,1)} custom-call(bf16[512,64]{1,0:T(8,128)(2,1)S(1)} %get-tuple-element.41.gated_ref, bf16[16,2048]{1,0:T(8,128)(2,1)S(1)} %copy-done, bf16[16,2048]{1,0:T(8,128)(2,1)S(1)} %collective-permute-done.3.b1, bf16[16,2048]{1,0:T(8,128)(2,1)S(1)} %collective-permute-done.4.b2, ...), custom_call_target="tpu_custom_call" | custom-call | flops 134217728 | bytes 2097152 | tf_op jit(solution)/shard_map/pallas_call | solution.py:31
  32.4 22.3 %all-to-all-done = bf16[32,16,2176]{2,1,0:T(8,128)(2,1)} async-done(((bf16[32,16,2176]{2,1,0:T(8,128)(2,1)}), bf16[32,16,2176]{2,1,0:T(8,128)(2,1)}, u32[]{:S(2)}, u32[]{:S(2)}) %all-to-all-start) | async-done | bytes 2228256 | tf_op jit(solution)/shard_map/all_to_all | solution.py:417
  54.8 4.9 %all-to-all-start.1 = ((bf16[32,16,2048]{2,1,0:T(8,128)(2,1)}), bf16[32,16,2048]{2,1,0:T(8,128)(2,1)}, u32[]{:S(2)}, u32[]{:S(2)}) async-start(bf16[32,16,2048]{2,1,0:T(8,128)(2,1)} %bitcast.11), calls=%async_computation.1 | async-start | bytes 4194304 | tf_op jit(solution)/shard_map/all_to_all | solution.py:417
  59.7 6.5 %shard_map.167 = (bf16[384,768]{1,0:T(8,128)(2,1)S(1)}, bf16[384,512]{1,0:T(8,128)(2,1)S(1)}) custom-call(f32[6,16]{1,0:T(8,128)S(1)} %get-tuple-element.72.sg_ref, bf16[512,2176]{1,0:T(8,128)(2,1)} %bitcast.7.x_hbm.dy_hbm, bf16[2048,768]{1,0:T(8,128)(2,1)} %bitcast.42), custom_call_target="tpu_custom_call" | custom-call | flops 1207959552 | bytes 7340032 | tf_op jit(solution)/shard_map/pallas_call | solution.py:31
  66.3 5.2 %shard_map.168 = (bf16[384,2048]{1,0:T(8,128)(2,1)}, bf16[384,768]{1,0:T(8,128)(2,1)S(1)}) custom-call(f32[6,16]{1,0:T(8,128)S(1)} %get-tuple-element.71.sv_ref.su_ref, bf16[384,512]{1,0:T(8,128)(2,1)S(1)} %get-tuple-element.46.slot_ref, bf16[512,2176]{1,0:T(8,128)(2,1)} %bitcast.7.x_hbm.dy_hbm, bf16[2048,768]{1,0:T(8,128)(2,1)} %bitcast.44), custom_call_target="tpu_custom_call" | custom-call | flops 1207959552 | bytes 7340032 | tf_op jit(solution)/shard_map/pallas_call | solution.py:31
  71.5 10.1 %collective-permute-done.6.a_in = bf16[384,768]{1,0:T(8,128)(2,1)S(1)} collective-permute-done((bf16[384,768]{1,0:T(8,128)(2,1)S(1)}, bf16[384,768]{1,0:T(8,128)(2,1)S(1)}, u32[]{:S(2)}, u32[]{:S(2)}) %collective-permute-start.6) | collective-permute-done | bytes 589856 | tf_op jit(solution)/shard_map/ppermute | solution.py:414
  81.9 7.8 %all-to-all-done.1 = bf16[32,16,2048]{2,1,0:T(8,128)(2,1)} async-done(((bf16[32,16,2048]{2,1,0:T(8,128)(2,1)}), bf16[32,16,2048]{2,1,0:T(8,128)(2,1)}, u32[]{:S(2)}, u32[]{:S(2)}) %all-to-all-start.1) | async-done | bytes 2097184 | tf_op jit(solution)/shard_map/all_to_all | solution.py:417
  89.6 5.2 %shard_map.170 = (bf16[384,2048]{1,0:T(8,128)(2,1)}, bf16[384,768]{1,0:T(8,128)(2,1)S(1)}) custom-call(f32[6,16]{1,0:T(8,128)S(1)} %bitcast.41, bf16[384,512]{1,0:T(8,128)(2,1)S(1)} %get-tuple-element.46.slot_ref, bf16[512,2048]{1,0:T(8,128)(2,1)} %bitcast.12.dy_hbm, bf16[2048,768]{1,0:T(8,128)(2,1)} %bitcast.46), custom_call_target="tpu_custom_call" | custom-call | flops 1207959552 | bytes 7340032 | tf_op jit(solution)/shard_map/pallas_call | solution.py:31
  96.7 7.7 %shard_map.169 = (bf16[2,384,768]{2,1,0:T(8,128)(2,1)}, bf16[384,768]{1,0:T(8,128)(2,1)S(1)}, bf16[2048,1536]{1,0:T(8,128)(2,1)}) custom-call(f32[6,16]{1,0:T(8,128)S(1)} %get-tuple-element.72.sg_ref, f32[6,16]{1,0:T(8,128)S(1)} %get-tuple-element.71.sv_ref.su_ref, bf16[384,768]{1,0:T(8,128)(2,1)S(1)} %get-tuple-element.45.a_ref, ...), custom_call_target="tpu_custom_call" | custom-call | flops 4718592 | bytes 12582912 | tf_op jit(solution)/shard_map/pallas_call | solution.py:31
  104.4 4.4 %collective-permute-done.8.dh_in = bf16[384,768]{1,0:T(8,128)(2,1)S(1)} collective-permute-done((bf16[384,768]{1,0:T(8,128)(2,1)S(1)}, bf16[384,768]{1,0:T(8,128)(2,1)S(1)}, u32[]{:S(2)}, u32[]{:S(2)}) %collective-permute-start.8) | collective-permute-done | bytes 589856 | tf_op jit(solution)/shard_map/ppermute | solution.py:414
  108.8 8.4 %shard_map.171 = (bf16[2,384,768]{2,1,0:T(8,128)(2,1)}, bf16[512,2176]{1,0:T(8,128)(2,1)}) custom-call(bf16[2,384,768]{2,1,0:T(8,128)(2,1)} %get-tuple-element.50.factor_ref, bf16[384,768]{1,0:T(8,128)(2,1)S(1)} %get-tuple-element.51.hid_ref, bf16[384,768]{1,0:T(8,128)(2,1)S(1)} %get-tuple-element.53.dh_ref, ...), custom_call_target="tpu_custom_call" | custom-call | flops 3221225472 | bytes 8388608 | tf_op jit(solution)/shard_map/pallas_call | solution.py:31
  117.2 7.6 %all-to-all-start.2 = ((bf16[32,16,2176]{2,1,0:T(8,128)(2,1)}), bf16[32,16,2176]{2,1,0:T(8,128)(2,1)S(1)}, u32[]{:S(2)}, u32[]{:S(2)}) async-start(bf16[32,16,2176]{2,1,0:T(8,128)(2,1)} %bitcast.47), calls=%async_computation.2 | async-start | bytes 4456448 | tf_op jit(solution)/shard_map/all_to_all | solution.py:417
  124.9 5.1 %convolution_convert_fusion = bf16[2048,768]{1,0:T(8,128)(2,1)} fusion(bf16[384,2048]{1,0:T(8,128)(2,1)} %get-tuple-element.58, bf16[384,768]{1,0:T(8,128)(2,1)S(1)} %get-tuple-element.51.hid_ref), kind=kOutput, calls=%fused_computation | convolution fusion | flops 1209532416 | bytes 5308416 | tf_op jit(solution)/shard_map/dot_general | solution.py:27
  130.0 3.5 %convolution_convert_fusion.1 = bf16[2048,768]{1,0:T(8,128)(2,1)} fusion(bf16[384,2048]{1,0:T(8,128)(2,1)S(1)} %copy-done.6, bf16[2,384,768]{2,1,0:T(8,128)(2,1)S(1)} %copy-done.8), kind=kOutput, calls=%fused_computation.1 | convolution fusion | flops 1209532416 | bytes 5308416 | tf_op jit(solution)/shard_map/dot_general | solution.py:27
  133.5 3.5 %convolution_convert_fusion.2 = bf16[2048,768]{1,0:T(8,128)(2,1)} fusion(bf16[384,2048]{1,0:T(8,128)(2,1)S(1)} %copy-done.6, bf16[2,384,768]{2,1,0:T(8,128)(2,1)S(1)} %copy-done.8), kind=kOutput, calls=%fused_computation.2 | convolution fusion | flops 1209532416 | bytes 5308416 | tf_op jit(solution)/shard_map/dot_general | solution.py:27
  137.0 19.3 %all-to-all-done.2 = bf16[32,16,2176]{2,1,0:T(8,128)(2,1)S(1)} async-done(((bf16[32,16,2176]{2,1,0:T(8,128)(2,1)}), bf16[32,16,2176]{2,1,0:T(8,128)(2,1)S(1)}, u32[]{:S(2)}, u32[]{:S(2)}) %all-to-all-start.2) | async-done | bytes 2228256 | tf_op jit(solution)/shard_map/all_to_all | solution.py:417
  158.0 2.9 %collective-permute-start.10 = (bf16[16,2176]{1,0:T(8,128)(2,1)S(1)}, bf16[16,2176]{1,0:T(8,128)(2,1)S(1)}, u32[]{:S(2)}, u32[]{:S(2)}) collective-permute-start(bf16[16,2176]{1,0:T(8,128)(2,1)S(1)} %get-tuple-element.64), channel_id=1, source_target_pairs={{0,64},{32,96},{64,0},{96,32},{1,65},{33,97},{65,1},{97,33},{2,66}... | collective-permute-start | bytes 208904 | tf_op jit(solution)/shard_map/ppermute | solution.py:414
  163.9 2.5 %collective-permute-done.11.b3 = bf16[16,2176]{1,0:T(8,128)(2,1)S(1)} collective-permute-done((bf16[16,2176]{1,0:T(8,128)(2,1)S(1)}, bf16[16,2176]{1,0:T(8,128)(2,1)S(1)}, u32[]{:S(2)}, u32[]{:S(2)}) %collective-permute-start.11) | collective-permute-done | bytes 69664 | tf_op jit(solution)/shard_map/ppermute | solution.py:414
  (39 shorter events, 16.5 us)
Async XLA Ops:
  2.5 6.0 %collective-permute-start.1 = (bf16[16,2176]{1,0:T(8,128)(2,1)}, bf16[16,2176]{1,0:T(8,128)(2,1)S(1)}, u32[]{:S(2)}, u32[]{:S(2)}) collective-permute-start(bf16[16,2176]{1,0:T(8,128)(2,1)} %get-tuple-element.38.b0), channel_id=1, source_target_pairs={{0,64},{32,96},{64,0},{96,32},{1,65},{33,97},{65,1},{97,33},{2,66}... | collective-permute-start | bytes 208904 | tf_op jit(solution)/shard_map/ppermute | solution.py:414
  5.6 5.7 %collective-permute-start.2 = (bf16[16,2176]{1,0:T(8,128)(2,1)}, bf16[16,2176]{1,0:T(8,128)(2,1)S(1)}, u32[]{:S(2)}, u32[]{:S(2)}) collective-permute-start(bf16[16,2176]{1,0:T(8,128)(2,1)} %get-tuple-element.39), channel_id=1, source_target_pairs={{0,96},{32,64},{64,32},{96,0},{1,97},{33,65},{65,33},{97,1},{2,98}... | collective-permute-start | bytes 208904 | tf_op jit(solution)/shard_map/ppermute | solution.py:414
  6.8 4.6 %collective-permute-start = (bf16[16,2176]{1,0:T(8,128)(2,1)}, bf16[16,2176]{1,0:T(8,128)(2,1)S(1)}, u32[]{:S(2)}, u32[]{:S(2)}) collective-permute-start(bf16[16,2176]{1,0:T(8,128)(2,1)} %get-tuple-element.39), channel_id=1, source_target_pairs={{0,32},{32,0},{64,96},{96,64},{1,33},{33,1},{65,97},{97,65},{2,34}... | collective-permute-start | bytes 208904 | tf_op jit(solution)/shard_map/ppermute | solution.py:414
  11.4 0.9 copy-start.1
  14.6 8.6 %copy-start = (bf16[16,2048]{1,0:T(8,128)(2,1)S(1)}, bf16[16,2048]{1,0:T(8,128)(2,1)}, u32[]{:S(2)}) copy-start(bf16[16,2048]{1,0:T(8,128)(2,1)} %get-tuple-element.42.b0) | copy-start | bytes 196612
  14.6 10.2 %copy-start.7 = (bf16[16,2048]{1,0:T(8,128)(2,1)S(1)}, bf16[16,2048]{1,0:T(8,128)(2,1)}, u32[]{:S(2)}) copy-start(bf16[16,2048]{1,0:T(8,128)(2,1)} %get-tuple-element.43) | copy-start | bytes 196612
  14.6 40.2 %all-to-all-start = ((bf16[32,16,2176]{2,1,0:T(8,128)(2,1)}), bf16[32,16,2176]{2,1,0:T(8,128)(2,1)}, u32[]{:S(2)}, u32[]{:S(2)}) async-start(bf16[32,16,2176]{2,1,0:T(8,128)(2,1)} %bitcast.6), calls=%async_computation | async-start | bytes 4456448 | tf_op jit(solution)/shard_map/all_to_all | solution.py:417
  23.2 5.9 %collective-permute-start.4 = (bf16[16,2048]{1,0:T(8,128)(2,1)S(1)}, bf16[16,2048]{1,0:T(8,128)(2,1)S(1)}, u32[]{:S(2)}, u32[]{:S(2)}) collective-permute-start(bf16[16,2048]{1,0:T(8,128)(2,1)S(1)} %copy-done), channel_id=1, source_target_pairs={{0,64},{32,96},{64,0},{96,32},{1,65},{33,97},{65,1},{97,33},{2,66}... | collective-permute-start | bytes 196616 | tf_op jit(solution)/shard_map/ppermute | solution.py:414
  24.8 5.7 %collective-permute-start.5 = (bf16[16,2048]{1,0:T(8,128)(2,1)S(1)}, bf16[16,2048]{1,0:T(8,128)(2,1)S(1)}, u32[]{:S(2)}, u32[]{:S(2)}) collective-permute-start(bf16[16,2048]{1,0:T(8,128)(2,1)S(1)} %copy-done.7), channel_id=1, source_target_pairs={{0,96},{32,64},{64,32},{96,0},{1,97},{33,65},{65,33},{97,1},{2,98}... | collective-permute-start | bytes 196616 | tf_op jit(solution)/shard_map/ppermute | solution.py:414
  26.0 4.5 %collective-permute-start.3 = (bf16[16,2048]{1,0:T(8,128)(2,1)S(1)}, bf16[16,2048]{1,0:T(8,128)(2,1)S(1)}, u32[]{:S(2)}, u32[]{:S(2)}) collective-permute-start(bf16[16,2048]{1,0:T(8,128)(2,1)S(1)} %copy-done.7), channel_id=1, source_target_pairs={{0,32},{32,0},{64,96},{96,64},{1,33},{33,1},{65,97},{97,65},{2,34}... | collective-permute-start | bytes 196616 | tf_op jit(solution)/shard_map/ppermute | solution.py:414
  54.8 4.9 %copy-start.3 = (f32[16,1,6]{0,1,2:T(1,128)S(1)}, f32[16,1,6]{0,1,2:T(1,128)}, u32[]{:S(2)}) copy-start(f32[16,1,6]{0,1,2:T(1,128)} %param.24) | copy-start | bytes 1156
  54.8 4.9 %copy-start.4 = (f32[16,1,6]{0,1,2:T(1,128)S(1)}, f32[16,1,6]{0,1,2:T(1,128)}, u32[]{:S(2)}) copy-start(f32[16,1,6]{0,1,2:T(1,128)} %param.23) | copy-start | bytes 1156
  54.8 34.9 %all-to-all-start.1 = ((bf16[32,16,2048]{2,1,0:T(8,128)(2,1)}), bf16[32,16,2048]{2,1,0:T(8,128)(2,1)}, u32[]{:S(2)}, u32[]{:S(2)}) async-start(bf16[32,16,2048]{2,1,0:T(8,128)(2,1)} %bitcast.11), calls=%async_computation.1 | async-start | bytes 4194304 | tf_op jit(solution)/shard_map/all_to_all | solution.py:417
  59.7 6.6 %copy-start.5 = (f32[16,1,6]{0,1,2:T(1,128)S(1)}, f32[16,1,6]{0,1,2:T(1,128)}, u32[]{:S(2)}) copy-start(f32[16,1,6]{0,1,2:T(1,128)} %param.25) | copy-start | bytes 1156
  66.2 15.4 %collective-permute-start.6 = (bf16[384,768]{1,0:T(8,128)(2,1)S(1)}, bf16[384,768]{1,0:T(8,128)(2,1)S(1)}, u32[]{:S(2)}, u32[]{:S(2)}) collective-permute-start(bf16[384,768]{1,0:T(8,128)(2,1)S(1)} %get-tuple-element.45.a_ref), channel_id=1, source_target_pairs={{0,32},{32,0},{64,96},{96,64},{1,33},{33,1},{65,97},{97,65},{2,34}... | collective-permute-start | bytes 1769480 | tf_op jit(solution)/shard_map/ppermute | solution.py:414
  81.6 13.3 %copy-start.2 = (bf16[384,768]{1,0:T(8,128)(2,1)}, bf16[384,768]{1,0:T(8,128)(2,1)S(1)}, u32[]{:S(2)}) copy-start(bf16[384,768]{1,0:T(8,128)(2,1)S(1)} %collective-permute-done.6.a_in) | copy-start | bytes 1769476
  81.6 15.1 %collective-permute-start.7 = (bf16[384,768]{1,0:T(8,128)(2,1)S(1)}, bf16[384,768]{1,0:T(8,128)(2,1)}, u32[]{:S(2)}, u32[]{:S(2)}) collective-permute-start(bf16[384,768]{1,0:T(8,128)(2,1)S(1)} %get-tuple-element.48.b_ref), channel_id=1, source_target_pairs={{0,32},{32,0},{64,96},{96,64},{1,33},{33,1},{65,97},{97,65},{2,34}... | collective-permute-start | bytes 1769480 | tf_op jit(solution)/shard_map/ppermute | solution.py:414
  94.9 13.9 %collective-permute-start.8 = (bf16[384,768]{1,0:T(8,128)(2,1)S(1)}, bf16[384,768]{1,0:T(8,128)(2,1)S(1)}, u32[]{:S(2)}, u32[]{:S(2)}) collective-permute-start(bf16[384,768]{1,0:T(8,128)(2,1)S(1)} %get-tuple-element.53.dh_ref), channel_id=1, source_target_pairs={{0,32},{32,0},{64,96},{96,64},{1,33},{33,1},{65,97},{97,65},{2,34}... | collective-permute-start | bytes 1769480 | tf_op jit(solution)/shard_map/ppermute | solution.py:414
  117.2 39.0 %all-to-all-start.2 = ((bf16[32,16,2176]{2,1,0:T(8,128)(2,1)}), bf16[32,16,2176]{2,1,0:T(8,128)(2,1)S(1)}, u32[]{:S(2)}, u32[]{:S(2)}) async-start(bf16[32,16,2176]{2,1,0:T(8,128)(2,1)} %bitcast.47), calls=%async_computation.2 | async-start | bytes 4456448 | tf_op jit(solution)/shard_map/all_to_all | solution.py:417
  124.9 5.1 %copy-start.6 = (bf16[384,2048]{1,0:T(8,128)(2,1)S(1)}, bf16[384,2048]{1,0:T(8,128)(2,1)}, u32[]{:S(2)}) copy-start(bf16[384,2048]{1,0:T(8,128)(2,1)} %get-tuple-element.56) | copy-start | bytes 4718596
  124.9 5.1 %copy-start.8 = (bf16[2,384,768]{2,1,0:T(8,128)(2,1)S(1)}, bf16[2,384,768]{2,1,0:T(8,128)(2,1)}, u32[]{:S(2)}) copy-start(bf16[2,384,768]{2,1,0:T(8,128)(2,1)} %get-tuple-element.57) | copy-start | bytes 3538948
  157.3 4.8 %collective-permute-start.9 = (bf16[16,2176]{1,0:T(8,128)(2,1)S(1)}, bf16[16,2176]{1,0:T(8,128)(2,1)S(1)}, u32[]{:S(2)}, u32[]{:S(2)}) collective-permute-start(bf16[16,2176]{1,0:T(8,128)(2,1)S(1)} %get-tuple-element.63), channel_id=1, source_target_pairs={{0,32},{32,0},{64,96},{96,64},{1,33},{33,1},{65,97},{97,65},{2,34}... | collective-permute-start | bytes 208904 | tf_op jit(solution)/shard_map/ppermute | solution.py:414
  158.0 6.0 %collective-permute-start.10 = (bf16[16,2176]{1,0:T(8,128)(2,1)S(1)}, bf16[16,2176]{1,0:T(8,128)(2,1)S(1)}, u32[]{:S(2)}, u32[]{:S(2)}) collective-permute-start(bf16[16,2176]{1,0:T(8,128)(2,1)S(1)} %get-tuple-element.64), channel_id=1, source_target_pairs={{0,64},{32,96},{64,0},{96,32},{1,65},{33,97},{65,1},{97,33},{2,66}... | collective-permute-start | bytes 208904 | tf_op jit(solution)/shard_map/ppermute | solution.py:414
  160.9 5.5 %collective-permute-start.11 = (bf16[16,2176]{1,0:T(8,128)(2,1)S(1)}, bf16[16,2176]{1,0:T(8,128)(2,1)S(1)}, u32[]{:S(2)}, u32[]{:S(2)}) collective-permute-start(bf16[16,2176]{1,0:T(8,128)(2,1)S(1)} %get-tuple-element.65), channel_id=1, source_target_pairs={{0,96},{32,64},{64,32},{96,0},{1,97},{33,65},{65,33},{97,1},{2,98}... | collective-permute-start | bytes 208904 | tf_op jit(solution)/shard_map/ppermute | solution.py:414
